TPU v7x, 32 devices: a whole 2x2x4 slice. The times are simulated.
32 devices in a mesh: groups: 2 (over y), scanx: 4 (over z), scany: 2 (over x), pos: 2 (over core).
Axes of the slice: x: 2, y: 2, z: 4, core: 2. Of those that a mesh axis runs over, the one named last changes fastest.
Arguments:
- specimen: float32 [2, 2048, 512], P(None, ('groups', 'scanx'), 'scany'), parts along dimension 1, may hold values from -5 to 5
- probe_wave: float32 [2, 512, 256], P(None, 'groups'), parts along dimension 1, may hold values from -6 to 6
- amplitudes: bfloat16 [64, 256, 256], P(('groups', 'scanx', 'scany', 'pos')), parts along dimension 0, may hold values from 0 to 2
- offsets: int32 [64, 2], P(('groups', 'scanx', 'scany', 'pos')), parts along dimension 0, may hold values from 0 to 255
Outputs:
- new_specimen: float32 [2, 2048, 512], P(None, ('groups', 'scanx'), 'scany'), parts along dimension 1
- new_probe: float32 [2, 512, 256], P(None, 'groups'), parts along dimension 1
There are 2 independent parts, one for each index of `groups`. A program takes and returns all parts, laid end to end along the dimension named above; each array names one. Nothing has to cross between parts.
Inputs may be any that keep to these rules, and one draw needn't show every extreme that they name: offsets are pixels from the top-left corner of the position's tile.
All inputs are finite; a program needn't handle non-finite values.
Results may differ from a plain program's by a relative error of at most 0.002.
The roundings to bfloat16 on the way count: a program that leaves them out, or rounds other values in their place, can miss the bound.
Values sent between devices are 32-bit elements; how exact they have to be, the bound alone decides.
No kernel may reach another device: no remote copies, remote signals or barrier semaphores. Data moves between devices by JAX's collectives and lax.ppermute only.
A program may use at most 64 MiB of HBM per device.

v0:
```python
import math

import jax
import jax.numpy as jnp
from jax import lax
from jax.sharding import PartitionSpec as P


def padded_2(block, sides, width):
    for axis, dim in sides:
        count = lax.axis_size(axis)
        forward = [(i, i + 1) for i in range(count - 1)]
        backward = [(target, source) for source, target in forward]
        low = lax.ppermute(
            lax.slice_in_dim(block, block.shape[dim] - width, None, axis=dim), axis, forward
        )
        high = lax.ppermute(lax.slice_in_dim(block, 0, width, axis=dim), axis, backward)
        block = jnp.concatenate([low, block, high], axis=dim)
    return block


def dft_tables(length):
    positions_index = jnp.arange(length, dtype=jnp.int32)
    phase_index = positions_index[:, None] * positions_index[None, :] % length
    angle_rad = phase_index.astype(jnp.float32) * (2.0 * math.pi / length)
    scale_factor = 1.0 / math.sqrt(length)
    cosine = (jnp.cos(angle_rad) * scale_factor).astype(jnp.bfloat16)
    sine_part = (jnp.sin(angle_rad) * scale_factor).astype(jnp.bfloat16)
    forward_left = jnp.stack(
        [jnp.stack([cosine, sine_part], 1), jnp.stack([-sine_part, cosine], 1)], 0
    )
    forward_right = jnp.stack(
        [jnp.stack([cosine, -sine_part], 1), jnp.stack([sine_part, cosine], 1)], 0
    )
    inverse_left = jnp.stack(
        [jnp.stack([cosine, -sine_part], 1), jnp.stack([sine_part, cosine], 1)], 0
    )
    inverse_right = jnp.stack(
        [jnp.stack([cosine, sine_part], 1), jnp.stack([-sine_part, cosine], 1)], 0
    )
    return (forward_left, forward_right, inverse_left, inverse_right)


def project_exit(patch_wave, probe_real, probe_imag, amplitude, tables):
    forward_left, forward_right, inverse_left, inverse_right = tables
    patch_real = patch_wave[0]
    patch_imag = patch_wave[1]
    exit_real = probe_real * patch_real - probe_imag * patch_imag
    exit_imag = probe_real * patch_imag + probe_imag * patch_real
    exit_wave = jnp.stack([exit_real, exit_imag]).astype(jnp.bfloat16)
    half_done = jnp.einsum(
        "akbr,brv->akv", forward_left, exit_wave, preferred_element_type=jnp.float32
    ).astype(jnp.bfloat16)
    far_field = jnp.einsum(
        "bkv,bval->akl", half_done, forward_right, preferred_element_type=jnp.float32
    )
    magnitude = jnp.sqrt(far_field[0] * far_field[0] + far_field[1] * far_field[1])
    scale_ratio = amplitude.astype(jnp.float32) / jnp.maximum(magnitude, 0.2)
    projected = (far_field * scale_ratio[None]).astype(jnp.bfloat16)
    back_half = jnp.einsum(
        "akbr,brv->akv", inverse_left, projected, preferred_element_type=jnp.float32
    ).astype(jnp.bfloat16)
    back_wave = jnp.einsum(
        "bkv,bval->akl", back_half, inverse_right, preferred_element_type=jnp.float32
    )
    return (back_wave[0] - exit_real, back_wave[1] - exit_imag, patch_real, patch_imag)


def fold_margin(field_in, axis_dim, margin, tile_len):
    extent = field_in.shape[axis_dim]
    inner_part = lax.slice_in_dim(field_in, 2 * margin, 2 * margin + tile_len, axis=axis_dim)
    lower_rim = lax.slice_in_dim(field_in, 0, margin, axis=axis_dim)
    upper_rim = lax.slice_in_dim(field_in, extent - margin, extent, axis=axis_dim)
    lower_widths = [(0, 0)] * field_in.ndim
    upper_widths = [(0, 0)] * field_in.ndim
    lower_widths[axis_dim] = (0, tile_len - margin)
    upper_widths[axis_dim] = (tile_len - margin, 0)
    return inner_part + jnp.pad(lower_rim, lower_widths) + jnp.pad(upper_rim, upper_widths)


def shards(specimen, probe_wave, amplitudes, offsets):
    pattern = probe_wave.shape[1]
    margin = pattern // 2
    tile_len = specimen.shape[1]
    tables = dft_tables(pattern)
    padded = padded_2(specimen, (("scanx", 1), ("scany", 2)), margin)
    probe_real = probe_wave[0]
    probe_imag = probe_wave[1]
    probe_power = probe_real * probe_real + probe_imag * probe_imag
    zero_index = jnp.zeros((), jnp.int32)

    def visit_position(carried, inputs):
        object_grad, probe_grad = carried
        amplitude, offset = inputs
        row_start = offset[0]
        col_start = offset[1]
        patch_wave = lax.dynamic_slice(
            padded, (zero_index, row_start, col_start), (2, pattern, pattern)
        )
        diff_real, diff_imag, patch_real, patch_imag = project_exit(
            patch_wave, probe_real, probe_imag, amplitude, tables
        )
        object_term = jnp.stack(
            [
                probe_real * diff_real + probe_imag * diff_imag,
                probe_real * diff_imag - probe_imag * diff_real,
                probe_power,
            ]
        )
        current = lax.dynamic_slice(
            object_grad, (zero_index, row_start, col_start), (3, pattern, pattern)
        )
        object_grad = lax.dynamic_update_slice(
            object_grad, current + object_term, (zero_index, row_start, col_start)
        )
        probe_term = jnp.stack(
            [
                patch_real * diff_real + patch_imag * diff_imag,
                patch_real * diff_imag - patch_imag * diff_real,
            ]
        )
        return ((object_grad, probe_grad + probe_term), None)

    start_grad = jnp.zeros((3, tile_len + pattern, tile_len + pattern), jnp.float32)
    start_probe = jnp.zeros((2, pattern, pattern), jnp.float32)
    (object_grad, probe_grad), unused = lax.scan(
        visit_position, (start_grad, start_probe), (amplitudes, offsets)
    )
    row_halo = padded_2(object_grad, (("scanx", 1),), margin)
    row_folded = fold_margin(row_halo, 1, margin, tile_len)
    col_halo = padded_2(row_folded, (("scany", 2),), margin)
    core_sum = fold_margin(col_halo, 2, margin, tile_len)
    core_sum = lax.psum(core_sum, "pos")
    new_specimen = specimen + core_sum[0:2] / (core_sum[2:3] + 1.0)
    devices_count = lax.axis_size("scanx") * lax.axis_size("scany") * lax.axis_size("pos")
    step_size = 1.0 / math.sqrt(offsets.shape[0] * devices_count)
    total_grad = lax.psum(probe_grad, ("scanx", "scany", "pos"))
    new_probe = probe_wave + total_grad * step_size
    return (new_specimen, new_probe)


def solution(mesh):
    placed = (
        P(None, ("groups", "scanx"), "scany"),
        P(None, "groups", None),
        P(("groups", "scanx", "scany", "pos"), None, None),
        P(("groups", "scanx", "scany", "pos"), None),
    )
    return jax.shard_map(
        shards,
        mesh=mesh,
        in_specs=placed,
        out_specs=(P(None, ("groups", "scanx"), "scany"), P(None, "groups", None)),
        check_vma=False,
    )
```

profile of v0, /device:TPU:0, one launch (start us, length us, event | category | flops | bytes accessed | tf_op | source)
XLA Modules:
  0.0 248.9 jit_solution(168859406196740415)
XLA Ops:
  7.2 0.0 copy-start.3
  7.2 0.0 all-reduce.9.cloned.1.call-start
  7.2 1.1 fusion.50
  8.3 1.3 collective-permute-start.1
  9.6 5.6 %collective-permute-start = (f32[2,128,256]{2,1,0:T(8,128)S(1)}, f32[2,128,256]{2,1,0:T(8,128)S(1)}, u32[]{:S(2)}, u32[]{:S(2)}) collective-permute-start(f32[2,128,256]{2,1,0:T(8,128)S(1)} %get-tuple-element.187), channel_id=1, source_target_pairs={{0,4},{4,8},{8,12},{1,5},{5,9},{9,13},{2,6},{6,10},{10,14},{3,7},{... | collective-permute-start | bytes 786440 | tf_op jit(solution)/shard_map/ppermute | solution.py:14
  15.2 1.0 fusion.41
  16.2 1.1 multiply_convert_fusion.1
  17.3 0.1 fusion.33
  17.4 0.8 pad_maximum_fusion.2
  18.3 2.5 collective-permute-done
  20.9 0.0 copy-start.1
  20.9 0.9 fusion.49
  21.7 4.4 %collective-permute-start.2 = (f32[2,512,128]{2,1,0:T(8,128)}, f32[2,512,128]{2,1,0:T(8,128)}, u32[]{:S(2)}, u32[]{:S(2)}) collective-permute-start(f32[2,512,128]{2,1,0:T(8,128)} %get-tuple-element.182), channel_id=1, source_target_pairs={{0,2},{1,3},{4,6},{5,7},{8,10},{9,11},{12,14},{13,15},{16,18},{17,... | collective-permute-start | bytes 1572872 | tf_op jit(solution)/shard_map/ppermute | solution.py:14
  26.1 1.3 collective-permute-start.3
  27.4 0.1 pad_maximum_fusion.1
  27.5 0.8 copy.7
  28.3 0.7 multiply_add_fusion.2
  29.0 0.7 slice_bitcast_fusion
  29.8 5.8 %collective-permute-done.2 = f32[2,512,128]{2,1,0:T(8,128)} collective-permute-done((f32[2,512,128]{2,1,0:T(8,128)}, f32[2,512,128]{2,1,0:T(8,128)}, u32[]{:S(2)}, u32[]{:S(2)}) %collective-permute-start.2) | collective-permute-done | bytes 524320 | tf_op jit(solution)/shard_map/ppermute | solution.py:14
  35.6 4.7 %collective-permute-done.3 = f32[2,512,128]{2,1,0:T(8,128)} collective-permute-done((f32[2,512,128]{2,1,0:T(8,128)S(1)}, f32[2,512,128]{2,1,0:T(8,128)}, u32[]{:S(2)}, u32[]{:S(2)}) %collective-permute-start.3) | collective-permute-done | bytes 524320 | tf_op jit(solution)/shard_map/ppermute | solution.py:17
  40.3 1.4 pad_maximum_fusion
  41.7 0.0 copy-start.5
  41.7 2.0 broadcast_in_dim.10
  43.7 53.2 %while.14 = (s32[]{:T(128)}, f32[3,512,512]{2,1,0:T(8,128)}, f32[2,256,256]{2,1,0:T(8,128)}, s32[2,2]{1,0:T(2,128)S(1)}, f32[256,256]{1,0:T(8,128)}, /*index=5*/...) while((s32[]{:T(128)}, f32[3,512,512]{2,1,0:T(8,128)}, ...), condition=%wide.region_1.2_spmd.clone, body=%wide.region_0.1_spmd.clone.sunk | while | flops 540737536 | bytes 17170760 | solution.py:126
  43.7 0.6 fusion.71
  48.1 2.0 fusion.72
  50.0 1.9 convolution_bitcast_fusion.6
  52.0 1.8 fusion.73
  53.7 2.0 convolution_bitcast_fusion.7
  55.7 1.3 multiply_add_fusion.4
  57.0 1.2 fusion.74
  58.2 0.9 maximum_add_fusion.5
  59.1 1.7 maximum_add_fusion.4
  60.7 9.1 %dynamic_update_slice.6 = f32[3,512,512]{2,1,0:T(8,128)} dynamic-update-slice(f32[3,512,512]{2,1,0:T(8,128)} %get-tuple-element.303, f32[3,256,256]{2,1,0:T(8,128)S(1)} %maximum_add_fusion.4, s32[]{:T(128)} %constant.39.clone.1..sunk, s32[]{:T(128)S(6)} %select_n.64, s32[]{:T(128)S(6)} %select_n.65) | dynamic-update-slice | bytes 1572868 | tf_op jit(solution)/shard_map/while/body/eval_jaxpr/dynamic_update_slice | solution.py:113
  69.8 0.6 fusion.71
  74.1 2.0 fusion.72
  76.1 1.9 convolution_bitcast_fusion.6
  78.0 1.8 fusion.73
  79.8 2.0 convolution_bitcast_fusion.7
  81.7 1.3 multiply_add_fusion.4
  83.0 1.2 fusion.74
  84.2 1.9 maximum_add_fusion.5
  86.1 1.7 maximum_add_fusion.4
  87.8 9.1 %dynamic_update_slice.6 = f32[3,512,512]{2,1,0:T(8,128)} dynamic-update-slice(f32[3,512,512]{2,1,0:T(8,128)} %get-tuple-element.303, f32[3,256,256]{2,1,0:T(8,128)S(1)} %maximum_add_fusion.4, s32[]{:T(128)} %constant.39.clone.1..sunk, s32[]{:T(128)S(6)} %select_n.64, s32[]{:T(128)S(6)} %select_n.65) | dynamic-update-slice | bytes 1572868 | tf_op jit(solution)/shard_map/while/body/eval_jaxpr/dynamic_update_slice | solution.py:113
  96.9 1.6 fusion.47
  98.6 3.5 %collective-permute-start.4 = (f32[3,128,512]{2,1,0:T(8,128)S(1)}, f32[3,128,512]{2,1,0:T(8,128)S(1)}, u32[]{:S(2)}, u32[]{:S(2)}) collective-permute-start(f32[3,128,512]{2,1,0:T(8,128)S(1)} %get-tuple-element.178), channel_id=1, source_target_pairs={{0,4},{4,8},{8,12},{1,5},{5,9},{9,13},{2,6},{6,10},{10,14},{3,7},{... | collective-permute-start | bytes 2359304 | tf_op jit(solution)/shard_map/ppermute | solution.py:14
  102.1 1.3 collective-permute-start.5
  103.4 13.0 %collective-permute-done.4 = f32[3,128,512]{2,1,0:T(8,128)S(1)} collective-permute-done((f32[3,128,512]{2,1,0:T(8,128)S(1)}, f32[3,128,512]{2,1,0:T(8,128)S(1)}, u32[]{:S(2)}, u32[]{:S(2)}) %collective-permute-start.4) | collective-permute-done | bytes 786464 | tf_op jit(solution)/shard_map/ppermute | solution.py:14
  116.4 4.7 %collective-permute-done.5 = f32[3,128,512]{2,1,0:T(8,128)S(1)} collective-permute-done((f32[3,128,512]{2,1,0:T(8,128)S(1)}, f32[3,128,512]{2,1,0:T(8,128)S(1)}, u32[]{:S(2)}, u32[]{:S(2)}) %collective-permute-start.5) | collective-permute-done | bytes 786464 | tf_op jit(solution)/shard_map/ppermute | solution.py:17
  121.0 0.3 pad_add_fusion
  121.4 0.9 fusion.48
  122.3 2.1 collective-permute-start.6
  124.4 1.3 collective-permute-start.7
  125.7 0.0 all-reduce.9.cloned.1.call-update
  125.8 0.0 all-reduce.7.cloned.1.call-start
  125.8 4.2 %collective-permute-done.6 = f32[3,256,128]{2,1,0:T(8,128)S(1)} collective-permute-done((f32[3,256,128]{2,1,0:T(8,128)}, f32[3,256,128]{2,1,0:T(8,128)S(1)}, u32[]{:S(2)}, u32[]{:S(2)}) %collective-permute-start.6) | collective-permute-done | bytes 393248 | tf_op jit(solution)/shard_map/ppermute | solution.py:14
  130.0 4.3 %collective-permute-done.7 = f32[3,256,128]{2,1,0:T(8,128)S(1)} collective-permute-done((f32[3,256,128]{2,1,0:T(8,128)}, f32[3,256,128]{2,1,0:T(8,128)S(1)}, u32[]{:S(2)}, u32[]{:S(2)}) %collective-permute-start.7) | collective-permute-done | bytes 393248 | tf_op jit(solution)/shard_map/ppermute | solution.py:17
  134.3 1.1 fusion.28
  135.4 0.0 all-reduce.7.cloned.1.call-update
  135.4 81.7 %all-reduce.9.cloned.1.call-done = f32[2,256,256]{2,1,0:T(8,128)} async-done(((f32[2,256,256]{2,1,0:T(8,128)}), f32[2,256,256]{2,1,0:T(8,128)}) %all-reduce.9.cloned.1.call-update) | async-done | bytes 524304 | tf_op jit(solution)/shard_map/psum | solution.py:137
  217.1 1.9 multiply_add_fusion.1
  219.0 20.2 %all-reduce.7.cloned.1.call-done = f32[3,256,256]{2,1,0:T(8,128)} async-done(((f32[3,256,256]{2,1,0:T(8,128)}), f32[3,256,256]{2,1,0:T(8,128)}) %all-reduce.7.cloned.1.call-update) | async-done | bytes 786448 | tf_op jit(solution)/shard_map/psum | solution.py:133
  239.2 1.0 fusion.37
  240.1 1.9 fusion.29
  (16 shorter events, 0.1 us)
Async XLA Ops:
  7.2 13.6 %copy-start.3 = (f32[2,256,256]{2,1,0:T(8,128)S(1)}, f32[2,256,256]{2,1,0:T(8,128)}, u32[]{:S(2)}) copy-start(f32[2,256,256]{2,1,0:T(8,128)} %param.6) | copy-start | bytes 1572868
  7.2 209.9 %all-reduce.9.cloned.1.call-start = ((), (), s32[]{:S(2)}) async-start(), calls=%async_computation.1 | async-start | bytes 1048576 | tf_op jit(solution)/shard_map/psum | solution.py:137
  8.3 12.5 %collective-permute-start.1 = (f32[2,128,256]{2,1,0:T(8,128)S(1)}, f32[2,128,256]{2,1,0:T(8,128)S(1)}, u32[]{:S(2)}, u32[]{:S(2)}) collective-permute-start(f32[2,128,256]{2,1,0:T(8,128)S(1)} %get-tuple-element.186), channel_id=1, source_target_pairs={{4,0},{8,4},{12,8},{5,1},{9,5},{13,9},{6,2},{10,6},{14,10},{7,3},{... | collective-permute-start | bytes 786440 | tf_op jit(solution)/shard_map/ppermute | solution.py:17
  9.6 11.1 %collective-permute-start = (f32[2,128,256]{2,1,0:T(8,128)S(1)}, f32[2,128,256]{2,1,0:T(8,128)S(1)}, u32[]{:S(2)}, u32[]{:S(2)}) collective-permute-start(f32[2,128,256]{2,1,0:T(8,128)S(1)} %get-tuple-element.187), channel_id=1, source_target_pairs={{0,4},{4,8},{8,12},{1,5},{5,9},{9,13},{2,6},{6,10},{10,14},{3,7},{... | collective-permute-start | bytes 786440 | tf_op jit(solution)/shard_map/ppermute | solution.py:14
  20.9 7.4 %copy-start.1 = (f32[2,256,256]{2,1,0:T(8,128)S(1)}, f32[2,256,256]{2,1,0:T(8,128)}, u32[]{:S(2)}) copy-start(f32[2,256,256]{2,1,0:T(8,128)} %param.7) | copy-start | bytes 1572868
  21.7 13.8 %collective-permute-start.2 = (f32[2,512,128]{2,1,0:T(8,128)}, f32[2,512,128]{2,1,0:T(8,128)}, u32[]{:S(2)}, u32[]{:S(2)}) collective-permute-start(f32[2,512,128]{2,1,0:T(8,128)} %get-tuple-element.182), channel_id=1, source_target_pairs={{0,2},{1,3},{4,6},{5,7},{8,10},{9,11},{12,14},{13,15},{16,18},{17,... | collective-permute-start | bytes 1572872 | tf_op jit(solution)/shard_map/ppermute | solution.py:14
  26.1 14.2 %collective-permute-start.3 = (f32[2,512,128]{2,1,0:T(8,128)S(1)}, f32[2,512,128]{2,1,0:T(8,128)}, u32[]{:S(2)}, u32[]{:S(2)}) collective-permute-start(f32[2,512,128]{2,1,0:T(8,128)S(1)} %get-tuple-element.183), channel_id=1, source_target_pairs={{2,0},{3,1},{6,4},{7,5},{10,8},{11,9},{14,12},{15,13},{18,16},{19,... | collective-permute-start | bytes 1572872 | tf_op jit(solution)/shard_map/ppermute | solution.py:17
  41.7 2.0 copy-start.5
  96.9 24.1 %copy-start = (f32[3,512,512]{2,1,0:T(8,128)S(1)}, f32[3,512,512]{2,1,0:T(8,128)}, u32[]{:S(2)}) copy-start(f32[3,512,512]{2,1,0:T(8,128)} %get-tuple-element.93) | copy-start | bytes 9437188
  98.6 17.8 %collective-permute-start.4 = (f32[3,128,512]{2,1,0:T(8,128)S(1)}, f32[3,128,512]{2,1,0:T(8,128)S(1)}, u32[]{:S(2)}, u32[]{:S(2)}) collective-permute-start(f32[3,128,512]{2,1,0:T(8,128)S(1)} %get-tuple-element.178), channel_id=1, source_target_pairs={{0,4},{4,8},{8,12},{1,5},{5,9},{9,13},{2,6},{6,10},{10,14},{3,7},{... | collective-permute-start | bytes 2359304 | tf_op jit(solution)/shard_map/ppermute | solution.py:14
  102.1 18.9 %collective-permute-start.5 = (f32[3,128,512]{2,1,0:T(8,128)S(1)}, f32[3,128,512]{2,1,0:T(8,128)S(1)}, u32[]{:S(2)}, u32[]{:S(2)}) collective-permute-start(f32[3,128,512]{2,1,0:T(8,128)S(1)} %get-tuple-element.179), channel_id=1, source_target_pairs={{4,0},{8,4},{12,8},{5,1},{9,5},{13,9},{6,2},{10,6},{14,10},{7,3},{... | collective-permute-start | bytes 2359304 | tf_op jit(solution)/shard_map/ppermute | solution.py:17
  122.3 94.8 %copy-start.2 = (f32[2,256,256]{2,1,0:T(8,128)S(1)}, f32[2,256,256]{2,1,0:T(8,128)}, u32[]{:S(2)}) copy-start(f32[2,256,256]{2,1,0:T(8,128)} %param.7) | copy-start | bytes 1572868
  122.3 7.7 %collective-permute-start.6 = (f32[3,256,128]{2,1,0:T(8,128)}, f32[3,256,128]{2,1,0:T(8,128)S(1)}, u32[]{:S(2)}, u32[]{:S(2)}) collective-permute-start(f32[3,256,128]{2,1,0:T(8,128)} %get-tuple-element.180), channel_id=1, source_target_pairs={{0,2},{1,3},{4,6},{5,7},{8,10},{9,11},{12,14},{13,15},{16,18},{17,... | collective-permute-start | bytes 1179656 | tf_op jit(solution)/shard_map/ppermute | solution.py:14
  124.4 9.9 %collective-permute-start.7 = (f32[3,256,128]{2,1,0:T(8,128)}, f32[3,256,128]{2,1,0:T(8,128)S(1)}, u32[]{:S(2)}, u32[]{:S(2)}) collective-permute-start(f32[3,256,128]{2,1,0:T(8,128)} %get-tuple-element.181), channel_id=1, source_target_pairs={{2,0},{3,1},{6,4},{7,5},{10,8},{11,9},{14,12},{15,13},{18,16},{19,... | collective-permute-start | bytes 1179656 | tf_op jit(solution)/shard_map/ppermute | solution.py:17
  125.7 114.4 %copy-start.4 = (f32[2,256,256]{2,1,0:T(8,128)S(1)}, f32[2,256,256]{2,1,0:T(8,128)}, u32[]{:S(2)}) copy-start(f32[2,256,256]{2,1,0:T(8,128)} %param.6) | copy-start | bytes 1572868
  125.8 113.4 %all-reduce.7.cloned.1.call-start = ((), (), s32[]{:S(2)}) async-start(), calls=%async_computation | async-start | bytes 1572864 | tf_op jit(solution)/shard_map/psum | solution.py:133
Sparse Core Ops, SparseCore 0:
  125.9 91.1 all-reduce.8
  219.4 19.7 all-reduce.6
where the time goes:
time: 251 us; the launch traced here: 249 us
  waiting for transfers between devices  141 us (56%)
  other arithmetic  29.9 us (12%)
  local copies, waits for them, and re-layouts  27.6 us (11%)
  starting transfers between devices  20.7 us (8%)
  between operations  14.2 us (6%)
  matrix products  7.75 us (3%)
  loops' own time  7.59 us (3%)
    psum x1, waiting for transfers between devices, shards(): total_grad = lax.psum(probe_grad, ('scanx', 'scany', 'pos'))  81.7 us
    ppermute x4, waiting for transfers between devices, padded_2(): lax.ppermute(lax.slice_in_dim(block, block.shape[dim] - width, None, axis...  25.5 us
    psum x1, waiting for transfers between devices, shards(): core_sum = lax.psum(core_sum, 'pos')  20.2 us
    dynamic_update_slice x2, local copies, waits for them, and re-layouts, visit_position(): lax.dynamic_update_slice(object_grad, current + object_term, (zero_index,...  18.2 us
    ppermute x4, starting transfers between devices, padded_2(): lax.ppermute(lax.slice_in_dim(block, block.shape[dim] - width, None, axis...  15.5 us
    ppermute x4, waiting for transfers between devices, padded_2(): lax.ppermute(lax.slice_in_dim(block, 0, width, axis=dim), axis, backward)  13.7 us
    another operation x1, loops' own time, shards(): lax.scan(visit_position, (start_grad, start_probe), (amplitudes, offsets))  7.59 us
    ppermute x4, starting transfers between devices, padded_2(): lax.ppermute(lax.slice_in_dim(block, 0, width, axis=dim), axis, backward)  5.16 us
  transfers between devices with their start and end apart: 10, of which 9 were waited for; matrix products, arithmetic and copies ran while one was open for 3% of the time, Pallas kernels for 0%

commit v1 on v0

v1 whole, which is shorter than its diff:
```python
import functools
import math

import jax
import jax.numpy as jnp
import numpy as np
from jax import lax
from jax.experimental import pallas as pl
from jax.experimental.pallas import tpu as pltpu
from jax.sharding import PartitionSpec as P

GROUP = ("scanx", "scany", "pos")
PART_SWAP = ((0, 1), (1, 0))
VMEM = pl.BlockSpec(memory_space=pltpu.VMEM)
SMEM = pl.BlockSpec(memory_space=pltpu.SMEM)
OFFSET_ROWS = 8


def f32(*shape):
    return jax.ShapeDtypeStruct(shape, jnp.float32)


def partner(index, way, count):
    step = 1 if (index + way) % 2 == 0 else -1
    return (index + step) % count


def ways_of(count):
    return (0,) if count == 2 else (0, 1)


def side_of(index, way):
    return lax.rem(index + way + 1, 2)


def valid_of(index, way, count):
    neighbour = index + 2 * side_of(index, way) - 1
    return jnp.logical_and(neighbour >= 0, neighbour < count)


def permutation(sizes, target):
    nz, nx, nc = sizes
    pairs = []
    for z in range(nz):
        for x in range(nx):
            for c in range(nc):
                tz, tx, tc = target(z, x, c)
                pairs.append(((z * nx + x) * nc + c, (tz * nx + tx) * nc + tc))
    return pairs


def dft_tables(length):
    index = np.arange(length, dtype=np.int32)
    phase = (index[:, None] * index[None, :]) % length
    angle = phase.astype(np.float32) * np.float32(2.0 * math.pi / length)
    scale = np.float32(1.0 / math.sqrt(length))
    cosine = (np.cos(angle) * scale).astype(jnp.bfloat16)
    sine = (np.sin(angle) * scale).astype(jnp.bfloat16)
    table_a = np.block([[cosine, sine], [-sine, cosine]])
    table_b = np.block([[cosine, -sine], [sine, cosine]])
    return table_a.astype(jnp.bfloat16), table_b.astype(jnp.bfloat16)


def aligned(row):
    return pl.multiple_of((row // 8) * 8, 8), lax.rem(row, 8)


def rows_up(block, shift):
    count, width = block.shape
    groups = pltpu.roll(block.reshape(count // 8, 8, width), lax.rem(8 - shift, 8), axis=1)
    at = lax.broadcasted_iota(jnp.int32, (count // 8 - 1, 8, width), 1)
    return jnp.where(at < 8 - shift, groups[:-1], groups[1:]).reshape(count - 8, width)


def rows_down(block, shift):
    count, width = block.shape
    groups = pltpu.roll(block.reshape(count // 8, 8, width), shift, axis=1)
    blank = jnp.zeros((1, 8, width), block.dtype)
    at = lax.broadcasted_iota(jnp.int32, (count // 8 + 1, 8, width), 1)
    early = jnp.concatenate([groups, blank])
    late = jnp.concatenate([blank, groups])
    return jnp.where(at >= shift, early, late).reshape(count + 8, width)


def halo_blocks_kernel(nz, nx, off_ref, spec_ref, *outs):
    z, x, c = (lax.axis_index(a) for a in GROUP)
    margin = spec_ref.shape[1] // 2
    xways = ways_of(nx)
    rows_at = pl.multiple_of(side_of(z, c) * margin, margin)

    def note(width):
        lane = lax.broadcasted_iota(jnp.int32, (OFFSET_ROWS, width), 1)
        row = jnp.zeros((OFFSET_ROWS, width), jnp.float32)
        for k in range(off_ref.shape[0]):
            row = jnp.where(lane == k, off_ref[k].astype(jnp.float32), row)
        return row

    own = note(margin)
    for k, way in enumerate(xways):
        cols_at = pl.multiple_of(side_of(x, way) * margin, margin)
        out = outs[k]
        out[: 2 * margin, :] = spec_ref[c, :, pl.ds(cols_at, margin)]
        out[2 * margin :, :] = own
        corner = outs[len(xways) + 1 + k]
        for p in range(2):
            corner[p, :margin, :] = spec_ref[p, pl.ds(rows_at, margin), pl.ds(cols_at, margin)]
            corner[p, margin:, :] = own
    wide = note(2 * margin)
    out = outs[len(xways)]
    for p in range(2):
        out[p, :margin, :] = spec_ref[p, pl.ds(rows_at, margin), :]
        out[p, margin:, :] = wide


def positions_kernel(nz, nx, off_ref, spec_ref, probe_ref, amp_ref, ta_ref, tb_ref, *refs):
    z, x, c = (lax.axis_index(a) for a in GROUP)
    xways = ways_of(nx)
    nw = len(xways)
    recv_x, recv_z, recv_c = refs[:nw], refs[nw], refs[nw + 1 : 2 * nw + 1]
    refs = refs[2 * nw + 1 :]
    other_x, other_z, other_c = refs[:nw], refs[nw], refs[nw + 1 : 2 * nw + 1]
    obj_own, obj_other, probe_own, probe_other, padded = refs[2 * nw + 1 :]
    size = probe_ref.shape[1]
    margin = size // 2
    tile = spec_ref.shape[1]
    npos = amp_ref.shape[0]

    blank = jnp.zeros((margin, tile + size), jnp.float32)
    slim = jnp.zeros((tile, margin), jnp.float32)
    for p in range(2):
        padded[p, :margin, :] = blank
        padded[p, margin + tile :, :] = blank
        if nw == 1:
            padded[p, margin : margin + tile, :margin] = slim
            padded[p, margin : margin + tile, margin + tile :] = slim
        padded[p, margin : margin + tile, margin : margin + tile] = spec_ref[p]

    def place(part, rows_at, height, cols_at, width, valid, value):
        @pl.when(valid)
        def _():
            padded[part, pl.ds(rows_at, height), pl.ds(cols_at, width)] = value()

    def halo_at(index, way):
        return pl.multiple_of(side_of(index, way) * (margin + tile), margin)

    for k, way in enumerate(xways):
        cols_at = halo_at(x, way)
        x_ok = valid_of(x, way, nx)
        if nw > 1:
            @pl.when(jnp.logical_not(x_ok))
            def _():
                for p in range(2):
                    padded[p, margin : margin + tile, pl.ds(cols_at, margin)] = slim
        place(c, margin, tile, cols_at, margin, x_ok, lambda: recv_x[k][:tile, :])
        place(1 - c, margin, tile, cols_at, margin, x_ok, lambda: other_x[k][:tile, :])
        for zway, corner in ((c, recv_c[k]), (1 - c, other_c[k])):
            ok = jnp.logical_and(x_ok, valid_of(z, zway, nz))
            for p in range(2):
                place(p, halo_at(z, zway), margin, cols_at, margin, ok, lambda: corner[p, :margin, :])
    for zway, edge in ((c, recv_z), (1 - c, other_z)):
        for p in range(2):
            place(p, halo_at(z, zway), margin, margin, tile, valid_of(z, zway, nz), lambda: edge[p, :margin, :])

    lane = lax.broadcasted_iota(jnp.int32, (size + 8, size), 1)
    first = c == 0
    table_a = ta_ref[...]
    table_b = tb_ref[...]
    probe_real = probe_ref[0]
    probe_imag = probe_ref[1]

    def side_by_side(both):
        return jnp.concatenate([both[:size], both[size:]], axis=1)

    grad_real = jnp.zeros((size, size), jnp.float32)
    grad_imag = jnp.zeros((size, size), jnp.float32)
    for j in range(npos):
        row, col = off_ref[j, 0], off_ref[j, 1]

        base, shift = aligned(row)

        def patch(part):
            rows = padded[part, pl.ds(base, size + 8), :]
            mixed = rows_up(jnp.where(lane >= col, rows[:, :size], rows[:, size:]), shift)
            return pltpu.roll(mixed, lax.rem(size - col, size), axis=1)

        patch_real, patch_imag = patch(0), patch(1)
        exit_real = probe_real * patch_real - probe_imag * patch_imag
        exit_imag = probe_real * patch_imag + probe_imag * patch_real
        wave = jnp.concatenate([exit_real, exit_imag], axis=0).astype(jnp.bfloat16)
        half = jnp.dot(table_a, wave, preferred_element_type=jnp.float32).astype(jnp.bfloat16)
        far = jnp.dot(side_by_side(half), table_b, preferred_element_type=jnp.float32)
        far_real, far_imag = far[:, :size], far[:, size:]
        power = far_real * far_real + far_imag * far_imag
        ratio = amp_ref[j].astype(jnp.float32) * jnp.minimum(lax.rsqrt(power), 1.0 / 0.2)
        projected = jnp.concatenate([far_real * ratio, far_imag * ratio], axis=0).astype(jnp.bfloat16)
        back_half = jnp.dot(table_b, projected, preferred_element_type=jnp.float32).astype(jnp.bfloat16)
        back = jnp.dot(side_by_side(back_half), table_a, preferred_element_type=jnp.float32)
        diff_real = back[:, :size] - exit_real
        diff_imag = back[:, size:] - exit_imag
        term_real = probe_real * diff_real + probe_imag * diff_imag
        term_imag = probe_real * diff_imag - probe_imag * diff_real
        obj_own[j] = jnp.where(first, term_real, term_imag)
        obj_other[j] = jnp.where(first, term_imag, term_real)
        grad_real += patch_real * diff_real + patch_imag * diff_imag
        grad_imag += patch_real * diff_imag - patch_imag * diff_real
    probe_own[...] = jnp.where(first, grad_real, grad_imag)
    probe_other[...] = jnp.where(first, grad_imag, grad_real)


def gather_kernel(nz, nx, off_ref, own_ref, other_ref, center_ref, *refs):
    z, x = lax.axis_index("scanx"), lax.axis_index("scany")
    xways = ways_of(nx)
    *blocks, grad = refs
    npos, size, _ = own_ref.shape
    margin = size // 2
    tile = center_ref.shape[0]
    lane = lax.broadcasted_iota(jnp.int32, (size + 8, size), 1)
    grad[...] = jnp.zeros_like(grad)
    for j in range(2 * npos):
        row, col = off_ref[2 * j], off_ref[2 * j + 1]
        term = own_ref[j] if j < npos else other_ref[j - npos]
        base, shift = aligned(row)
        term = rows_down(pltpu.roll(term, col, axis=1), shift)
        low = jnp.where(lane >= col, term, 0.0)
        rows = pl.ds(base, size + 8)
        grad[rows, :size] += low
        grad[rows, size:] += term - low
    center_ref[...] = grad[margin : margin + tile, margin : margin + tile]

    def halo_at(index, way):
        return pl.multiple_of(side_of(index, way) * (margin + tile), margin)

    blocks = iter(blocks)
    for xway in xways:
        next(blocks)[...] = grad[margin : margin + tile, pl.ds(halo_at(x, xway), margin)]
    for zway in (0, 1):
        next(blocks)[...] = grad[pl.ds(halo_at(z, zway), margin), margin : margin + tile]
    for xway in xways:
        for zway in (0, 1):
            next(blocks)[...] = grad[pl.ds(halo_at(z, zway), margin), pl.ds(halo_at(x, xway), margin)]


def light_kernel(nz, nx, npos, off_ref, probe_ref, light_ref, power_ref, total):
    z, x, c = (lax.axis_index(a) for a in GROUP)
    xways = ways_of(nx)
    size = probe_ref.shape[1]
    margin = size // 2
    tile = light_ref.shape[0]
    power_ref[...] = probe_ref[0] * probe_ref[0] + probe_ref[1] * probe_ref[1]
    total[...] = jnp.zeros_like(total)
    lane = lax.broadcasted_iota(jnp.int32, (size, size), 1)

    def add(row, col, ok):
        ok = jnp.logical_and(ok, jnp.logical_and(jnp.abs(row) < tile, jnp.abs(col) < tile))

        @pl.when(ok)
        def _():
            base, shift = aligned(row + tile)
            moved = pltpu.roll(power_ref[...], lax.rem(col + size, size), axis=1)
            keep = jnp.logical_and(lane >= col, lane < col + size)
            total[pl.ds(base, size + 8), :] += rows_down(jnp.where(keep, moved, 0.0), shift)

    def visit(at, count, dz, dx, ok):
        for j in range(count):
            add(off_ref[at + 2 * j] + dz * tile - margin, off_ref[at + 2 * j + 1] + dx * tile - margin, ok)

    zero = jnp.int32(0)
    span = 4 * npos
    visit(0, npos, zero, zero, True)
    zstep = 2 * side_of(z, c) - 1
    z_ok = valid_of(z, c, nz)
    at = span
    for way in xways:
        visit(at, npos, zero, 2 * side_of(x, way) - 1, valid_of(x, way, nx))
        at += span
    visit(at, 2 * npos, zstep, zero, z_ok)
    at += span
    for way in xways:
        visit(at, 2 * npos, zstep, 2 * side_of(x, way) - 1, jnp.logical_and(z_ok, valid_of(x, way, nx)))
        at += span
    light_ref[...] = total[tile : 2 * tile, :]


def update_kernel(nz, nx, spec_ref, center_ref, light_ref, other_light_ref, *refs):
    z, x, c = (lax.axis_index(a) for a in GROUP)
    xways = ways_of(nx)
    *blocks, out_ref, grad = refs
    tile = center_ref.shape[0]
    margin = tile // 2
    grad[...] = center_ref[...]

    def edge_at(index, way):
        return pl.multiple_of(side_of(index, way) * (tile - margin), margin)

    def add(rows, cols, ok, block):
        @pl.when(ok)
        def _():
            grad[rows, cols] += block[...]

    blocks = iter(blocks)
    for xway in xways:
        add(pl.ds(0, tile), pl.ds(edge_at(x, xway), margin), valid_of(x, xway, nx), next(blocks))
    for zway in (0, 1):
        add(pl.ds(edge_at(z, zway), margin), pl.ds(0, tile), valid_of(z, zway, nz), next(blocks))
    for xway in xways:
        for zway in (0, 1):
            ok = jnp.logical_and(valid_of(x, xway, nx), valid_of(z, zway, nz))
            add(pl.ds(edge_at(z, zway), margin), pl.ds(edge_at(x, xway), margin), ok, next(blocks))
    out_ref[...] = spec_ref[c] + grad[...] / (light_ref[...] + other_light_ref[...] + 1.0)


def call(kernel, out_shape, specs, scratch=()):
    return pl.pallas_call(
        kernel,
        out_shape=out_shape,
        in_specs=specs,
        out_specs=jax.tree.map(lambda _: VMEM, out_shape),
        scratch_shapes=list(scratch),
        compiler_params=pltpu.CompilerParams(vmem_limit_bytes=32 * 1024 * 1024),
    )


def shards(sizes, specimen, probe_wave, amplitudes, offsets):
    nz, nx, nc = sizes
    size = probe_wave.shape[1]
    margin = size // 2
    tile = specimen.shape[1]
    npos = offsets.shape[0]
    xways = ways_of(nx)
    z, x, c = (lax.axis_index(a) for a in GROUP)

    def send(value, target):
        return lax.ppermute(value, GROUP, permutation(sizes, target))

    def to_core(value):
        return lax.ppermute(value, "pos", PART_SWAP)

    def zto(index, way):
        return partner(index, way, nz)

    def xto(index, way):
        return partner(index, way, nx)

    flat = jnp.concatenate([offsets.reshape(-1), to_core(offsets).reshape(-1)])

    high = OFFSET_ROWS + margin
    blocks = call(
        functools.partial(halo_blocks_kernel, nz, nx),
        [f32(tile + OFFSET_ROWS, margin)] * len(xways) + [f32(2, high, tile)] + [f32(2, high, margin)] * len(xways),
        [SMEM, VMEM],
    )(flat, specimen)
    nw = len(xways)
    recv = [send(blocks[k], lambda z, x, c, w=way: (z, xto(x, w), c)) for k, way in enumerate(xways)]
    recv.append(send(blocks[nw], lambda z, x, c: (zto(z, c), x, c)))
    recv += [
        send(blocks[nw + 1 + k], lambda z, x, c, w=way: (zto(z, c), xto(x, w), c)) for k, way in enumerate(xways)
    ]
    other = [to_core(block) for block in recv]

    table_a, table_b = dft_tables(size)
    obj_own, obj_other, probe_own, probe_other = call(
        functools.partial(positions_kernel, nz, nx),
        [f32(npos, size, size), f32(npos, size, size), f32(size, size), f32(size, size)],
        [SMEM] + [VMEM] * (5 + 2 * len(recv)),
        [pltpu.VMEM((2, tile + size, tile + size), jnp.float32)],
    )(offsets, specimen, probe_wave, amplitudes, jnp.asarray(table_a), jnp.asarray(table_b), *recv, *other)

    held = probe_own + to_core(probe_other)
    obj_recv = to_core(obj_other)
    zbits = [("z", 1 << k) for k in range(nz.bit_length() - 1)]
    xbits = [("x", 1 << k) for k in range(nx.bit_length() - 1)]
    orders = (xbits[:1] + zbits + xbits[1:], zbits + xbits)

    def stage(k):
        def target(z, x, c):
            axis, bit = orders[c][k]
            return (z ^ bit, x, c) if axis == "z" else (z, x ^ bit, c)

        return target

    rows = size // 2
    mine = jnp.where(c == 0, lax.rem(x, 2), lax.rem(z, 2))
    keep = lax.dynamic_slice_in_dim(held, mine * rows, rows, 0)
    give = lax.dynamic_slice_in_dim(held, (1 - mine) * rows, rows, 0)
    keep = keep + send(give, stage(0))
    for k in range(1, len(orders[0])):
        keep = keep + send(keep, stage(k))
    away = send(keep, stage(0))
    summed = jnp.where(mine == 0, jnp.concatenate([keep, away]), jnp.concatenate([away, keep]))
    summed_other = to_core(summed)
    total_grad = jnp.where(c == 0, jnp.stack([summed, summed_other]), jnp.stack([summed_other, summed]))
    step_size = 1.0 / math.sqrt(npos * nz * nx * nc)
    new_probe = probe_wave + total_grad * step_size

    grad_shapes = (
        [f32(tile, tile)] + [f32(tile, margin)] * nw + [f32(margin, tile)] * 2 + [f32(margin, margin)] * (2 * nw)
    )
    center, *pieces = call(
        functools.partial(gather_kernel, nz, nx),
        grad_shapes,
        [SMEM, VMEM, VMEM],
        [pltpu.VMEM((tile + size, tile + size), jnp.float32)],
    )(flat, obj_own, obj_recv)
    targets = [lambda z, x, c, w=way: (z, xto(x, w), c) for way in xways]
    targets += [lambda z, x, c, w=way: (zto(z, w), x, c) for way in (0, 1)]
    targets += [lambda z, x, c, v=xway, w=zway: (zto(z, w), xto(x, v), c) for xway in xways for zway in (0, 1)]
    arrived = [send(piece, target) for piece, target in zip(pieces, targets)]

    notes = [flat]
    for k, block in enumerate(recv):
        notes.append((block[tile, : 4 * npos] if k < nw else block[0, margin, : 4 * npos]).astype(jnp.int32))
    light, unused = call(
        functools.partial(light_kernel, nz, nx, npos),
        [f32(tile, tile), f32(size, size)],
        [SMEM, VMEM],
        [pltpu.VMEM((3 * tile, size), jnp.float32)],
    )(jnp.concatenate(notes), probe_wave)
    other_light = to_core(light)

    part = call(
        functools.partial(update_kernel, nz, nx),
        [f32(tile, tile)],
        [VMEM] * (4 + len(arrived)),
        [pltpu.VMEM((tile, tile), jnp.float32)],
    )(specimen, center, light, other_light, *arrived)[0]
    part_other = to_core(part)
    new_specimen = jnp.where(c == 0, jnp.stack([part, part_other]), jnp.stack([part_other, part]))
    return (new_specimen, new_probe)


def solution(mesh):
    sizes = tuple(mesh.shape[a] for a in GROUP)
    placed = (
        P(None, ("groups", "scanx"), "scany"),
        P(None, "groups", None),
        P(("groups", "scanx", "scany", "pos"), None, None),
        P(("groups", "scanx", "scany", "pos"), None),
    )
    return jax.shard_map(
        functools.partial(shards, sizes),
        mesh=mesh,
        in_specs=placed,
        out_specs=(P(None, ("groups", "scanx"), "scany"), P(None, "groups", None)),
        check_vma=False,
    )
```

time: 251 us -> 66.4 us (0.26)
  waiting for transfers between devices: 141 us -> 26.8 us
  other arithmetic: 29.9 us -> 1.91 us
  local copies, waits for them, and re-layouts: 27.6 us -> 6.06 us
  between operations: 14.2 us -> 0.79 us
  Pallas kernels: 0 us -> 7.82 us
  matrix products: 7.75 us -> 0 us
  loops' own time: 7.59 us -> 0 us
    psum x2 -> x0, waiting for transfers between devices: 102 us -> none  [the longest x1 81.7 us: shards(): total_grad = lax.psum(probe_grad, ('scanx', 'scany', 'pos'))]
    dynamic_update_slice x2 -> x0, local copies, waits for them, and re-layouts: 18.2 us -> none  [visit_position(): lax.dynamic_update_slice(object_grad, current + object_term, (zero_index,...]
    add x12 -> x4, other arithmetic: 15.1 us -> 0.09 us  [the longest x2 0.04 us: shards(): keep = keep + send(keep, stage(k))]
    ppermute x8 -> x21, waiting for transfers between devices: 39.1 us -> 26.8 us  [the longest x12 22.9 us: send(): return lax.ppermute(value, GROUP, permutation(sizes, target))]
    pallas_call x0 -> x5, Pallas kernels: none -> 7.82 us  [the longest x1 3.55 us: shards(): call(functools.partial(positions_kernel, nz, nx), [f32(npos, size, size),...]
    dot_general x4 -> x0, matrix products: 7.75 us -> none  [the longest x2 3.96 us: project_exit(): jnp.einsum('bkv,bval->akl', back_half, inverse_right, preferred_element_t...]
    another operation x1 -> x0, loops' own time: 7.59 us -> none  [shards(): lax.scan(visit_position, (start_grad, start_probe), (amplitudes, offsets))]
    slice x6 -> x0, local copies, waits for them, and re-layouts: 5.72 us -> none  [the longest x3 3.43 us: padded_2(): lax.slice_in_dim(block, block.shape[dim] - width, None, axis=dim)]
  transfers between devices with their start and end apart: 10 -> 21, of which waited for: 9 -> 10; matrix products, arithmetic and copies ran while one was open for 3% -> 3% of each run, Pallas kernels for 0% -> 6%
where the time goes in v1:
time: 66.4 us; the launch traced here: 66.1 us
  waiting for transfers between devices  26.8 us (40%)
  starting transfers between devices  22.7 us (34%)
  Pallas kernels  7.82 us (12%)
  local copies, waits for them, and re-layouts  6.06 us (9%)
  other arithmetic  1.91 us (3%)
  between operations  0.79 us (1%)
    ppermute x12, waiting for transfers between devices, send(): return lax.ppermute(value, GROUP, permutation(sizes, target))  22.9 us
    ppermute x12, starting transfers between devices, send(): return lax.ppermute(value, GROUP, permutation(sizes, target))  19.5 us
    unnamed x16, local copies, waits for them, and re-layouts  5.12 us
    ppermute x9, waiting for transfers between devices, to_core(): return lax.ppermute(value, 'pos', PART_SWAP)  3.93 us
    pallas_call x1, Pallas kernels, shards(): call(functools.partial(positions_kernel, nz, nx), [f32(npos, size, size),...  3.55 us
    ppermute x9, starting transfers between devices, to_core(): return lax.ppermute(value, 'pos', PART_SWAP)  3.17 us
    pallas_call x1, Pallas kernels, shards(): call(functools.partial(light_kernel, nz, nx, npos), [f32(tile, tile), f32...  2.52 us
  transfers between devices with their start and end apart: 21, of which 10 were waited for; matrix products, arithmetic and copies ran while one was open for 3% of the time, Pallas kernels for 6%

profile of v1, /device:TPU:0, one launch (start us, length us, event | category | flops | bytes accessed | tf_op | source)
XLA Modules:
  0.0 66.1 jit_solution(8495742110264346673)
XLA Ops:
  0.6 0.0 copy-start
  0.6 0.5 collective-permute-start
  1.2 0.8 %reshape.68 = s32[4]{0:T(128)S(1)} reshape(s32[2,2]{1,0:T(2,128)} %off_ref.1) | data formatting | bytes 32 | tf_op jit(solution)/shard_map/reshape | solution.py:344
  1.9 0.3 collective-permute-done
  2.2 0.1 reshape.69
  2.3 0.1 pad_add_fusion.off_ref
  2.3 0.0 copy-start.1
  2.3 1.0 %copy-done.1 = f32[2,256,256]{2,1,0:T(8,128)S(1)} copy-done((f32[2,256,256]{2,1,0:T(8,128)S(1)}, f32[2,256,256]{2,1,0:T(8,128)}, u32[]{:S(2)}) %copy-start.1) | copy-done | bytes 524312
  3.4 0.6 shard_map.77
  4.0 3.0 %collective-permute-start.2 = (f32[2,136,256]{2,1,0:T(8,128)S(1)}, f32[2,136,256]{2,1,0:T(8,128)S(1)}, u32[]{:S(2)}, u32[]{:S(2)}) collective-permute-start(f32[2,136,256]{2,1,0:T(8,128)S(1)} %get-tuple-element.17), channel_id=1, source_target_pairs={{0,4},{1,13},{2,6},{3,15},{4,0},{5,9},{6,2},{7,11},{8,12},{9,5},{1... | collective-permute-start | bytes 835592 | tf_op jit(solution)/shard_map/ppermute | solution.py:333
  6.9 1.4 %collective-permute-start.3 = (f32[2,136,128]{2,1,0:T(8,128)S(1)}, f32[2,136,128]{2,1,0:T(8,128)S(1)}, u32[]{:S(2)}, u32[]{:S(2)}) collective-permute-start(f32[2,136,128]{2,1,0:T(8,128)S(1)} %get-tuple-element.18), channel_id=1, source_target_pairs={{0,6},{1,15},{2,4},{3,13},{4,2},{5,11},{6,0},{7,9},{8,14},{9,7},{1... | collective-permute-start | bytes 417800 | tf_op jit(solution)/shard_map/ppermute | solution.py:333
  8.3 5.5 %collective-permute-done.2.refs_1_ = f32[2,136,256]{2,1,0:T(8,128)S(1)} collective-permute-done((f32[2,136,256]{2,1,0:T(8,128)S(1)}, f32[2,136,256]{2,1,0:T(8,128)S(1)}, u32[]{:S(2)}, u32[]{:S(2)}) %collective-permute-start.2) | collective-permute-done | bytes 278560 | tf_op jit(solution)/shard_map/ppermute | solution.py:333
  13.8 1.5 %collective-permute-start.5 = (f32[2,136,256]{2,1,0:T(8,128)S(1)}, f32[2,136,256]{2,1,0:T(8,128)S(1)}, u32[]{:S(2)}, u32[]{:S(2)}) collective-permute-start(f32[2,136,256]{2,1,0:T(8,128)S(1)} %collective-permute-done.2.refs_1_), channel_id=1, source_target_pairs={{0,1},{1,0},{2,3},{3,2},{4,5},{5,4},{6,7},{7,6},{8,9},{9,8},{10,11... | collective-permute-start | bytes 835592 | tf_op jit(solution)/shard_map/ppermute | solution.py:336
  15.4 1.5 %collective-permute-start.1 = (f32[264,128]{1,0:T(8,128)S(1)}, f32[264,128]{1,0:T(8,128)S(1)}, u32[]{:S(2)}, u32[]{:S(2)}) collective-permute-start(f32[264,128]{1,0:T(8,128)S(1)} %get-tuple-element.16), channel_id=1, source_target_pairs={{0,2},{1,3},{2,0},{3,1},{4,6},{5,7},{6,4},{7,5},{8,10},{9,11},{10,... | collective-permute-start | bytes 405512 | tf_op jit(solution)/shard_map/ppermute | solution.py:333
  16.9 1.8 %collective-permute-done.3.refs_2_ = f32[2,136,128]{2,1,0:T(8,128)S(1)} collective-permute-done((f32[2,136,128]{2,1,0:T(8,128)S(1)}, f32[2,136,128]{2,1,0:T(8,128)S(1)}, u32[]{:S(2)}, u32[]{:S(2)}) %collective-permute-start.3) | collective-permute-done | bytes 139296 | tf_op jit(solution)/shard_map/ppermute | solution.py:333
  18.7 0.1 collective-permute-start.6
  18.8 2.9 %collective-permute-done.1.refs_0_ = f32[264,128]{1,0:T(8,128)S(1)} collective-permute-done((f32[264,128]{1,0:T(8,128)S(1)}, f32[264,128]{1,0:T(8,128)S(1)}, u32[]{:S(2)}, u32[]{:S(2)}) %collective-permute-start.1) | collective-permute-done | bytes 135200 | tf_op jit(solution)/shard_map/ppermute | solution.py:333
  21.7 0.0 collective-permute-start.4
  21.7 1.4 %collective-permute-done.4.refs_3_ = f32[264,128]{1,0:T(8,128)S(1)} collective-permute-done((f32[264,128]{1,0:T(8,128)S(1)}, f32[264,128]{1,0:T(8,128)S(1)}, u32[]{:S(2)}, u32[]{:S(2)}) %collective-permute-start.4) | collective-permute-done | bytes 135200 | tf_op jit(solution)/shard_map/ppermute | solution.py:336
  23.1 0.0 collective-permute-done.6.refs_5_
  23.1 0.0 collective-permute-done.5.refs_4_
  23.1 0.0 copy-done
  23.1 0.0 copy-done.7
  23.1 0.0 copy-start.2
  23.1 1.0 %copy-done.2 = f32[2,256,256]{2,1,0:T(8,128)S(1)} copy-done((f32[2,256,256]{2,1,0:T(8,128)S(1)}, f32[2,256,256]{2,1,0:T(8,128)}, u32[]{:S(2)}) %copy-start.2) | copy-done | bytes 524312
  24.1 1.0 %copy-done.4 = bf16[512,512]{1,0:T(8,128)(2,1)S(1)} copy-done((bf16[512,512]{1,0:T(8,128)(2,1)S(1)}, bf16[512,512]{1,0:T(8,128)(2,1)}, u32[]{:S(2)}) %copy-start.4) | copy-done | bytes 524312
  25.2 1.0 %copy-done.5 = bf16[512,512]{1,0:T(8,128)(2,1)S(1)} copy-done((bf16[512,512]{1,0:T(8,128)(2,1)S(1)}, bf16[512,512]{1,0:T(8,128)(2,1)}, u32[]{:S(2)}) %copy-start.5) | copy-done | bytes 524312
  26.2 0.9 %copy-done.6 = bf16[2,256,256]{2,1,0:T(8,128)(2,1)S(1)} copy-done((bf16[2,256,256]{2,1,0:T(8,128)(2,1)S(1)}, bf16[2,256,256]{2,1,0:T(8,128)(2,1)}, u32[]{:S(2)}) %copy-start.6) | copy-done | bytes 262168
  27.2 3.6 %shard_map.78 = (f32[2,256,256]{2,1,0:T(8,128)S(1)}, f32[2,256,256]{2,1,0:T(8,128)S(1)}, f32[256,256]{1,0:T(8,128)S(1)}, f32[256,256]{1,0:T(8,128)S(1)}) custom-call(s32[2,2]{1,0:T(2,128)S(1)} %copy-done.7, f32[2,256,256]{2,1,0:T(8,128)S(1)} %copy-done.2, f32[2,256,256]{2,1,0:T(8,128)S(1)} %copy-done, bf16[2,256,256]{2,1,0:T(8,128)(2,1)S(1)} %copy-done.6, ...), custom_call_target="tpu_custom_call" | custom-call | tf_op jit(solution)/shard_map/pallas_call | solution.py:361
  30.7 0.2 collective-permute-start.15
  30.9 1.4 %collective-permute-done.15 = f32[256,256]{1,0:T(8,128)S(1)} collective-permute-done((f32[256,256]{1,0:T(8,128)S(1)}, f32[256,256]{1,0:T(8,128)S(1)}, u32[]{:S(2)}, u32[]{:S(2)}) %collective-permute-start.15) | collective-permute-done | bytes 262176 | tf_op jit(solution)/shard_map/ppermute | solution.py:336
  32.4 0.7 %collective-permute-start.16 = (f32[128,256]{1,0:T(8,128)S(1)}, f32[128,256]{1,0:T(8,128)S(1)}, u32[]{:S(2)}, u32[]{:S(2)}) collective-permute-start(f32[128,256]{1,0:T(8,128)S(1)} %constant_dynamic-slice_fusion), channel_id=1, source_target_pairs={{0,2},{1,5},{2,0},{3,7},{4,6},{5,1},{6,4},{7,3},{8,10},{9,13},{10,... | collective-permute-start | bytes 393224 | tf_op jit(solution)/shard_map/ppermute | solution.py:333
  33.1 0.0 collective-permute-start.7
  33.1 4.3 %collective-permute-done.16 = f32[128,256]{1,0:T(8,128)S(1)} collective-permute-done((f32[128,256]{1,0:T(8,128)S(1)}, f32[128,256]{1,0:T(8,128)S(1)}, u32[]{:S(2)}, u32[]{:S(2)}) %collective-permute-start.16) | collective-permute-done | bytes 131104 | tf_op jit(solution)/shard_map/ppermute | solution.py:333
  37.4 0.7 %collective-permute-start.17 = (f32[128,256]{1,0:T(8,128)S(1)}, f32[128,256]{1,0:T(8,128)S(1)}, u32[]{:S(2)}, u32[]{:S(2)}) collective-permute-start(f32[128,256]{1,0:T(8,128)S(1)} %dynamic-slice_add_fusion), channel_id=1, source_target_pairs={{0,4},{1,9},{2,6},{3,11},{4,0},{5,13},{6,2},{7,15},{8,12},{9,1},{1... | collective-permute-start | bytes 393224 | tf_op jit(solution)/shard_map/ppermute | solution.py:333
  38.1 0.1 concatenate.36.off_ref
  38.2 2.5 %shard_map.80 = (f32[256,256]{1,0:T(8,128)S(1)}, f32[256,256]{1,0:T(8,128)}) custom-call(s32[32]{0:T(128)S(1)} %concatenate.36.off_ref, f32[2,256,256]{2,1,0:T(8,128)S(1)} %copy-done), custom_call_target="tpu_custom_call" | custom-call | tf_op jit(solution)/shard_map/pallas_call | solution.py:412
  40.7 0.2 collective-permute-start.8
  41.0 1.8 %collective-permute-done.17 = f32[128,256]{1,0:T(8,128)S(1)} collective-permute-done((f32[128,256]{1,0:T(8,128)S(1)}, f32[128,256]{1,0:T(8,128)S(1)}, u32[]{:S(2)}, u32[]{:S(2)}) %collective-permute-start.17) | collective-permute-done | bytes 131104 | tf_op jit(solution)/shard_map/ppermute | solution.py:333
  42.8 2.5 %collective-permute-start.18 = (f32[128,256]{1,0:T(8,128)S(1)}, f32[128,256]{1,0:T(8,128)S(1)}, u32[]{:S(2)}, u32[]{:S(2)}) collective-permute-start(f32[128,256]{1,0:T(8,128)S(1)} %add.25), channel_id=1, source_target_pairs={{0,8},{1,3},{2,10},{3,1},{4,12},{5,7},{6,14},{7,5},{8,0},{9,11},{1... | collective-permute-start | bytes 393224 | tf_op jit(solution)/shard_map/ppermute | solution.py:333
  45.3 0.0 collective-permute-done.7.other_ref
  45.3 1.0 %shard_map.79 = (f32[256,256]{1,0:T(8,128)S(1)}, f32[256,128]{1,0:T(8,128)S(1)}, f32[128,256]{1,0:T(8,128)S(1)}, f32[128,256]{1,0:T(8,128)S(1)}, f32[128,128]{1,0:T(8,128)S(1)}, /*index=5*/f32[128,128]{1,0:T(8,128)S(1)}) custom-call(s32[8]{0:T(128)S(1)} %pad_add_fusion.off_ref, f32[2,256,256]{2,1,0:T(8,128)S(1)} %get-tuple-element.19.own_ref, ...), custom_call_target="tpu_custom_call" | custom-call | tf_op jit(solution)/shard_map/pallas_call | solution.py:398
  46.3 3.0 %collective-permute-start.12 = (f32[128,128]{1,0:T(8,128)S(1)}, f32[128,128]{1,0:T(8,128)S(1)}, u32[]{:S(2)}, u32[]{:S(2)}) collective-permute-start(f32[128,128]{1,0:T(8,128)S(1)} %get-tuple-element.26), channel_id=1, source_target_pairs={{0,6},{1,7},{2,4},{3,5},{4,2},{5,3},{6,0},{7,1},{8,14},{9,15},{10,... | collective-permute-start | bytes 196616 | tf_op jit(solution)/shard_map/ppermute | solution.py:333
  49.3 1.0 %collective-permute-start.9 = (f32[256,128]{1,0:T(8,128)S(1)}, f32[256,128]{1,0:T(8,128)S(1)}, u32[]{:S(2)}, u32[]{:S(2)}) collective-permute-start(f32[256,128]{1,0:T(8,128)S(1)} %get-tuple-element.23), channel_id=1, source_target_pairs={{0,2},{1,3},{2,0},{3,1},{4,6},{5,7},{6,4},{7,5},{8,10},{9,11},{10,... | collective-permute-start | bytes 393224 | tf_op jit(solution)/shard_map/ppermute | solution.py:333
  50.3 0.0 collective-permute-start.10
  50.3 0.0 collective-permute-done.18
  50.3 4.2 %collective-permute-start.11 = (f32[128,256]{1,0:T(8,128)S(1)}, f32[128,256]{1,0:T(8,128)S(1)}, u32[]{:S(2)}, u32[]{:S(2)}) collective-permute-start(f32[128,256]{1,0:T(8,128)S(1)} %get-tuple-element.25), channel_id=1, source_target_pairs={{0,12},{1,13},{2,14},{3,15},{4,8},{5,9},{6,10},{7,11},{8,4},{9,5},... | collective-permute-start | bytes 393224 | tf_op jit(solution)/shard_map/ppermute | solution.py:333
  54.6 0.0 collective-permute-done.8.other_light_ref
  54.6 1.1 %collective-permute-start.19 = (f32[128,256]{1,0:T(8,128)S(1)}, f32[128,256]{1,0:T(8,128)S(1)}, u32[]{:S(2)}, u32[]{:S(2)}) collective-permute-start(f32[128,256]{1,0:T(8,128)S(1)} %add.26), channel_id=1, source_target_pairs={{0,2},{1,5},{2,0},{3,7},{4,6},{5,1},{6,4},{7,3},{8,10},{9,13},{10,... | collective-permute-start | bytes 393224 | tf_op jit(solution)/shard_map/ppermute | solution.py:333
  55.7 0.0 collective-permute-done.12.refs_3_
  55.7 0.5 collective-permute-start.13
  56.1 6.5 %collective-permute-done.13.refs_4_ = f32[128,128]{1,0:T(8,128)S(1)} collective-permute-done((f32[128,128]{1,0:T(8,128)S(1)}, f32[128,128]{1,0:T(8,128)S(1)}, u32[]{:S(2)}, u32[]{:S(2)}) %collective-permute-start.13) | collective-permute-done | bytes 65568 | tf_op jit(solution)/shard_map/ppermute | solution.py:333
  62.6 0.0 collective-permute-done.9.refs_0_
  62.6 0.0 collective-permute-done.10.refs_1_
  62.6 0.0 collective-permute-done.11.refs_2_
  62.6 0.0 copy-done.3
  62.6 0.1 shard_map.81
  62.8 0.1 collective-permute-start.14
  62.9 0.0 collective-permute-done.19
  62.9 0.5 collective-permute-start.20
  63.5 0.9 %collective-permute-done.14 = f32[256,256]{1,0:T(8,128)S(1)} collective-permute-done((f32[256,256]{1,0:T(8,128)S(1)}, f32[256,256]{1,0:T(8,128)S(1)}, u32[]{:S(2)}, u32[]{:S(2)}) %collective-permute-start.14) | collective-permute-done | bytes 262176 | tf_op jit(solution)/shard_map/ppermute | solution.py:336
  64.4 0.8 %maximum_select_fusion = f32[2,256,256]{2,1,0:T(8,128)} fusion(f32[1,256,256]{2,1,0:T(8,128)S(1)} %bitcast.14, f32[1,256,256]{2,1,0:T(8,128)S(1)} %bitcast.11, pred[]{:T(512)S(6)} %eq.8), kind=kLoop, calls=%fused_computation | loop fusion | flops 393216 | bytes 1048577 | tf_op jit(solution)/shard_map/jit(_where)/select_n | solution.py:427
  65.2 0.0 collective-permute-done.20
  65.2 0.9 %fusion.1 = f32[2,256,256]{2,1,0:T(8,128)} fusion(f32[2,256,256]{2,1,0:T(8,128)S(1)} %copy-done, f32[1,256,256]{2,1,0:T(8,128)S(1)} %bitcast.15, f32[1,256,256]{2,1,0:T(8,128)S(1)} %maximum_select_fusion.2, pred[]{:T(512)S(6)} %eq.8), kind=kLoop, calls=%fused_computation.3 | loop fusion | flops 655360 | bytes 1572865 | tf_op jit(solution)/shard_map/add | solution.py:393
  (15 shorter events, 0.2 us)
Async XLA Ops:
  0.6 22.4 %copy-start = (f32[2,256,256]{2,1,0:T(8,128)S(1)}, f32[2,256,256]{2,1,0:T(8,128)}, u32[]{:S(2)}) copy-start(f32[2,256,256]{2,1,0:T(8,128)} %probe_ref.3) | copy-start | bytes 1572868
  0.6 1.5 %collective-permute-start = (s32[2,2]{1,0:T(2,128)}, s32[2,2]{1,0:T(2,128)S(1)}, u32[]{:S(2)}, u32[]{:S(2)}) collective-permute-start(s32[2,2]{1,0:T(2,128)} %off_ref.1), channel_id=1, source_target_pairs={{0,1},{1,0},{2,3},{3,2},{4,5},{5,4},{6,7},{7,6},{8,9},{9,8},{10,11... | collective-permute-start | bytes 56 | tf_op jit(solution)/shard_map/ppermute | solution.py:336
  2.3 1.0 %copy-start.1 = (f32[2,256,256]{2,1,0:T(8,128)S(1)}, f32[2,256,256]{2,1,0:T(8,128)}, u32[]{:S(2)}) copy-start(f32[2,256,256]{2,1,0:T(8,128)} %spec_ref.5) | copy-start | bytes 1572868
  4.0 9.9 %collective-permute-start.2 = (f32[2,136,256]{2,1,0:T(8,128)S(1)}, f32[2,136,256]{2,1,0:T(8,128)S(1)}, u32[]{:S(2)}, u32[]{:S(2)}) collective-permute-start(f32[2,136,256]{2,1,0:T(8,128)S(1)} %get-tuple-element.17), channel_id=1, source_target_pairs={{0,4},{1,13},{2,6},{3,15},{4,0},{5,9},{6,2},{7,11},{8,12},{9,5},{1... | collective-permute-start | bytes 835592 | tf_op jit(solution)/shard_map/ppermute | solution.py:333
  6.9 16.1 %copy-start.7 = (s32[2,2]{1,0:T(2,128)S(1)}, s32[2,2]{1,0:T(2,128)}, u32[]{:S(2)}) copy-start(s32[2,2]{1,0:T(2,128)} %off_ref.1) | copy-start | bytes 52
  6.9 11.8 %collective-permute-start.3 = (f32[2,136,128]{2,1,0:T(8,128)S(1)}, f32[2,136,128]{2,1,0:T(8,128)S(1)}, u32[]{:S(2)}, u32[]{:S(2)}) collective-permute-start(f32[2,136,128]{2,1,0:T(8,128)S(1)} %get-tuple-element.18), channel_id=1, source_target_pairs={{0,6},{1,15},{2,4},{3,13},{4,2},{5,11},{6,0},{7,9},{8,14},{9,7},{1... | collective-permute-start | bytes 417800 | tf_op jit(solution)/shard_map/ppermute | solution.py:333
  13.8 9.2 %collective-permute-start.5 = (f32[2,136,256]{2,1,0:T(8,128)S(1)}, f32[2,136,256]{2,1,0:T(8,128)S(1)}, u32[]{:S(2)}, u32[]{:S(2)}) collective-permute-start(f32[2,136,256]{2,1,0:T(8,128)S(1)} %collective-permute-done.2.refs_1_), channel_id=1, source_target_pairs={{0,1},{1,0},{2,3},{3,2},{4,5},{5,4},{6,7},{7,6},{8,9},{9,8},{10,11... | collective-permute-start | bytes 835592 | tf_op jit(solution)/shard_map/ppermute | solution.py:336
  15.4 6.3 %collective-permute-start.1 = (f32[264,128]{1,0:T(8,128)S(1)}, f32[264,128]{1,0:T(8,128)S(1)}, u32[]{:S(2)}, u32[]{:S(2)}) collective-permute-start(f32[264,128]{1,0:T(8,128)S(1)} %get-tuple-element.16), channel_id=1, source_target_pairs={{0,2},{1,3},{2,0},{3,1},{4,6},{5,7},{6,4},{7,5},{8,10},{9,11},{10,... | collective-permute-start | bytes 405512 | tf_op jit(solution)/shard_map/ppermute | solution.py:333
  18.7 4.3 %collective-permute-start.6 = (f32[2,136,128]{2,1,0:T(8,128)S(1)}, f32[2,136,128]{2,1,0:T(8,128)S(1)}, u32[]{:S(2)}, u32[]{:S(2)}) collective-permute-start(f32[2,136,128]{2,1,0:T(8,128)S(1)} %collective-permute-done.3.refs_2_), channel_id=1, source_target_pairs={{0,1},{1,0},{2,3},{3,2},{4,5},{5,4},{6,7},{7,6},{8,9},{9,8},{10,11... | collective-permute-start | bytes 417800 | tf_op jit(solution)/shard_map/ppermute | solution.py:336
  21.7 1.4 %collective-permute-start.4 = (f32[264,128]{1,0:T(8,128)S(1)}, f32[264,128]{1,0:T(8,128)S(1)}, u32[]{:S(2)}, u32[]{:S(2)}) collective-permute-start(f32[264,128]{1,0:T(8,128)S(1)} %collective-permute-done.1.refs_0_), channel_id=1, source_target_pairs={{0,1},{1,0},{2,3},{3,2},{4,5},{5,4},{6,7},{7,6},{8,9},{9,8},{10,11... | collective-permute-start | bytes 405512 | tf_op jit(solution)/shard_map/ppermute | solution.py:336
  23.1 1.0 %copy-start.2 = (f32[2,256,256]{2,1,0:T(8,128)S(1)}, f32[2,256,256]{2,1,0:T(8,128)}, u32[]{:S(2)}) copy-start(f32[2,256,256]{2,1,0:T(8,128)} %spec_ref.5) | copy-start | bytes 1572868
  24.1 1.0 %copy-start.4 = (bf16[512,512]{1,0:T(8,128)(2,1)S(1)}, bf16[512,512]{1,0:T(8,128)(2,1)}, u32[]{:S(2)}) copy-start(bf16[512,512]{1,0:T(8,128)(2,1)} %constant.31.clone.tb_ref) | copy-start | bytes 1572868
  25.2 1.0 %copy-start.5 = (bf16[512,512]{1,0:T(8,128)(2,1)S(1)}, bf16[512,512]{1,0:T(8,128)(2,1)}, u32[]{:S(2)}) copy-start(bf16[512,512]{1,0:T(8,128)(2,1)} %constant.30.clone.ta_ref) | copy-start | bytes 1572868
  26.2 0.9 %copy-start.6 = (bf16[2,256,256]{2,1,0:T(8,128)(2,1)S(1)}, bf16[2,256,256]{2,1,0:T(8,128)(2,1)}, u32[]{:S(2)}) copy-start(bf16[2,256,256]{2,1,0:T(8,128)(2,1)} %amp_ref.1) | copy-start | bytes 786436
  30.7 1.6 %collective-permute-start.15 = (f32[256,256]{1,0:T(8,128)S(1)}, f32[256,256]{1,0:T(8,128)S(1)}, u32[]{:S(2)}, u32[]{:S(2)}) collective-permute-start(f32[256,256]{1,0:T(8,128)S(1)} %get-tuple-element.29), channel_id=1, source_target_pairs={{0,1},{1,0},{2,3},{3,2},{4,5},{5,4},{6,7},{7,6},{8,9},{9,8},{10,11... | collective-permute-start | bytes 786440 | tf_op jit(solution)/shard_map/ppermute | solution.py:336
  32.4 5.0 %collective-permute-start.16 = (f32[128,256]{1,0:T(8,128)S(1)}, f32[128,256]{1,0:T(8,128)S(1)}, u32[]{:S(2)}, u32[]{:S(2)}) collective-permute-start(f32[128,256]{1,0:T(8,128)S(1)} %constant_dynamic-slice_fusion), channel_id=1, source_target_pairs={{0,2},{1,5},{2,0},{3,7},{4,6},{5,1},{6,4},{7,3},{8,10},{9,13},{10,... | collective-permute-start | bytes 393224 | tf_op jit(solution)/shard_map/ppermute | solution.py:333
  33.1 12.2 %collective-permute-start.7 = (f32[2,256,256]{2,1,0:T(8,128)S(1)}, f32[2,256,256]{2,1,0:T(8,128)S(1)}, u32[]{:S(2)}, u32[]{:S(2)}) collective-permute-start(f32[2,256,256]{2,1,0:T(8,128)S(1)} %get-tuple-element.20), channel_id=1, source_target_pairs={{0,1},{1,0},{2,3},{3,2},{4,5},{5,4},{6,7},{7,6},{8,9},{9,8},{10,11... | collective-permute-start | bytes 1572872 | tf_op jit(solution)/shard_map/ppermute | solution.py:336
  37.4 5.3 %collective-permute-start.17 = (f32[128,256]{1,0:T(8,128)S(1)}, f32[128,256]{1,0:T(8,128)S(1)}, u32[]{:S(2)}, u32[]{:S(2)}) collective-permute-start(f32[128,256]{1,0:T(8,128)S(1)} %dynamic-slice_add_fusion), channel_id=1, source_target_pairs={{0,4},{1,9},{2,6},{3,11},{4,0},{5,13},{6,2},{7,15},{8,12},{9,1},{1... | collective-permute-start | bytes 393224 | tf_op jit(solution)/shard_map/ppermute | solution.py:333
  40.7 13.8 %collective-permute-start.8 = (f32[256,256]{1,0:T(8,128)S(1)}, f32[256,256]{1,0:T(8,128)S(1)}, u32[]{:S(2)}, u32[]{:S(2)}) collective-permute-start(f32[256,256]{1,0:T(8,128)S(1)} %get-tuple-element.22.light_ref), channel_id=1, source_target_pairs={{0,1},{1,0},{2,3},{3,2},{4,5},{5,4},{6,7},{7,6},{8,9},{9,8},{10,11... | collective-permute-start | bytes 786440 | tf_op jit(solution)/shard_map/ppermute | solution.py:336
  42.8 7.5 %collective-permute-start.18 = (f32[128,256]{1,0:T(8,128)S(1)}, f32[128,256]{1,0:T(8,128)S(1)}, u32[]{:S(2)}, u32[]{:S(2)}) collective-permute-start(f32[128,256]{1,0:T(8,128)S(1)} %add.25), channel_id=1, source_target_pairs={{0,8},{1,3},{2,10},{3,1},{4,12},{5,7},{6,14},{7,5},{8,0},{9,11},{1... | collective-permute-start | bytes 393224 | tf_op jit(solution)/shard_map/ppermute | solution.py:333
  45.3 17.3 %copy-start.3 = (f32[2,256,256]{2,1,0:T(8,128)S(1)}, f32[2,256,256]{2,1,0:T(8,128)}, u32[]{:S(2)}) copy-start(f32[2,256,256]{2,1,0:T(8,128)} %spec_ref.5) | copy-start | bytes 1572868
  46.3 9.3 %collective-permute-start.12 = (f32[128,128]{1,0:T(8,128)S(1)}, f32[128,128]{1,0:T(8,128)S(1)}, u32[]{:S(2)}, u32[]{:S(2)}) collective-permute-start(f32[128,128]{1,0:T(8,128)S(1)} %get-tuple-element.26), channel_id=1, source_target_pairs={{0,6},{1,7},{2,4},{3,5},{4,2},{5,3},{6,0},{7,1},{8,14},{9,15},{10,... | collective-permute-start | bytes 196616 | tf_op jit(solution)/shard_map/ppermute | solution.py:333
  49.3 13.3 %collective-permute-start.9 = (f32[256,128]{1,0:T(8,128)S(1)}, f32[256,128]{1,0:T(8,128)S(1)}, u32[]{:S(2)}, u32[]{:S(2)}) collective-permute-start(f32[256,128]{1,0:T(8,128)S(1)} %get-tuple-element.23), channel_id=1, source_target_pairs={{0,2},{1,3},{2,0},{3,1},{4,6},{5,7},{6,4},{7,5},{8,10},{9,11},{10,... | collective-permute-start | bytes 393224 | tf_op jit(solution)/shard_map/ppermute | solution.py:333
  50.3 12.3 %collective-permute-start.10 = (f32[128,256]{1,0:T(8,128)S(1)}, f32[128,256]{1,0:T(8,128)S(1)}, u32[]{:S(2)}, u32[]{:S(2)}) collective-permute-start(f32[128,256]{1,0:T(8,128)S(1)} %get-tuple-element.24), channel_id=1, source_target_pairs={{0,4},{1,5},{2,6},{3,7},{4,0},{5,1},{6,2},{7,3},{8,12},{9,13},{10,... | collective-permute-start | bytes 393224 | tf_op jit(solution)/shard_map/ppermute | solution.py:333
  50.3 12.3 %collective-permute-start.11 = (f32[128,256]{1,0:T(8,128)S(1)}, f32[128,256]{1,0:T(8,128)S(1)}, u32[]{:S(2)}, u32[]{:S(2)}) collective-permute-start(f32[128,256]{1,0:T(8,128)S(1)} %get-tuple-element.25), channel_id=1, source_target_pairs={{0,12},{1,13},{2,14},{3,15},{4,8},{5,9},{6,10},{7,11},{8,4},{9,5},... | collective-permute-start | bytes 393224 | tf_op jit(solution)/shard_map/ppermute | solution.py:333
  54.6 8.3 %collective-permute-start.19 = (f32[128,256]{1,0:T(8,128)S(1)}, f32[128,256]{1,0:T(8,128)S(1)}, u32[]{:S(2)}, u32[]{:S(2)}) collective-permute-start(f32[128,256]{1,0:T(8,128)S(1)} %add.26), channel_id=1, source_target_pairs={{0,2},{1,5},{2,0},{3,7},{4,6},{5,1},{6,4},{7,3},{8,10},{9,13},{10,... | collective-permute-start | bytes 393224 | tf_op jit(solution)/shard_map/ppermute | solution.py:333
  55.7 7.0 %collective-permute-start.13 = (f32[128,128]{1,0:T(8,128)S(1)}, f32[128,128]{1,0:T(8,128)S(1)}, u32[]{:S(2)}, u32[]{:S(2)}) collective-permute-start(f32[128,128]{1,0:T(8,128)S(1)} %get-tuple-element.27), channel_id=1, source_target_pairs={{0,14},{1,15},{2,12},{3,13},{4,10},{5,11},{6,8},{7,9},{8,6},{9,7},... | collective-permute-start | bytes 196616 | tf_op jit(solution)/shard_map/ppermute | solution.py:333
  62.8 1.6 %collective-permute-start.14 = (f32[256,256]{1,0:T(8,128)S(1)}, f32[256,256]{1,0:T(8,128)S(1)}, u32[]{:S(2)}, u32[]{:S(2)}) collective-permute-start(f32[256,256]{1,0:T(8,128)S(1)} %shard_map.81), channel_id=1, source_target_pairs={{0,1},{1,0},{2,3},{3,2},{4,5},{5,4},{6,7},{7,6},{8,9},{9,8},{10,11... | collective-permute-start | bytes 786440 | tf_op jit(solution)/shard_map/ppermute | solution.py:336
  62.9 2.3 %collective-permute-start.20 = (f32[256,256]{1,0:T(8,128)S(1)}, f32[256,256]{1,0:T(8,128)S(1)}, u32[]{:S(2)}, u32[]{:S(2)}) collective-permute-start(f32[256,256]{1,0:T(8,128)S(1)} %maximum_select_fusion.3), channel_id=1, source_target_pairs={{0,1},{1,0},{2,3},{3,2},{4,5},{5,4},{6,7},{7,6},{8,9},{9,8},{10,11... | collective-permute-start | bytes 786440 | tf_op jit(solution)/shard_map/ppermute | solution.py:336

commit v2 on v1

v2 whole, which is shorter than its diff:
```python
import functools
import math

import jax
import jax.numpy as jnp
import numpy as np
from jax import lax
from jax.experimental import pallas as pl
from jax.experimental.pallas import tpu as pltpu
from jax.sharding import PartitionSpec as P

GROUP = ("scanx", "scany", "pos")
PART_SWAP = ((0, 1), (1, 0))
VMEM = pl.BlockSpec(memory_space=pltpu.VMEM)
SMEM = pl.BlockSpec(memory_space=pltpu.SMEM)
ANY = pl.BlockSpec(memory_space=pl.ANY)
OFFSET_ROWS = 8


def f32(*shape):
    return jax.ShapeDtypeStruct(shape, jnp.float32)


def ways_of(count):
    return (0,) if count == 2 else (0, 1)


def side_of(index, way):
    return lax.rem(index + way + 1, 2)


def valid_of(index, way, count):
    neighbour = index + 2 * side_of(index, way) - 1
    return jnp.logical_and(neighbour >= 0, neighbour < count)


def block_ways(nz, nx):
    xways, zways = ways_of(nx), (0, 1)
    order = [(None, w) for w in xways] + [(w, None) for w in zways]
    return order + [(v, w) for w in xways for v in zways]


def block_places(z, x, nz, nx, origin, extent, margin):
    places = []
    for zway, xway in block_ways(nz, nx):
        span = []
        for index, way in ((z, zway), (x, xway)):
            if way is None:
                span.append(pl.ds(origin, 2 * margin))
            else:
                span.append(pl.ds(pl.multiple_of(side_of(index, way) * extent, margin), margin))
        places.append(tuple(span))
    return places


def block_valid(z, x, nz, nx):
    result = []
    for zway, xway in block_ways(nz, nx):
        ok = True
        if zway is not None:
            ok = valid_of(z, zway, nz)
        if xway is not None:
            ok = jnp.logical_and(ok, valid_of(x, xway, nx))
        result.append(ok)
    return result


def block_targets(nz, nx):
    def step(index, way, count):
        if way is None:
            return index
        to = index + (1 if (index + way) % 2 == 0 else -1)
        return to if 0 <= to < count else None

    def target(ways, z, x, c):
        tz, tx = step(z, ways[0], nz), step(x, ways[1], nx)
        return (z, x, 1 - c) if tz is None or tx is None else (tz, tx, c)

    return [functools.partial(target, ways) for ways in block_ways(nz, nx)]


def pack_places(shapes):
    lanes = min(width for _, width in shapes)
    at, places = 0, []
    for height, width in shapes:
        height -= OFFSET_ROWS
        places.append([])
        for col in range(0, width, lanes):
            places[-1].append((at, col, height))
            at += height
    return places


def permutation(sizes, target):
    nz, nx, nc = sizes
    pairs = []
    for z in range(nz):
        for x in range(nx):
            for c in range(nc):
                tz, tx, tc = target(z, x, c)
                pairs.append(((z * nx + x) * nc + c, (tz * nx + tx) * nc + tc))
    return pairs


def dft_tables(length):
    index = np.arange(length, dtype=np.int32)
    phase = (index[:, None] * index[None, :]) % length
    angle = phase.astype(np.float32) * np.float32(2.0 * math.pi / length)
    scale = np.float32(1.0 / math.sqrt(length))
    cosine = (np.cos(angle) * scale).astype(jnp.bfloat16)
    sine = (np.sin(angle) * scale).astype(jnp.bfloat16)
    table_a = np.block([[cosine, sine], [-sine, cosine]])
    table_b = np.block([[cosine, -sine], [sine, cosine]])
    return table_a.astype(jnp.bfloat16), table_b.astype(jnp.bfloat16)


def aligned(row):
    return pl.multiple_of((row // 8) * 8, 8), lax.rem(row, 8)


def rows_up(block, shift):
    count, width = block.shape
    groups = pltpu.roll(block.reshape(count // 8, 8, width), lax.rem(8 - shift, 8), axis=1)
    at = lax.broadcasted_iota(jnp.int32, (count // 8 - 1, 8, width), 1)
    return jnp.where(at < 8 - shift, groups[:-1], groups[1:]).reshape(count - 8, width)


def rows_down(block, shift):
    count, width = block.shape
    groups = pltpu.roll(block.reshape(count // 8, 8, width), shift, axis=1)
    blank = jnp.zeros((1, 8, width), block.dtype)
    at = lax.broadcasted_iota(jnp.int32, (count // 8 + 1, 8, width), 1)
    early = jnp.concatenate([groups, blank])
    late = jnp.concatenate([blank, groups])
    return jnp.where(at >= shift, early, late).reshape(count + 8, width)


def halo_blocks_kernel(nz, nx, off_ref, spec_ref, *refs):
    z, x, c = (lax.axis_index(a) for a in GROUP)
    *outs, sems = refs
    margin = spec_ref.shape[1] // 2
    copies = []
    for k, (rows, cols) in enumerate(block_places(z, x, nz, nx, 0, margin, margin)):
        height, width = outs[k].shape
        height -= OFFSET_ROWS
        copies.append(
            pltpu.make_async_copy(spec_ref.at[c, rows, cols], outs[k].at[pl.ds(0, height), :], sems.at[k])
        )
        copies[-1].start()
    for out in outs:
        height, width = out.shape
        lane = lax.broadcasted_iota(jnp.int32, (OFFSET_ROWS, width), 1)
        note = jnp.zeros((OFFSET_ROWS, width), jnp.float32)
        for j in range(off_ref.shape[0]):
            for k in range(2):
                note = jnp.where(lane == 2 * j + k, off_ref[j, k].astype(jnp.float32), note)
        out[height - OFFSET_ROWS :, :] = note
    for copy in copies:
        copy.wait()


def fetch_kernel(*refs):
    *refs, sems = refs
    count = len(refs) // 2
    copies = [pltpu.make_async_copy(refs[k], refs[count + k], sems.at[k]) for k in range(count)]
    for copy in copies:
        copy.start()
    for copy in copies:
        copy.wait()


def pack_kernel(unused_ref, *refs):
    *blocks, out = refs
    for part, places in zip(blocks, pack_places([b.shape for b in blocks])):
        for at, col, height in places:
            out[at : at + height, :] = part[:height, col : col + out.shape[1]]


def positions_kernel(nz, nx, off_ref, spec_ref, probe_ref, amp_ref, ta_ref, tb_ref, unused_ref, packed_ref, *refs):
    z, x, c = (lax.axis_index(a) for a in GROUP)
    *blocks, obj_own, obj_other, probe_own, probe_other, padded = refs
    size = probe_ref.shape[1]
    margin = size // 2
    tile = spec_ref.shape[1]
    npos = amp_ref.shape[0]

    padded[:, margin : margin + tile, margin : margin + tile] = spec_ref[...]
    ways = block_ways(nz, nx)
    if len(ways_of(nx)) == 1:
        far_cols = pl.ds(pl.multiple_of((1 - side_of(x, 0)) * (margin + tile), margin), margin)
        padded[:, :, far_cols] = jnp.zeros((2, tile + size, margin), jnp.float32)
    places = block_places(z, x, nz, nx, margin, margin + tile, margin)
    for block, (rows, cols), ok, packed in zip(
        blocks, places, block_valid(z, x, nz, nx), pack_places([b.shape for b in blocks])
    ):
        height, width = block.shape[0] - OFFSET_ROWS, block.shape[1]

        @pl.when(ok)
        def _():
            padded[c, rows, cols] = block[:height, :]
            pieces = [packed_ref[at : at + height, :] for at, _, _ in packed]
            padded[1 - c, rows, cols] = jnp.concatenate(pieces, axis=1) if len(pieces) > 1 else pieces[0]

        @pl.when(jnp.logical_not(ok))
        def _():
            padded[:, rows, cols] = jnp.zeros((2, height, width), jnp.float32)

    lane = lax.broadcasted_iota(jnp.int32, (size + 8, size), 1)
    first = c == 0
    table_a = ta_ref[...]
    table_b = tb_ref[...]
    probe_real = probe_ref[0]
    probe_imag = probe_ref[1]

    def side_by_side(both):
        return jnp.concatenate([both[:size], both[size:]], axis=1)

    grad_real = jnp.zeros((size, size), jnp.float32)
    grad_imag = jnp.zeros((size, size), jnp.float32)
    for j in range(npos):
        row, col = off_ref[j, 0], off_ref[j, 1]

        base, shift = aligned(row)

        def patch(part):
            rows = padded[part, pl.ds(base, size + 8), :]
            mixed = rows_up(jnp.where(lane >= col, rows[:, :size], rows[:, size:]), shift)
            return pltpu.roll(mixed, lax.rem(size - col, size), axis=1)

        patch_real, patch_imag = patch(0), patch(1)
        exit_real = probe_real * patch_real - probe_imag * patch_imag
        exit_imag = probe_real * patch_imag + probe_imag * patch_real
        wave = jnp.concatenate([exit_real, exit_imag], axis=0).astype(jnp.bfloat16)
        half = jnp.dot(table_a, wave, preferred_element_type=jnp.float32).astype(jnp.bfloat16)
        far = jnp.dot(side_by_side(half), table_b, preferred_element_type=jnp.float32)
        far_real, far_imag = far[:, :size], far[:, size:]
        power = far_real * far_real + far_imag * far_imag
        ratio = amp_ref[j].astype(jnp.float32) * jnp.minimum(lax.rsqrt(power), 1.0 / 0.2)
        projected = jnp.concatenate([far_real * ratio, far_imag * ratio], axis=0).astype(jnp.bfloat16)
        back_half = jnp.dot(table_b, projected, preferred_element_type=jnp.float32).astype(jnp.bfloat16)
        back = jnp.dot(side_by_side(back_half), table_a, preferred_element_type=jnp.float32)
        diff_real = back[:, :size] - exit_real
        diff_imag = back[:, size:] - exit_imag
        term_real = probe_real * diff_real + probe_imag * diff_imag
        term_imag = probe_real * diff_imag - probe_imag * diff_real
        obj_own[j] = jnp.where(first, term_real, term_imag)
        obj_other[j] = jnp.where(first, term_imag, term_real)
        grad_real += patch_real * diff_real + patch_imag * diff_imag
        grad_imag += patch_real * diff_imag - patch_imag * diff_real
    probe_own[...] = jnp.where(first, grad_real, grad_imag)
    probe_other[...] = jnp.where(first, grad_imag, grad_real)


def gather_kernel(nz, nx, off_ref, off_other_ref, own_ref, other_ref, center_ref, *refs):
    z, x = lax.axis_index("scanx"), lax.axis_index("scany")
    *blocks, grad = refs
    npos, size, _ = own_ref.shape
    margin = size // 2
    tile = center_ref.shape[0]
    lane = lax.broadcasted_iota(jnp.int32, (size + 8, size), 1)
    grad[...] = jnp.zeros_like(grad)
    for offs, terms in ((off_ref, own_ref), (off_other_ref, other_ref)):
        for j in range(npos):
            row, col = offs[j, 0], offs[j, 1]
            base, shift = aligned(row)
            term = rows_down(pltpu.roll(terms[j], col, axis=1), shift)
            low = jnp.where(lane >= col, term, 0.0)
            rows = pl.ds(base, size + 8)
            grad[rows, :size] += low
            grad[rows, size:] += term - low
    center_ref[...] = grad[margin : margin + tile, margin : margin + tile]
    for block, (rows, cols) in zip(blocks, block_places(z, x, nz, nx, margin, margin + tile, margin)):
        block[...] = grad[rows, cols]


def light_kernel(nz, nx, off_ref, note_ref, probe_ref, unused_ref, light_ref, power_ref, total):
    z, x, c = (lax.axis_index(a) for a in GROUP)
    size = probe_ref.shape[1]
    margin = size // 2
    tile = light_ref.shape[0]
    npos = off_ref.shape[0]
    power_ref[...] = probe_ref[0] * probe_ref[0] + probe_ref[1] * probe_ref[1]
    total[...] = jnp.zeros_like(total)
    lane = lax.broadcasted_iota(jnp.int32, (size, size), 1)

    def add(row, col, ok):
        ok = jnp.logical_and(ok, jnp.logical_and(jnp.abs(row) < tile, jnp.abs(col) < tile))

        @pl.when(ok)
        def _():
            base, shift = aligned(row + tile)
            moved = pltpu.roll(power_ref[...], lax.rem(col + size, size), axis=1)
            keep = jnp.logical_and(lane >= col, lane < col + size)
            total[pl.ds(base, size + 8), :] += rows_down(jnp.where(keep, moved, 0.0), shift)

    for j in range(npos):
        add(off_ref[j, 0] - margin, off_ref[j, 1] - margin, True)
    for k, ((zway, xway), ok) in enumerate(zip(block_ways(nz, nx), block_valid(z, x, nz, nx))):
        down = 0 if zway is None else (2 * side_of(z, zway) - 1) * tile
        right = 0 if xway is None else (2 * side_of(x, xway) - 1) * tile
        for j in range(npos):
            at = 2 * (k * npos + j)
            add(note_ref[at] + down - margin, note_ref[at + 1] + right - margin, ok)
    light_ref[...] = total[tile : 2 * tile, :]


def update_kernel(nz, nx, spec_ref, center_ref, light_ref, other_light_ref, *refs):
    z, x, c = (lax.axis_index(a) for a in GROUP)
    *blocks, out_ref, grad = refs
    tile = center_ref.shape[0]
    margin = tile // 2
    grad[...] = center_ref[...]
    places = block_places(z, x, nz, nx, 0, tile - margin, margin)
    for block, (rows, cols), ok in zip(blocks, places, block_valid(z, x, nz, nx)):

        @pl.when(ok)
        def _():
            grad[rows, cols] += block[...]

    out_ref[...] = spec_ref[c] + grad[...] / (light_ref[...] + other_light_ref[...] + 1.0)


def add_kernel(a_ref, b_ref, *refs):
    refs[-1][...] = a_ref[...] + b_ref[...]


def add_after(a, b, *earlier):
    return call(add_kernel, [f32(*a.shape)], [VMEM, VMEM] + [ANY] * len(earlier))(a, b, *earlier)[0]


def call(kernel, out_shape, specs, scratch=()):
    return pl.pallas_call(
        kernel,
        out_shape=out_shape,
        in_specs=specs,
        out_specs=jax.tree.map(lambda _: VMEM, out_shape),
        scratch_shapes=list(scratch),
        compiler_params=pltpu.CompilerParams(vmem_limit_bytes=32 * 1024 * 1024),
    )


def shards(sizes, specimen, probe_wave, amplitudes, offsets):
    nz, nx, nc = sizes
    size = probe_wave.shape[1]
    margin = size // 2
    tile = specimen.shape[1]
    npos = offsets.shape[0]
    z, x, c = (lax.axis_index(a) for a in GROUP)
    ways = block_ways(nz, nx)
    targets = block_targets(nz, nx)

    def send(value, target):
        return lax.ppermute(value, GROUP, permutation(sizes, target))

    def to_core(value):
        return lax.ppermute(value, "pos", PART_SWAP)

    shapes = [(tile if v is None else margin, tile if w is None else margin) for v, w in ways]
    blocks = call(
        functools.partial(halo_blocks_kernel, nz, nx),
        [f32(h + OFFSET_ROWS, w) for h, w in shapes],
        [SMEM, ANY],
        [pltpu.SemaphoreType.DMA((len(ways),))],
    )(offsets, specimen)
    recv = [send(block, target) for block, target in zip(blocks, targets)]

    table_a, table_b = (jnp.asarray(t) for t in dft_tables(size))
    late = (specimen, probe_wave, amplitudes, table_a, table_b)
    specimen_v, probe_v, amp_v, ta_v, tb_v = call(
        fetch_kernel,
        [jax.ShapeDtypeStruct(a.shape, a.dtype) for a in late],
        [ANY] * len(late),
        [pltpu.SemaphoreType.DMA((len(late),))],
    )(*late)

    lanes = min(w for _, w in shapes)
    packed = call(
        pack_kernel,
        [f32(sum(h * w for h, w in shapes) // lanes, lanes)],
        [ANY] + [VMEM] * len(recv),
    )(probe_v, *recv)[0]
    packed_other = to_core(packed)
    off_other = to_core(offsets)

    notes = jnp.concatenate([r[h, : 2 * npos] for r, (h, _) in zip(recv, shapes)]).astype(jnp.int32)
    light = call(
        functools.partial(light_kernel, nz, nx),
        [f32(tile, tile)],
        [SMEM, SMEM, VMEM, ANY],
        [pltpu.VMEM((size, size), jnp.float32), pltpu.VMEM((3 * tile, size), jnp.float32)],
    )(offsets, notes, probe_v, packed)[0]

    obj_own, obj_other, probe_own, probe_other = call(
        functools.partial(positions_kernel, nz, nx),
        [f32(npos, size, size), f32(npos, size, size), f32(size, size), f32(size, size)],
        [SMEM] + [VMEM] * 5 + [ANY] + [VMEM] * (1 + len(recv)),
        [pltpu.VMEM((2, tile + size, tile + size), jnp.float32)],
    )(offsets, specimen_v, probe_v, amp_v, ta_v, tb_v, light, packed_other, *recv)

    obj_recv = to_core(obj_other)
    held = probe_own + to_core(probe_other)
    other_light = to_core(light)
    zbits = [("z", 1 << k) for k in range(nz.bit_length() - 1)]
    xbits = [("x", 1 << k) for k in range(nx.bit_length() - 1)]
    orders = (xbits[:1] + zbits + xbits[1:], zbits + xbits)

    def stage(k):
        def target(z, x, c):
            axis, bit = orders[c][k]
            return (z ^ bit, x, c) if axis == "z" else (z, x ^ bit, c)

        return target

    center, *pieces = call(
        functools.partial(gather_kernel, nz, nx),
        [f32(tile, tile)] + [f32(h, w) for h, w in shapes],
        [SMEM, SMEM, VMEM, VMEM],
        [pltpu.VMEM((tile + size, tile + size), jnp.float32)],
    )(offsets, off_other, obj_own, obj_recv)
    arrived = [send(piece, target) for piece, target in zip(pieces, targets)]

    rows = size // 2
    mine = jnp.where(c == 0, lax.rem(x, 2), lax.rem(z, 2))
    keep = lax.dynamic_slice_in_dim(held, mine * rows, rows, 0)
    give = lax.dynamic_slice_in_dim(held, (1 - mine) * rows, rows, 0)
    earlier = [(center,), tuple(arrived[:2])]
    keep = add_after(keep, send(give, stage(0)), *earlier[0])
    for k in range(1, len(orders[0])):
        keep = add_after(keep, send(keep, stage(k)), *(earlier[k] if k < len(earlier) else ()))
    away = send(keep, stage(0))
    summed = jnp.where(mine == 0, jnp.concatenate([keep, away]), jnp.concatenate([away, keep]))
    summed_other = to_core(summed)
    total_grad = jnp.where(c == 0, jnp.stack([summed, summed_other]), jnp.stack([summed_other, summed]))
    step_size = 1.0 / math.sqrt(npos * nz * nx * nc)
    new_probe = probe_wave + total_grad * step_size

    part = call(
        functools.partial(update_kernel, nz, nx),
        [f32(tile, tile)],
        [VMEM] * (4 + len(arrived)),
        [pltpu.VMEM((tile, tile), jnp.float32)],
    )(specimen_v, center, light, other_light, *arrived)[0]
    part_other = to_core(part)
    new_specimen = jnp.where(c == 0, jnp.stack([part, part_other]), jnp.stack([part_other, part]))
    return (new_specimen, new_probe)


def solution(mesh):
    sizes = tuple(mesh.shape[a] for a in GROUP)
    placed = (
        P(None, ("groups", "scanx"), "scany"),
        P(None, "groups", None),
        P(("groups", "scanx", "scany", "pos"), None, None),
        P(("groups", "scanx", "scany", "pos"), None),
    )
    return jax.shard_map(
        functools.partial(shards, sizes),
        mesh=mesh,
        in_specs=placed,
        out_specs=(P(None, ("groups", "scanx"), "scany"), P(None, "groups", None)),
        check_vma=False,
    )
```

time: 66.4 us -> 59.1 us (0.89)
  starting transfers between devices: 22.7 us -> 16.2 us
  waiting for transfers between devices: 26.8 us -> 22.2 us
  local copies, waits for them, and re-layouts: 6.06 us -> 7.73 us
  Pallas kernels: 7.82 us -> 8.88 us
  other arithmetic: 1.91 us -> 2.72 us
    ppermute x12 -> x14, waiting for transfers between devices: 22.9 us -> 18.1 us  [send(): return lax.ppermute(value, GROUP, permutation(sizes, target))]
    ppermute x12 -> x14, starting transfers between devices: 19.5 us -> 15 us  [send(): return lax.ppermute(value, GROUP, permutation(sizes, target))]
    unnamed x16 -> x24, local copies, waits for them, and re-layouts: 5.12 us -> 7.61 us
    ppermute x9 -> x7, starting transfers between devices: 3.17 us -> 1.2 us  [to_core(): return lax.ppermute(value, 'pos', PART_SWAP)]
    pallas_call x1, Pallas kernels: 3.55 us -> 4.89 us  [shards(): call(functools.partial(positions_kernel, nz, nx), [f32(npos, size, size),...]
    add x1, other arithmetic: 0.03 us -> 0.98 us  [shards(): held = probe_own + to_core(probe_other)]
    reshape x2 -> x0, local copies, waits for them, and re-layouts: 0.84 us -> none  [shards(): flat = jnp.concatenate([offsets.reshape(-1), to_core(offsets).reshape(-1)])]
    pallas_call x3 -> x8, Pallas kernels: 4.13 us -> 3.87 us  [the longest x1 1.55 us: shards(): call(functools.partial(light_kernel, nz, nx), [f32(tile, tile)], [SMEM, S...]
  transfers between devices with their start and end apart: 21 -> 21, of which waited for: 10 -> 9; matrix products, arithmetic and copies ran while one was open for 3% -> 3% of each run, Pallas kernels for 6% -> 5%
where the time goes in v2:
time: 59.1 us; the launch traced here: 58.6 us
  waiting for transfers between devices  22.2 us (38%)
  starting transfers between devices  16.2 us (27%)
  Pallas kernels  8.88 us (15%)
  local copies, waits for them, and re-layouts  7.73 us (13%)
  other arithmetic  2.72 us (5%)
  between operations  0.85 us (1%)
    ppermute x14, waiting for transfers between devices, send(): return lax.ppermute(value, GROUP, permutation(sizes, target))  18.1 us
    ppermute x14, starting transfers between devices, send(): return lax.ppermute(value, GROUP, permutation(sizes, target))  15 us
    unnamed x24, local copies, waits for them, and re-layouts  7.61 us
    pallas_call x1, Pallas kernels, shards(): call(functools.partial(positions_kernel, nz, nx), [f32(npos, size, size),...  4.89 us
    ppermute x7, waiting for transfers between devices, to_core(): return lax.ppermute(value, 'pos', PART_SWAP)  4.14 us
    pallas_call x1, Pallas kernels, shards(): call(functools.partial(light_kernel, nz, nx), [f32(tile, tile)], [SMEM, S...  1.55 us
    ppermute x7, starting transfers between devices, to_core(): return lax.ppermute(value, 'pos', PART_SWAP)  1.2 us
  transfers between devices with their start and end apart: 21, of which 9 were waited for; matrix products, arithmetic and copies ran while one was open for 3% of the time, Pallas kernels for 5%

profile of v2, /device:TPU:0, one launch (start us, length us, event | category | flops | bytes accessed | tf_op | source)
XLA Modules:
  0.0 58.6 jit_solution(4983487667972022523)
XLA Ops:
  0.6 0.0 copy-start
  0.6 1.0 %copy-done = f32[2,256,256]{2,1,0:T(8,128)S(1)} copy-done((f32[2,256,256]{2,1,0:T(8,128)S(1)}, f32[2,256,256]{2,1,0:T(8,128)}, u32[]{:S(2)}) %copy-start) | copy-done | bytes 524312
  1.7 0.7 %copy-done.10 = s32[2,2]{1,0:T(2,128)S(1)} copy-done((s32[2,2]{1,0:T(2,128)S(1)}, s32[2,2]{1,0:T(2,128)}, u32[]{:S(2)}) %copy-start.10) | copy-done | bytes 40
  2.4 1.0 %shard_map.78 = (f32[264,128]{1,0:T(8,128)S(1)}, f32[136,256]{1,0:T(8,128)S(1)}, f32[136,256]{1,0:T(8,128)S(1)}, f32[136,128]{1,0:T(8,128)S(1)}, f32[136,128]{1,0:T(8,128)S(1)}) custom-call(s32[2,2]{1,0:T(2,128)S(1)} %copy-done.10, f32[2,256,256]{2,1,0:T(8,128)S(1)} %copy-done), custom_call_target="tpu_custom_call" | custom-call | tf_op jit(solution)/shard_map/pallas_call | solution.py:359
  3.4 0.5 collective-permute-start.5
  3.9 5.1 %collective-permute-start.2 = (f32[136,256]{1,0:T(8,128)S(1)}, f32[136,256]{1,0:T(8,128)S(1)}, u32[]{:S(2)}, u32[]{:S(2)}) collective-permute-start(f32[136,256]{1,0:T(8,128)S(1)} %get-tuple-element.28), channel_id=1, source_target_pairs={{0,4},{1,5},{2,6},{3,7},{4,0},{5,1},{6,2},{7,3},{8,12},{9,13},{10,... | collective-permute-start | bytes 417800 | tf_op jit(solution)/shard_map/ppermute | solution.py:353
  8.9 0.0 collective-permute-start.3
  9.0 0.5 collective-permute-start.1
  9.5 1.7 %collective-permute-start.4 = (f32[136,128]{1,0:T(8,128)S(1)}, f32[136,128]{1,0:T(8,128)S(1)}, u32[]{:S(2)}, u32[]{:S(2)}) collective-permute-start(f32[136,128]{1,0:T(8,128)S(1)} %get-tuple-element.30), channel_id=1, source_target_pairs={{0,6},{1,7},{2,4},{3,5},{4,2},{5,3},{6,0},{7,1},{8,14},{9,15},{10,... | collective-permute-start | bytes 208904 | tf_op jit(solution)/shard_map/ppermute | solution.py:353
  11.1 0.0 copy-done.1
  11.1 1.0 %copy-done.4 = bf16[512,512]{1,0:T(8,128)(2,1)S(1)} copy-done((bf16[512,512]{1,0:T(8,128)(2,1)S(1)}, bf16[512,512]{1,0:T(8,128)(2,1)}, u32[]{:S(2)}) %copy-start.4) | copy-done | bytes 524312
  12.2 1.0 %copy-done.5 = bf16[512,512]{1,0:T(8,128)(2,1)S(1)} copy-done((bf16[512,512]{1,0:T(8,128)(2,1)S(1)}, bf16[512,512]{1,0:T(8,128)(2,1)}, u32[]{:S(2)}) %copy-start.5) | copy-done | bytes 524312
  13.2 0.9 %copy-done.6 = bf16[2,256,256]{2,1,0:T(8,128)(2,1)S(1)} copy-done((bf16[2,256,256]{2,1,0:T(8,128)(2,1)S(1)}, bf16[2,256,256]{2,1,0:T(8,128)(2,1)}, u32[]{:S(2)}) %copy-start.6) | copy-done | bytes 262168
  14.2 0.2 shard_map.77
  14.4 0.0 copy-start.2
  14.4 0.8 %copy-done.2 = bf16[512,512]{1,0:T(8,128)(2,1)} copy-done((bf16[512,512]{1,0:T(8,128)(2,1)}, bf16[512,512]{1,0:T(8,128)(2,1)S(1)}, u32[]{:S(2)}) %copy-start.2) | copy-done | bytes 524312
  15.2 0.7 %copy-done.8 = bf16[2,256,256]{2,1,0:T(8,128)(2,1)} copy-done((bf16[2,256,256]{2,1,0:T(8,128)(2,1)}, bf16[2,256,256]{2,1,0:T(8,128)(2,1)S(1)}, u32[]{:S(2)}) %copy-start.8) | copy-done | bytes 262168
  15.9 0.0 collective-permute-done.5.refs_4_
  15.9 0.0 collective-permute-done.4.refs_3_
  15.9 0.5 collective-permute-done.1.refs_0_
  16.4 0.0 collective-permute-done.2.refs_1_
  16.4 0.0 collective-permute-done.3.refs_2_
  16.5 0.1 collective-permute-start.6
  16.6 0.1 concatenate.31
  16.7 0.7 %copy-done.11 = s32[2,2]{1,0:T(2,128)S(1)} copy-done((s32[2,2]{1,0:T(2,128)S(1)}, s32[2,2]{1,0:T(2,128)}, u32[]{:S(2)}) %copy-start.11) | copy-done | bytes 40
  17.4 1.5 %shard_map.80.unused_ref.light_ref = f32[256,256]{1,0:T(8,128)S(1)} custom-call(s32[2,2]{1,0:T(2,128)S(1)} %copy-done.11, s32[20]{0:T(128)S(1)} %convert_element_type.3.note_ref, f32[2,256,256]{2,1,0:T(8,128)S(1)} %get-tuple-element.23.unused_ref.probe_ref, f32[1024,128]{1,0:T(8,128)S(1)} %shard_map.79.unused_ref), custom_call_target="tpu_custom_call" | custom-call | tf_op jit(solution)/shard_map/pallas_call | solution.py:386
  18.9 0.0 collective-permute-done.6.packed_ref
  19.0 4.9 %shard_map.81 = (f32[2,256,256]{2,1,0:T(8,128)S(1)}, f32[2,256,256]{2,1,0:T(8,128)}, f32[256,256]{1,0:T(8,128)S(1)}, f32[256,256]{1,0:T(8,128)}) custom-call(s32[2,2]{1,0:T(2,128)S(1)} %copy-done.11, f32[2,256,256]{2,1,0:T(8,128)S(1)} %get-tuple-element.22.spec_ref, f32[2,256,256]{2,1,0:T(8,128)S(1)} %get-tuple-element.23.unused_ref.probe_ref, ...), custom_call_target="tpu_custom_call" | custom-call | tf_op jit(solution)/shard_map/pallas_call | solution.py:393
  23.8 0.7 %copy-done.7 = f32[256,256]{1,0:T(8,128)} copy-done((f32[256,256]{1,0:T(8,128)}, f32[256,256]{1,0:T(8,128)S(1)}, u32[]{:S(2)}) %copy-start.7) | copy-done | bytes 262168
  24.5 0.5 collective-permute-start.7
  25.0 0.0 collective-permute-start.15
  25.0 2.1 %collective-permute-done.15 = f32[256,256]{1,0:T(8,128)S(1)} collective-permute-done((f32[256,256]{1,0:T(8,128)}, f32[256,256]{1,0:T(8,128)S(1)}, u32[]{:S(2)}, u32[]{:S(2)}) %collective-permute-start.15) | collective-permute-done | bytes 262176 | tf_op jit(solution)/shard_map/ppermute | solution.py:356
  27.1 1.0 %add.12 = f32[256,256]{1,0:T(8,128)S(1)} add(f32[256,256]{1,0:T(8,128)} %copy-done.7, f32[256,256]{1,0:T(8,128)S(1)} %collective-permute-done.15) | non-fusion elementwise | flops 65536 | bytes 786432 | tf_op jit(solution)/shard_map/add | solution.py:401
  28.1 1.2 %collective-permute-start.16 = (f32[128,256]{1,0:T(8,128)S(1)}, f32[128,256]{1,0:T(8,128)S(1)}, u32[]{:S(2)}, u32[]{:S(2)}) collective-permute-start(f32[128,256]{1,0:T(8,128)S(1)} %get-tuple-element.42), channel_id=1, source_target_pairs={{0,2},{1,5},{2,0},{3,7},{4,6},{5,1},{6,4},{7,3},{8,10},{9,13},{10,... | collective-permute-start | bytes 393224 | tf_op jit(solution)/shard_map/ppermute | solution.py:353
  29.4 0.0 collective-permute-start
  29.4 1.1 %collective-permute-done.off_other_ref = s32[2,2]{1,0:T(2,128)S(1)} collective-permute-done((s32[2,2]{1,0:T(2,128)S(1)}, s32[2,2]{1,0:T(2,128)S(1)}, u32[]{:S(2)}, u32[]{:S(2)}) %collective-permute-start) | collective-permute-done | bytes 48 | tf_op jit(solution)/shard_map/ppermute | solution.py:356
  30.5 0.0 collective-permute-done.7.other_ref
  30.5 1.0 %shard_map.82 = (f32[256,256]{1,0:T(8,128)S(1)}, f32[256,128]{1,0:T(8,128)S(1)}, f32[128,256]{1,0:T(8,128)S(1)}, f32[128,256]{1,0:T(8,128)S(1)}, f32[128,128]{1,0:T(8,128)S(1)}, /*index=5*/f32[128,128]{1,0:T(8,128)S(1)}) custom-call(s32[2,2]{1,0:T(2,128)S(1)} %copy-done.11, s32[2,2]{1,0:T(2,128)S(1)} %collective-permute-done.off_other_ref, ...), custom_call_target="tpu_custom_call" | custom-call | tf_op jit(solution)/shard_map/pallas_call | solution.py:414
  31.5 1.6 %collective-permute-done.16.b_ref = f32[128,256]{1,0:T(8,128)S(1)} collective-permute-done((f32[128,256]{1,0:T(8,128)S(1)}, f32[128,256]{1,0:T(8,128)S(1)}, u32[]{:S(2)}, u32[]{:S(2)}) %collective-permute-start.16) | collective-permute-done | bytes 131104 | tf_op jit(solution)/shard_map/ppermute | solution.py:353
  33.2 0.9 %collective-permute-start.17 = (f32[128,256]{1,0:T(8,128)S(1)}, f32[128,256]{1,0:T(8,128)S(1)}, u32[]{:S(2)}, u32[]{:S(2)}) collective-permute-start(f32[128,256]{1,0:T(8,128)S(1)} %shard_map.84.a_ref), channel_id=1, source_target_pairs={{0,4},{1,9},{2,6},{3,11},{4,0},{5,13},{6,2},{7,15},{8,12},{9,1},{1... | collective-permute-start | bytes 393224 | tf_op jit(solution)/shard_map/ppermute | solution.py:353
  34.1 1.2 %collective-permute-start.10 = (f32[128,256]{1,0:T(8,128)S(1)}, f32[128,256]{1,0:T(8,128)S(1)}, u32[]{:S(2)}, u32[]{:S(2)}) collective-permute-start(f32[128,256]{1,0:T(8,128)S(1)} %get-tuple-element.36), channel_id=1, source_target_pairs={{0,4},{1,5},{2,6},{3,7},{4,0},{5,1},{6,2},{7,3},{8,12},{9,13},{10,... | collective-permute-start | bytes 393224 | tf_op jit(solution)/shard_map/ppermute | solution.py:353
  35.3 1.1 %collective-permute-start.9 = (f32[256,128]{1,0:T(8,128)S(1)}, f32[256,128]{1,0:T(8,128)S(1)}, u32[]{:S(2)}, u32[]{:S(2)}) collective-permute-start(f32[256,128]{1,0:T(8,128)S(1)} %get-tuple-element.35), channel_id=1, source_target_pairs={{0,2},{1,3},{2,0},{3,1},{4,6},{5,7},{6,4},{7,5},{8,10},{9,11},{10,... | collective-permute-start | bytes 393224 | tf_op jit(solution)/shard_map/ppermute | solution.py:353
  36.4 0.0 collective-permute-start.8
  36.4 3.6 %collective-permute-done.17.b_ref = f32[128,256]{1,0:T(8,128)S(1)} collective-permute-done((f32[128,256]{1,0:T(8,128)S(1)}, f32[128,256]{1,0:T(8,128)S(1)}, u32[]{:S(2)}, u32[]{:S(2)}) %collective-permute-start.17) | collective-permute-done | bytes 131104 | tf_op jit(solution)/shard_map/ppermute | solution.py:353
  40.0 1.4 %collective-permute-done.10.refs_1_ = f32[128,256]{1,0:T(8,128)S(1)} collective-permute-done((f32[128,256]{1,0:T(8,128)S(1)}, f32[128,256]{1,0:T(8,128)S(1)}, u32[]{:S(2)}, u32[]{:S(2)}) %collective-permute-start.10) | collective-permute-done | bytes 131104 | tf_op jit(solution)/shard_map/ppermute | solution.py:353
  41.4 0.0 collective-permute-done.9.refs_0_
  41.4 1.4 %collective-permute-start.18 = (f32[128,256]{1,0:T(8,128)S(1)}, f32[128,256]{1,0:T(8,128)S(1)}, u32[]{:S(2)}, u32[]{:S(2)}) collective-permute-start(f32[128,256]{1,0:T(8,128)S(1)} %shard_map.85.a_ref), channel_id=1, source_target_pairs={{0,8},{1,3},{2,10},{3,1},{4,12},{5,7},{6,14},{7,5},{8,0},{9,11},{1... | collective-permute-start | bytes 393224 | tf_op jit(solution)/shard_map/ppermute | solution.py:353
  42.8 0.0 collective-permute-start.11
  42.8 5.8 %collective-permute-done.18.b_ref = f32[128,256]{1,0:T(8,128)S(1)} collective-permute-done((f32[128,256]{1,0:T(8,128)S(1)}, f32[128,256]{1,0:T(8,128)S(1)}, u32[]{:S(2)}, u32[]{:S(2)}) %collective-permute-start.18) | collective-permute-done | bytes 131104 | tf_op jit(solution)/shard_map/ppermute | solution.py:353
  48.6 1.4 %collective-permute-start.19 = (f32[128,256]{1,0:T(8,128)S(1)}, f32[128,256]{1,0:T(8,128)S(1)}, u32[]{:S(2)}, u32[]{:S(2)}) collective-permute-start(f32[128,256]{1,0:T(8,128)S(1)} %shard_map.86), channel_id=1, source_target_pairs={{0,2},{1,5},{2,0},{3,7},{4,6},{5,1},{6,4},{7,3},{8,10},{9,13},{10,... | collective-permute-start | bytes 393224 | tf_op jit(solution)/shard_map/ppermute | solution.py:353
  50.0 0.0 collective-permute-start.12
  50.1 0.0 collective-permute-start.13
  50.1 0.0 collective-permute-done.8.other_light_ref
  50.1 5.2 %collective-permute-done.12.refs_3_ = f32[128,128]{1,0:T(8,128)S(1)} collective-permute-done((f32[128,128]{1,0:T(8,128)S(1)}, f32[128,128]{1,0:T(8,128)S(1)}, u32[]{:S(2)}, u32[]{:S(2)}) %collective-permute-start.12) | collective-permute-done | bytes 65568 | tf_op jit(solution)/shard_map/ppermute | solution.py:353
  55.2 0.0 collective-permute-done.13.refs_4_
  55.2 0.0 collective-permute-done.11.refs_2_
  55.2 0.1 shard_map.83
  55.3 0.1 collective-permute-start.14
  55.4 0.0 collective-permute-done.19
  55.5 0.5 collective-permute-start.20
  56.0 0.9 %collective-permute-done.14 = f32[256,256]{1,0:T(8,128)S(1)} collective-permute-done((f32[256,256]{1,0:T(8,128)S(1)}, f32[256,256]{1,0:T(8,128)S(1)}, u32[]{:S(2)}, u32[]{:S(2)}) %collective-permute-start.14) | collective-permute-done | bytes 262176 | tf_op jit(solution)/shard_map/ppermute | solution.py:356
  56.9 0.8 %maximum_select_fusion = f32[2,256,256]{2,1,0:T(8,128)} fusion(f32[1,256,256]{2,1,0:T(8,128)S(1)} %bitcast.18, f32[1,256,256]{2,1,0:T(8,128)S(1)} %bitcast.16, pred[]{:T(512)S(6)} %eq.8), kind=kLoop, calls=%fused_computation | loop fusion | flops 393216 | bytes 1048577 | tf_op jit(solution)/shard_map/jit(_where)/select_n | solution.py:444
  57.8 0.0 collective-permute-done.20
  57.8 0.9 %fusion.1 = f32[2,256,256]{2,1,0:T(8,128)} fusion(f32[2,256,256]{2,1,0:T(8,128)S(1)} %copy-done.1, f32[1,256,256]{2,1,0:T(8,128)S(1)} %bitcast.19, f32[1,256,256]{2,1,0:T(8,128)S(1)} %maximum_select_fusion.2, pred[]{:T(512)S(6)} %eq.8), kind=kLoop, calls=%fused_computation.3 | loop fusion | flops 655360 | bytes 1572865 | tf_op jit(solution)/shard_map/add | solution.py:435
  (25 shorter events, 0.2 us)
Async XLA Ops:
  0.6 1.0 %copy-start = (f32[2,256,256]{2,1,0:T(8,128)S(1)}, f32[2,256,256]{2,1,0:T(8,128)}, u32[]{:S(2)}) copy-start(f32[2,256,256]{2,1,0:T(8,128)} %spec_ref.1) | copy-start | bytes 1572868
  1.7 0.7 %copy-start.10 = (s32[2,2]{1,0:T(2,128)S(1)}, s32[2,2]{1,0:T(2,128)}, u32[]{:S(2)}) copy-start(s32[2,2]{1,0:T(2,128)} %off_ref.7) | copy-start | bytes 52
  2.4 8.8 %copy-start.1 = (f32[2,256,256]{2,1,0:T(8,128)S(1)}, f32[2,256,256]{2,1,0:T(8,128)}, u32[]{:S(2)}) copy-start(f32[2,256,256]{2,1,0:T(8,128)} %refs_1_.1) | copy-start | bytes 1572868
  3.4 12.5 %collective-permute-start.5 = (f32[136,128]{1,0:T(8,128)S(1)}, f32[136,128]{1,0:T(8,128)S(1)}, u32[]{:S(2)}, u32[]{:S(2)}) collective-permute-start(f32[136,128]{1,0:T(8,128)S(1)} %get-tuple-element.31), channel_id=1, source_target_pairs={{0,1},{1,0},{2,3},{3,2},{4,10},{5,11},{6,8},{7,9},{8,6},{9,7},{10,... | collective-permute-start | bytes 208904 | tf_op jit(solution)/shard_map/ppermute | solution.py:353
  3.9 12.6 %collective-permute-start.2 = (f32[136,256]{1,0:T(8,128)S(1)}, f32[136,256]{1,0:T(8,128)S(1)}, u32[]{:S(2)}, u32[]{:S(2)}) collective-permute-start(f32[136,256]{1,0:T(8,128)S(1)} %get-tuple-element.28), channel_id=1, source_target_pairs={{0,4},{1,5},{2,6},{3,7},{4,0},{5,1},{6,2},{7,3},{8,12},{9,13},{10,... | collective-permute-start | bytes 417800 | tf_op jit(solution)/shard_map/ppermute | solution.py:353
  8.9 7.5 %collective-permute-start.3 = (f32[136,256]{1,0:T(8,128)S(1)}, f32[136,256]{1,0:T(8,128)S(1)}, u32[]{:S(2)}, u32[]{:S(2)}) collective-permute-start(f32[136,256]{1,0:T(8,128)S(1)} %get-tuple-element.29), channel_id=1, source_target_pairs={{0,1},{1,0},{2,3},{3,2},{4,8},{5,9},{6,10},{7,11},{8,4},{9,5},{10,... | collective-permute-start | bytes 417800 | tf_op jit(solution)/shard_map/ppermute | solution.py:353
  9.0 7.5 %collective-permute-start.1 = (f32[264,128]{1,0:T(8,128)S(1)}, f32[264,128]{1,0:T(8,128)S(1)}, u32[]{:S(2)}, u32[]{:S(2)}) collective-permute-start(f32[264,128]{1,0:T(8,128)S(1)} %get-tuple-element.27), channel_id=1, source_target_pairs={{0,2},{1,3},{2,0},{3,1},{4,6},{5,7},{6,4},{7,5},{8,10},{9,11},{10,... | collective-permute-start | bytes 405512 | tf_op jit(solution)/shard_map/ppermute | solution.py:353
  9.5 6.4 %collective-permute-start.4 = (f32[136,128]{1,0:T(8,128)S(1)}, f32[136,128]{1,0:T(8,128)S(1)}, u32[]{:S(2)}, u32[]{:S(2)}) collective-permute-start(f32[136,128]{1,0:T(8,128)S(1)} %get-tuple-element.30), channel_id=1, source_target_pairs={{0,6},{1,7},{2,4},{3,5},{4,2},{5,3},{6,0},{7,1},{8,14},{9,15},{10,... | collective-permute-start | bytes 208904 | tf_op jit(solution)/shard_map/ppermute | solution.py:353
  11.1 1.0 %copy-start.4 = (bf16[512,512]{1,0:T(8,128)(2,1)S(1)}, bf16[512,512]{1,0:T(8,128)(2,1)}, u32[]{:S(2)}) copy-start(bf16[512,512]{1,0:T(8,128)(2,1)} %constant.30.clone.refs_3_) | copy-start | bytes 1572868
  12.2 1.0 %copy-start.5 = (bf16[512,512]{1,0:T(8,128)(2,1)S(1)}, bf16[512,512]{1,0:T(8,128)(2,1)}, u32[]{:S(2)}) copy-start(bf16[512,512]{1,0:T(8,128)(2,1)} %constant.31.clone.refs_4_) | copy-start | bytes 1572868
  13.2 0.9 %copy-start.6 = (bf16[2,256,256]{2,1,0:T(8,128)(2,1)S(1)}, bf16[2,256,256]{2,1,0:T(8,128)(2,1)}, u32[]{:S(2)}) copy-start(bf16[2,256,256]{2,1,0:T(8,128)(2,1)} %refs_2_.1) | copy-start | bytes 786436
  14.4 0.8 %copy-start.2 = (bf16[512,512]{1,0:T(8,128)(2,1)}, bf16[512,512]{1,0:T(8,128)(2,1)S(1)}, u32[]{:S(2)}) copy-start(bf16[512,512]{1,0:T(8,128)(2,1)S(1)} %get-tuple-element.26.tb_ref) | copy-start | bytes 1572868
  15.2 0.7 %copy-start.8 = (bf16[2,256,256]{2,1,0:T(8,128)(2,1)}, bf16[2,256,256]{2,1,0:T(8,128)(2,1)S(1)}, u32[]{:S(2)}) copy-start(bf16[2,256,256]{2,1,0:T(8,128)(2,1)S(1)} %get-tuple-element.24.amp_ref) | copy-start | bytes 786436
  16.5 2.4 %collective-permute-start.6 = (f32[1024,128]{1,0:T(8,128)S(1)}, f32[1024,128]{1,0:T(8,128)}, u32[]{:S(2)}, u32[]{:S(2)}) collective-permute-start(f32[1024,128]{1,0:T(8,128)S(1)} %shard_map.79.unused_ref), channel_id=1, source_target_pairs={{0,1},{1,0},{2,3},{3,2},{4,5},{5,4},{6,7},{7,6},{8,9},{9,8},{10,11... | collective-permute-start | bytes 1572872 | tf_op jit(solution)/shard_map/ppermute | solution.py:356
  16.7 0.7 %copy-start.11 = (s32[2,2]{1,0:T(2,128)S(1)}, s32[2,2]{1,0:T(2,128)}, u32[]{:S(2)}) copy-start(s32[2,2]{1,0:T(2,128)} %off_ref.7) | copy-start | bytes 52
  17.4 1.6 %copy-start.3 = (bf16[512,512]{1,0:T(8,128)(2,1)S(1)}, bf16[512,512]{1,0:T(8,128)(2,1)}, u32[]{:S(2)}) copy-start(bf16[512,512]{1,0:T(8,128)(2,1)} %copy-done.2) | copy-start | bytes 1572868
  17.4 1.6 %copy-start.9 = (bf16[2,256,256]{2,1,0:T(8,128)(2,1)S(1)}, bf16[2,256,256]{2,1,0:T(8,128)(2,1)}, u32[]{:S(2)}) copy-start(bf16[2,256,256]{2,1,0:T(8,128)(2,1)} %copy-done.8) | copy-start | bytes 786436
  23.8 0.7 %copy-start.7 = (f32[256,256]{1,0:T(8,128)}, f32[256,256]{1,0:T(8,128)S(1)}, u32[]{:S(2)}) copy-start(f32[256,256]{1,0:T(8,128)S(1)} %get-tuple-element.40) | copy-start | bytes 786436
  24.5 6.0 %collective-permute-start.7 = (f32[2,256,256]{2,1,0:T(8,128)}, f32[2,256,256]{2,1,0:T(8,128)S(1)}, u32[]{:S(2)}, u32[]{:S(2)}) collective-permute-start(f32[2,256,256]{2,1,0:T(8,128)} %get-tuple-element.33), channel_id=1, source_target_pairs={{0,1},{1,0},{2,3},{3,2},{4,5},{5,4},{6,7},{7,6},{8,9},{9,8},{10,11... | collective-permute-start | bytes 1572872 | tf_op jit(solution)/shard_map/ppermute | solution.py:356
  25.0 2.1 %collective-permute-start.15 = (f32[256,256]{1,0:T(8,128)}, f32[256,256]{1,0:T(8,128)S(1)}, u32[]{:S(2)}, u32[]{:S(2)}) collective-permute-start(f32[256,256]{1,0:T(8,128)} %get-tuple-element.41), channel_id=1, source_target_pairs={{0,1},{1,0},{2,3},{3,2},{4,5},{5,4},{6,7},{7,6},{8,9},{9,8},{10,11... | collective-permute-start | bytes 786440 | tf_op jit(solution)/shard_map/ppermute | solution.py:356
  28.1 5.0 %collective-permute-start.16 = (f32[128,256]{1,0:T(8,128)S(1)}, f32[128,256]{1,0:T(8,128)S(1)}, u32[]{:S(2)}, u32[]{:S(2)}) collective-permute-start(f32[128,256]{1,0:T(8,128)S(1)} %get-tuple-element.42), channel_id=1, source_target_pairs={{0,2},{1,5},{2,0},{3,7},{4,6},{5,1},{6,4},{7,3},{8,10},{9,13},{10,... | collective-permute-start | bytes 393224 | tf_op jit(solution)/shard_map/ppermute | solution.py:353
  29.4 1.1 %collective-permute-start = (s32[2,2]{1,0:T(2,128)S(1)}, s32[2,2]{1,0:T(2,128)S(1)}, u32[]{:S(2)}, u32[]{:S(2)}) collective-permute-start(s32[2,2]{1,0:T(2,128)S(1)} %copy-done.11), channel_id=1, source_target_pairs={{0,1},{1,0},{2,3},{3,2},{4,5},{5,4},{6,7},{7,6},{8,9},{9,8},{10,11... | collective-permute-start | bytes 56 | tf_op jit(solution)/shard_map/ppermute | solution.py:356
  33.2 6.8 %collective-permute-start.17 = (f32[128,256]{1,0:T(8,128)S(1)}, f32[128,256]{1,0:T(8,128)S(1)}, u32[]{:S(2)}, u32[]{:S(2)}) collective-permute-start(f32[128,256]{1,0:T(8,128)S(1)} %shard_map.84.a_ref), channel_id=1, source_target_pairs={{0,4},{1,9},{2,6},{3,11},{4,0},{5,13},{6,2},{7,15},{8,12},{9,1},{1... | collective-permute-start | bytes 393224 | tf_op jit(solution)/shard_map/ppermute | solution.py:353
  34.1 7.3 %collective-permute-start.10 = (f32[128,256]{1,0:T(8,128)S(1)}, f32[128,256]{1,0:T(8,128)S(1)}, u32[]{:S(2)}, u32[]{:S(2)}) collective-permute-start(f32[128,256]{1,0:T(8,128)S(1)} %get-tuple-element.36), channel_id=1, source_target_pairs={{0,4},{1,5},{2,6},{3,7},{4,0},{5,1},{6,2},{7,3},{8,12},{9,13},{10,... | collective-permute-start | bytes 393224 | tf_op jit(solution)/shard_map/ppermute | solution.py:353
  35.3 6.1 %collective-permute-start.9 = (f32[256,128]{1,0:T(8,128)S(1)}, f32[256,128]{1,0:T(8,128)S(1)}, u32[]{:S(2)}, u32[]{:S(2)}) collective-permute-start(f32[256,128]{1,0:T(8,128)S(1)} %get-tuple-element.35), channel_id=1, source_target_pairs={{0,2},{1,3},{2,0},{3,1},{4,6},{5,7},{6,4},{7,5},{8,10},{9,11},{10,... | collective-permute-start | bytes 393224 | tf_op jit(solution)/shard_map/ppermute | solution.py:353
  36.4 13.6 %collective-permute-start.8 = (f32[256,256]{1,0:T(8,128)S(1)}, f32[256,256]{1,0:T(8,128)S(1)}, u32[]{:S(2)}, u32[]{:S(2)}) collective-permute-start(f32[256,256]{1,0:T(8,128)S(1)} %shard_map.80.unused_ref.light_ref), channel_id=1, source_target_pairs={{0,1},{1,0},{2,3},{3,2},{4,5},{5,4},{6,7},{7,6},{8,9},{9,8},{10,11... | collective-permute-start | bytes 786440 | tf_op jit(solution)/shard_map/ppermute | solution.py:356
  41.4 7.2 %collective-permute-start.18 = (f32[128,256]{1,0:T(8,128)S(1)}, f32[128,256]{1,0:T(8,128)S(1)}, u32[]{:S(2)}, u32[]{:S(2)}) collective-permute-start(f32[128,256]{1,0:T(8,128)S(1)} %shard_map.85.a_ref), channel_id=1, source_target_pairs={{0,8},{1,3},{2,10},{3,1},{4,12},{5,7},{6,14},{7,5},{8,0},{9,11},{1... | collective-permute-start | bytes 393224 | tf_op jit(solution)/shard_map/ppermute | solution.py:353
  42.8 12.4 %collective-permute-start.11 = (f32[128,256]{1,0:T(8,128)S(1)}, f32[128,256]{1,0:T(8,128)S(1)}, u32[]{:S(2)}, u32[]{:S(2)}) collective-permute-start(f32[128,256]{1,0:T(8,128)S(1)} %get-tuple-element.37), channel_id=1, source_target_pairs={{0,1},{1,0},{2,3},{3,2},{4,8},{5,9},{6,10},{7,11},{8,4},{9,5},{10,... | collective-permute-start | bytes 393224 | tf_op jit(solution)/shard_map/ppermute | solution.py:353
  48.6 6.8 %collective-permute-start.19 = (f32[128,256]{1,0:T(8,128)S(1)}, f32[128,256]{1,0:T(8,128)S(1)}, u32[]{:S(2)}, u32[]{:S(2)}) collective-permute-start(f32[128,256]{1,0:T(8,128)S(1)} %shard_map.86), channel_id=1, source_target_pairs={{0,2},{1,5},{2,0},{3,7},{4,6},{5,1},{6,4},{7,3},{8,10},{9,13},{10,... | collective-permute-start | bytes 393224 | tf_op jit(solution)/shard_map/ppermute | solution.py:353
  50.0 5.2 %collective-permute-start.12 = (f32[128,128]{1,0:T(8,128)S(1)}, f32[128,128]{1,0:T(8,128)S(1)}, u32[]{:S(2)}, u32[]{:S(2)}) collective-permute-start(f32[128,128]{1,0:T(8,128)S(1)} %get-tuple-element.38), channel_id=1, source_target_pairs={{0,6},{1,7},{2,4},{3,5},{4,2},{5,3},{6,0},{7,1},{8,14},{9,15},{10,... | collective-permute-start | bytes 196616 | tf_op jit(solution)/shard_map/ppermute | solution.py:353
  50.1 5.2 %collective-permute-start.13 = (f32[128,128]{1,0:T(8,128)S(1)}, f32[128,128]{1,0:T(8,128)S(1)}, u32[]{:S(2)}, u32[]{:S(2)}) collective-permute-start(f32[128,128]{1,0:T(8,128)S(1)} %get-tuple-element.39), channel_id=1, source_target_pairs={{0,1},{1,0},{2,3},{3,2},{4,10},{5,11},{6,8},{7,9},{8,6},{9,7},{10,... | collective-permute-start | bytes 196616 | tf_op jit(solution)/shard_map/ppermute | solution.py:353
  55.3 1.6 %collective-permute-start.14 = (f32[256,256]{1,0:T(8,128)S(1)}, f32[256,256]{1,0:T(8,128)S(1)}, u32[]{:S(2)}, u32[]{:S(2)}) collective-permute-start(f32[256,256]{1,0:T(8,128)S(1)} %shard_map.83), channel_id=1, source_target_pairs={{0,1},{1,0},{2,3},{3,2},{4,5},{5,4},{6,7},{7,6},{8,9},{9,8},{10,11... | collective-permute-start | bytes 786440 | tf_op jit(solution)/shard_map/ppermute | solution.py:356
  55.5 2.3 %collective-permute-start.20 = (f32[256,256]{1,0:T(8,128)S(1)}, f32[256,256]{1,0:T(8,128)S(1)}, u32[]{:S(2)}, u32[]{:S(2)}) collective-permute-start(f32[256,256]{1,0:T(8,128)S(1)} %maximum_select_fusion.3), channel_id=1, source_target_pairs={{0,1},{1,0},{2,3},{3,2},{4,5},{5,4},{6,7},{7,6},{8,9},{9,8},{10,11... | collective-permute-start | bytes 786440 | tf_op jit(solution)/shard_map/ppermute | solution.py:356

commit v3 on v2

--- a/solution.py
+++ b/solution.py
@@ -14,6 +14,7 @@
 VMEM = pl.BlockSpec(memory_space=pltpu.VMEM)
 SMEM = pl.BlockSpec(memory_space=pltpu.SMEM)
 ANY = pl.BlockSpec(memory_space=pl.ANY)
+HBM = pl.BlockSpec(memory_space=pltpu.HBM)
 OFFSET_ROWS = 8
 
 
@@ -135,10 +136,12 @@
     return jnp.where(at >= shift, early, late).reshape(count + 8, width)
 
 
-def halo_blocks_kernel(nz, nx, off_ref, spec_ref, *refs):
+def halo_blocks_kernel(nz, nx, off_hbm, spec_ref, *refs):
     z, x, c = (lax.axis_index(a) for a in GROUP)
-    *outs, sems = refs
+    *outs, off_ref, off_sem, sems = refs
     margin = spec_ref.shape[1] // 2
+    off_copy = pltpu.make_async_copy(off_hbm, off_ref, off_sem)
+    off_copy.start()
     copies = []
     for k, (rows, cols) in enumerate(block_places(z, x, nz, nx, 0, margin, margin)):
         height, width = outs[k].shape
@@ -147,6 +150,7 @@
             pltpu.make_async_copy(spec_ref.at[c, rows, cols], outs[k].at[pl.ds(0, height), :], sems.at[k])
         )
         copies[-1].start()
+    off_copy.wait()
     for out in outs:
         height, width = out.shape
         lane = lax.broadcasted_iota(jnp.int32, (OFFSET_ROWS, width), 1)
@@ -176,9 +180,11 @@
             out[at : at + height, :] = part[:height, col : col + out.shape[1]]
 
 
-def positions_kernel(nz, nx, off_ref, spec_ref, probe_ref, amp_ref, ta_ref, tb_ref, unused_ref, packed_ref, *refs):
+def positions_kernel(nz, nx, off_hbm, spec_ref, probe_ref, amp_ref, ta_ref, tb_ref, unused_ref, packed_ref, *refs):
     z, x, c = (lax.axis_index(a) for a in GROUP)
-    *blocks, obj_own, obj_other, probe_own, probe_other, padded = refs
+    *blocks, obj_own, obj_other, probe_own, probe_other, padded, off_ref, off_sem = refs
+    off_copy = pltpu.make_async_copy(off_hbm, off_ref, off_sem)
+    off_copy.start()
     size = probe_ref.shape[1]
     margin = size // 2
     tile = spec_ref.shape[1]
@@ -207,6 +213,7 @@
 
     lane = lax.broadcasted_iota(jnp.int32, (size + 8, size), 1)
     first = c == 0
+    off_copy.wait()
     table_a = ta_ref[...]
     table_b = tb_ref[...]
     probe_real = probe_ref[0]
@@ -251,15 +258,22 @@
     probe_other[...] = jnp.where(first, grad_imag, grad_real)
 
 
-def gather_kernel(nz, nx, off_ref, off_other_ref, own_ref, other_ref, center_ref, *refs):
-    z, x = lax.axis_index("scanx"), lax.axis_index("scany")
-    *blocks, grad = refs
+def gather_kernel(nz, nx, off_hbm, off_other_hbm, own_ref, other_ref, middle_ref, *refs):
+    x = lax.axis_index("scany")
+    *blocks, grad, off_ref, off_other_ref, sems = refs
+    copies = [
+        pltpu.make_async_copy(off_hbm, off_ref, sems.at[0]),
+        pltpu.make_async_copy(off_other_hbm, off_other_ref, sems.at[1]),
+    ]
+    for copy in copies:
+        copy.start()
     npos, size, _ = own_ref.shape
     margin = size // 2
-    tile = center_ref.shape[0]
+    tile = middle_ref.shape[1]
     lane = lax.broadcasted_iota(jnp.int32, (size + 8, size), 1)
     grad[...] = jnp.zeros_like(grad)
-    for offs, terms in ((off_ref, own_ref), (off_other_ref, other_ref)):
+    for copy, offs, terms in zip(copies, (off_ref, off_other_ref), (own_ref, other_ref)):
+        copy.wait()
         for j in range(npos):
             row, col = offs[j, 0], offs[j, 1]
             base, shift = aligned(row)
@@ -268,12 +282,34 @@
             rows = pl.ds(base, size + 8)
             grad[rows, :size] += low
             grad[rows, size:] += term - low
-    center_ref[...] = grad[margin : margin + tile, margin : margin + tile]
-    for block, (rows, cols) in zip(blocks, block_places(z, x, nz, nx, margin, margin + tile, margin)):
-        block[...] = grad[rows, cols]
-
-
-def light_kernel(nz, nx, off_ref, note_ref, probe_ref, unused_ref, light_ref, power_ref, total):
+    middle_ref[...] = grad[:, margin : margin + tile]
+    for block, way in zip(blocks, ways_of(nx)):
+        at = pl.multiple_of(side_of(x, way) * (margin + tile), margin)
+        block[...] = grad[:, pl.ds(at, margin)]
+
+
+def fold_kernel(nz, nx, middle_ref, *refs):
+    z, x = lax.axis_index("scanx"), lax.axis_index("scany")
+    ways = ways_of(nx)
+    blocks, (center_ref, *edges, total) = refs[: len(ways)], refs[len(ways) :]
+    tile = center_ref.shape[0]
+    margin = tile // 2
+    total[...] = middle_ref[...]
+    for block, way in zip(blocks, ways):
+        at = pl.multiple_of(side_of(x, way) * (tile - margin), margin)
+
+        @pl.when(valid_of(x, way, nx))
+        def _():
+            total[:, pl.ds(at, margin)] += block[...]
+
+    center_ref[...] = total[margin : margin + tile, :]
+    for way, edge in enumerate(edges):
+        edge[...] = total[pl.ds(pl.multiple_of(side_of(z, way) * (margin + tile), margin), margin), :]
+
+
+def light_kernel(nz, nx, off_hbm, note_ref, probe_ref, unused_ref, light_ref, power_ref, total, off_ref, off_sem):
+    off_copy = pltpu.make_async_copy(off_hbm, off_ref, off_sem)
+    off_copy.start()
     z, x, c = (lax.axis_index(a) for a in GROUP)
     size = probe_ref.shape[1]
     margin = size // 2
@@ -293,6 +329,7 @@
             keep = jnp.logical_and(lane >= col, lane < col + size)
             total[pl.ds(base, size + 8), :] += rows_down(jnp.where(keep, moved, 0.0), shift)
 
+    off_copy.wait()
     for j in range(npos):
         add(off_ref[j, 0] - margin, off_ref[j, 1] - margin, True)
     for k, ((zway, xway), ok) in enumerate(zip(block_ways(nz, nx), block_valid(z, x, nz, nx))):
@@ -304,18 +341,18 @@
     light_ref[...] = total[tile : 2 * tile, :]
 
 
-def update_kernel(nz, nx, spec_ref, center_ref, light_ref, other_light_ref, *refs):
-    z, x, c = (lax.axis_index(a) for a in GROUP)
-    *blocks, out_ref, grad = refs
+def update_kernel(nz, spec_ref, center_ref, light_ref, other_light_ref, *refs):
+    z, c = lax.axis_index("scanx"), lax.axis_index("pos")
+    *edges, out_ref, grad = refs
     tile = center_ref.shape[0]
     margin = tile // 2
     grad[...] = center_ref[...]
-    places = block_places(z, x, nz, nx, 0, tile - margin, margin)
-    for block, (rows, cols), ok in zip(blocks, places, block_valid(z, x, nz, nx)):
-
-        @pl.when(ok)
+    for way, edge in enumerate(edges):
+        at = pl.multiple_of(side_of(z, way) * (tile - margin), margin)
+
+        @pl.when(valid_of(z, way, nz))
         def _():
-            grad[rows, cols] += block[...]
+            grad[pl.ds(at, margin), :] += edge[...]
 
     out_ref[...] = spec_ref[c] + grad[...] / (light_ref[...] + other_light_ref[...] + 1.0)
 
@@ -335,7 +372,7 @@
         in_specs=specs,
         out_specs=jax.tree.map(lambda _: VMEM, out_shape),
         scratch_shapes=list(scratch),
-        compiler_params=pltpu.CompilerParams(vmem_limit_bytes=32 * 1024 * 1024),
+        compiler_params=pltpu.CompilerParams(vmem_limit_bytes=16 * 1024 * 1024),
     )
 
 
@@ -355,12 +392,13 @@
     def to_core(value):
         return lax.ppermute(value, "pos", PART_SWAP)
 
+    off_scratch = pltpu.SMEM(offsets.shape, jnp.int32)
     shapes = [(tile if v is None else margin, tile if w is None else margin) for v, w in ways]
     blocks = call(
         functools.partial(halo_blocks_kernel, nz, nx),
         [f32(h + OFFSET_ROWS, w) for h, w in shapes],
-        [SMEM, ANY],
-        [pltpu.SemaphoreType.DMA((len(ways),))],
+        [HBM, HBM],
+        [off_scratch, pltpu.SemaphoreType.DMA, pltpu.SemaphoreType.DMA((len(ways),))],
     )(offsets, specimen)
     recv = [send(block, target) for block, target in zip(blocks, targets)]
 
@@ -369,7 +407,7 @@
     specimen_v, probe_v, amp_v, ta_v, tb_v = call(
         fetch_kernel,
         [jax.ShapeDtypeStruct(a.shape, a.dtype) for a in late],
-        [ANY] * len(late),
+        [HBM] * len(late),
         [pltpu.SemaphoreType.DMA((len(late),))],
     )(*late)
 
@@ -386,15 +424,20 @@
     light = call(
         functools.partial(light_kernel, nz, nx),
         [f32(tile, tile)],
-        [SMEM, SMEM, VMEM, ANY],
-        [pltpu.VMEM((size, size), jnp.float32), pltpu.VMEM((3 * tile, size), jnp.float32)],
+        [HBM, SMEM, VMEM, ANY],
+        [
+            pltpu.VMEM((size, size), jnp.float32),
+            pltpu.VMEM((3 * tile, size), jnp.float32),
+            off_scratch,
+            pltpu.SemaphoreType.DMA,
+        ],
     )(offsets, notes, probe_v, packed)[0]
 
     obj_own, obj_other, probe_own, probe_other = call(
         functools.partial(positions_kernel, nz, nx),
         [f32(npos, size, size), f32(npos, size, size), f32(size, size), f32(size, size)],
-        [SMEM] + [VMEM] * 5 + [ANY] + [VMEM] * (1 + len(recv)),
-        [pltpu.VMEM((2, tile + size, tile + size), jnp.float32)],
+        [HBM] + [VMEM] * 5 + [ANY] + [VMEM] * (1 + len(recv)),
+        [pltpu.VMEM((2, tile + size, tile + size), jnp.float32), off_scratch, pltpu.SemaphoreType.DMA],
     )(offsets, specimen_v, probe_v, amp_v, ta_v, tb_v, light, packed_other, *recv)
 
     obj_recv = to_core(obj_other)
@@ -411,37 +454,56 @@
 
         return target
 
-    center, *pieces = call(
+    xways = ways_of(nx)
+    middle, *beyond = call(
         functools.partial(gather_kernel, nz, nx),
-        [f32(tile, tile)] + [f32(h, w) for h, w in shapes],
-        [SMEM, SMEM, VMEM, VMEM],
-        [pltpu.VMEM((tile + size, tile + size), jnp.float32)],
+        [f32(tile + size, tile)] + [f32(tile + size, margin)] * len(xways),
+        [HBM, HBM, VMEM, VMEM],
+        [
+            pltpu.VMEM((tile + size, tile + size), jnp.float32),
+            off_scratch,
+            off_scratch,
+            pltpu.SemaphoreType.DMA((2,)),
+        ],
     )(offsets, off_other, obj_own, obj_recv)
-    arrived = [send(piece, target) for piece, target in zip(pieces, targets)]
+    beside = [send(piece, targets[ways.index((None, way))]) for piece, way in zip(beyond, xways)]
+    center, *edges = call(
+        functools.partial(fold_kernel, nz, nx),
+        [f32(tile, tile)] + [f32(margin, tile)] * 2,
+        [VMEM] * (1 + len(beside)),
+        [pltpu.VMEM((tile + size, tile), jnp.float32)],
+    )(middle, *beside)
+    arrived = [send(edge, targets[ways.index((way, None))]) for way, edge in enumerate(edges)]
 
     rows = size // 2
-    mine = jnp.where(c == 0, lax.rem(x, 2), lax.rem(z, 2))
+    halves = (lax.rem(x, 2), lax.rem(z, 2))
+    mine = jnp.where(c == 0, halves[0], halves[1])
+    theirs = jnp.where(c == 0, halves[1], halves[0])
     keep = lax.dynamic_slice_in_dim(held, mine * rows, rows, 0)
     give = lax.dynamic_slice_in_dim(held, (1 - mine) * rows, rows, 0)
-    earlier = [(center,), tuple(arrived[:2])]
-    keep = add_after(keep, send(give, stage(0)), *earlier[0])
-    for k in range(1, len(orders[0])):
-        keep = add_after(keep, send(keep, stage(k)), *(earlier[k] if k < len(earlier) else ()))
+    last = len(orders[0]) - 1
+    earlier = {0: (middle,), 1: (center,), last: tuple(arrived)}
+    for k in range(last + 1):
+        keep = add_after(keep, send(give if k == 0 else keep, stage(k)), *earlier.get(k, ()))
     away = send(keep, stage(0))
-    summed = jnp.where(mine == 0, jnp.concatenate([keep, away]), jnp.concatenate([away, keep]))
-    summed_other = to_core(summed)
-    total_grad = jnp.where(c == 0, jnp.stack([summed, summed_other]), jnp.stack([summed_other, summed]))
-    step_size = 1.0 / math.sqrt(npos * nz * nx * nc)
-    new_probe = probe_wave + total_grad * step_size
+
+    def joined(half, keep, away):
+        return jnp.where(half == 0, jnp.concatenate([keep, away]), jnp.concatenate([away, keep]))
+
+    def in_order(own, other):
+        return jnp.where(c == 0, jnp.stack([own, other]), jnp.stack([other, own]))
 
     part = call(
-        functools.partial(update_kernel, nz, nx),
+        functools.partial(update_kernel, nz),
         [f32(tile, tile)],
         [VMEM] * (4 + len(arrived)),
         [pltpu.VMEM((tile, tile), jnp.float32)],
     )(specimen_v, center, light, other_light, *arrived)[0]
-    part_other = to_core(part)
-    new_specimen = jnp.where(c == 0, jnp.stack([part, part_other]), jnp.stack([part_other, part]))
+    new_specimen = in_order(part, to_core(part))
+
+    step_size = 1.0 / math.sqrt(npos * nz * nx * nc)
+    total_grad = in_order(joined(mine, keep, away), joined(theirs, to_core(keep), to_core(away)))
+    new_probe = probe_v + total_grad * step_size
     return (new_specimen, new_probe)
 
 

time: 59.1 us -> 59.7 us (1.010)
  waiting for transfers between devices: 22.2 us -> 25.1 us
  local copies, waits for them, and re-layouts: 7.73 us -> 6.23 us
  starting transfers between devices: 16.2 us -> 15 us
    ppermute x14 -> x12, waiting for transfers between devices: 18.1 us -> 23 us  [send(): return lax.ppermute(value, GROUP, permutation(sizes, target))]
    ppermute x7 -> x8, waiting for transfers between devices: 4.14 us -> 2.1 us  [to_core(): return lax.ppermute(value, 'pos', PART_SWAP)]
    unnamed x24 -> x20, local copies, waits for them, and re-layouts: 7.61 us -> 6.12 us
    ppermute x14 -> x12, starting transfers between devices: 15 us -> 13.9 us  [send(): return lax.ppermute(value, GROUP, permutation(sizes, target))]
    pallas_call x3 -> x4, Pallas kernels: 2.7 us -> 3.24 us  [the longest x1 1.88 us: shards(): call(functools.partial(light_kernel, nz, nx), [f32(tile, tile)], [HBM, SM...]
    ppermute x7 -> x8, starting transfers between devices: 1.2 us -> 1.13 us  [to_core(): return lax.ppermute(value, 'pos', PART_SWAP)]
  transfers between devices with their start and end apart: 21 -> 20, of which waited for: 9 -> 9; matrix products, arithmetic and copies ran while one was open for 3% -> 3% of each run, Pallas kernels for 5% -> 4%
where the time goes in v3:
time: 59.7 us; the launch traced here: 59.3 us
  waiting for transfers between devices  25.1 us (42%)
  starting transfers between devices  15 us (25%)
  Pallas kernels  9.4 us (16%)
  local copies, waits for them, and re-layouts  6.23 us (10%)
  other arithmetic  2.73 us (5%)
  between operations  0.87 us (1%)
    ppermute x12, waiting for transfers between devices, send(): return lax.ppermute(value, GROUP, permutation(sizes, target))  23 us
    ppermute x12, starting transfers between devices, send(): return lax.ppermute(value, GROUP, permutation(sizes, target))  13.9 us
    unnamed x20, local copies, waits for them, and re-layouts  6.12 us
    pallas_call x1, Pallas kernels, shards(): call(functools.partial(positions_kernel, nz, nx), [f32(npos, size, size),...  5.26 us
    ppermute x8, waiting for transfers between devices, to_core(): return lax.ppermute(value, 'pos', PART_SWAP)  2.1 us
    pallas_call x1, Pallas kernels, shards(): call(functools.partial(light_kernel, nz, nx), [f32(tile, tile)], [HBM, SM...  1.88 us
  transfers between devices with their start and end apart: 20, of which 9 were waited for; matrix products, arithmetic and copies ran while one was open for 3% of the time, Pallas kernels for 4%

profile of v3, /device:TPU:0, one launch (start us, length us, event | category | flops | bytes accessed | tf_op | source)
XLA Modules:
  0.0 59.3 jit_solution(8876882872161129616)
XLA Ops:
  0.6 0.0 copy-start
  0.6 1.0 %copy-done = f32[2,256,256]{2,1,0:T(8,128)S(1)} copy-done((f32[2,256,256]{2,1,0:T(8,128)S(1)}, f32[2,256,256]{2,1,0:T(8,128)}, u32[]{:S(2)}) %copy-start) | copy-done | bytes 524312
  1.7 0.7 %copy-done.8 = s32[2,2]{1,0:T(2,128)S(1)} copy-done((s32[2,2]{1,0:T(2,128)S(1)}, s32[2,2]{1,0:T(2,128)}, u32[]{:S(2)}) %copy-start.8) | copy-done | bytes 40
  2.4 0.6 %shard_map.78 = (f32[264,128]{1,0:T(8,128)S(1)}, f32[136,256]{1,0:T(8,128)S(1)}, f32[136,256]{1,0:T(8,128)S(1)}, f32[136,128]{1,0:T(8,128)S(1)}, f32[136,128]{1,0:T(8,128)S(1)}) custom-call(s32[2,2]{1,0:T(2,128)S(1)} %copy-done.8, f32[2,256,256]{2,1,0:T(8,128)S(1)} %copy-done), custom_call_target="tpu_custom_call" | custom-call | tf_op jit(solution)/shard_map/pallas_call | solution.py:397
  3.0 0.5 collective-permute-start.5
  3.5 5.1 %collective-permute-start.2 = (f32[136,256]{1,0:T(8,128)S(1)}, f32[136,256]{1,0:T(8,128)S(1)}, u32[]{:S(2)}, u32[]{:S(2)}) collective-permute-start(f32[136,256]{1,0:T(8,128)S(1)} %get-tuple-element.27), channel_id=1, source_target_pairs={{0,4},{1,5},{2,6},{3,7},{4,0},{5,1},{6,2},{7,3},{8,12},{9,13},{10,... | collective-permute-start | bytes 417800 | tf_op jit(solution)/shard_map/ppermute | solution.py:390
  8.6 0.0 collective-permute-start.3
  8.6 0.5 collective-permute-start.1
  9.1 1.7 %collective-permute-start.4 = (f32[136,128]{1,0:T(8,128)S(1)}, f32[136,128]{1,0:T(8,128)S(1)}, u32[]{:S(2)}, u32[]{:S(2)}) collective-permute-start(f32[136,128]{1,0:T(8,128)S(1)} %get-tuple-element.29), channel_id=1, source_target_pairs={{0,6},{1,7},{2,4},{3,5},{4,2},{5,3},{6,0},{7,1},{8,14},{9,15},{10,... | collective-permute-start | bytes 208904 | tf_op jit(solution)/shard_map/ppermute | solution.py:390
  10.8 0.0 copy-done.1
  10.8 1.0 %copy-done.2 = bf16[512,512]{1,0:T(8,128)(2,1)S(1)} copy-done((bf16[512,512]{1,0:T(8,128)(2,1)S(1)}, bf16[512,512]{1,0:T(8,128)(2,1)}, u32[]{:S(2)}) %copy-start.2) | copy-done | bytes 524312
  11.8 1.0 %copy-done.3 = bf16[512,512]{1,0:T(8,128)(2,1)S(1)} copy-done((bf16[512,512]{1,0:T(8,128)(2,1)S(1)}, bf16[512,512]{1,0:T(8,128)(2,1)}, u32[]{:S(2)}) %copy-start.3) | copy-done | bytes 524312
  12.9 0.9 %copy-done.4 = bf16[2,256,256]{2,1,0:T(8,128)(2,1)S(1)} copy-done((bf16[2,256,256]{2,1,0:T(8,128)(2,1)S(1)}, bf16[2,256,256]{2,1,0:T(8,128)(2,1)}, u32[]{:S(2)}) %copy-start.4) | copy-done | bytes 262168
  13.8 0.2 shard_map.77
  14.0 0.0 copy-start.6
  14.0 0.0 collective-permute-done.5.refs_4_
  14.1 0.4 collective-permute-done.4.refs_3_
  14.4 1.6 %collective-permute-done.1.refs_0_ = f32[264,128]{1,0:T(8,128)S(1)} collective-permute-done((f32[264,128]{1,0:T(8,128)S(1)}, f32[264,128]{1,0:T(8,128)S(1)}, u32[]{:S(2)}, u32[]{:S(2)}) %collective-permute-start.1) | collective-permute-done | bytes 135200 | tf_op jit(solution)/shard_map/ppermute | solution.py:390
  16.1 0.0 collective-permute-done.2.refs_1_
  16.1 0.0 collective-permute-done.3.refs_2_
  16.1 0.0 copy-done.6
  16.1 0.1 collective-permute-start.6
  16.2 0.1 concatenate.51
  16.3 0.7 %copy-done.9 = s32[2,2]{1,0:T(2,128)S(1)} copy-done((s32[2,2]{1,0:T(2,128)S(1)}, s32[2,2]{1,0:T(2,128)}, u32[]{:S(2)}) %copy-start.9) | copy-done | bytes 40
  17.0 1.9 %shard_map.80.unused_ref.light_ref = f32[256,256]{1,0:T(8,128)S(1)} custom-call(s32[2,2]{1,0:T(2,128)S(1)} %copy-done.9, s32[20]{0:T(128)S(1)} %convert_element_type.3.note_ref, f32[2,256,256]{2,1,0:T(8,128)S(1)} %get-tuple-element.22.unused_ref.probe_ref, f32[1024,128]{1,0:T(8,128)S(1)} %shard_map.79.unused_ref), custom_call_target="tpu_custom_call" | custom-call | tf_op jit(solution)/shard_map/pallas_call | solution.py:424
  18.9 0.0 collective-permute-done.6.packed_ref
  18.9 0.0 copy-done.7
  18.9 5.3 %shard_map.81 = (f32[2,256,256]{2,1,0:T(8,128)S(1)}, f32[2,256,256]{2,1,0:T(8,128)}, f32[256,256]{1,0:T(8,128)S(1)}, f32[256,256]{1,0:T(8,128)}) custom-call(s32[2,2]{1,0:T(2,128)S(1)} %copy-done.9, f32[2,256,256]{2,1,0:T(8,128)S(1)} %get-tuple-element.21.spec_ref, f32[2,256,256]{2,1,0:T(8,128)S(1)} %get-tuple-element.22.unused_ref.probe_ref, ...), custom_call_target="tpu_custom_call" | custom-call | tf_op jit(solution)/shard_map/pallas_call | solution.py:436
  24.2 0.0 copy-start.5
  24.2 0.7 %copy-done.5 = f32[256,256]{1,0:T(8,128)} copy-done((f32[256,256]{1,0:T(8,128)}, f32[256,256]{1,0:T(8,128)S(1)}, u32[]{:S(2)}) %copy-start.5) | copy-done | bytes 262168
  24.9 0.5 collective-permute-start.7
  25.3 0.0 collective-permute-start.13
  25.4 0.5 collective-permute-start
  25.8 1.6 %collective-permute-done.13 = f32[256,256]{1,0:T(8,128)S(1)} collective-permute-done((f32[256,256]{1,0:T(8,128)}, f32[256,256]{1,0:T(8,128)S(1)}, u32[]{:S(2)}, u32[]{:S(2)}) %collective-permute-start.13) | collective-permute-done | bytes 262176 | tf_op jit(solution)/shard_map/ppermute | solution.py:393
  27.5 1.0 %add.12 = f32[256,256]{1,0:T(8,128)S(1)} add(f32[256,256]{1,0:T(8,128)} %copy-done.5, f32[256,256]{1,0:T(8,128)S(1)} %collective-permute-done.13) | non-fusion elementwise | flops 65536 | bytes 786432 | tf_op jit(solution)/shard_map/add | solution.py:444
  28.4 0.0 collective-permute-done.off_other_hbm
  28.5 0.0 collective-permute-done.7.other_ref
  28.5 1.2 %shard_map.82 = (f32[512,256]{1,0:T(8,128)S(1)}, f32[512,128]{1,0:T(8,128)S(1)}) custom-call(s32[2,2]{1,0:T(2,128)S(1)} %copy-done.9, s32[2,2]{1,0:T(2,128)S(1)} %collective-permute-done.off_other_hbm, f32[2,256,256]{2,1,0:T(8,128)S(1)} %get-tuple-element.31.own_ref, f32[2,256,256]{2,1,0:T(8,128)S(1)} %collective-permute-done.7.other_ref), custom_call_target="tpu_custom_call" | custom-call | tf_op jit(solution)/shard_map/pallas_call | solution.py:458
  29.6 0.8 %collective-permute-start.8 = (f32[512,128]{1,0:T(8,128)S(1)}, f32[512,128]{1,0:T(8,128)S(1)}, u32[]{:S(2)}, u32[]{:S(2)}) collective-permute-start(f32[512,128]{1,0:T(8,128)S(1)} %get-tuple-element.34), channel_id=1, source_target_pairs={{0,2},{1,3},{2,0},{3,1},{4,6},{5,7},{6,4},{7,5},{8,10},{9,11},{10,... | collective-permute-start | bytes 786440 | tf_op jit(solution)/shard_map/ppermute | solution.py:390
  30.4 1.4 %collective-permute-start.14 = (f32[128,256]{1,0:T(8,128)S(1)}, f32[128,256]{1,0:T(8,128)S(1)}, u32[]{:S(2)}, u32[]{:S(2)}) collective-permute-start(f32[128,256]{1,0:T(8,128)S(1)} %get-tuple-element.40), channel_id=1, source_target_pairs={{0,2},{1,5},{2,0},{3,7},{4,6},{5,1},{6,4},{7,3},{8,10},{9,13},{10,... | collective-permute-start | bytes 393224 | tf_op jit(solution)/shard_map/ppermute | solution.py:390
  31.8 0.0 collective-permute-start.9
  31.8 7.9 %collective-permute-done.14.b_ref = f32[128,256]{1,0:T(8,128)S(1)} collective-permute-done((f32[128,256]{1,0:T(8,128)S(1)}, f32[128,256]{1,0:T(8,128)S(1)}, u32[]{:S(2)}, u32[]{:S(2)}) %collective-permute-start.14) | collective-permute-done | bytes 131104 | tf_op jit(solution)/shard_map/ppermute | solution.py:390
  39.7 0.5 collective-permute-start.15
  40.2 0.0 collective-permute-done.8.refs_0_
  40.2 0.1 shard_map.83
  40.3 1.7 %collective-permute-start.10 = (f32[128,256]{1,0:T(8,128)S(1)}, f32[128,256]{1,0:T(8,128)S(1)}, u32[]{:S(2)}, u32[]{:S(2)}) collective-permute-start(f32[128,256]{1,0:T(8,128)S(1)} %get-tuple-element.36), channel_id=1, source_target_pairs={{0,4},{1,5},{2,6},{3,7},{4,0},{5,1},{6,2},{7,3},{8,12},{9,13},{10,... | collective-permute-start | bytes 393224 | tf_op jit(solution)/shard_map/ppermute | solution.py:390
  42.0 0.0 collective-permute-start.11
  42.0 2.8 %collective-permute-done.15.b_ref = f32[128,256]{1,0:T(8,128)S(1)} collective-permute-done((f32[128,256]{1,0:T(8,128)S(1)}, f32[128,256]{1,0:T(8,128)S(1)}, u32[]{:S(2)}, u32[]{:S(2)}) %collective-permute-start.15) | collective-permute-done | bytes 131104 | tf_op jit(solution)/shard_map/ppermute | solution.py:390
  44.8 1.0 %collective-permute-start.16 = (f32[128,256]{1,0:T(8,128)S(1)}, f32[128,256]{1,0:T(8,128)S(1)}, u32[]{:S(2)}, u32[]{:S(2)}) collective-permute-start(f32[128,256]{1,0:T(8,128)S(1)} %shard_map.86.a_ref), channel_id=1, source_target_pairs={{0,8},{1,3},{2,10},{3,1},{4,12},{5,7},{6,14},{7,5},{8,0},{9,11},{1... | collective-permute-start | bytes 393224 | tf_op jit(solution)/shard_map/ppermute | solution.py:390
  45.8 0.0 collective-permute-done.9.other_light_ref
  45.8 0.4 collective-permute-done.10.refs_0_
  46.2 0.0 collective-permute-done.11.refs_1_
  46.2 0.1 shard_map.84
  46.3 0.1 collective-permute-start.12
  46.3 5.7 %collective-permute-done.16.b_ref = f32[128,256]{1,0:T(8,128)S(1)} collective-permute-done((f32[128,256]{1,0:T(8,128)S(1)}, f32[128,256]{1,0:T(8,128)S(1)}, u32[]{:S(2)}, u32[]{:S(2)}) %collective-permute-start.16) | collective-permute-done | bytes 131104 | tf_op jit(solution)/shard_map/ppermute | solution.py:390
  52.1 0.8 %collective-permute-start.17 = (f32[128,256]{1,0:T(8,128)S(1)}, f32[128,256]{1,0:T(8,128)S(1)}, u32[]{:S(2)}, u32[]{:S(2)}) collective-permute-start(f32[128,256]{1,0:T(8,128)S(1)} %shard_map.87), channel_id=1, source_target_pairs={{0,2},{1,5},{2,0},{3,7},{4,6},{5,1},{6,4},{7,3},{8,10},{9,13},{10,... | collective-permute-start | bytes 393224 | tf_op jit(solution)/shard_map/ppermute | solution.py:390
  52.9 0.0 collective-permute-start.18
  52.9 4.2 %collective-permute-done.17 = f32[128,256]{1,0:T(8,128)S(1)} collective-permute-done((f32[128,256]{1,0:T(8,128)S(1)}, f32[128,256]{1,0:T(8,128)S(1)}, u32[]{:S(2)}, u32[]{:S(2)}) %collective-permute-start.17) | collective-permute-done | bytes 131104 | tf_op jit(solution)/shard_map/ppermute | solution.py:390
  57.1 0.0 collective-permute-start.19
  57.1 0.0 collective-permute-done.12
  57.1 0.8 %maximum_select_fusion = f32[2,256,256]{2,1,0:T(8,128)} fusion(f32[1,256,256]{2,1,0:T(8,128)S(1)} %bitcast.18, f32[1,256,256]{2,1,0:T(8,128)S(1)} %bitcast.16, pred[]{:T(512)S(6)} %eq.12), kind=kLoop, calls=%fused_computation | loop fusion | flops 393216 | bytes 1048577 | tf_op jit(solution)/shard_map/jit(_where)/select_n | solution.py:494
  58.0 0.0 collective-permute-done.18
  58.0 0.5 collective-permute-done.19
  58.5 0.9 %fusion.1 = f32[2,256,256]{2,1,0:T(8,128)} fusion(f32[2,256,256]{2,1,0:T(8,128)S(1)} %get-tuple-element.22.unused_ref.probe_ref, f32[1,256,256]{2,1,0:T(8,128)S(1)} %maximum_select_fusion.3, f32[1,256,256]{2,1,0:T(8,128)S(1)} %maximum_select_fusion.2, pred[]{:T(512)S(6)} %eq.12), kind=kLoop, calls=%fused_computation.3 | loop fusion | flops 655360 | bytes 1572865 | tf_op jit(solution)/shard_map/add | solution.py:506
  (20 shorter events, 0.2 us)
Async XLA Ops:
  0.6 1.0 %copy-start = (f32[2,256,256]{2,1,0:T(8,128)S(1)}, f32[2,256,256]{2,1,0:T(8,128)}, u32[]{:S(2)}) copy-start(f32[2,256,256]{2,1,0:T(8,128)} %spec_ref.1) | copy-start | bytes 1572868
  1.7 0.7 %copy-start.8 = (s32[2,2]{1,0:T(2,128)S(1)}, s32[2,2]{1,0:T(2,128)}, u32[]{:S(2)}) copy-start(s32[2,2]{1,0:T(2,128)} %off_hbm.7) | copy-start | bytes 52
  2.4 8.4 %copy-start.1 = (f32[2,256,256]{2,1,0:T(8,128)S(1)}, f32[2,256,256]{2,1,0:T(8,128)}, u32[]{:S(2)}) copy-start(f32[2,256,256]{2,1,0:T(8,128)} %refs_1_.1) | copy-start | bytes 1572868
  3.0 11.1 %collective-permute-start.5 = (f32[136,128]{1,0:T(8,128)S(1)}, f32[136,128]{1,0:T(8,128)S(1)}, u32[]{:S(2)}, u32[]{:S(2)}) collective-permute-start(f32[136,128]{1,0:T(8,128)S(1)} %get-tuple-element.30), channel_id=1, source_target_pairs={{0,1},{1,0},{2,3},{3,2},{4,10},{5,11},{6,8},{7,9},{8,6},{9,7},{10,... | collective-permute-start | bytes 208904 | tf_op jit(solution)/shard_map/ppermute | solution.py:390
  3.5 12.6 %collective-permute-start.2 = (f32[136,256]{1,0:T(8,128)S(1)}, f32[136,256]{1,0:T(8,128)S(1)}, u32[]{:S(2)}, u32[]{:S(2)}) collective-permute-start(f32[136,256]{1,0:T(8,128)S(1)} %get-tuple-element.27), channel_id=1, source_target_pairs={{0,4},{1,5},{2,6},{3,7},{4,0},{5,1},{6,2},{7,3},{8,12},{9,13},{10,... | collective-permute-start | bytes 417800 | tf_op jit(solution)/shard_map/ppermute | solution.py:390
  8.6 7.5 %collective-permute-start.3 = (f32[136,256]{1,0:T(8,128)S(1)}, f32[136,256]{1,0:T(8,128)S(1)}, u32[]{:S(2)}, u32[]{:S(2)}) collective-permute-start(f32[136,256]{1,0:T(8,128)S(1)} %get-tuple-element.28), channel_id=1, source_target_pairs={{0,1},{1,0},{2,3},{3,2},{4,8},{5,9},{6,10},{7,11},{8,4},{9,5},{10,... | collective-permute-start | bytes 417800 | tf_op jit(solution)/shard_map/ppermute | solution.py:390
  8.6 7.5 %collective-permute-start.1 = (f32[264,128]{1,0:T(8,128)S(1)}, f32[264,128]{1,0:T(8,128)S(1)}, u32[]{:S(2)}, u32[]{:S(2)}) collective-permute-start(f32[264,128]{1,0:T(8,128)S(1)} %get-tuple-element.26), channel_id=1, source_target_pairs={{0,2},{1,3},{2,0},{3,1},{4,6},{5,7},{6,4},{7,5},{8,10},{9,11},{10,... | collective-permute-start | bytes 405512 | tf_op jit(solution)/shard_map/ppermute | solution.py:390
  9.1 5.3 %collective-permute-start.4 = (f32[136,128]{1,0:T(8,128)S(1)}, f32[136,128]{1,0:T(8,128)S(1)}, u32[]{:S(2)}, u32[]{:S(2)}) collective-permute-start(f32[136,128]{1,0:T(8,128)S(1)} %get-tuple-element.29), channel_id=1, source_target_pairs={{0,6},{1,7},{2,4},{3,5},{4,2},{5,3},{6,0},{7,1},{8,14},{9,15},{10,... | collective-permute-start | bytes 208904 | tf_op jit(solution)/shard_map/ppermute | solution.py:390
  10.8 1.0 %copy-start.2 = (bf16[512,512]{1,0:T(8,128)(2,1)S(1)}, bf16[512,512]{1,0:T(8,128)(2,1)}, u32[]{:S(2)}) copy-start(bf16[512,512]{1,0:T(8,128)(2,1)} %constant.30.clone.refs_3_) | copy-start | bytes 1572868
  11.8 1.0 %copy-start.3 = (bf16[512,512]{1,0:T(8,128)(2,1)S(1)}, bf16[512,512]{1,0:T(8,128)(2,1)}, u32[]{:S(2)}) copy-start(bf16[512,512]{1,0:T(8,128)(2,1)} %constant.31.clone.refs_4_) | copy-start | bytes 1572868
  12.9 0.9 %copy-start.4 = (bf16[2,256,256]{2,1,0:T(8,128)(2,1)S(1)}, bf16[2,256,256]{2,1,0:T(8,128)(2,1)}, u32[]{:S(2)}) copy-start(bf16[2,256,256]{2,1,0:T(8,128)(2,1)} %refs_2_.1) | copy-start | bytes 786436
  14.0 2.1 %copy-start.6 = (bf16[2,256,256]{2,1,0:T(8,128)(2,1)}, bf16[2,256,256]{2,1,0:T(8,128)(2,1)S(1)}, u32[]{:S(2)}) copy-start(bf16[2,256,256]{2,1,0:T(8,128)(2,1)S(1)} %get-tuple-element.23.amp_ref) | copy-start | bytes 786436
  16.1 2.8 %collective-permute-start.6 = (f32[1024,128]{1,0:T(8,128)S(1)}, f32[1024,128]{1,0:T(8,128)}, u32[]{:S(2)}, u32[]{:S(2)}) collective-permute-start(f32[1024,128]{1,0:T(8,128)S(1)} %shard_map.79.unused_ref), channel_id=1, source_target_pairs={{0,1},{1,0},{2,3},{3,2},{4,5},{5,4},{6,7},{7,6},{8,9},{9,8},{10,11... | collective-permute-start | bytes 1572872 | tf_op jit(solution)/shard_map/ppermute | solution.py:393
  16.3 0.7 %copy-start.9 = (s32[2,2]{1,0:T(2,128)S(1)}, s32[2,2]{1,0:T(2,128)}, u32[]{:S(2)}) copy-start(s32[2,2]{1,0:T(2,128)} %off_hbm.7) | copy-start | bytes 52
  17.0 1.9 %copy-start.7 = (bf16[2,256,256]{2,1,0:T(8,128)(2,1)S(1)}, bf16[2,256,256]{2,1,0:T(8,128)(2,1)}, u32[]{:S(2)}) copy-start(bf16[2,256,256]{2,1,0:T(8,128)(2,1)} %copy-done.6) | copy-start | bytes 786436
  24.2 0.7 %copy-start.5 = (f32[256,256]{1,0:T(8,128)}, f32[256,256]{1,0:T(8,128)S(1)}, u32[]{:S(2)}) copy-start(f32[256,256]{1,0:T(8,128)S(1)} %get-tuple-element.38) | copy-start | bytes 786436
  24.9 3.6 %collective-permute-start.7 = (f32[2,256,256]{2,1,0:T(8,128)}, f32[2,256,256]{2,1,0:T(8,128)S(1)}, u32[]{:S(2)}, u32[]{:S(2)}) collective-permute-start(f32[2,256,256]{2,1,0:T(8,128)} %get-tuple-element.32), channel_id=1, source_target_pairs={{0,1},{1,0},{2,3},{3,2},{4,5},{5,4},{6,7},{7,6},{8,9},{9,8},{10,11... | collective-permute-start | bytes 1572872 | tf_op jit(solution)/shard_map/ppermute | solution.py:393
  25.3 2.1 %collective-permute-start.13 = (f32[256,256]{1,0:T(8,128)}, f32[256,256]{1,0:T(8,128)S(1)}, u32[]{:S(2)}, u32[]{:S(2)}) collective-permute-start(f32[256,256]{1,0:T(8,128)} %get-tuple-element.39), channel_id=1, source_target_pairs={{0,1},{1,0},{2,3},{3,2},{4,5},{5,4},{6,7},{7,6},{8,9},{9,8},{10,11... | collective-permute-start | bytes 786440 | tf_op jit(solution)/shard_map/ppermute | solution.py:393
  25.4 3.1 %collective-permute-start = (s32[2,2]{1,0:T(2,128)S(1)}, s32[2,2]{1,0:T(2,128)S(1)}, u32[]{:S(2)}, u32[]{:S(2)}) collective-permute-start(s32[2,2]{1,0:T(2,128)S(1)} %copy-done.9), channel_id=1, source_target_pairs={{0,1},{1,0},{2,3},{3,2},{4,5},{5,4},{6,7},{7,6},{8,9},{9,8},{10,11... | collective-permute-start | bytes 56 | tf_op jit(solution)/shard_map/ppermute | solution.py:393
  29.6 10.5 %collective-permute-start.8 = (f32[512,128]{1,0:T(8,128)S(1)}, f32[512,128]{1,0:T(8,128)S(1)}, u32[]{:S(2)}, u32[]{:S(2)}) collective-permute-start(f32[512,128]{1,0:T(8,128)S(1)} %get-tuple-element.34), channel_id=1, source_target_pairs={{0,2},{1,3},{2,0},{3,1},{4,6},{5,7},{6,4},{7,5},{8,10},{9,11},{10,... | collective-permute-start | bytes 786440 | tf_op jit(solution)/shard_map/ppermute | solution.py:390
  30.4 9.3 %collective-permute-start.14 = (f32[128,256]{1,0:T(8,128)S(1)}, f32[128,256]{1,0:T(8,128)S(1)}, u32[]{:S(2)}, u32[]{:S(2)}) collective-permute-start(f32[128,256]{1,0:T(8,128)S(1)} %get-tuple-element.40), channel_id=1, source_target_pairs={{0,2},{1,5},{2,0},{3,7},{4,6},{5,1},{6,4},{7,3},{8,10},{9,13},{10,... | collective-permute-start | bytes 393224 | tf_op jit(solution)/shard_map/ppermute | solution.py:390
  31.8 13.9 %collective-permute-start.9 = (f32[256,256]{1,0:T(8,128)S(1)}, f32[256,256]{1,0:T(8,128)S(1)}, u32[]{:S(2)}, u32[]{:S(2)}) collective-permute-start(f32[256,256]{1,0:T(8,128)S(1)} %shard_map.80.unused_ref.light_ref), channel_id=1, source_target_pairs={{0,1},{1,0},{2,3},{3,2},{4,5},{5,4},{6,7},{7,6},{8,9},{9,8},{10,11... | collective-permute-start | bytes 786440 | tf_op jit(solution)/shard_map/ppermute | solution.py:393
  39.7 5.0 %collective-permute-start.15 = (f32[128,256]{1,0:T(8,128)S(1)}, f32[128,256]{1,0:T(8,128)S(1)}, u32[]{:S(2)}, u32[]{:S(2)}) collective-permute-start(f32[128,256]{1,0:T(8,128)S(1)} %shard_map.85.a_ref), channel_id=1, source_target_pairs={{0,4},{1,9},{2,6},{3,11},{4,0},{5,13},{6,2},{7,15},{8,12},{9,1},{1... | collective-permute-start | bytes 393224 | tf_op jit(solution)/shard_map/ppermute | solution.py:390
  40.3 5.9 %collective-permute-start.10 = (f32[128,256]{1,0:T(8,128)S(1)}, f32[128,256]{1,0:T(8,128)S(1)}, u32[]{:S(2)}, u32[]{:S(2)}) collective-permute-start(f32[128,256]{1,0:T(8,128)S(1)} %get-tuple-element.36), channel_id=1, source_target_pairs={{0,4},{1,5},{2,6},{3,7},{4,0},{5,1},{6,2},{7,3},{8,12},{9,13},{10,... | collective-permute-start | bytes 393224 | tf_op jit(solution)/shard_map/ppermute | solution.py:390
  42.0 4.2 %collective-permute-start.11 = (f32[128,256]{1,0:T(8,128)S(1)}, f32[128,256]{1,0:T(8,128)S(1)}, u32[]{:S(2)}, u32[]{:S(2)}) collective-permute-start(f32[128,256]{1,0:T(8,128)S(1)} %get-tuple-element.37), channel_id=1, source_target_pairs={{0,1},{1,0},{2,3},{3,2},{4,8},{5,9},{6,10},{7,11},{8,4},{9,5},{10,... | collective-permute-start | bytes 393224 | tf_op jit(solution)/shard_map/ppermute | solution.py:390
  44.8 7.3 %collective-permute-start.16 = (f32[128,256]{1,0:T(8,128)S(1)}, f32[128,256]{1,0:T(8,128)S(1)}, u32[]{:S(2)}, u32[]{:S(2)}) collective-permute-start(f32[128,256]{1,0:T(8,128)S(1)} %shard_map.86.a_ref), channel_id=1, source_target_pairs={{0,8},{1,3},{2,10},{3,1},{4,12},{5,7},{6,14},{7,5},{8,0},{9,11},{1... | collective-permute-start | bytes 393224 | tf_op jit(solution)/shard_map/ppermute | solution.py:390
  46.3 10.9 %collective-permute-start.12 = (f32[256,256]{1,0:T(8,128)S(1)}, f32[256,256]{1,0:T(8,128)S(1)}, u32[]{:S(2)}, u32[]{:S(2)}) collective-permute-start(f32[256,256]{1,0:T(8,128)S(1)} %shard_map.84), channel_id=1, source_target_pairs={{0,1},{1,0},{2,3},{3,2},{4,5},{5,4},{6,7},{7,6},{8,9},{9,8},{10,11... | collective-permute-start | bytes 786440 | tf_op jit(solution)/shard_map/ppermute | solution.py:393
  52.1 5.0 %collective-permute-start.17 = (f32[128,256]{1,0:T(8,128)S(1)}, f32[128,256]{1,0:T(8,128)S(1)}, u32[]{:S(2)}, u32[]{:S(2)}) collective-permute-start(f32[128,256]{1,0:T(8,128)S(1)} %shard_map.87), channel_id=1, source_target_pairs={{0,2},{1,5},{2,0},{3,7},{4,6},{5,1},{6,4},{7,3},{8,10},{9,13},{10,... | collective-permute-start | bytes 393224 | tf_op jit(solution)/shard_map/ppermute | solution.py:390
  52.9 5.1 %collective-permute-start.18 = (f32[128,256]{1,0:T(8,128)S(1)}, f32[128,256]{1,0:T(8,128)S(1)}, u32[]{:S(2)}, u32[]{:S(2)}) collective-permute-start(f32[128,256]{1,0:T(8,128)S(1)} %shard_map.87), channel_id=1, source_target_pairs={{0,1},{1,0},{2,3},{3,2},{4,5},{5,4},{6,7},{7,6},{8,9},{9,8},{10,11... | collective-permute-start | bytes 393224 | tf_op jit(solution)/shard_map/ppermute | solution.py:393
  57.1 1.3 %collective-permute-start.19 = (f32[128,256]{1,0:T(8,128)S(1)}, f32[128,256]{1,0:T(8,128)S(1)}, u32[]{:S(2)}, u32[]{:S(2)}) collective-permute-start(f32[128,256]{1,0:T(8,128)S(1)} %collective-permute-done.17), channel_id=1, source_target_pairs={{0,1},{1,0},{2,3},{3,2},{4,5},{5,4},{6,7},{7,6},{8,9},{9,8},{10,11... | collective-permute-start | bytes 393224 | tf_op jit(solution)/shard_map/ppermute | solution.py:393

commit v4 on v2

v4 whole, which is shorter than its diff:
```python
import functools
import math

import jax
import jax.numpy as jnp
import numpy as np
from jax import lax
from jax.experimental import pallas as pl
from jax.experimental.pallas import tpu as pltpu
from jax.sharding import PartitionSpec as P

GROUP = ("scanx", "scany", "pos")
PART_SWAP = ((0, 1), (1, 0))
VMEM = pl.BlockSpec(memory_space=pltpu.VMEM)
ANY = pl.BlockSpec(memory_space=pl.ANY)
HBM = pl.BlockSpec(memory_space=pltpu.HBM)
NOTE = (8, 128)
NOTE_SMEM = pltpu.SMEM(NOTE, jnp.float32)


def f32(*shape):
    return jax.ShapeDtypeStruct(shape, jnp.float32)


def ways_of(count):
    return (0,) if count == 2 else (0, 1)


def side_of(index, way):
    return lax.rem(index + way + 1, 2)


def valid_of(index, way, count):
    neighbour = index + 2 * side_of(index, way) - 1
    return jnp.logical_and(neighbour >= 0, neighbour < count)


def block_ways(nz, nx):
    xways, zways = ways_of(nx), (0, 1)
    order = [(None, w) for w in xways] + [(w, None) for w in zways]
    return order + [(v, w) for w in xways for v in zways]


def block_places(z, x, nz, nx, origin, extent, margin):
    places = []
    for zway, xway in block_ways(nz, nx):
        span = []
        for index, way in ((z, zway), (x, xway)):
            if way is None:
                span.append(pl.ds(origin, 2 * margin))
            else:
                span.append(pl.ds(pl.multiple_of(side_of(index, way) * extent, margin), margin))
        places.append(tuple(span))
    return places


def block_valid(z, x, nz, nx):
    result = []
    for zway, xway in block_ways(nz, nx):
        ok = True
        if zway is not None:
            ok = valid_of(z, zway, nz)
        if xway is not None:
            ok = jnp.logical_and(ok, valid_of(x, xway, nx))
        result.append(ok)
    return result


def block_targets(nz, nx):
    def step(index, way, count):
        if way is None:
            return index
        to = index + (1 if (index + way) % 2 == 0 else -1)
        return to if 0 <= to < count else None

    def target(ways, z, x, c):
        tz, tx = step(z, ways[0], nz), step(x, ways[1], nx)
        return (z, x, 1 - c) if tz is None or tx is None else (tz, tx, c)

    return [functools.partial(target, ways) for ways in block_ways(nz, nx)]


def permutation(sizes, target):
    nz, nx, nc = sizes
    pairs = []
    for z in range(nz):
        for x in range(nx):
            for c in range(nc):
                tz, tx, tc = target(z, x, c)
                pairs.append(((z * nx + x) * nc + c, (tz * nx + tx) * nc + tc))
    return pairs


def dft_tables(length):
    index = np.arange(length, dtype=np.int32)
    phase = (index[:, None] * index[None, :]) % length
    angle = phase.astype(np.float32) * np.float32(2.0 * math.pi / length)
    scale = np.float32(1.0 / math.sqrt(length))
    cosine = (np.cos(angle) * scale).astype(jnp.bfloat16)
    sine = (np.sin(angle) * scale).astype(jnp.bfloat16)
    table_a = np.block([[cosine, sine], [-sine, cosine]])
    table_b = np.block([[cosine, -sine], [sine, cosine]])
    return table_a.astype(jnp.bfloat16), table_b.astype(jnp.bfloat16)


def aligned(row):
    return pl.multiple_of((row // 8) * 8, 8), lax.rem(row, 8)


def rows_up(block, shift):
    count, width = block.shape
    groups = pltpu.roll(block.reshape(count // 8, 8, width), lax.rem(8 - shift, 8), axis=1)
    at = lax.broadcasted_iota(jnp.int32, (count // 8 - 1, 8, width), 1)
    return jnp.where(at < 8 - shift, groups[:-1], groups[1:]).reshape(count - 8, width)


def rows_down(block, shift):
    count, width = block.shape
    groups = pltpu.roll(block.reshape(count // 8, 8, width), shift, axis=1)
    blank = jnp.zeros((1, 8, width), block.dtype)
    at = lax.broadcasted_iota(jnp.int32, (count // 8 + 1, 8, width), 1)
    early = jnp.concatenate([groups, blank])
    late = jnp.concatenate([blank, groups])
    return jnp.where(at >= shift, early, late).reshape(count + 8, width)


def halo_blocks_kernel(nz, nx, off_hbm, spec_ref, *refs):
    z, x, c = (lax.axis_index(a) for a in GROUP)
    *outs, note_ref, off_ref, sems = refs
    margin = spec_ref.shape[1] // 2
    off_copy = pltpu.make_async_copy(off_hbm, off_ref, sems.at[len(outs)])
    off_copy.start()
    copies = []
    for k, (rows, cols) in enumerate(block_places(z, x, nz, nx, 0, margin, margin)):
        height = outs[k].shape[0] - NOTE[0]
        copies.append(
            pltpu.make_async_copy(spec_ref.at[c, rows, cols], outs[k].at[pl.ds(0, height), :], sems.at[k])
        )
        copies[-1].start()
    off_copy.wait()
    lane = lax.broadcasted_iota(jnp.int32, NOTE, 1)
    note = jnp.zeros(NOTE, jnp.float32)
    for j in range(off_ref.shape[0]):
        for k in range(2):
            note = jnp.where(lane == 2 * j + k, off_ref[j, k].astype(jnp.float32), note)
    note_ref[...] = note
    for out in outs:
        out[out.shape[0] - NOTE[0] :, : NOTE[1]] = note
    for copy in copies:
        copy.wait()


def read_notes(notes, smems, sems):
    copies = [pltpu.make_async_copy(note, smem, sems.at[k]) for k, (note, smem) in enumerate(zip(notes, smems))]
    for copy in copies:
        copy.start()
    return copies


def note_of(block):
    return block.at[pl.ds(block.shape[0] - NOTE[0], NOTE[0]), pl.ds(0, NOTE[1])]


def offset_in(note, j):
    return note[0, 2 * j].astype(jnp.int32), note[0, 2 * j + 1].astype(jnp.int32)


def fetch_kernel(*refs):
    *refs, sems = refs
    count = len(refs) // 2
    copies = [pltpu.make_async_copy(refs[k], refs[count + k], sems.at[k]) for k in range(count)]
    for copy in copies:
        copy.start()
    for copy in copies:
        copy.wait()


def cut_patches(note, padded, out):
    npos, size, _ = out.shape
    lane = lax.broadcasted_iota(jnp.int32, (size + 8, size), 1)
    for j in range(npos):
        row, col = offset_in(note, j)
        base, shift = aligned(row)
        rows = padded[pl.ds(base, size + 8), :]
        mixed = rows_up(jnp.where(lane >= col, rows[:, :size], rows[:, size:]), shift)
        out[j] = pltpu.roll(mixed, lax.rem(size - col, size), axis=1)


def other_patches_kernel(nz, nx, note_ref, spec_ref, *refs):
    z, x, c = (lax.axis_index(a) for a in GROUP)
    *blocks, out, padded, note, sems = refs
    copies = read_notes([note_ref], [note], sems)
    tile = spec_ref.shape[1]
    margin = (padded.shape[0] - tile) // 2
    padded[margin : margin + tile, margin : margin + tile] = spec_ref[c]
    if len(ways_of(nx)) == 1:
        far_cols = pl.ds(pl.multiple_of((1 - side_of(x, 0)) * (margin + tile), margin), margin)
        padded[:, far_cols] = jnp.zeros((padded.shape[0], margin), jnp.float32)
    places = block_places(z, x, nz, nx, margin, margin + tile, margin)
    for block, (rows, cols), ok in zip(blocks, places, block_valid(z, x, nz, nx)):
        height, width = block.shape[0] - NOTE[0], block.shape[1]

        @pl.when(ok)
        def _():
            padded[rows, cols] = block[:height, :]

        @pl.when(jnp.logical_not(ok))
        def _():
            padded[rows, cols] = jnp.zeros((height, width), jnp.float32)

    copies[0].wait()
    cut_patches(note, padded, out)


def own_patches_kernel(note_ref, padded, unused_ref, out, note, sems):
    read_notes([note_ref], [note], sems)[0].wait()
    cut_patches(note, padded, out)


def positions_kernel(patch_ref, patch_other_ref, probe_ref, amp_ref, ta_ref, tb_ref, own_ref, other_ref):
    first = lax.axis_index("pos") == 0
    npos, size, _ = patch_ref.shape
    table_a = ta_ref[...]
    table_b = tb_ref[...]
    probe_real = probe_ref[0]
    probe_imag = probe_ref[1]

    def side_by_side(both):
        return jnp.concatenate([both[:size], both[size:]], axis=1)

    grad_real = jnp.zeros((size, size), jnp.float32)
    grad_imag = jnp.zeros((size, size), jnp.float32)
    for j in range(npos):
        patch_real = jnp.where(first, patch_ref[j], patch_other_ref[j])
        patch_imag = jnp.where(first, patch_other_ref[j], patch_ref[j])
        exit_real = probe_real * patch_real - probe_imag * patch_imag
        exit_imag = probe_real * patch_imag + probe_imag * patch_real
        wave = jnp.concatenate([exit_real, exit_imag], axis=0).astype(jnp.bfloat16)
        half = jnp.dot(table_a, wave, preferred_element_type=jnp.float32).astype(jnp.bfloat16)
        far = jnp.dot(side_by_side(half), table_b, preferred_element_type=jnp.float32)
        far_real, far_imag = far[:, :size], far[:, size:]
        power = far_real * far_real + far_imag * far_imag
        ratio = amp_ref[j].astype(jnp.float32) * jnp.minimum(lax.rsqrt(power), 1.0 / 0.2)
        projected = jnp.concatenate([far_real * ratio, far_imag * ratio], axis=0).astype(jnp.bfloat16)
        back_half = jnp.dot(table_b, projected, preferred_element_type=jnp.float32).astype(jnp.bfloat16)
        back = jnp.dot(side_by_side(back_half), table_a, preferred_element_type=jnp.float32)
        diff_real = back[:, :size] - exit_real
        diff_imag = back[:, size:] - exit_imag
        term_real = probe_real * diff_real + probe_imag * diff_imag
        term_imag = probe_real * diff_imag - probe_imag * diff_real
        own_ref[j] = jnp.where(first, term_real, term_imag)
        other_ref[j] = jnp.where(first, term_imag, term_real)
        grad_real += patch_real * diff_real + patch_imag * diff_imag
        grad_imag += patch_real * diff_imag - patch_imag * diff_real
    own_ref[npos] = jnp.where(first, grad_real, grad_imag)
    other_ref[npos] = jnp.where(first, grad_imag, grad_real)


def half_of(z, x, c):
    return jnp.where(c == 0, lax.rem(x, 2), lax.rem(z, 2))


def halve_kernel(own_ref, recv_ref, keep_ref, give_ref):
    half = half_of(*(lax.axis_index(a) for a in GROUP))
    rows = keep_ref.shape[0]
    last = own_ref.shape[0] - 1
    for at, out in ((half, keep_ref), (1 - half, give_ref)):
        span = pl.ds(pl.multiple_of(at * rows, rows), rows)
        out[...] = own_ref[last, span, :] + recv_ref[last, span, :]


def gather_kernel(note_ref, other_note_ref, own_ref, recv_ref, unused_ref, grad, note, other_note, sems):
    copies = read_notes([note_ref, other_note_ref], [note, other_note], sems)
    count, size, _ = own_ref.shape
    lane = lax.broadcasted_iota(jnp.int32, (size + 8, size), 1)
    grad[...] = jnp.zeros_like(grad)
    for copy, offs, terms in zip(copies, (note, other_note), (own_ref, recv_ref)):
        copy.wait()
        for j in range(count - 1):
            row, col = offset_in(offs, j)
            base, shift = aligned(row)
            term = rows_down(pltpu.roll(terms[j], col, axis=1), shift)
            low = jnp.where(lane >= col, term, 0.0)
            rows = pl.ds(base, size + 8)
            grad[rows, :size] += low
            grad[rows, size:] += term - low


def cut_step_kernel(nx, keep_ref, recv_ref, grad_ref, out_ref, middle_ref, *blocks):
    x = lax.axis_index("scany")
    out_ref[...] = keep_ref[...] + recv_ref[...]
    tile = middle_ref.shape[1]
    margin = (middle_ref.shape[0] - tile) // 2
    middle_ref[...] = grad_ref[:, margin : margin + tile]
    for block, way in zip(blocks, ways_of(nx)):
        block[...] = grad_ref[:, pl.ds(pl.multiple_of(side_of(x, way) * (margin + tile), margin), margin)]


def fold_step_kernel(nz, nx, keep_ref, recv_ref, unused_ref, middle_ref, *refs):
    z, x = lax.axis_index("scanx"), lax.axis_index("scany")
    ways = ways_of(nx)
    blocks, (out_ref, center_ref, *edges, total) = refs[: len(ways)], refs[len(ways) :]
    out_ref[...] = keep_ref[...] + recv_ref[...]
    tile = center_ref.shape[0]
    margin = (middle_ref.shape[0] - tile) // 2
    total[...] = middle_ref[...]
    for block, way in zip(blocks, ways):
        at = pl.multiple_of(side_of(x, way) * (tile - margin), margin)

        @pl.when(valid_of(x, way, nx))
        def _():
            total[:, pl.ds(at, margin)] += block[...]

    center_ref[...] = total[margin : margin + tile, :]
    for way, edge in enumerate(edges):
        edge[...] = total[pl.ds(pl.multiple_of(side_of(z, way) * (margin + tile), margin), margin), :]


def update_step_kernel(nz, keep_ref, recv_ref, spec_ref, center_ref, light_ref, other_light_ref, *refs):
    z, c = lax.axis_index("scanx"), lax.axis_index("pos")
    *edges, out_ref, part_ref, grad = refs
    out_ref[...] = keep_ref[...] + recv_ref[...]
    tile = center_ref.shape[0]
    grad[...] = center_ref[...]
    for way, edge in enumerate(edges):
        margin = edge.shape[0]
        at = pl.multiple_of(side_of(z, way) * (tile - margin), margin)

        @pl.when(valid_of(z, way, nz))
        def _():
            grad[pl.ds(at, margin), :] += edge[...]

    part_ref[...] = spec_ref[c] + grad[...] / (light_ref[...] + other_light_ref[...] + 1.0)


def add_kernel(a_ref, b_ref, out_ref):
    out_ref[...] = a_ref[...] + b_ref[...]


def specimen_kernel(part_ref, part_other_ref, out_ref):
    c = lax.axis_index("pos")
    out_ref[c] = part_ref[...]
    out_ref[1 - c] = part_other_ref[...]


def probe_kernel(step_size, probe_ref, keep_ref, away_ref, keep_other_ref, away_other_ref, out_ref):
    z, x, c = (lax.axis_index(a) for a in GROUP)
    rows = keep_ref.shape[0]
    for part, keep, away in ((c, keep_ref, away_ref), (1 - c, keep_other_ref, away_other_ref)):
        half = half_of(z, x, part)
        for at, term in ((half, keep), (1 - half, away)):
            span = pl.ds(pl.multiple_of(at * rows, rows), rows)
            out_ref[part, span, :] = probe_ref[part, span, :] + term[...] * step_size


def light_kernel(npos, nz, nx, note_ref, probe_ref, unused_ref, *refs):
    z, x, c = (lax.axis_index(a) for a in GROUP)
    ways = block_ways(nz, nx)
    blocks, (light_ref, power_ref, total, *notes, sems) = refs[: len(ways)], refs[len(ways) :]
    copies = read_notes([note_ref] + [note_of(b) for b in blocks], notes, sems)
    size = probe_ref.shape[1]
    margin = size // 2
    tile = light_ref.shape[0]
    power_ref[...] = probe_ref[0] * probe_ref[0] + probe_ref[1] * probe_ref[1]
    total[...] = jnp.zeros_like(total)
    lane = lax.broadcasted_iota(jnp.int32, (size, size), 1)

    def add(row, col, ok):
        ok = jnp.logical_and(ok, jnp.logical_and(jnp.abs(row) < tile, jnp.abs(col) < tile))

        @pl.when(ok)
        def _():
            base, shift = aligned(row + tile)
            moved = pltpu.roll(power_ref[...], lax.rem(col + size, size), axis=1)
            keep = jnp.logical_and(lane >= col, lane < col + size)
            total[pl.ds(base, size + 8), :] += rows_down(jnp.where(keep, moved, 0.0), shift)

    places = [((None, None), True)] + list(zip(ways, block_valid(z, x, nz, nx)))
    for copy, note, ((zway, xway), ok) in zip(copies, notes, places):
        copy.wait()
        down = 0 if zway is None else (2 * side_of(z, zway) - 1) * tile
        right = 0 if xway is None else (2 * side_of(x, xway) - 1) * tile
        for j in range(npos):
            row, col = offset_in(note, j)
            add(row + down - margin, col + right - margin, ok)
    light_ref[...] = total[tile : 2 * tile, :]


def call(kernel, out_shape, specs, *operands, scratch=(), vmem=16):
    return pl.pallas_call(
        kernel,
        out_shape=out_shape,
        in_specs=specs,
        out_specs=[VMEM] * len(out_shape),
        scratch_shapes=list(scratch),
        compiler_params=pltpu.CompilerParams(vmem_limit_bytes=vmem * 1024 * 1024),
    )(*operands)


def dma(count):
    return pltpu.SemaphoreType.DMA((count,))


def shards(sizes, specimen, probe_wave, amplitudes, offsets):
    nz, nx, nc = sizes
    size = probe_wave.shape[1]
    margin = size // 2
    tile = specimen.shape[1]
    npos = offsets.shape[0]
    ways = block_ways(nz, nx)
    xways = ways_of(nx)
    targets = block_targets(nz, nx)

    def send(value, target):
        return lax.ppermute(value, GROUP, permutation(sizes, target))

    def to_core(value):
        return lax.ppermute(value, "pos", PART_SWAP)

    shapes = [(tile if v is None else margin, tile if w is None else margin) for v, w in ways]
    *blocks, note = call(
        functools.partial(halo_blocks_kernel, nz, nx),
        [f32(h + NOTE[0], w) for h, w in shapes] + [f32(*NOTE)],
        [HBM, HBM],
        offsets,
        specimen,
        scratch=[pltpu.SMEM(offsets.shape, jnp.int32), dma(len(ways) + 1)],
    )
    recv = [send(block, target) for block, target in zip(blocks, targets)]
    other_note = to_core(note)

    table_a, table_b = (jnp.asarray(t) for t in dft_tables(size))
    late = (specimen, probe_wave, amplitudes, table_a, table_b)
    specimen_v, probe_v, amp_v, ta_v, tb_v = call(
        fetch_kernel,
        [jax.ShapeDtypeStruct(a.shape, a.dtype) for a in late],
        [HBM] * len(late),
        *late,
        scratch=[dma(len(late))],
    )

    give, padded = call(
        functools.partial(other_patches_kernel, nz, nx),
        [f32(npos, size, size), f32(tile + size, tile + size)],
        [VMEM] * (2 + len(recv)),
        other_note,
        specimen_v,
        *recv,
        scratch=[NOTE_SMEM, dma(1)],
    )
    patches_other = to_core(give)
    (patches,) = call(
        own_patches_kernel,
        [f32(npos, size, size)],
        [VMEM, VMEM, ANY],
        note,
        padded,
        give,
        scratch=[NOTE_SMEM, dma(1)],
    )
    own, other = call(
        positions_kernel,
        [f32(npos + 1, size, size)] * 2,
        [VMEM] * 6,
        patches,
        patches_other,
        probe_v,
        amp_v,
        ta_v,
        tb_v,
    )
    terms = to_core(other)

    zbits = [("z", 1 << k) for k in range(nz.bit_length() - 1)]
    xbits = [("x", 1 << k) for k in range(nx.bit_length() - 1)]
    orders = (xbits[:1] + zbits + xbits[1:], zbits + xbits)

    def stage(k):
        def target(z, x, c):
            axis, bit = orders[c][k]
            return (z ^ bit, x, c) if axis == "z" else (z, x ^ bit, c)

        return target

    half = f32(size // 2, size)
    keep, away = call(halve_kernel, [half] * 2, [VMEM] * 2, own, terms)
    (grad,) = call(
        gather_kernel,
        [f32(tile + size, tile + size)],
        [VMEM] * 4 + [ANY],
        note,
        other_note,
        own,
        terms,
        keep,
        scratch=[NOTE_SMEM, NOTE_SMEM, dma(2)],
    )
    keep, middle, *beyond = call(
        functools.partial(cut_step_kernel, nx),
        [half, f32(tile + size, tile)] + [f32(tile + size, margin)] * len(xways),
        [VMEM] * 3,
        keep,
        send(away, stage(0)),
        grad,
    )
    (light,) = call(
        functools.partial(light_kernel, npos, nz, nx),
        [f32(tile, tile)],
        [VMEM, VMEM, ANY] + [VMEM] * len(recv),
        note,
        probe_v,
        keep,
        *recv,
        scratch=[
            pltpu.VMEM((size, size), jnp.float32),
            pltpu.VMEM((3 * tile, size), jnp.float32),
            *[NOTE_SMEM] * (1 + len(recv)),
            dma(1 + len(recv)),
        ],
    )
    beside = [send(piece, targets[ways.index((None, way))]) for piece, way in zip(beyond, xways)]
    keep, center, *edges = call(
        functools.partial(fold_step_kernel, nz, nx),
        [half, f32(tile, tile)] + [f32(margin, tile)] * 2,
        [VMEM, VMEM, ANY, VMEM] + [VMEM] * len(beside),
        keep,
        send(keep, stage(1)),
        light,
        middle,
        *beside,
        scratch=[pltpu.VMEM((tile + size, tile), jnp.float32)],
    )
    arrived = [send(edge, targets[ways.index((way, None))]) for way, edge in enumerate(edges)]
    keep, part = call(
        functools.partial(update_step_kernel, nz),
        [half, f32(tile, tile)],
        [VMEM] * (6 + len(arrived)),
        keep,
        send(keep, stage(2)),
        specimen_v,
        center,
        light,
        to_core(light),
        *arrived,
        scratch=[pltpu.VMEM((tile, tile), jnp.float32)],
    )
    for k in range(3, len(orders[0])):
        (keep,) = call(add_kernel, [half], [VMEM] * 2, keep, send(keep, stage(k)))
    away = send(keep, stage(0))
    (new_specimen,) = call(specimen_kernel, [f32(2, tile, tile)], [VMEM] * 2, part, to_core(part))
    step_size = 1.0 / math.sqrt(npos * nz * nx * nc)
    (new_probe,) = call(
        functools.partial(probe_kernel, step_size),
        [f32(2, size, size)],
        [VMEM] * 5,
        probe_v,
        keep,
        away,
        to_core(keep),
        to_core(away),
    )
    return (new_specimen, new_probe)


def solution(mesh):
    sizes = tuple(mesh.shape[a] for a in GROUP)
    placed = (
        P(None, ("groups", "scanx"), "scany"),
        P(None, "groups", None),
        P(("groups", "scanx", "scany", "pos"), None, None),
        P(("groups", "scanx", "scany", "pos"), None),
    )
    return jax.shard_map(
        functools.partial(shards, sizes),
        mesh=mesh,
        in_specs=placed,
        out_specs=(P(None, ("groups", "scanx"), "scany"), P(None, "groups", None)),
        check_vma=False,
    )
```

time: 59.1 us -> 53.7 us (0.909)
  waiting for transfers between devices: 22.2 us -> 18.3 us
  other arithmetic: 2.72 us -> 0 us
  starting transfers between devices: 16.2 us -> 18.5 us
  local copies, waits for them, and re-layouts: 7.73 us -> 5.79 us
  Pallas kernels: 8.88 us -> 9.93 us
    ppermute x14 -> x12, waiting for transfers between devices: 18.1 us -> 15 us  [send(): return lax.ppermute(value, GROUP, permutation(sizes, target))]
    ppermute x14 -> x12, starting transfers between devices: 15 us -> 17.4 us  [send(): return lax.ppermute(value, GROUP, permutation(sizes, target))]
    add x2 -> x0, other arithmetic: 1.85 us -> none  [the longest x1 0.98 us: shards(): held = probe_own + to_core(probe_other)]
    unnamed x24 -> x14, local copies, waits for them, and re-layouts: 7.61 us -> 5.79 us
    pallas_call x10 -> x13, Pallas kernels: 8.88 us -> 9.93 us  [call(): pl.pallas_call(kernel, out_shape=out_shape, in_specs=specs, out_specs=[VM...]
    select_n x3 -> x0, other arithmetic: 0.87 us -> none  [the longest x1 0.83 us: shards(): jnp.where(c == 0, jnp.stack([part, part_other]), jnp.stack([part_other, p...]
    ppermute x7, waiting for transfers between devices: 4.14 us -> 3.31 us  [to_core(): return lax.ppermute(value, 'pos', PART_SWAP)]
  transfers between devices with their start and end apart: 21 -> 19, of which waited for: 9 -> 9; matrix products, arithmetic and copies ran while one was open for 3% -> 0% of each run, Pallas kernels for 5% -> 9%
where the time goes in v4:
time: 53.7 us; the launch traced here: 53.3 us
  starting transfers between devices  18.5 us (34%)
  waiting for transfers between devices  18.3 us (34%)
  Pallas kernels  9.93 us (18%)
  local copies, waits for them, and re-layouts  5.79 us (11%)
  between operations  0.79 us (1%)
    ppermute x12, starting transfers between devices, send(): return lax.ppermute(value, GROUP, permutation(sizes, target))  17.4 us
    ppermute x12, waiting for transfers between devices, send(): return lax.ppermute(value, GROUP, permutation(sizes, target))  15 us
    pallas_call x13, Pallas kernels, call(): pl.pallas_call(kernel, out_shape=out_shape, in_specs=specs, out_specs=[VM...  9.93 us
    unnamed x14, local copies, waits for them, and re-layouts  5.79 us
    ppermute x7, waiting for transfers between devices, to_core(): return lax.ppermute(value, 'pos', PART_SWAP)  3.31 us
  transfers between devices with their start and end apart: 19, of which 9 were waited for; matrix products, arithmetic and copies ran while one was open for 0% of the time, Pallas kernels for 9%

profile of v4, /device:TPU:0, one launch (start us, length us, event | category | flops | bytes accessed | tf_op | source)
XLA Modules:
  0.0 53.3 jit_solution(5318873058746581553)
XLA Ops:
  0.6 0.0 copy-start
  0.6 1.0 %copy-done = f32[2,256,256]{2,1,0:T(8,128)S(1)} copy-done((f32[2,256,256]{2,1,0:T(8,128)S(1)}, f32[2,256,256]{2,1,0:T(8,128)}, u32[]{:S(2)}) %copy-start) | copy-done | bytes 524312
  1.7 0.0 copy-start.6
  1.7 0.7 %copy-done.6 = s32[2,2]{1,0:T(2,128)S(1)} copy-done((s32[2,2]{1,0:T(2,128)S(1)}, s32[2,2]{1,0:T(2,128)}, u32[]{:S(2)}) %copy-start.6) | copy-done | bytes 40
  2.4 0.0 copy-start.1
  2.4 0.6 %shard_map.77 = (f32[264,128]{1,0:T(8,128)S(1)}, f32[136,256]{1,0:T(8,128)S(1)}, f32[136,256]{1,0:T(8,128)S(1)}, f32[136,128]{1,0:T(8,128)S(1)}, f32[136,128]{1,0:T(8,128)S(1)}, /*index=5*/f32[8,128]{1,0:T(8,128)S(1)}) custom-call(s32[2,2]{1,0:T(2,128)S(1)} %copy-done.6, f32[2,256,256]{2,1,0:T(8,128)S(1)} %copy-done), custom_call_target="tpu_custom_call" | custom-call | tf_op jit(solution)/shard_map/pallas_call | solution.py:390
  3.0 3.1 %collective-permute-start.2 = (f32[136,256]{1,0:T(8,128)S(1)}, f32[136,256]{1,0:T(8,128)S(1)}, u32[]{:S(2)}, u32[]{:S(2)}) collective-permute-start(f32[136,256]{1,0:T(8,128)S(1)} %get-tuple-element.31), channel_id=1, source_target_pairs={{0,4},{1,5},{2,6},{3,7},{4,0},{5,1},{6,2},{7,3},{8,12},{9,13},{10,... | collective-permute-start | bytes 417800 | tf_op jit(solution)/shard_map/ppermute | solution.py:415
  6.1 0.0 collective-permute-start.3
  6.1 1.5 %collective-permute-start.1 = (f32[264,128]{1,0:T(8,128)S(1)}, f32[264,128]{1,0:T(8,128)S(1)}, u32[]{:S(2)}, u32[]{:S(2)}) collective-permute-start(f32[264,128]{1,0:T(8,128)S(1)} %get-tuple-element.30), channel_id=1, source_target_pairs={{0,2},{1,3},{2,0},{3,1},{4,6},{5,7},{6,4},{7,5},{8,10},{9,11},{10,... | collective-permute-start | bytes 405512 | tf_op jit(solution)/shard_map/ppermute | solution.py:415
  7.6 0.2 collective-permute-start
  7.8 2.9 %collective-permute-start.4 = (f32[136,128]{1,0:T(8,128)S(1)}, f32[136,128]{1,0:T(8,128)S(1)}, u32[]{:S(2)}, u32[]{:S(2)}) collective-permute-start(f32[136,128]{1,0:T(8,128)S(1)} %get-tuple-element.33), channel_id=1, source_target_pairs={{0,6},{1,7},{2,4},{3,5},{4,2},{5,3},{6,0},{7,1},{8,14},{9,15},{10,... | collective-permute-start | bytes 208904 | tf_op jit(solution)/shard_map/ppermute | solution.py:415
  10.7 0.0 collective-permute-done.note_ref.other_note_ref
  10.7 0.2 collective-permute-start.5
  10.9 0.0 copy-done.1
  10.9 0.0 copy-start.2
  10.9 1.0 %copy-done.2 = f32[2,256,256]{2,1,0:T(8,128)S(1)} copy-done((f32[2,256,256]{2,1,0:T(8,128)S(1)}, f32[2,256,256]{2,1,0:T(8,128)}, u32[]{:S(2)}) %copy-start.2) | copy-done | bytes 524312
  12.0 0.0 copy-start.3
  12.0 1.0 %copy-done.3 = bf16[512,512]{1,0:T(8,128)(2,1)S(1)} copy-done((bf16[512,512]{1,0:T(8,128)(2,1)S(1)}, bf16[512,512]{1,0:T(8,128)(2,1)}, u32[]{:S(2)}) %copy-start.3) | copy-done | bytes 524312
  13.0 0.0 copy-start.4
  13.0 1.0 %copy-done.4 = bf16[512,512]{1,0:T(8,128)(2,1)S(1)} copy-done((bf16[512,512]{1,0:T(8,128)(2,1)S(1)}, bf16[512,512]{1,0:T(8,128)(2,1)}, u32[]{:S(2)}) %copy-start.4) | copy-done | bytes 524312
  14.0 0.0 copy-start.5
  14.1 0.9 %copy-done.5 = bf16[2,256,256]{2,1,0:T(8,128)(2,1)S(1)} copy-done((bf16[2,256,256]{2,1,0:T(8,128)(2,1)S(1)}, bf16[2,256,256]{2,1,0:T(8,128)(2,1)}, u32[]{:S(2)}) %copy-start.5) | copy-done | bytes 262168
  15.0 0.2 shard_map.78
  15.2 0.0 collective-permute-done.4.refs_3_
  15.2 0.0 collective-permute-done.5.refs_4_
  15.2 0.0 collective-permute-done.1.refs_0_
  15.2 0.0 collective-permute-done.2.refs_1_
  15.3 0.0 collective-permute-done.3.refs_2_
  15.3 0.8 %shard_map.79 = (f32[2,256,256]{2,1,0:T(8,128)S(1)}, f32[512,512]{1,0:T(8,128)S(1)}) custom-call(f32[8,128]{1,0:T(8,128)S(1)} %collective-permute-done.note_ref.other_note_ref, f32[2,256,256]{2,1,0:T(8,128)S(1)} %get-tuple-element.29.spec_ref, f32[264,128]{1,0:T(8,128)S(1)} %collective-permute-done.1.refs_0_, f32[136,256]{1,0:T(8,128)S(1)} %collective-permute-done.2.refs_1_, ...), custom_call_target="tpu_custom_call" | custom-call | tf_op jit(solution)/shard_map/pallas_call | solution.py:390
  16.1 0.3 collective-permute-start.6
  16.5 0.8 %shard_map.80.patch_ref = f32[2,256,256]{2,1,0:T(8,128)S(1)} custom-call(f32[8,128]{1,0:T(8,128)S(1)} %get-tuple-element.28.note_ref, f32[512,512]{1,0:T(8,128)S(1)} %get-tuple-element.35.padded, f32[2,256,256]{2,1,0:T(8,128)S(1)} %get-tuple-element.36.unused_ref), custom_call_target="tpu_custom_call" | custom-call | tf_op jit(solution)/shard_map/pallas_call | solution.py:390
  17.3 0.8 %collective-permute-done.6.patch_other_ref = f32[2,256,256]{2,1,0:T(8,128)S(1)} collective-permute-done((f32[2,256,256]{2,1,0:T(8,128)S(1)}, f32[2,256,256]{2,1,0:T(8,128)S(1)}, u32[]{:S(2)}, u32[]{:S(2)}) %collective-permute-start.6) | collective-permute-done | bytes 524320 | tf_op jit(solution)/shard_map/ppermute | solution.py:418
  18.1 2.6 %shard_map.81 = (f32[3,256,256]{2,1,0:T(8,128)S(1)}, f32[3,256,256]{2,1,0:T(8,128)S(1)}) custom-call(f32[2,256,256]{2,1,0:T(8,128)S(1)} %shard_map.80.patch_ref, f32[2,256,256]{2,1,0:T(8,128)S(1)} %collective-permute-done.6.patch_other_ref, f32[2,256,256]{2,1,0:T(8,128)S(1)} %get-tuple-element.37.probe_ref, ...), custom_call_target="tpu_custom_call" | custom-call | tf_op jit(solution)/shard_map/pallas_call | solution.py:390
  20.7 0.3 collective-permute-start.7
  21.0 2.0 %collective-permute-done.7.recv_ref = f32[3,256,256]{2,1,0:T(8,128)S(1)} collective-permute-done((f32[3,256,256]{2,1,0:T(8,128)S(1)}, f32[3,256,256]{2,1,0:T(8,128)S(1)}, u32[]{:S(2)}, u32[]{:S(2)}) %collective-permute-start.7) | collective-permute-done | bytes 786464 | tf_op jit(solution)/shard_map/ppermute | solution.py:418
  23.1 1.6 %collective-permute-start.8 = (f32[128,256]{1,0:T(8,128)S(1)}, f32[128,256]{1,0:T(8,128)S(1)}, u32[]{:S(2)}, u32[]{:S(2)}) collective-permute-start(f32[128,256]{1,0:T(8,128)S(1)} %get-tuple-element.44), channel_id=1, source_target_pairs={{0,2},{1,5},{2,0},{3,7},{4,6},{5,1},{6,4},{7,3},{8,10},{9,13},{10,... | collective-permute-start | bytes 393224 | tf_op jit(solution)/shard_map/ppermute | solution.py:415
  24.6 1.2 %shard_map.83.grad_ref = f32[512,512]{1,0:T(8,128)S(1)} custom-call(f32[8,128]{1,0:T(8,128)S(1)} %get-tuple-element.28.note_ref, f32[8,128]{1,0:T(8,128)S(1)} %collective-permute-done.note_ref.other_note_ref, f32[3,256,256]{2,1,0:T(8,128)S(1)} %get-tuple-element.41.own_ref, f32[3,256,256]{2,1,0:T(8,128)S(1)} %collective-permute-done.7.recv_ref, ...), custom_call_target="tpu_custom_call" | custom-call | tf_op jit(solution)/shard_map/pallas_call | solution.py:390
  25.8 2.3 %collective-permute-done.8.recv_ref = f32[128,256]{1,0:T(8,128)S(1)} collective-permute-done((f32[128,256]{1,0:T(8,128)S(1)}, f32[128,256]{1,0:T(8,128)S(1)}, u32[]{:S(2)}, u32[]{:S(2)}) %collective-permute-start.8) | collective-permute-done | bytes 131104 | tf_op jit(solution)/shard_map/ppermute | solution.py:415
  28.1 0.1 shard_map.84
  28.2 1.6 %collective-permute-start.10 = (f32[512,128]{1,0:T(8,128)S(1)}, f32[512,128]{1,0:T(8,128)S(1)}, u32[]{:S(2)}, u32[]{:S(2)}) collective-permute-start(f32[512,128]{1,0:T(8,128)S(1)} %get-tuple-element.47), channel_id=1, source_target_pairs={{0,2},{1,3},{2,0},{3,1},{4,6},{5,7},{6,4},{7,5},{8,10},{9,11},{10,... | collective-permute-start | bytes 786440 | tf_op jit(solution)/shard_map/ppermute | solution.py:415
  29.7 2.0 %collective-permute-start.9 = (f32[128,256]{1,0:T(8,128)S(1)}, f32[128,256]{1,0:T(8,128)S(1)}, u32[]{:S(2)}, u32[]{:S(2)}) collective-permute-start(f32[128,256]{1,0:T(8,128)S(1)} %get-tuple-element.45.unused_ref.keep_ref), channel_id=1, source_target_pairs={{0,4},{1,9},{2,6},{3,11},{4,0},{5,13},{6,2},{7,15},{8,12},{9,1},{1... | collective-permute-start | bytes 393224 | tf_op jit(solution)/shard_map/ppermute | solution.py:415
  31.7 1.7 %shard_map.85.unused_ref.light_ref = f32[256,256]{1,0:T(8,128)S(1)} custom-call(f32[8,128]{1,0:T(8,128)S(1)} %get-tuple-element.28.note_ref, f32[2,256,256]{2,1,0:T(8,128)S(1)} %get-tuple-element.37.probe_ref, f32[128,256]{1,0:T(8,128)S(1)} %get-tuple-element.45.unused_ref.keep_ref, f32[264,128]{1,0:T(8,128)S(1)} %collective-permute-done.1.refs_0_, ...), custom_call_target="tpu_custom_call" | custom-call | tf_op jit(solution)/shard_map/pallas_call | solution.py:390
  33.4 0.1 collective-permute-start.12
  33.5 1.7 %collective-permute-done.9.recv_ref = f32[128,256]{1,0:T(8,128)S(1)} collective-permute-done((f32[128,256]{1,0:T(8,128)S(1)}, f32[128,256]{1,0:T(8,128)S(1)}, u32[]{:S(2)}, u32[]{:S(2)}) %collective-permute-start.9) | collective-permute-done | bytes 131104 | tf_op jit(solution)/shard_map/ppermute | solution.py:415
  35.1 1.3 %collective-permute-done.10.refs_0_ = f32[512,128]{1,0:T(8,128)S(1)} collective-permute-done((f32[512,128]{1,0:T(8,128)S(1)}, f32[512,128]{1,0:T(8,128)S(1)}, u32[]{:S(2)}, u32[]{:S(2)}) %collective-permute-start.10) | collective-permute-done | bytes 262176 | tf_op jit(solution)/shard_map/ppermute | solution.py:415
  36.5 0.1 shard_map.86
  36.6 1.8 %collective-permute-start.13 = (f32[128,256]{1,0:T(8,128)S(1)}, f32[128,256]{1,0:T(8,128)S(1)}, u32[]{:S(2)}, u32[]{:S(2)}) collective-permute-start(f32[128,256]{1,0:T(8,128)S(1)} %get-tuple-element.50), channel_id=1, source_target_pairs={{0,4},{1,5},{2,6},{3,7},{4,0},{5,1},{6,2},{7,3},{8,12},{9,13},{10,... | collective-permute-start | bytes 393224 | tf_op jit(solution)/shard_map/ppermute | solution.py:415
  38.4 0.0 collective-permute-start.14
  38.4 1.7 %collective-permute-start.11 = (f32[128,256]{1,0:T(8,128)S(1)}, f32[128,256]{1,0:T(8,128)S(1)}, u32[]{:S(2)}, u32[]{:S(2)}) collective-permute-start(f32[128,256]{1,0:T(8,128)S(1)} %get-tuple-element.48.keep_ref), channel_id=1, source_target_pairs={{0,8},{1,3},{2,10},{3,1},{4,12},{5,7},{6,14},{7,5},{8,0},{9,11},{1... | collective-permute-start | bytes 393224 | tf_op jit(solution)/shard_map/ppermute | solution.py:415
  40.1 0.0 collective-permute-done.12.other_light_ref
  40.1 1.5 %collective-permute-done.13.refs_0_ = f32[128,256]{1,0:T(8,128)S(1)} collective-permute-done((f32[128,256]{1,0:T(8,128)S(1)}, f32[128,256]{1,0:T(8,128)S(1)}, u32[]{:S(2)}, u32[]{:S(2)}) %collective-permute-start.13) | collective-permute-done | bytes 131104 | tf_op jit(solution)/shard_map/ppermute | solution.py:415
  41.6 0.0 collective-permute-done.14.refs_1_
  41.6 4.3 %collective-permute-done.11.recv_ref = f32[128,256]{1,0:T(8,128)S(1)} collective-permute-done((f32[128,256]{1,0:T(8,128)S(1)}, f32[128,256]{1,0:T(8,128)S(1)}, u32[]{:S(2)}, u32[]{:S(2)}) %collective-permute-start.11) | collective-permute-done | bytes 131104 | tf_op jit(solution)/shard_map/ppermute | solution.py:415
  45.9 0.1 shard_map.87
  46.0 0.1 collective-permute-start.15
  46.1 1.1 %collective-permute-start.16 = (f32[128,256]{1,0:T(8,128)S(1)}, f32[128,256]{1,0:T(8,128)S(1)}, u32[]{:S(2)}, u32[]{:S(2)}) collective-permute-start(f32[128,256]{1,0:T(8,128)S(1)} %get-tuple-element.53.keep_ref), channel_id=1, source_target_pairs={{0,2},{1,5},{2,0},{3,7},{4,6},{5,1},{6,4},{7,3},{8,10},{9,13},{10,... | collective-permute-start | bytes 393224 | tf_op jit(solution)/shard_map/ppermute | solution.py:415
  47.1 0.0 collective-permute-start.17
  47.1 4.0 %collective-permute-done.16.away_ref = f32[128,256]{1,0:T(8,128)S(1)} collective-permute-done((f32[128,256]{1,0:T(8,128)S(1)}, f32[128,256]{1,0:T(8,128)S(1)}, u32[]{:S(2)}, u32[]{:S(2)}) %collective-permute-start.16) | collective-permute-done | bytes 131104 | tf_op jit(solution)/shard_map/ppermute | solution.py:415
  51.1 0.0 collective-permute-start.18
  51.1 0.0 collective-permute-done.15.part_other_ref
  51.1 0.8 %shard_map.88 = f32[2,256,256]{2,1,0:T(8,128)} custom-call(f32[256,256]{1,0:T(8,128)S(1)} %get-tuple-element.52.part_ref, f32[256,256]{1,0:T(8,128)S(1)} %collective-permute-done.15.part_other_ref), custom_call_target="tpu_custom_call" | custom-call | tf_op jit(solution)/shard_map/pallas_call | solution.py:390
  51.9 0.0 collective-permute-done.17.keep_other_ref
  51.9 0.5 collective-permute-done.18.away_other_ref
  52.4 0.9 %shard_map.89 = f32[2,256,256]{2,1,0:T(8,128)} custom-call(f32[2,256,256]{2,1,0:T(8,128)S(1)} %get-tuple-element.37.probe_ref, f32[128,256]{1,0:T(8,128)S(1)} %get-tuple-element.53.keep_ref, f32[128,256]{1,0:T(8,128)S(1)} %collective-permute-done.16.away_ref, f32[128,256]{1,0:T(8,128)S(1)} %collective-permute-done.17.keep_other_ref, ...), custom_call_target="tpu_custom_call" | custom-call | tf_op jit(solution)/shard_map/pallas_call | solution.py:390
  (1 shorter events, 0.0 us)
Async XLA Ops:
  0.6 1.0 %copy-start = (f32[2,256,256]{2,1,0:T(8,128)S(1)}, f32[2,256,256]{2,1,0:T(8,128)}, u32[]{:S(2)}) copy-start(f32[2,256,256]{2,1,0:T(8,128)} %refs_0_.1) | copy-start | bytes 1572868
  1.7 0.7 %copy-start.6 = (s32[2,2]{1,0:T(2,128)S(1)}, s32[2,2]{1,0:T(2,128)}, u32[]{:S(2)}) copy-start(s32[2,2]{1,0:T(2,128)} %off_hbm.1) | copy-start | bytes 52
  2.4 8.6 %copy-start.1 = (f32[2,256,256]{2,1,0:T(8,128)S(1)}, f32[2,256,256]{2,1,0:T(8,128)}, u32[]{:S(2)}) copy-start(f32[2,256,256]{2,1,0:T(8,128)} %refs_0_.1) | copy-start | bytes 1572868
  3.0 12.3 %collective-permute-start.2 = (f32[136,256]{1,0:T(8,128)S(1)}, f32[136,256]{1,0:T(8,128)S(1)}, u32[]{:S(2)}, u32[]{:S(2)}) collective-permute-start(f32[136,256]{1,0:T(8,128)S(1)} %get-tuple-element.31), channel_id=1, source_target_pairs={{0,4},{1,5},{2,6},{3,7},{4,0},{5,1},{6,2},{7,3},{8,12},{9,13},{10,... | collective-permute-start | bytes 417800 | tf_op jit(solution)/shard_map/ppermute | solution.py:415
  6.1 9.2 %collective-permute-start.3 = (f32[136,256]{1,0:T(8,128)S(1)}, f32[136,256]{1,0:T(8,128)S(1)}, u32[]{:S(2)}, u32[]{:S(2)}) collective-permute-start(f32[136,256]{1,0:T(8,128)S(1)} %get-tuple-element.32), channel_id=1, source_target_pairs={{0,1},{1,0},{2,3},{3,2},{4,8},{5,9},{6,10},{7,11},{8,4},{9,5},{10,... | collective-permute-start | bytes 417800 | tf_op jit(solution)/shard_map/ppermute | solution.py:415
  6.1 9.2 %collective-permute-start.1 = (f32[264,128]{1,0:T(8,128)S(1)}, f32[264,128]{1,0:T(8,128)S(1)}, u32[]{:S(2)}, u32[]{:S(2)}) collective-permute-start(f32[264,128]{1,0:T(8,128)S(1)} %get-tuple-element.30), channel_id=1, source_target_pairs={{0,2},{1,3},{2,0},{3,1},{4,6},{5,7},{6,4},{7,5},{8,10},{9,11},{10,... | collective-permute-start | bytes 405512 | tf_op jit(solution)/shard_map/ppermute | solution.py:415
  7.6 3.1 %collective-permute-start = (f32[8,128]{1,0:T(8,128)S(1)}, f32[8,128]{1,0:T(8,128)S(1)}, u32[]{:S(2)}, u32[]{:S(2)}) collective-permute-start(f32[8,128]{1,0:T(8,128)S(1)} %get-tuple-element.28.note_ref), channel_id=1, source_target_pairs={{0,1},{1,0},{2,3},{3,2},{4,5},{5,4},{6,7},{7,6},{8,9},{9,8},{10,11... | collective-permute-start | bytes 12296 | tf_op jit(solution)/shard_map/ppermute | solution.py:418
  7.8 7.4 %collective-permute-start.4 = (f32[136,128]{1,0:T(8,128)S(1)}, f32[136,128]{1,0:T(8,128)S(1)}, u32[]{:S(2)}, u32[]{:S(2)}) collective-permute-start(f32[136,128]{1,0:T(8,128)S(1)} %get-tuple-element.33), channel_id=1, source_target_pairs={{0,6},{1,7},{2,4},{3,5},{4,2},{5,3},{6,0},{7,1},{8,14},{9,15},{10,... | collective-permute-start | bytes 208904 | tf_op jit(solution)/shard_map/ppermute | solution.py:415
  10.7 4.5 %collective-permute-start.5 = (f32[136,128]{1,0:T(8,128)S(1)}, f32[136,128]{1,0:T(8,128)S(1)}, u32[]{:S(2)}, u32[]{:S(2)}) collective-permute-start(f32[136,128]{1,0:T(8,128)S(1)} %get-tuple-element.34), channel_id=1, source_target_pairs={{0,1},{1,0},{2,3},{3,2},{4,10},{5,11},{6,8},{7,9},{8,6},{9,7},{10,... | collective-permute-start | bytes 208904 | tf_op jit(solution)/shard_map/ppermute | solution.py:415
  10.9 1.0 %copy-start.2 = (f32[2,256,256]{2,1,0:T(8,128)S(1)}, f32[2,256,256]{2,1,0:T(8,128)}, u32[]{:S(2)}) copy-start(f32[2,256,256]{2,1,0:T(8,128)} %refs_1_.1) | copy-start | bytes 1572868
  12.0 1.0 %copy-start.3 = (bf16[512,512]{1,0:T(8,128)(2,1)S(1)}, bf16[512,512]{1,0:T(8,128)(2,1)}, u32[]{:S(2)}) copy-start(bf16[512,512]{1,0:T(8,128)(2,1)} %constant.5.clone.refs_4_) | copy-start | bytes 1572868
  13.0 1.0 %copy-start.4 = (bf16[512,512]{1,0:T(8,128)(2,1)S(1)}, bf16[512,512]{1,0:T(8,128)(2,1)}, u32[]{:S(2)}) copy-start(bf16[512,512]{1,0:T(8,128)(2,1)} %constant.4.clone.refs_3_) | copy-start | bytes 1572868
  14.0 0.9 %copy-start.5 = (bf16[2,256,256]{2,1,0:T(8,128)(2,1)S(1)}, bf16[2,256,256]{2,1,0:T(8,128)(2,1)}, u32[]{:S(2)}) copy-start(bf16[2,256,256]{2,1,0:T(8,128)(2,1)} %refs_2_.1) | copy-start | bytes 786436
  16.1 2.0 %collective-permute-start.6 = (f32[2,256,256]{2,1,0:T(8,128)S(1)}, f32[2,256,256]{2,1,0:T(8,128)S(1)}, u32[]{:S(2)}, u32[]{:S(2)}) collective-permute-start(f32[2,256,256]{2,1,0:T(8,128)S(1)} %get-tuple-element.36.unused_ref), channel_id=1, source_target_pairs={{0,1},{1,0},{2,3},{3,2},{4,5},{5,4},{6,7},{7,6},{8,9},{9,8},{10,11... | collective-permute-start | bytes 1572872 | tf_op jit(solution)/shard_map/ppermute | solution.py:418
  20.7 2.4 %collective-permute-start.7 = (f32[3,256,256]{2,1,0:T(8,128)S(1)}, f32[3,256,256]{2,1,0:T(8,128)S(1)}, u32[]{:S(2)}, u32[]{:S(2)}) collective-permute-start(f32[3,256,256]{2,1,0:T(8,128)S(1)} %get-tuple-element.42), channel_id=1, source_target_pairs={{0,1},{1,0},{2,3},{3,2},{4,5},{5,4},{6,7},{7,6},{8,9},{9,8},{10,11... | collective-permute-start | bytes 2359304 | tf_op jit(solution)/shard_map/ppermute | solution.py:418
  23.1 5.0 %collective-permute-start.8 = (f32[128,256]{1,0:T(8,128)S(1)}, f32[128,256]{1,0:T(8,128)S(1)}, u32[]{:S(2)}, u32[]{:S(2)}) collective-permute-start(f32[128,256]{1,0:T(8,128)S(1)} %get-tuple-element.44), channel_id=1, source_target_pairs={{0,2},{1,5},{2,0},{3,7},{4,6},{5,1},{6,4},{7,3},{8,10},{9,13},{10,... | collective-permute-start | bytes 393224 | tf_op jit(solution)/shard_map/ppermute | solution.py:415
  28.2 8.3 %collective-permute-start.10 = (f32[512,128]{1,0:T(8,128)S(1)}, f32[512,128]{1,0:T(8,128)S(1)}, u32[]{:S(2)}, u32[]{:S(2)}) collective-permute-start(f32[512,128]{1,0:T(8,128)S(1)} %get-tuple-element.47), channel_id=1, source_target_pairs={{0,2},{1,3},{2,0},{3,1},{4,6},{5,7},{6,4},{7,5},{8,10},{9,11},{10,... | collective-permute-start | bytes 786440 | tf_op jit(solution)/shard_map/ppermute | solution.py:415
  29.7 5.4 %collective-permute-start.9 = (f32[128,256]{1,0:T(8,128)S(1)}, f32[128,256]{1,0:T(8,128)S(1)}, u32[]{:S(2)}, u32[]{:S(2)}) collective-permute-start(f32[128,256]{1,0:T(8,128)S(1)} %get-tuple-element.45.unused_ref.keep_ref), channel_id=1, source_target_pairs={{0,4},{1,9},{2,6},{3,11},{4,0},{5,13},{6,2},{7,15},{8,12},{9,1},{1... | collective-permute-start | bytes 393224 | tf_op jit(solution)/shard_map/ppermute | solution.py:415
  33.4 6.7 %collective-permute-start.12 = (f32[256,256]{1,0:T(8,128)S(1)}, f32[256,256]{1,0:T(8,128)S(1)}, u32[]{:S(2)}, u32[]{:S(2)}) collective-permute-start(f32[256,256]{1,0:T(8,128)S(1)} %shard_map.85.unused_ref.light_ref), channel_id=1, source_target_pairs={{0,1},{1,0},{2,3},{3,2},{4,5},{5,4},{6,7},{7,6},{8,9},{9,8},{10,11... | collective-permute-start | bytes 786440 | tf_op jit(solution)/shard_map/ppermute | solution.py:418
  36.6 5.0 %collective-permute-start.13 = (f32[128,256]{1,0:T(8,128)S(1)}, f32[128,256]{1,0:T(8,128)S(1)}, u32[]{:S(2)}, u32[]{:S(2)}) collective-permute-start(f32[128,256]{1,0:T(8,128)S(1)} %get-tuple-element.50), channel_id=1, source_target_pairs={{0,4},{1,5},{2,6},{3,7},{4,0},{5,1},{6,2},{7,3},{8,12},{9,13},{10,... | collective-permute-start | bytes 393224 | tf_op jit(solution)/shard_map/ppermute | solution.py:415
  38.4 3.2 %collective-permute-start.14 = (f32[128,256]{1,0:T(8,128)S(1)}, f32[128,256]{1,0:T(8,128)S(1)}, u32[]{:S(2)}, u32[]{:S(2)}) collective-permute-start(f32[128,256]{1,0:T(8,128)S(1)} %get-tuple-element.51), channel_id=1, source_target_pairs={{0,1},{1,0},{2,3},{3,2},{4,8},{5,9},{6,10},{7,11},{8,4},{9,5},{10,... | collective-permute-start | bytes 393224 | tf_op jit(solution)/shard_map/ppermute | solution.py:415
  38.4 7.5 %collective-permute-start.11 = (f32[128,256]{1,0:T(8,128)S(1)}, f32[128,256]{1,0:T(8,128)S(1)}, u32[]{:S(2)}, u32[]{:S(2)}) collective-permute-start(f32[128,256]{1,0:T(8,128)S(1)} %get-tuple-element.48.keep_ref), channel_id=1, source_target_pairs={{0,8},{1,3},{2,10},{3,1},{4,12},{5,7},{6,14},{7,5},{8,0},{9,11},{1... | collective-permute-start | bytes 393224 | tf_op jit(solution)/shard_map/ppermute | solution.py:415
  46.0 5.1 %collective-permute-start.15 = (f32[256,256]{1,0:T(8,128)S(1)}, f32[256,256]{1,0:T(8,128)S(1)}, u32[]{:S(2)}, u32[]{:S(2)}) collective-permute-start(f32[256,256]{1,0:T(8,128)S(1)} %get-tuple-element.52.part_ref), channel_id=1, source_target_pairs={{0,1},{1,0},{2,3},{3,2},{4,5},{5,4},{6,7},{7,6},{8,9},{9,8},{10,11... | collective-permute-start | bytes 786440 | tf_op jit(solution)/shard_map/ppermute | solution.py:418
  46.1 5.0 %collective-permute-start.16 = (f32[128,256]{1,0:T(8,128)S(1)}, f32[128,256]{1,0:T(8,128)S(1)}, u32[]{:S(2)}, u32[]{:S(2)}) collective-permute-start(f32[128,256]{1,0:T(8,128)S(1)} %get-tuple-element.53.keep_ref), channel_id=1, source_target_pairs={{0,2},{1,5},{2,0},{3,7},{4,6},{5,1},{6,4},{7,3},{8,10},{9,13},{10,... | collective-permute-start | bytes 393224 | tf_op jit(solution)/shard_map/ppermute | solution.py:415
  47.1 4.8 %collective-permute-start.17 = (f32[128,256]{1,0:T(8,128)S(1)}, f32[128,256]{1,0:T(8,128)S(1)}, u32[]{:S(2)}, u32[]{:S(2)}) collective-permute-start(f32[128,256]{1,0:T(8,128)S(1)} %get-tuple-element.53.keep_ref), channel_id=1, source_target_pairs={{0,1},{1,0},{2,3},{3,2},{4,5},{5,4},{6,7},{7,6},{8,9},{9,8},{10,11... | collective-permute-start | bytes 393224 | tf_op jit(solution)/shard_map/ppermute | solution.py:418
  51.1 1.3 %collective-permute-start.18 = (f32[128,256]{1,0:T(8,128)S(1)}, f32[128,256]{1,0:T(8,128)S(1)}, u32[]{:S(2)}, u32[]{:S(2)}) collective-permute-start(f32[128,256]{1,0:T(8,128)S(1)} %collective-permute-done.16.away_ref), channel_id=1, source_target_pairs={{0,1},{1,0},{2,3},{3,2},{4,5},{5,4},{6,7},{7,6},{8,9},{9,8},{10,11... | collective-permute-start | bytes 393224 | tf_op jit(solution)/shard_map/ppermute | solution.py:418

commit v5 on v4

--- a/solution.py
+++ b/solution.py
@@ -10,6 +10,7 @@
 from jax.sharding import PartitionSpec as P
 
 GROUP = ("scanx", "scany", "pos")
+KEEP_IN_HBM = 64 * 1024 * 1024 - 448 * 1024
 PART_SWAP = ((0, 1), (1, 0))
 VMEM = pl.BlockSpec(memory_space=pltpu.VMEM)
 ANY = pl.BlockSpec(memory_space=pl.ANY)
@@ -54,6 +55,21 @@
     return places
 
 
+def block_shapes(nz, nx, tile):
+    return [tuple(tile if way is None else tile // 2 for way in ways) for ways in block_ways(nz, nx)]
+
+
+def packed_places(shapes):
+    lanes = min(width for _, width in shapes)
+    at, places = 0, []
+    for height, width in shapes:
+        places.append([])
+        for col in range(0, width, lanes):
+            places[-1].append((at, col, height))
+            at += height
+    return places
+
+
 def block_valid(z, x, nz, nx):
     result = []
     for zway, xway in block_ways(nz, nx):
@@ -91,16 +107,13 @@
     return pairs
 
 
-def dft_tables(length):
+def dft_waves(length):
     index = np.arange(length, dtype=np.int32)
     phase = (index[:, None] * index[None, :]) % length
     angle = phase.astype(np.float32) * np.float32(2.0 * math.pi / length)
     scale = np.float32(1.0 / math.sqrt(length))
-    cosine = (np.cos(angle) * scale).astype(jnp.bfloat16)
-    sine = (np.sin(angle) * scale).astype(jnp.bfloat16)
-    table_a = np.block([[cosine, sine], [-sine, cosine]])
-    table_b = np.block([[cosine, -sine], [sine, cosine]])
-    return table_a.astype(jnp.bfloat16), table_b.astype(jnp.bfloat16)
+    sine = np.sin(angle) * scale
+    return np.stack([np.cos(angle) * scale, sine, -sine]).astype(jnp.bfloat16)
 
 
 def aligned(row):
@@ -127,15 +140,14 @@
 def halo_blocks_kernel(nz, nx, off_hbm, spec_ref, *refs):
     z, x, c = (lax.axis_index(a) for a in GROUP)
     *outs, note_ref, off_ref, sems = refs
-    margin = spec_ref.shape[1] // 2
+    tile = spec_ref.shape[1]
+    margin = tile // 2
     off_copy = pltpu.make_async_copy(off_hbm, off_ref, sems.at[len(outs)])
     off_copy.start()
     copies = []
-    for k, (rows, cols) in enumerate(block_places(z, x, nz, nx, 0, margin, margin)):
-        height = outs[k].shape[0] - NOTE[0]
-        copies.append(
-            pltpu.make_async_copy(spec_ref.at[c, rows, cols], outs[k].at[pl.ds(0, height), :], sems.at[k])
-        )
+    places = block_places(z, x, nz, nx, 0, margin, margin)
+    for k, (out, (height, _), (rows, cols)) in enumerate(zip(outs, block_shapes(nz, nx, tile), places)):
+        copies.append(pltpu.make_async_copy(spec_ref.at[c, rows, cols], out.at[pl.ds(0, height), :], sems.at[k]))
         copies[-1].start()
     off_copy.wait()
     lane = lax.broadcasted_iota(jnp.int32, NOTE, 1)
@@ -166,11 +178,18 @@
 
 
 def fetch_kernel(*refs):
-    *refs, sems = refs
+    *refs, table_a, table_b, sems = refs
     count = len(refs) // 2
-    copies = [pltpu.make_async_copy(refs[k], refs[count + k], sems.at[k]) for k in range(count)]
+    *sources, waves = refs[: count + 1]
+    copies = [pltpu.make_async_copy(src, refs[count + 1 + k], sems.at[k]) for k, src in enumerate(sources)]
     for copy in copies:
         copy.start()
+    cosine, sine, minus = (waves[k] for k in range(3))
+    size = cosine.shape[0]
+    for table, blocks in ((table_a, (cosine, sine, minus, cosine)), (table_b, (cosine, minus, sine, cosine))):
+        for k, block in enumerate(blocks):
+            at, left = k // 2 * size, k % 2 * size
+            table[at : at + size, left : left + size] = block
     for copy in copies:
         copy.wait()
 
@@ -186,23 +205,28 @@
         out[j] = pltpu.roll(mixed, lax.rem(size - col, size), axis=1)
 
 
-def other_patches_kernel(nz, nx, note_ref, spec_ref, *refs):
+def patches_kernel(nz, nx, ours, note_ref, unused_ref, spec_ref, *refs):
     z, x, c = (lax.axis_index(a) for a in GROUP)
     *blocks, out, padded, note, sems = refs
     copies = read_notes([note_ref], [note], sems)
     tile = spec_ref.shape[1]
     margin = (padded.shape[0] - tile) // 2
-    padded[margin : margin + tile, margin : margin + tile] = spec_ref[c]
+    padded[margin : margin + tile, margin : margin + tile] = spec_ref[c if ours else 1 - c]
     if len(ways_of(nx)) == 1:
         far_cols = pl.ds(pl.multiple_of((1 - side_of(x, 0)) * (margin + tile), margin), margin)
         padded[:, far_cols] = jnp.zeros((padded.shape[0], margin), jnp.float32)
     places = block_places(z, x, nz, nx, margin, margin + tile, margin)
-    for block, (rows, cols), ok in zip(blocks, places, block_valid(z, x, nz, nx)):
-        height, width = block.shape[0] - NOTE[0], block.shape[1]
+    shapes = block_shapes(nz, nx, tile)
+    pieces = packed_places(shapes)
+    for k, ((height, width), (rows, cols), ok) in enumerate(zip(shapes, places, block_valid(z, x, nz, nx))):
 
         @pl.when(ok)
         def _():
-            padded[rows, cols] = block[:height, :]
+            if ours:
+                padded[rows, cols] = blocks[k][:height, :]
+            else:
+                parts = [blocks[0][at : at + height, :] for at, _, _ in pieces[k]]
+                padded[rows, cols] = parts[0] if len(parts) == 1 else jnp.concatenate(parts, axis=1)
 
         @pl.when(jnp.logical_not(ok))
         def _():
@@ -212,12 +236,14 @@
     cut_patches(note, padded, out)
 
 
-def own_patches_kernel(note_ref, padded, unused_ref, out, note, sems):
-    read_notes([note_ref], [note], sems)[0].wait()
-    cut_patches(note, padded, out)
-
-
-def positions_kernel(patch_ref, patch_other_ref, probe_ref, amp_ref, ta_ref, tb_ref, own_ref, other_ref):
+def pack_kernel(nz, nx, tile, unused_ref, *refs):
+    *blocks, out = refs
+    for block, pieces in zip(blocks, packed_places(block_shapes(nz, nx, tile))):
+        for at, col, height in pieces:
+            out[at : at + height, :] = block[:height, col : col + out.shape[1]]
+
+
+def positions_kernel(patch_ref, patch_other_ref, probe_ref, amp_ref, ta_ref, tb_ref, own_ref, other_ref, probe_own_ref, probe_other_ref):
     first = lax.axis_index("pos") == 0
     npos, size, _ = patch_ref.shape
     table_a = ta_ref[...]
@@ -252,8 +278,8 @@
         other_ref[j] = jnp.where(first, term_imag, term_real)
         grad_real += patch_real * diff_real + patch_imag * diff_imag
         grad_imag += patch_real * diff_imag - patch_imag * diff_real
-    own_ref[npos] = jnp.where(first, grad_real, grad_imag)
-    other_ref[npos] = jnp.where(first, grad_imag, grad_real)
+    probe_own_ref[...] = jnp.where(first, grad_real, grad_imag)
+    probe_other_ref[...] = jnp.where(first, grad_imag, grad_real)
 
 
 def half_of(z, x, c):
@@ -263,20 +289,19 @@
 def halve_kernel(own_ref, recv_ref, keep_ref, give_ref):
     half = half_of(*(lax.axis_index(a) for a in GROUP))
     rows = keep_ref.shape[0]
-    last = own_ref.shape[0] - 1
     for at, out in ((half, keep_ref), (1 - half, give_ref)):
         span = pl.ds(pl.multiple_of(at * rows, rows), rows)
-        out[...] = own_ref[last, span, :] + recv_ref[last, span, :]
+        out[...] = own_ref[span, :] + recv_ref[span, :]
 
 
 def gather_kernel(note_ref, other_note_ref, own_ref, recv_ref, unused_ref, grad, note, other_note, sems):
     copies = read_notes([note_ref, other_note_ref], [note, other_note], sems)
-    count, size, _ = own_ref.shape
+    npos, size, _ = own_ref.shape
     lane = lax.broadcasted_iota(jnp.int32, (size + 8, size), 1)
     grad[...] = jnp.zeros_like(grad)
     for copy, offs, terms in zip(copies, (note, other_note), (own_ref, recv_ref)):
         copy.wait()
-        for j in range(count - 1):
+        for j in range(npos):
             row, col = offset_in(offs, j)
             base, shift = aligned(row)
             term = rows_down(pltpu.roll(terms[j], col, axis=1), shift)
@@ -296,11 +321,10 @@
         block[...] = grad_ref[:, pl.ds(pl.multiple_of(side_of(x, way) * (margin + tile), margin), margin)]
 
 
-def fold_step_kernel(nz, nx, keep_ref, recv_ref, unused_ref, middle_ref, *refs):
+def fold_kernel(nz, nx, middle_ref, *refs):
     z, x = lax.axis_index("scanx"), lax.axis_index("scany")
     ways = ways_of(nx)
-    blocks, (out_ref, center_ref, *edges, total) = refs[: len(ways)], refs[len(ways) :]
-    out_ref[...] = keep_ref[...] + recv_ref[...]
+    blocks, (center_ref, *edges, total) = refs[: len(ways)], refs[len(ways) :]
     tile = center_ref.shape[0]
     margin = (middle_ref.shape[0] - tile) // 2
     total[...] = middle_ref[...]
@@ -316,13 +340,12 @@
         edge[...] = total[pl.ds(pl.multiple_of(side_of(z, way) * (margin + tile), margin), margin), :]
 
 
-def update_step_kernel(nz, keep_ref, recv_ref, spec_ref, center_ref, light_ref, other_light_ref, *refs):
+def update_kernel(nz, spec_ref, center_ref, light_ref, other_light_ref, edge_a, edge_b, *refs):
     z, c = lax.axis_index("scanx"), lax.axis_index("pos")
-    *edges, out_ref, part_ref, grad = refs
-    out_ref[...] = keep_ref[...] + recv_ref[...]
+    part_ref, grad = refs
     tile = center_ref.shape[0]
     grad[...] = center_ref[...]
-    for way, edge in enumerate(edges):
+    for way, edge in enumerate((edge_a, edge_b)):
         margin = edge.shape[0]
         at = pl.multiple_of(side_of(z, way) * (tile - margin), margin)
 
@@ -333,8 +356,8 @@
     part_ref[...] = spec_ref[c] + grad[...] / (light_ref[...] + other_light_ref[...] + 1.0)
 
 
-def add_kernel(a_ref, b_ref, out_ref):
-    out_ref[...] = a_ref[...] + b_ref[...]
+def add_kernel(a_ref, b_ref, *refs):
+    refs[-1][...] = a_ref[...] + b_ref[...]
 
 
 def specimen_kernel(part_ref, part_other_ref, out_ref):
@@ -386,14 +409,14 @@
     light_ref[...] = total[tile : 2 * tile, :]
 
 
-def call(kernel, out_shape, specs, *operands, scratch=(), vmem=16):
+def call(kernel, out_shape, specs, *operands, scratch=(), outs=VMEM, vmem=16 * 1024 * 1024):
     return pl.pallas_call(
         kernel,
         out_shape=out_shape,
         in_specs=specs,
-        out_specs=[VMEM] * len(out_shape),
+        out_specs=[outs] * len(out_shape),
         scratch_shapes=list(scratch),
-        compiler_params=pltpu.CompilerParams(vmem_limit_bytes=vmem * 1024 * 1024),
+        compiler_params=pltpu.CompilerParams(vmem_limit_bytes=vmem),
     )(*operands)
 
 
@@ -417,7 +440,7 @@
     def to_core(value):
         return lax.ppermute(value, "pos", PART_SWAP)
 
-    shapes = [(tile if v is None else margin, tile if w is None else margin) for v, w in ways]
+    shapes = block_shapes(nz, nx, tile)
     *blocks, note = call(
         functools.partial(halo_blocks_kernel, nz, nx),
         [f32(h + NOTE[0], w) for h, w in shapes] + [f32(*NOTE)],
@@ -425,42 +448,47 @@
         offsets,
         specimen,
         scratch=[pltpu.SMEM(offsets.shape, jnp.int32), dma(len(ways) + 1)],
+        vmem=KEEP_IN_HBM,
     )
     recv = [send(block, target) for block, target in zip(blocks, targets)]
-    other_note = to_core(note)
-
-    table_a, table_b = (jnp.asarray(t) for t in dft_tables(size))
-    late = (specimen, probe_wave, amplitudes, table_a, table_b)
+
+    waves = jnp.asarray(dft_waves(size))
+    late = (specimen, probe_wave, amplitudes)
     specimen_v, probe_v, amp_v, ta_v, tb_v = call(
         fetch_kernel,
-        [jax.ShapeDtypeStruct(a.shape, a.dtype) for a in late],
-        [HBM] * len(late),
+        [jax.ShapeDtypeStruct(a.shape, a.dtype) for a in late]
+        + [jax.ShapeDtypeStruct((2 * size, 2 * size), jnp.bfloat16)] * 2,
+        [ANY] * len(late) + [VMEM],
         *late,
+        waves,
         scratch=[dma(len(late))],
     )
-
-    give, padded = call(
-        functools.partial(other_patches_kernel, nz, nx),
-        [f32(npos, size, size), f32(tile + size, tile + size)],
-        [VMEM] * (2 + len(recv)),
-        other_note,
-        specimen_v,
+    lanes = min(w for _, w in shapes)
+    (packed,) = call(
+        functools.partial(pack_kernel, nz, nx, tile),
+        [f32(sum(h * w for h, w in shapes) // lanes, lanes)],
+        [ANY] + [VMEM] * len(recv),
+        probe_v,
         *recv,
-        scratch=[NOTE_SMEM, dma(1)],
-    )
-    patches_other = to_core(give)
-    (patches,) = call(
-        own_patches_kernel,
-        [f32(npos, size, size)],
-        [VMEM, VMEM, ANY],
-        note,
-        padded,
-        give,
-        scratch=[NOTE_SMEM, dma(1)],
-    )
-    own, other = call(
+    )
+
+    def patches_from(ours, after, *arrays):
+        return call(
+            functools.partial(patches_kernel, nz, nx, ours),
+            [f32(npos, size, size)],
+            [VMEM, ANY] + [VMEM] * (1 + len(arrays)),
+            note,
+            after,
+            specimen_v,
+            *arrays,
+            scratch=[pltpu.VMEM((tile + size, tile + size), jnp.float32), NOTE_SMEM, dma(1)],
+        )[0]
+
+    patches = patches_from(True, packed, *recv)
+    patches_other = patches_from(False, patches, to_core(packed))
+    own, other, probe_own, probe_other = call(
         positions_kernel,
-        [f32(npos + 1, size, size)] * 2,
+        [f32(npos, size, size)] * 2 + [f32(size, size)] * 2,
         [VMEM] * 6,
         patches,
         patches_other,
@@ -470,6 +498,7 @@
         tb_v,
     )
     terms = to_core(other)
+    other_note = to_core(note)
 
     zbits = [("z", 1 << k) for k in range(nz.bit_length() - 1)]
     xbits = [("x", 1 << k) for k in range(nx.bit_length() - 1)]
@@ -483,7 +512,7 @@
         return target
 
     half = f32(size // 2, size)
-    keep, away = call(halve_kernel, [half] * 2, [VMEM] * 2, own, terms)
+    keep, away = call(halve_kernel, [half] * 2, [VMEM] * 2, probe_own, to_core(probe_other))
     (grad,) = call(
         gather_kernel,
         [f32(tile + size, tile + size)],
@@ -519,24 +548,20 @@
         ],
     )
     beside = [send(piece, targets[ways.index((None, way))]) for piece, way in zip(beyond, xways)]
-    keep, center, *edges = call(
-        functools.partial(fold_step_kernel, nz, nx),
-        [half, f32(tile, tile)] + [f32(margin, tile)] * 2,
-        [VMEM, VMEM, ANY, VMEM] + [VMEM] * len(beside),
-        keep,
-        send(keep, stage(1)),
-        light,
+    (keep,) = call(add_kernel, [half], [VMEM, VMEM, ANY], keep, send(keep, stage(1)), light)
+    center, *edges = call(
+        functools.partial(fold_kernel, nz, nx),
+        [f32(tile, tile)] + [f32(margin, tile)] * 2,
+        [VMEM] * (1 + len(beside)),
         middle,
         *beside,
         scratch=[pltpu.VMEM((tile + size, tile), jnp.float32)],
     )
     arrived = [send(edge, targets[ways.index((way, None))]) for way, edge in enumerate(edges)]
-    keep, part = call(
-        functools.partial(update_step_kernel, nz),
-        [half, f32(tile, tile)],
-        [VMEM] * (6 + len(arrived)),
-        keep,
-        send(keep, stage(2)),
+    (part,) = call(
+        functools.partial(update_kernel, nz),
+        [f32(tile, tile)],
+        [VMEM] * (4 + len(arrived)),
         specimen_v,
         center,
         light,
@@ -544,7 +569,7 @@
         *arrived,
         scratch=[pltpu.VMEM((tile, tile), jnp.float32)],
     )
-    for k in range(3, len(orders[0])):
+    for k in range(2, len(orders[0])):
         (keep,) = call(add_kernel, [half], [VMEM] * 2, keep, send(keep, stage(k)))
     away = send(keep, stage(0))
     (new_specimen,) = call(specimen_kernel, [f32(2, tile, tile)], [VMEM] * 2, part, to_core(part))

time: 53.7 us -> 51.8 us (0.965)
  local copies, waits for them, and re-layouts: 5.79 us -> 3.09 us
  waiting for transfers between devices: 18.3 us -> 15.7 us
  starting transfers between devices: 18.5 us -> 20.7 us
  Pallas kernels: 9.93 us -> 11.2 us
    ppermute x12, waiting for transfers between devices: 15 us -> 11.1 us  [send(): return lax.ppermute(value, GROUP, permutation(sizes, target))]
    unnamed x14 -> x10, local copies, waits for them, and re-layouts: 5.79 us -> 3.09 us
    ppermute x7 -> x8, starting transfers between devices: 1.07 us -> 3.48 us  [to_core(): return lax.ppermute(value, 'pos', PART_SWAP)]
    ppermute x7 -> x8, waiting for transfers between devices: 3.31 us -> 4.61 us  [to_core(): return lax.ppermute(value, 'pos', PART_SWAP)]
    pallas_call x13 -> x16, Pallas kernels: 9.93 us -> 11.2 us  [call(): pl.pallas_call(kernel, out_shape=out_shape, in_specs=specs, out_specs=[ou...]
  transfers between devices with their start and end apart: 19 -> 20, of which waited for: 9 -> 7; matrix products, arithmetic and copies ran while one was open for 0% -> 0% of each run, Pallas kernels for 9% -> 9%
where the time goes in v5:
time: 51.8 us; the launch traced here: 51.5 us
  starting transfers between devices  20.7 us (40%)
  waiting for transfers between devices  15.7 us (30%)
  Pallas kernels  11.2 us (22%)
  local copies, waits for them, and re-layouts  3.09 us (6%)
  between operations  0.82 us (2%)
    ppermute x12, starting transfers between devices, send(): return lax.ppermute(value, GROUP, permutation(sizes, target))  17.2 us
    pallas_call x16, Pallas kernels, call(): pl.pallas_call(kernel, out_shape=out_shape, in_specs=specs, out_specs=[ou...  11.2 us
    ppermute x12, waiting for transfers between devices, send(): return lax.ppermute(value, GROUP, permutation(sizes, target))  11.1 us
    ppermute x8, waiting for transfers between devices, to_core(): return lax.ppermute(value, 'pos', PART_SWAP)  4.61 us
    ppermute x8, starting transfers between devices, to_core(): return lax.ppermute(value, 'pos', PART_SWAP)  3.48 us
    unnamed x10, local copies, waits for them, and re-layouts  3.09 us
  transfers between devices with their start and end apart: 20, of which 7 were waited for; matrix products, arithmetic and copies ran while one was open for 0% of the time, Pallas kernels for 9%

profile of v5, /device:TPU:0, one launch (start us, length us, event | category | flops | bytes accessed | tf_op | source)
XLA Modules:
  0.0 51.5 jit_solution(10559917964874973390)
XLA Ops:
  0.6 0.0 copy-start.2
  0.6 2.0 %shard_map.69 = (f32[264,128]{1,0:T(8,128)}, f32[136,256]{1,0:T(8,128)}, f32[136,256]{1,0:T(8,128)}, f32[136,128]{1,0:T(8,128)}, f32[136,128]{1,0:T(8,128)}, /*index=5*/f32[8,128]{1,0:T(8,128)}) custom-call(s32[2,2]{1,0:T(2,128)} %off_hbm.1, f32[2,256,256]{2,1,0:T(8,128)} %spec_ref.1), custom_call_target="tpu_custom_call" | custom-call | tf_op jit(solution)/shard_map/pallas_call | solution.py:413
  2.6 3.1 %collective-permute-start.1 = (f32[136,256]{1,0:T(8,128)}, f32[136,256]{1,0:T(8,128)S(1)}, u32[]{:S(2)}, u32[]{:S(2)}) collective-permute-start(f32[136,256]{1,0:T(8,128)} %get-tuple-element.29), channel_id=1, source_target_pairs={{0,4},{1,5},{2,6},{3,7},{4,0},{5,1},{6,2},{7,3},{8,12},{9,13},{10,... | collective-permute-start | bytes 417800 | tf_op jit(solution)/shard_map/ppermute | solution.py:438
  5.7 0.0 collective-permute-start.2
  5.7 1.5 %collective-permute-start = (f32[264,128]{1,0:T(8,128)}, f32[264,128]{1,0:T(8,128)S(1)}, u32[]{:S(2)}, u32[]{:S(2)}) collective-permute-start(f32[264,128]{1,0:T(8,128)} %get-tuple-element.28), channel_id=1, source_target_pairs={{0,2},{1,3},{2,0},{3,1},{4,6},{5,7},{6,4},{7,5},{8,10},{9,11},{10,... | collective-permute-start | bytes 405512 | tf_op jit(solution)/shard_map/ppermute | solution.py:438
  7.2 3.1 %collective-permute-start.3 = (f32[136,128]{1,0:T(8,128)}, f32[136,128]{1,0:T(8,128)S(1)}, u32[]{:S(2)}, u32[]{:S(2)}) collective-permute-start(f32[136,128]{1,0:T(8,128)} %get-tuple-element.31), channel_id=1, source_target_pairs={{0,6},{1,7},{2,4},{3,5},{4,2},{5,3},{6,0},{7,1},{8,14},{9,15},{10,... | collective-permute-start | bytes 208904 | tf_op jit(solution)/shard_map/ppermute | solution.py:438
  10.3 0.0 collective-permute-start.4
  10.3 0.0 copy-done.2
  10.3 0.0 copy-start
  10.3 1.0 %copy-done = f32[2,256,256]{2,1,0:T(8,128)S(1)} copy-done((f32[2,256,256]{2,1,0:T(8,128)S(1)}, f32[2,256,256]{2,1,0:T(8,128)}, u32[]{:S(2)}) %copy-start) | copy-done | bytes 524312
  11.4 0.0 copy-start.1
  11.4 1.0 %copy-done.1 = f32[2,256,256]{2,1,0:T(8,128)S(1)} copy-done((f32[2,256,256]{2,1,0:T(8,128)S(1)}, f32[2,256,256]{2,1,0:T(8,128)}, u32[]{:S(2)}) %copy-start.1) | copy-done | bytes 524312
  12.4 0.0 copy-start.3
  12.4 0.9 %copy-done.3 = bf16[2,256,256]{2,1,0:T(8,128)(2,1)S(1)} copy-done((bf16[2,256,256]{2,1,0:T(8,128)(2,1)S(1)}, bf16[2,256,256]{2,1,0:T(8,128)(2,1)}, u32[]{:S(2)}) %copy-start.3) | copy-done | bytes 262168
  13.4 0.2 shard_map.68
  13.6 0.0 collective-permute-done.3.refs_3_
  13.6 0.0 collective-permute-done.4.refs_4_
  13.6 0.0 collective-permute-done.refs_0_
  13.6 0.0 collective-permute-done.1.refs_1_
  13.6 0.0 collective-permute-done.2.refs_2_
  13.6 0.0 copy-start.4
  13.7 0.6 %collective-permute-start.5 = (f32[1024,128]{1,0:T(8,128)S(1)}, f32[1024,128]{1,0:T(8,128)S(1)}, u32[]{:S(2)}, u32[]{:S(2)}) collective-permute-start(f32[1024,128]{1,0:T(8,128)S(1)} %shard_map.70.unused_ref), channel_id=1, source_target_pairs={{0,1},{1,0},{2,3},{3,2},{4,5},{5,4},{6,7},{7,6},{8,9},{9,8},{10,11... | collective-permute-start | bytes 1572872 | tf_op jit(solution)/shard_map/ppermute | solution.py:441
  14.2 0.0 copy-done.4
  14.3 0.8 %shard_map.71.unused_ref.patch_ref = f32[2,256,256]{2,1,0:T(8,128)S(1)} custom-call(f32[8,128]{1,0:T(8,128)S(1)} %copy-done.4, f32[1024,128]{1,0:T(8,128)S(1)} %shard_map.70.unused_ref, f32[2,256,256]{2,1,0:T(8,128)S(1)} %get-tuple-element.25.spec_ref, f32[264,128]{1,0:T(8,128)S(1)} %collective-permute-done.refs_0_, ...), custom_call_target="tpu_custom_call" | custom-call | tf_op jit(solution)/shard_map/pallas_call | solution.py:413
  15.1 0.7 %collective-permute-done.5.refs_0_ = f32[1024,128]{1,0:T(8,128)S(1)} collective-permute-done((f32[1024,128]{1,0:T(8,128)S(1)}, f32[1024,128]{1,0:T(8,128)S(1)}, u32[]{:S(2)}, u32[]{:S(2)}) %collective-permute-start.5) | collective-permute-done | bytes 524320 | tf_op jit(solution)/shard_map/ppermute | solution.py:441
  15.8 0.8 %shard_map.72.patch_other_ref = f32[2,256,256]{2,1,0:T(8,128)S(1)} custom-call(f32[8,128]{1,0:T(8,128)S(1)} %copy-done.4, f32[2,256,256]{2,1,0:T(8,128)S(1)} %shard_map.71.unused_ref.patch_ref, f32[2,256,256]{2,1,0:T(8,128)S(1)} %get-tuple-element.25.spec_ref, f32[1024,128]{1,0:T(8,128)S(1)} %collective-permute-done.5.refs_0_), custom_call_target="tpu_custom_call" | custom-call | tf_op jit(solution)/shard_map/pallas_call | solution.py:413
  16.6 2.6 %shard_map.73 = (f32[2,256,256]{2,1,0:T(8,128)S(1)}, f32[2,256,256]{2,1,0:T(8,128)S(1)}, f32[256,256]{1,0:T(8,128)S(1)}, f32[256,256]{1,0:T(8,128)S(1)}) custom-call(f32[2,256,256]{2,1,0:T(8,128)S(1)} %shard_map.71.unused_ref.patch_ref, f32[2,256,256]{2,1,0:T(8,128)S(1)} %shard_map.72.patch_other_ref, ...), custom_call_target="tpu_custom_call" | custom-call | tf_op jit(solution)/shard_map/pallas_call | solution.py:413
  19.2 0.4 collective-permute-start.9
  19.7 0.1 collective-permute-start.6
  19.8 1.8 %collective-permute-done.6.recv_ref = f32[256,256]{1,0:T(8,128)S(1)} collective-permute-done((f32[256,256]{1,0:T(8,128)S(1)}, f32[256,256]{1,0:T(8,128)S(1)}, u32[]{:S(2)}, u32[]{:S(2)}) %collective-permute-start.6) | collective-permute-done | bytes 262176 | tf_op jit(solution)/shard_map/ppermute | solution.py:441
  21.6 1.6 %collective-permute-start.7 = (f32[128,256]{1,0:T(8,128)S(1)}, f32[128,256]{1,0:T(8,128)S(1)}, u32[]{:S(2)}, u32[]{:S(2)}) collective-permute-start(f32[128,256]{1,0:T(8,128)S(1)} %get-tuple-element.39), channel_id=1, source_target_pairs={{0,2},{1,5},{2,0},{3,7},{4,6},{5,1},{6,4},{7,3},{8,10},{9,13},{10,... | collective-permute-start | bytes 393224 | tf_op jit(solution)/shard_map/ppermute | solution.py:438
  23.2 1.7 %collective-permute-start.8 = (f32[8,128]{1,0:T(8,128)S(1)}, f32[8,128]{1,0:T(8,128)S(1)}, u32[]{:S(2)}, u32[]{:S(2)}) collective-permute-start(f32[8,128]{1,0:T(8,128)S(1)} %copy-done.4), channel_id=1, source_target_pairs={{0,1},{1,0},{2,3},{3,2},{4,5},{5,4},{6,7},{7,6},{8,9},{9,8},{10,11... | collective-permute-start | bytes 12296 | tf_op jit(solution)/shard_map/ppermute | solution.py:441
  24.9 0.8 %collective-permute-done.8.other_note_ref = f32[8,128]{1,0:T(8,128)S(1)} collective-permute-done((f32[8,128]{1,0:T(8,128)S(1)}, f32[8,128]{1,0:T(8,128)S(1)}, u32[]{:S(2)}, u32[]{:S(2)}) %collective-permute-start.8) | collective-permute-done | bytes 4128 | tf_op jit(solution)/shard_map/ppermute | solution.py:441
  25.7 0.0 collective-permute-done.9.recv_ref
  25.7 1.2 %shard_map.75.grad_ref = f32[512,512]{1,0:T(8,128)S(1)} custom-call(f32[8,128]{1,0:T(8,128)S(1)} %copy-done.4, f32[8,128]{1,0:T(8,128)S(1)} %collective-permute-done.8.other_note_ref, f32[2,256,256]{2,1,0:T(8,128)S(1)} %get-tuple-element.40.own_ref, f32[2,256,256]{2,1,0:T(8,128)S(1)} %collective-permute-done.9.recv_ref, ...), custom_call_target="tpu_custom_call" | custom-call | tf_op jit(solution)/shard_map/pallas_call | solution.py:413
  26.8 0.0 collective-permute-done.7.recv_ref
  26.9 0.1 shard_map.76
  27.0 1.3 %collective-permute-start.10 = (f32[512,128]{1,0:T(8,128)S(1)}, f32[512,128]{1,0:T(8,128)S(1)}, u32[]{:S(2)}, u32[]{:S(2)}) collective-permute-start(f32[512,128]{1,0:T(8,128)S(1)} %get-tuple-element.43), channel_id=1, source_target_pairs={{0,2},{1,3},{2,0},{3,1},{4,6},{5,7},{6,4},{7,5},{8,10},{9,11},{10,... | collective-permute-start | bytes 786440 | tf_op jit(solution)/shard_map/ppermute | solution.py:438
  28.3 3.1 %collective-permute-start.15 = (f32[128,256]{1,0:T(8,128)S(1)}, f32[128,256]{1,0:T(8,128)S(1)}, u32[]{:S(2)}, u32[]{:S(2)}) collective-permute-start(f32[128,256]{1,0:T(8,128)S(1)} %get-tuple-element.45.unused_ref.a_ref), channel_id=1, source_target_pairs={{0,4},{1,9},{2,6},{3,11},{4,0},{5,13},{6,2},{7,15},{8,12},{9,1},{1... | collective-permute-start | bytes 393224 | tf_op jit(solution)/shard_map/ppermute | solution.py:438
  31.4 1.5 %shard_map.78.light_ref.refs_0_ = f32[256,256]{1,0:T(8,128)S(1)} custom-call(f32[8,128]{1,0:T(8,128)S(1)} %copy-done.4, f32[2,256,256]{2,1,0:T(8,128)S(1)} %get-tuple-element.27.unused_ref.probe_ref, f32[128,256]{1,0:T(8,128)S(1)} %get-tuple-element.45.unused_ref.a_ref, f32[264,128]{1,0:T(8,128)S(1)} %collective-permute-done.refs_0_, ...), custom_call_target="tpu_custom_call" | custom-call | tf_op jit(solution)/shard_map/pallas_call | solution.py:413
  32.9 0.1 collective-permute-start.11
  33.0 1.7 %collective-permute-done.15.b_ref = f32[128,256]{1,0:T(8,128)S(1)} collective-permute-done((f32[128,256]{1,0:T(8,128)S(1)}, f32[128,256]{1,0:T(8,128)S(1)}, u32[]{:S(2)}, u32[]{:S(2)}) %collective-permute-start.15) | collective-permute-done | bytes 131104 | tf_op jit(solution)/shard_map/ppermute | solution.py:438
  34.6 2.1 %collective-permute-start.16 = (f32[128,256]{1,0:T(8,128)S(1)}, f32[128,256]{1,0:T(8,128)S(1)}, u32[]{:S(2)}, u32[]{:S(2)}) collective-permute-start(f32[128,256]{1,0:T(8,128)S(1)} %shard_map.81.a_ref), channel_id=1, source_target_pairs={{0,8},{1,3},{2,10},{3,1},{4,12},{5,7},{6,14},{7,5},{8,0},{9,11},{1... | collective-permute-start | bytes 393224 | tf_op jit(solution)/shard_map/ppermute | solution.py:438
  36.8 0.0 collective-permute-done.10.refs_0_
  36.8 0.1 shard_map.77
  36.9 0.9 %collective-permute-start.12 = (f32[128,256]{1,0:T(8,128)S(1)}, f32[128,256]{1,0:T(8,128)S(1)}, u32[]{:S(2)}, u32[]{:S(2)}) collective-permute-start(f32[128,256]{1,0:T(8,128)S(1)} %get-tuple-element.46), channel_id=1, source_target_pairs={{0,4},{1,5},{2,6},{3,7},{4,0},{5,1},{6,2},{7,3},{8,12},{9,13},{10,... | collective-permute-start | bytes 393224 | tf_op jit(solution)/shard_map/ppermute | solution.py:438
  37.8 0.0 collective-permute-start.13
  37.8 5.6 %collective-permute-done.16.b_ref = f32[128,256]{1,0:T(8,128)S(1)} collective-permute-done((f32[128,256]{1,0:T(8,128)S(1)}, f32[128,256]{1,0:T(8,128)S(1)}, u32[]{:S(2)}, u32[]{:S(2)}) %collective-permute-start.16) | collective-permute-done | bytes 131104 | tf_op jit(solution)/shard_map/ppermute | solution.py:438
  43.4 0.5 %collective-permute-start.17 = (f32[128,256]{1,0:T(8,128)S(1)}, f32[128,256]{1,0:T(8,128)S(1)}, u32[]{:S(2)}, u32[]{:S(2)}) collective-permute-start(f32[128,256]{1,0:T(8,128)S(1)} %shard_map.82.keep_ref), channel_id=1, source_target_pairs={{0,2},{1,5},{2,0},{3,7},{4,6},{5,1},{6,4},{7,3},{8,10},{9,13},{10,... | collective-permute-start | bytes 393224 | tf_op jit(solution)/shard_map/ppermute | solution.py:438
  43.9 0.0 collective-permute-done.11.other_light_ref
  43.9 0.0 collective-permute-done.12.edge_a
  43.9 0.0 collective-permute-done.13.edge_b
  43.9 0.1 shard_map.79.part_ref
  44.1 0.1 collective-permute-start.14
  44.1 0.5 collective-permute-start.18
  44.6 3.8 %collective-permute-done.17.away_ref = f32[128,256]{1,0:T(8,128)S(1)} collective-permute-done((f32[128,256]{1,0:T(8,128)S(1)}, f32[128,256]{1,0:T(8,128)S(1)}, u32[]{:S(2)}, u32[]{:S(2)}) %collective-permute-start.17) | collective-permute-done | bytes 131104 | tf_op jit(solution)/shard_map/ppermute | solution.py:438
  48.4 0.0 collective-permute-start.19
  48.4 0.0 collective-permute-done.18.keep_other_ref
  48.4 1.3 %collective-permute-done.19.away_other_ref = f32[128,256]{1,0:T(8,128)S(1)} collective-permute-done((f32[128,256]{1,0:T(8,128)S(1)}, f32[128,256]{1,0:T(8,128)S(1)}, u32[]{:S(2)}, u32[]{:S(2)}) %collective-permute-start.19) | collective-permute-done | bytes 131104 | tf_op jit(solution)/shard_map/ppermute | solution.py:441
  49.8 0.9 %shard_map.83 = f32[2,256,256]{2,1,0:T(8,128)} custom-call(f32[2,256,256]{2,1,0:T(8,128)S(1)} %get-tuple-element.27.unused_ref.probe_ref, f32[128,256]{1,0:T(8,128)S(1)} %shard_map.82.keep_ref, f32[128,256]{1,0:T(8,128)S(1)} %collective-permute-done.17.away_ref, f32[128,256]{1,0:T(8,128)S(1)} %collective-permute-done.18.keep_other_ref, ...), custom_call_target="tpu_custom_call" | custom-call | tf_op jit(solution)/shard_map/pallas_call | solution.py:413
  50.7 0.0 collective-permute-done.14.part_other_ref
  50.7 0.8 %shard_map.80 = f32[2,256,256]{2,1,0:T(8,128)} custom-call(f32[256,256]{1,0:T(8,128)S(1)} %shard_map.79.part_ref, f32[256,256]{1,0:T(8,128)S(1)} %collective-permute-done.14.part_other_ref), custom_call_target="tpu_custom_call" | custom-call | tf_op jit(solution)/shard_map/pallas_call | solution.py:413
  (4 shorter events, 0.1 us)
Async XLA Ops:
  0.6 9.7 %copy-start.2 = (bf16[3,256,256]{2,1,0:T(8,128)(2,1)S(1)}, bf16[3,256,256]{2,1,0:T(8,128)(2,1)}, u32[]{:S(2)}) copy-start(bf16[3,256,256]{2,1,0:T(8,128)(2,1)} %constant.2.clone.refs_3_) | copy-start | bytes 1179652
  2.6 11.0 %collective-permute-start.1 = (f32[136,256]{1,0:T(8,128)}, f32[136,256]{1,0:T(8,128)S(1)}, u32[]{:S(2)}, u32[]{:S(2)}) collective-permute-start(f32[136,256]{1,0:T(8,128)} %get-tuple-element.29), channel_id=1, source_target_pairs={{0,4},{1,5},{2,6},{3,7},{4,0},{5,1},{6,2},{7,3},{8,12},{9,13},{10,... | collective-permute-start | bytes 417800 | tf_op jit(solution)/shard_map/ppermute | solution.py:438
  5.7 7.9 %collective-permute-start.2 = (f32[136,256]{1,0:T(8,128)}, f32[136,256]{1,0:T(8,128)S(1)}, u32[]{:S(2)}, u32[]{:S(2)}) collective-permute-start(f32[136,256]{1,0:T(8,128)} %get-tuple-element.30), channel_id=1, source_target_pairs={{0,1},{1,0},{2,3},{3,2},{4,8},{5,9},{6,10},{7,11},{8,4},{9,5},{10,... | collective-permute-start | bytes 417800 | tf_op jit(solution)/shard_map/ppermute | solution.py:438
  5.7 7.9 %collective-permute-start = (f32[264,128]{1,0:T(8,128)}, f32[264,128]{1,0:T(8,128)S(1)}, u32[]{:S(2)}, u32[]{:S(2)}) collective-permute-start(f32[264,128]{1,0:T(8,128)} %get-tuple-element.28), channel_id=1, source_target_pairs={{0,2},{1,3},{2,0},{3,1},{4,6},{5,7},{6,4},{7,5},{8,10},{9,11},{10,... | collective-permute-start | bytes 405512 | tf_op jit(solution)/shard_map/ppermute | solution.py:438
  7.2 6.4 %collective-permute-start.3 = (f32[136,128]{1,0:T(8,128)}, f32[136,128]{1,0:T(8,128)S(1)}, u32[]{:S(2)}, u32[]{:S(2)}) collective-permute-start(f32[136,128]{1,0:T(8,128)} %get-tuple-element.31), channel_id=1, source_target_pairs={{0,6},{1,7},{2,4},{3,5},{4,2},{5,3},{6,0},{7,1},{8,14},{9,15},{10,... | collective-permute-start | bytes 208904 | tf_op jit(solution)/shard_map/ppermute | solution.py:438
  10.3 3.2 %collective-permute-start.4 = (f32[136,128]{1,0:T(8,128)}, f32[136,128]{1,0:T(8,128)S(1)}, u32[]{:S(2)}, u32[]{:S(2)}) collective-permute-start(f32[136,128]{1,0:T(8,128)} %get-tuple-element.32), channel_id=1, source_target_pairs={{0,1},{1,0},{2,3},{3,2},{4,10},{5,11},{6,8},{7,9},{8,6},{9,7},{10,... | collective-permute-start | bytes 208904 | tf_op jit(solution)/shard_map/ppermute | solution.py:438
  10.3 1.0 %copy-start = (f32[2,256,256]{2,1,0:T(8,128)S(1)}, f32[2,256,256]{2,1,0:T(8,128)}, u32[]{:S(2)}) copy-start(f32[2,256,256]{2,1,0:T(8,128)} %spec_ref.1) | copy-start | bytes 1572868
  11.4 1.0 %copy-start.1 = (f32[2,256,256]{2,1,0:T(8,128)S(1)}, f32[2,256,256]{2,1,0:T(8,128)}, u32[]{:S(2)}) copy-start(f32[2,256,256]{2,1,0:T(8,128)} %refs_1_.1) | copy-start | bytes 1572868
  12.4 0.9 %copy-start.3 = (bf16[2,256,256]{2,1,0:T(8,128)(2,1)S(1)}, bf16[2,256,256]{2,1,0:T(8,128)(2,1)}, u32[]{:S(2)}) copy-start(bf16[2,256,256]{2,1,0:T(8,128)(2,1)} %refs_2_.1) | copy-start | bytes 786436
  13.6 0.7 %copy-start.4 = (f32[8,128]{1,0:T(8,128)S(1)}, f32[8,128]{1,0:T(8,128)}, u32[]{:S(2)}) copy-start(f32[8,128]{1,0:T(8,128)} %get-tuple-element.26.note_ref) | copy-start | bytes 12292
  13.7 2.1 %collective-permute-start.5 = (f32[1024,128]{1,0:T(8,128)S(1)}, f32[1024,128]{1,0:T(8,128)S(1)}, u32[]{:S(2)}, u32[]{:S(2)}) collective-permute-start(f32[1024,128]{1,0:T(8,128)S(1)} %shard_map.70.unused_ref), channel_id=1, source_target_pairs={{0,1},{1,0},{2,3},{3,2},{4,5},{5,4},{6,7},{7,6},{8,9},{9,8},{10,11... | collective-permute-start | bytes 1572872 | tf_op jit(solution)/shard_map/ppermute | solution.py:441
  19.2 6.5 %collective-permute-start.9 = (f32[2,256,256]{2,1,0:T(8,128)S(1)}, f32[2,256,256]{2,1,0:T(8,128)S(1)}, u32[]{:S(2)}, u32[]{:S(2)}) collective-permute-start(f32[2,256,256]{2,1,0:T(8,128)S(1)} %get-tuple-element.41), channel_id=1, source_target_pairs={{0,1},{1,0},{2,3},{3,2},{4,5},{5,4},{6,7},{7,6},{8,9},{9,8},{10,11... | collective-permute-start | bytes 1572872 | tf_op jit(solution)/shard_map/ppermute | solution.py:441
  19.7 1.9 %collective-permute-start.6 = (f32[256,256]{1,0:T(8,128)S(1)}, f32[256,256]{1,0:T(8,128)S(1)}, u32[]{:S(2)}, u32[]{:S(2)}) collective-permute-start(f32[256,256]{1,0:T(8,128)S(1)} %get-tuple-element.37), channel_id=1, source_target_pairs={{0,1},{1,0},{2,3},{3,2},{4,5},{5,4},{6,7},{7,6},{8,9},{9,8},{10,11... | collective-permute-start | bytes 786440 | tf_op jit(solution)/shard_map/ppermute | solution.py:441
  21.6 5.2 %collective-permute-start.7 = (f32[128,256]{1,0:T(8,128)S(1)}, f32[128,256]{1,0:T(8,128)S(1)}, u32[]{:S(2)}, u32[]{:S(2)}) collective-permute-start(f32[128,256]{1,0:T(8,128)S(1)} %get-tuple-element.39), channel_id=1, source_target_pairs={{0,2},{1,5},{2,0},{3,7},{4,6},{5,1},{6,4},{7,3},{8,10},{9,13},{10,... | collective-permute-start | bytes 393224 | tf_op jit(solution)/shard_map/ppermute | solution.py:438
  23.2 2.5 %collective-permute-start.8 = (f32[8,128]{1,0:T(8,128)S(1)}, f32[8,128]{1,0:T(8,128)S(1)}, u32[]{:S(2)}, u32[]{:S(2)}) collective-permute-start(f32[8,128]{1,0:T(8,128)S(1)} %copy-done.4), channel_id=1, source_target_pairs={{0,1},{1,0},{2,3},{3,2},{4,5},{5,4},{6,7},{7,6},{8,9},{9,8},{10,11... | collective-permute-start | bytes 12296 | tf_op jit(solution)/shard_map/ppermute | solution.py:441
  27.0 9.8 %collective-permute-start.10 = (f32[512,128]{1,0:T(8,128)S(1)}, f32[512,128]{1,0:T(8,128)S(1)}, u32[]{:S(2)}, u32[]{:S(2)}) collective-permute-start(f32[512,128]{1,0:T(8,128)S(1)} %get-tuple-element.43), channel_id=1, source_target_pairs={{0,2},{1,3},{2,0},{3,1},{4,6},{5,7},{6,4},{7,5},{8,10},{9,11},{10,... | collective-permute-start | bytes 786440 | tf_op jit(solution)/shard_map/ppermute | solution.py:438
  28.3 6.3 %collective-permute-start.15 = (f32[128,256]{1,0:T(8,128)S(1)}, f32[128,256]{1,0:T(8,128)S(1)}, u32[]{:S(2)}, u32[]{:S(2)}) collective-permute-start(f32[128,256]{1,0:T(8,128)S(1)} %get-tuple-element.45.unused_ref.a_ref), channel_id=1, source_target_pairs={{0,4},{1,9},{2,6},{3,11},{4,0},{5,13},{6,2},{7,15},{8,12},{9,1},{1... | collective-permute-start | bytes 393224 | tf_op jit(solution)/shard_map/ppermute | solution.py:438
  32.9 11.1 %collective-permute-start.11 = (f32[256,256]{1,0:T(8,128)S(1)}, f32[256,256]{1,0:T(8,128)S(1)}, u32[]{:S(2)}, u32[]{:S(2)}) collective-permute-start(f32[256,256]{1,0:T(8,128)S(1)} %shard_map.78.light_ref.refs_0_), channel_id=1, source_target_pairs={{0,1},{1,0},{2,3},{3,2},{4,5},{5,4},{6,7},{7,6},{8,9},{9,8},{10,11... | collective-permute-start | bytes 786440 | tf_op jit(solution)/shard_map/ppermute | solution.py:441
  34.6 8.7 %collective-permute-start.16 = (f32[128,256]{1,0:T(8,128)S(1)}, f32[128,256]{1,0:T(8,128)S(1)}, u32[]{:S(2)}, u32[]{:S(2)}) collective-permute-start(f32[128,256]{1,0:T(8,128)S(1)} %shard_map.81.a_ref), channel_id=1, source_target_pairs={{0,8},{1,3},{2,10},{3,1},{4,12},{5,7},{6,14},{7,5},{8,0},{9,11},{1... | collective-permute-start | bytes 393224 | tf_op jit(solution)/shard_map/ppermute | solution.py:438
  36.9 7.1 %collective-permute-start.12 = (f32[128,256]{1,0:T(8,128)S(1)}, f32[128,256]{1,0:T(8,128)S(1)}, u32[]{:S(2)}, u32[]{:S(2)}) collective-permute-start(f32[128,256]{1,0:T(8,128)S(1)} %get-tuple-element.46), channel_id=1, source_target_pairs={{0,4},{1,5},{2,6},{3,7},{4,0},{5,1},{6,2},{7,3},{8,12},{9,13},{10,... | collective-permute-start | bytes 393224 | tf_op jit(solution)/shard_map/ppermute | solution.py:438
  37.8 6.2 %collective-permute-start.13 = (f32[128,256]{1,0:T(8,128)S(1)}, f32[128,256]{1,0:T(8,128)S(1)}, u32[]{:S(2)}, u32[]{:S(2)}) collective-permute-start(f32[128,256]{1,0:T(8,128)S(1)} %get-tuple-element.47), channel_id=1, source_target_pairs={{0,1},{1,0},{2,3},{3,2},{4,8},{5,9},{6,10},{7,11},{8,4},{9,5},{10,... | collective-permute-start | bytes 393224 | tf_op jit(solution)/shard_map/ppermute | solution.py:438
  43.4 5.0 %collective-permute-start.17 = (f32[128,256]{1,0:T(8,128)S(1)}, f32[128,256]{1,0:T(8,128)S(1)}, u32[]{:S(2)}, u32[]{:S(2)}) collective-permute-start(f32[128,256]{1,0:T(8,128)S(1)} %shard_map.82.keep_ref), channel_id=1, source_target_pairs={{0,2},{1,5},{2,0},{3,7},{4,6},{5,1},{6,4},{7,3},{8,10},{9,13},{10,... | collective-permute-start | bytes 393224 | tf_op jit(solution)/shard_map/ppermute | solution.py:438
  44.1 6.6 %collective-permute-start.14 = (f32[256,256]{1,0:T(8,128)S(1)}, f32[256,256]{1,0:T(8,128)S(1)}, u32[]{:S(2)}, u32[]{:S(2)}) collective-permute-start(f32[256,256]{1,0:T(8,128)S(1)} %shard_map.79.part_ref), channel_id=1, source_target_pairs={{0,1},{1,0},{2,3},{3,2},{4,5},{5,4},{6,7},{7,6},{8,9},{9,8},{10,11... | collective-permute-start | bytes 786440 | tf_op jit(solution)/shard_map/ppermute | solution.py:441
  44.1 4.3 %collective-permute-start.18 = (f32[128,256]{1,0:T(8,128)S(1)}, f32[128,256]{1,0:T(8,128)S(1)}, u32[]{:S(2)}, u32[]{:S(2)}) collective-permute-start(f32[128,256]{1,0:T(8,128)S(1)} %shard_map.82.keep_ref), channel_id=1, source_target_pairs={{0,1},{1,0},{2,3},{3,2},{4,5},{5,4},{6,7},{7,6},{8,9},{9,8},{10,11... | collective-permute-start | bytes 393224 | tf_op jit(solution)/shard_map/ppermute | solution.py:441
  48.4 1.3 %collective-permute-start.19 = (f32[128,256]{1,0:T(8,128)S(1)}, f32[128,256]{1,0:T(8,128)S(1)}, u32[]{:S(2)}, u32[]{:S(2)}) collective-permute-start(f32[128,256]{1,0:T(8,128)S(1)} %collective-permute-done.17.away_ref), channel_id=1, source_target_pairs={{0,1},{1,0},{2,3},{3,2},{4,5},{5,4},{6,7},{7,6},{8,9},{9,8},{10,11... | collective-permute-start | bytes 393224 | tf_op jit(solution)/shard_map/ppermute | solution.py:441

commit v6 on v5

--- a/solution.py
+++ b/solution.py
@@ -286,7 +286,7 @@
     return jnp.where(c == 0, lax.rem(x, 2), lax.rem(z, 2))
 
 
-def halve_kernel(own_ref, recv_ref, keep_ref, give_ref):
+def halve_kernel(own_ref, recv_ref, unused_ref, unused_light_ref, keep_ref, give_ref, handed_on_ref):
     half = half_of(*(lax.axis_index(a) for a in GROUP))
     rows = keep_ref.shape[0]
     for at, out in ((half, keep_ref), (1 - half, give_ref)):
@@ -294,7 +294,9 @@
         out[...] = own_ref[span, :] + recv_ref[span, :]
 
 
-def gather_kernel(note_ref, other_note_ref, own_ref, recv_ref, unused_ref, grad, note, other_note, sems):
+def gather_kernel(nx, note_ref, other_note_ref, own_ref, recv_ref, unused_ref, middle_ref, *refs):
+    x = lax.axis_index("scany")
+    *blocks, grad, note, other_note, sems = refs
     copies = read_notes([note_ref, other_note_ref], [note, other_note], sems)
     npos, size, _ = own_ref.shape
     lane = lax.broadcasted_iota(jnp.int32, (size + 8, size), 1)
@@ -309,19 +311,14 @@
             rows = pl.ds(base, size + 8)
             grad[rows, :size] += low
             grad[rows, size:] += term - low
-
-
-def cut_step_kernel(nx, keep_ref, recv_ref, grad_ref, out_ref, middle_ref, *blocks):
-    x = lax.axis_index("scany")
-    out_ref[...] = keep_ref[...] + recv_ref[...]
     tile = middle_ref.shape[1]
     margin = (middle_ref.shape[0] - tile) // 2
-    middle_ref[...] = grad_ref[:, margin : margin + tile]
+    middle_ref[...] = grad[:, margin : margin + tile]
     for block, way in zip(blocks, ways_of(nx)):
-        block[...] = grad_ref[:, pl.ds(pl.multiple_of(side_of(x, way) * (margin + tile), margin), margin)]
-
-
-def fold_kernel(nz, nx, middle_ref, *refs):
+        block[...] = grad[:, pl.ds(pl.multiple_of(side_of(x, way) * (margin + tile), margin), margin)]
+
+
+def fold_kernel(nz, nx, unused_ref, middle_ref, *refs):
     z, x = lax.axis_index("scanx"), lax.axis_index("scany")
     ways = ways_of(nx)
     blocks, (center_ref, *edges, total) = refs[: len(ways)], refs[len(ways) :]
@@ -340,7 +337,7 @@
         edge[...] = total[pl.ds(pl.multiple_of(side_of(z, way) * (margin + tile), margin), margin), :]
 
 
-def update_kernel(nz, spec_ref, center_ref, light_ref, other_light_ref, edge_a, edge_b, *refs):
+def update_kernel(nz, unused_ref, spec_ref, center_ref, light_ref, other_light_ref, edge_a, edge_b, *refs):
     z, c = lax.axis_index("scanx"), lax.axis_index("pos")
     part_ref, grad = refs
     tile = center_ref.shape[0]
@@ -360,13 +357,14 @@
     refs[-1][...] = a_ref[...] + b_ref[...]
 
 
-def specimen_kernel(part_ref, part_other_ref, out_ref):
+def specimen_kernel(part_ref, part_other_ref, out_ref, done_ref):
+    done_ref[...] = jnp.zeros(done_ref.shape, done_ref.dtype)
     c = lax.axis_index("pos")
     out_ref[c] = part_ref[...]
     out_ref[1 - c] = part_other_ref[...]
 
 
-def probe_kernel(step_size, probe_ref, keep_ref, away_ref, keep_other_ref, away_other_ref, out_ref):
+def probe_kernel(step_size, probe_ref, keep_ref, away_ref, keep_other_ref, away_other_ref, unused_ref, out_ref):
     z, x, c = (lax.axis_index(a) for a in GROUP)
     rows = keep_ref.shape[0]
     for part, keep, away in ((c, keep_ref, away_ref), (1 - c, keep_other_ref, away_other_ref)):
@@ -376,11 +374,11 @@
             out_ref[part, span, :] = probe_ref[part, span, :] + term[...] * step_size
 
 
-def light_kernel(npos, nz, nx, note_ref, probe_ref, unused_ref, *refs):
+def light_kernel(npos, nz, nx, which, note_ref, probe_ref, before_ref, unused_ref, *refs):
     z, x, c = (lax.axis_index(a) for a in GROUP)
-    ways = block_ways(nz, nx)
-    blocks, (light_ref, power_ref, total, *notes, sems) = refs[: len(ways)], refs[len(ways) :]
-    copies = read_notes([note_ref] + [note_of(b) for b in blocks], notes, sems)
+    blocks, (light_ref, power_ref, total, *notes, sems) = refs[: len(which)], refs[len(which) :]
+    own = len(notes) > len(which)
+    copies = read_notes(([note_ref] if own else []) + [note_of(b) for b in blocks], notes, sems)
     size = probe_ref.shape[1]
     margin = size // 2
     tile = light_ref.shape[0]
@@ -398,7 +396,8 @@
             keep = jnp.logical_and(lane >= col, lane < col + size)
             total[pl.ds(base, size + 8), :] += rows_down(jnp.where(keep, moved, 0.0), shift)
 
-    places = [((None, None), True)] + list(zip(ways, block_valid(z, x, nz, nx)))
+    ways, valid = block_ways(nz, nx), block_valid(z, x, nz, nx)
+    places = [((None, None), True)] * own + [(ways[k], valid[k]) for k in which]
     for copy, note, ((zway, xway), ok) in zip(copies, notes, places):
         copy.wait()
         down = 0 if zway is None else (2 * side_of(z, zway) - 1) * tile
@@ -406,16 +405,20 @@
         for j in range(npos):
             row, col = offset_in(note, j)
             add(row + down - margin, col + right - margin, ok)
-    light_ref[...] = total[tile : 2 * tile, :]
-
-
-def call(kernel, out_shape, specs, *operands, scratch=(), outs=VMEM, vmem=16 * 1024 * 1024):
+    if own:
+        light_ref[...] = total[tile : 2 * tile, :]
+    else:
+        light_ref[...] = before_ref[...] + total[tile : 2 * tile, :]
+
+
+def call(kernel, out_shape, specs, *operands, scratch=(), outs=None, aliases={}, vmem=16 * 1024 * 1024):
     return pl.pallas_call(
         kernel,
         out_shape=out_shape,
         in_specs=specs,
-        out_specs=[outs] * len(out_shape),
+        out_specs=outs or [VMEM] * len(out_shape),
         scratch_shapes=list(scratch),
+        input_output_aliases=aliases,
         compiler_params=pltpu.CompilerParams(vmem_limit_bytes=vmem),
     )(*operands)
 
@@ -453,8 +456,8 @@
     recv = [send(block, target) for block, target in zip(blocks, targets)]
 
     waves = jnp.asarray(dft_waves(size))
-    late = (specimen, probe_wave, amplitudes)
-    specimen_v, probe_v, amp_v, ta_v, tb_v = call(
+    late = (note, specimen, probe_wave, amplitudes)
+    note, specimen_v, probe_v, amp_v, ta_v, tb_v = call(
         fetch_kernel,
         [jax.ShapeDtypeStruct(a.shape, a.dtype) for a in late]
         + [jax.ShapeDtypeStruct((2 * size, 2 * size), jnp.bfloat16)] * 2,
@@ -484,8 +487,27 @@
             scratch=[pltpu.VMEM((tile + size, tile + size), jnp.float32), NOTE_SMEM, dma(1)],
         )[0]
 
+    def light_from(which, own, before, after):
+        return call(
+            functools.partial(light_kernel, npos, nz, nx, which),
+            [f32(tile, tile)],
+            [VMEM, VMEM, ANY if own else VMEM, ANY] + [VMEM] * len(which),
+            note,
+            probe_v,
+            before,
+            after,
+            *[recv[k] for k in which],
+            scratch=[
+                pltpu.VMEM((size, size), jnp.float32),
+                pltpu.VMEM((3 * tile, size), jnp.float32),
+                *[NOTE_SMEM] * (own + len(which)),
+                dma(own + len(which)),
+            ],
+        )[0]
+
     patches = patches_from(True, packed, *recv)
-    patches_other = patches_from(False, patches, to_core(packed))
+    light = light_from([k for k, (_, w) in enumerate(ways) if w is None], True, packed, patches)
+    patches_other = patches_from(False, light, to_core(packed))
     own, other, probe_own, probe_other = call(
         positions_kernel,
         [f32(npos, size, size)] * 2 + [f32(size, size)] * 2,
@@ -497,8 +519,8 @@
         ta_v,
         tb_v,
     )
-    terms = to_core(other)
     other_note = to_core(note)
+    light = light_from([k for k, (_, w) in enumerate(ways) if w is not None], False, light, own)
 
     zbits = [("z", 1 << k) for k in range(nz.bit_length() - 1)]
     xbits = [("x", 1 << k) for k in range(nx.bit_length() - 1)]
@@ -512,56 +534,49 @@
         return target
 
     half = f32(size // 2, size)
-    keep, away = call(halve_kernel, [half] * 2, [VMEM] * 2, probe_own, to_core(probe_other))
-    (grad,) = call(
-        gather_kernel,
-        [f32(tile + size, tile + size)],
+    keep, away, other = call(
+        halve_kernel,
+        [half] * 2 + [f32(npos, size, size)],
+        [VMEM, VMEM, ANY, ANY],
+        probe_own,
+        to_core(probe_other),
+        other,
+        light,
+        outs=[VMEM, VMEM, ANY],
+        aliases={2: 2},
+    )
+    terms = to_core(other)
+    middle, *beyond = call(
+        functools.partial(gather_kernel, nx),
+        [f32(tile + size, tile)] + [f32(tile + size, margin)] * len(xways),
         [VMEM] * 4 + [ANY],
         note,
         other_note,
         own,
         terms,
         keep,
-        scratch=[NOTE_SMEM, NOTE_SMEM, dma(2)],
-    )
-    keep, middle, *beyond = call(
-        functools.partial(cut_step_kernel, nx),
-        [half, f32(tile + size, tile)] + [f32(tile + size, margin)] * len(xways),
-        [VMEM] * 3,
-        keep,
-        send(away, stage(0)),
-        grad,
-    )
-    (light,) = call(
-        functools.partial(light_kernel, npos, nz, nx),
-        [f32(tile, tile)],
-        [VMEM, VMEM, ANY] + [VMEM] * len(recv),
-        note,
-        probe_v,
-        keep,
-        *recv,
-        scratch=[
-            pltpu.VMEM((size, size), jnp.float32),
-            pltpu.VMEM((3 * tile, size), jnp.float32),
-            *[NOTE_SMEM] * (1 + len(recv)),
-            dma(1 + len(recv)),
-        ],
-    )
+        scratch=[pltpu.VMEM((tile + size, tile + size), jnp.float32), NOTE_SMEM, NOTE_SMEM, dma(2)],
+    )
+    (keep,) = call(add_kernel, [half], [VMEM] * 2 + [ANY], keep, send(away, stage(0)), middle)
     beside = [send(piece, targets[ways.index((None, way))]) for piece, way in zip(beyond, xways)]
-    (keep,) = call(add_kernel, [half], [VMEM, VMEM, ANY], keep, send(keep, stage(1)), light)
+    (keep,) = call(add_kernel, [half], [VMEM] * 2, keep, send(keep, stage(1)))
     center, *edges = call(
         functools.partial(fold_kernel, nz, nx),
         [f32(tile, tile)] + [f32(margin, tile)] * 2,
-        [VMEM] * (1 + len(beside)),
+        [ANY] + [VMEM] * (1 + len(beside)),
+        keep,
         middle,
         *beside,
         scratch=[pltpu.VMEM((tile + size, tile), jnp.float32)],
     )
     arrived = [send(edge, targets[ways.index((way, None))]) for way, edge in enumerate(edges)]
+    for k in range(2, len(orders[0])):
+        (keep,) = call(add_kernel, [half], [VMEM] * 2, keep, send(keep, stage(k)))
     (part,) = call(
         functools.partial(update_kernel, nz),
         [f32(tile, tile)],
-        [VMEM] * (4 + len(arrived)),
+        [ANY] + [VMEM] * (4 + len(arrived)),
+        keep,
         specimen_v,
         center,
         light,
@@ -569,20 +584,19 @@
         *arrived,
         scratch=[pltpu.VMEM((tile, tile), jnp.float32)],
     )
-    for k in range(2, len(orders[0])):
-        (keep,) = call(add_kernel, [half], [VMEM] * 2, keep, send(keep, stage(k)))
     away = send(keep, stage(0))
-    (new_specimen,) = call(specimen_kernel, [f32(2, tile, tile)], [VMEM] * 2, part, to_core(part))
+    new_specimen, done = call(specimen_kernel, [f32(2, tile, tile), f32(*NOTE)], [VMEM] * 2, part, to_core(part))
     step_size = 1.0 / math.sqrt(npos * nz * nx * nc)
     (new_probe,) = call(
         functools.partial(probe_kernel, step_size),
         [f32(2, size, size)],
-        [VMEM] * 5,
+        [VMEM] * 5 + [ANY],
         probe_v,
         keep,
         away,
         to_core(keep),
         to_core(away),
+        done,
     )
     return (new_specimen, new_probe)
 

time: 51.8 us -> 50.1 us (0.967)
  waiting for transfers between devices: 15.7 us -> 13.4 us
  Pallas kernels: 11.2 us -> 12.1 us
    ppermute x8, waiting for transfers between devices: 4.61 us -> 0.84 us  [to_core(): return lax.ppermute(value, 'pos', PART_SWAP)]
    ppermute x12, waiting for transfers between devices: 11.1 us -> 12.6 us  [send(): return lax.ppermute(value, GROUP, permutation(sizes, target))]
    ppermute x8, starting transfers between devices: 3.48 us -> 2.16 us  [to_core(): return lax.ppermute(value, 'pos', PART_SWAP)]
    pallas_call x16 -> x17, Pallas kernels: 11.2 us -> 12.1 us  [call(): pl.pallas_call(kernel, out_shape=out_shape, in_specs=specs, out_specs=out...]
    ppermute x12, starting transfers between devices: 17.2 us -> 18.1 us  [send(): return lax.ppermute(value, GROUP, permutation(sizes, target))]
  transfers between devices with their start and end apart: 20 -> 20, of which waited for: 7 -> 6; matrix products, arithmetic and copies ran while one was open for 0% -> 0% of each run, Pallas kernels for 9% -> 11%
where the time goes in v6:
time: 50.1 us; the launch traced here: 49.7 us
  starting transfers between devices  20.3 us (41%)
  waiting for transfers between devices  13.4 us (27%)
  Pallas kernels  12.1 us (24%)
  local copies, waits for them, and re-layouts  3.04 us (6%)
  between operations  0.85 us (2%)
    ppermute x12, starting transfers between devices, send(): return lax.ppermute(value, GROUP, permutation(sizes, target))  18.1 us
    ppermute x12, waiting for transfers between devices, send(): return lax.ppermute(value, GROUP, permutation(sizes, target))  12.6 us
    pallas_call x17, Pallas kernels, call(): pl.pallas_call(kernel, out_shape=out_shape, in_specs=specs, out_specs=out...  12.1 us
    unnamed x10, local copies, waits for them, and re-layouts  3.04 us
    ppermute x8, starting transfers between devices, to_core(): return lax.ppermute(value, 'pos', PART_SWAP)  2.16 us
  transfers between devices with their start and end apart: 20, of which 6 were waited for; matrix products, arithmetic and copies ran while one was open for 0% of the time, Pallas kernels for 11%

profile of v6, /device:TPU:0, one launch (start us, length us, event | category | flops | bytes accessed | tf_op | source)
XLA Modules:
  0.0 49.7 jit_solution(17162009718486763036)
XLA Ops:
  0.6 0.0 copy-start.2
  0.6 2.0 %shard_map.68 = (f32[264,128]{1,0:T(8,128)}, f32[136,256]{1,0:T(8,128)}, f32[136,256]{1,0:T(8,128)}, f32[136,128]{1,0:T(8,128)}, f32[136,128]{1,0:T(8,128)}, /*index=5*/f32[8,128]{1,0:T(8,128)}) custom-call(s32[2,2]{1,0:T(2,128)} %off_hbm.1, f32[2,256,256]{2,1,0:T(8,128)} %refs_1_.1), custom_call_target="tpu_custom_call" | custom-call | tf_op jit(solution)/shard_map/pallas_call | solution.py:415
  2.6 3.1 %collective-permute-start.1 = (f32[136,256]{1,0:T(8,128)}, f32[136,256]{1,0:T(8,128)S(1)}, u32[]{:S(2)}, u32[]{:S(2)}) collective-permute-start(f32[136,256]{1,0:T(8,128)} %get-tuple-element.32), channel_id=1, source_target_pairs={{0,4},{1,5},{2,6},{3,7},{4,0},{5,1},{6,2},{7,3},{8,12},{9,13},{10,... | collective-permute-start | bytes 417800 | tf_op jit(solution)/shard_map/ppermute | solution.py:441
  5.7 0.0 copy-start.4
  5.7 0.0 collective-permute-start.2
  5.7 1.5 %collective-permute-start = (f32[264,128]{1,0:T(8,128)}, f32[264,128]{1,0:T(8,128)S(1)}, u32[]{:S(2)}, u32[]{:S(2)}) collective-permute-start(f32[264,128]{1,0:T(8,128)} %get-tuple-element.31), channel_id=1, source_target_pairs={{0,2},{1,3},{2,0},{3,1},{4,6},{5,7},{6,4},{7,5},{8,10},{9,11},{10,... | collective-permute-start | bytes 405512 | tf_op jit(solution)/shard_map/ppermute | solution.py:441
  7.2 3.1 %collective-permute-start.3 = (f32[136,128]{1,0:T(8,128)}, f32[136,128]{1,0:T(8,128)S(1)}, u32[]{:S(2)}, u32[]{:S(2)}) collective-permute-start(f32[136,128]{1,0:T(8,128)} %get-tuple-element.34), channel_id=1, source_target_pairs={{0,6},{1,7},{2,4},{3,5},{4,2},{5,3},{6,0},{7,1},{8,14},{9,15},{10,... | collective-permute-start | bytes 208904 | tf_op jit(solution)/shard_map/ppermute | solution.py:441
  10.3 0.0 collective-permute-start.4
  10.3 0.0 copy-done.2
  10.3 0.0 copy-done.4
  10.3 0.0 copy-start
  10.4 1.0 %copy-done = f32[2,256,256]{2,1,0:T(8,128)S(1)} copy-done((f32[2,256,256]{2,1,0:T(8,128)S(1)}, f32[2,256,256]{2,1,0:T(8,128)}, u32[]{:S(2)}) %copy-start) | copy-done | bytes 524312
  11.4 0.0 copy-start.1
  11.4 1.0 %copy-done.1 = f32[2,256,256]{2,1,0:T(8,128)S(1)} copy-done((f32[2,256,256]{2,1,0:T(8,128)S(1)}, f32[2,256,256]{2,1,0:T(8,128)}, u32[]{:S(2)}) %copy-start.1) | copy-done | bytes 524312
  12.4 0.0 copy-start.3
  12.4 0.9 %copy-done.3 = bf16[2,256,256]{2,1,0:T(8,128)(2,1)S(1)} copy-done((bf16[2,256,256]{2,1,0:T(8,128)(2,1)S(1)}, bf16[2,256,256]{2,1,0:T(8,128)(2,1)}, u32[]{:S(2)}) %copy-start.3) | copy-done | bytes 262168
  13.4 0.2 shard_map.69
  13.6 0.0 collective-permute-done.3.refs_3_.refs_1_
  13.6 0.0 collective-permute-done.4.refs_4_.refs_2_
  13.6 0.0 collective-permute-done.refs_0_
  13.6 0.0 collective-permute-done.1.refs_1_.refs_0_
  13.6 0.0 collective-permute-done.2.refs_2_.refs_1_
  13.7 0.6 %collective-permute-start.5 = (f32[1024,128]{1,0:T(8,128)S(1)}, f32[1024,128]{1,0:T(8,128)S(1)}, u32[]{:S(2)}, u32[]{:S(2)}) collective-permute-start(f32[1024,128]{1,0:T(8,128)S(1)} %shard_map.70.unused_ref.before_ref), channel_id=1, source_target_pairs={{0,1},{1,0},{2,3},{3,2},{4,5},{5,4},{6,7},{7,6},{8,9},{9,8},{10,11... | collective-permute-start | bytes 1572872 | tf_op jit(solution)/shard_map/ppermute | solution.py:444
  14.3 0.8 %shard_map.71.unused_ref.patch_ref = f32[2,256,256]{2,1,0:T(8,128)S(1)} custom-call(f32[8,128]{1,0:T(8,128)S(1)} %get-tuple-element.29.note_ref, f32[1024,128]{1,0:T(8,128)S(1)} %shard_map.70.unused_ref.before_ref, f32[2,256,256]{2,1,0:T(8,128)S(1)} %get-tuple-element.36.spec_ref, f32[264,128]{1,0:T(8,128)S(1)} %collective-permute-done.refs_0_, ...), custom_call_target="tpu_custom_call" | custom-call | tf_op jit(solution)/shard_map/pallas_call | solution.py:415
  15.1 1.4 %shard_map.72.unused_ref.before_ref = f32[256,256]{1,0:T(8,128)S(1)} custom-call(f32[8,128]{1,0:T(8,128)S(1)} %get-tuple-element.29.note_ref, f32[2,256,256]{2,1,0:T(8,128)S(1)} %get-tuple-element.30.unused_ref.probe_ref, f32[1024,128]{1,0:T(8,128)S(1)} %shard_map.70.unused_ref.before_ref, f32[2,256,256]{2,1,0:T(8,128)S(1)} %shard_map.71.unused_ref.patch_ref, ...), custom_call_target="tpu_custom_call" | custom-call | tf_op jit(solution)/shard_map/pallas_call | solution.py:415
  16.5 0.0 collective-permute-done.5.refs_0_
  16.5 0.8 %shard_map.73.patch_other_ref = f32[2,256,256]{2,1,0:T(8,128)S(1)} custom-call(f32[8,128]{1,0:T(8,128)S(1)} %get-tuple-element.29.note_ref, f32[256,256]{1,0:T(8,128)S(1)} %shard_map.72.unused_ref.before_ref, f32[2,256,256]{2,1,0:T(8,128)S(1)} %get-tuple-element.36.spec_ref, f32[1024,128]{1,0:T(8,128)S(1)} %collective-permute-done.5.refs_0_), custom_call_target="tpu_custom_call" | custom-call | tf_op jit(solution)/shard_map/pallas_call | solution.py:415
  17.3 2.5 %shard_map.74 = (f32[2,256,256]{2,1,0:T(8,128)S(1)}, f32[2,256,256]{2,1,0:T(8,128)S(1)}, f32[256,256]{1,0:T(8,128)S(1)}, f32[256,256]{1,0:T(8,128)S(1)}) custom-call(f32[2,256,256]{2,1,0:T(8,128)S(1)} %shard_map.71.unused_ref.patch_ref, f32[2,256,256]{2,1,0:T(8,128)S(1)} %shard_map.73.patch_other_ref, ...), custom_call_target="tpu_custom_call" | custom-call | tf_op jit(solution)/shard_map/pallas_call | solution.py:415
  19.9 0.1 collective-permute-start.6
  19.9 1.1 %shard_map.75.unused_light_ref.light_ref = f32[256,256]{1,0:T(8,128)S(1)} custom-call(f32[8,128]{1,0:T(8,128)S(1)} %get-tuple-element.29.note_ref, f32[2,256,256]{2,1,0:T(8,128)S(1)} %get-tuple-element.30.unused_ref.probe_ref, f32[256,256]{1,0:T(8,128)S(1)} %shard_map.72.unused_ref.before_ref, f32[2,256,256]{2,1,0:T(8,128)S(1)} %get-tuple-element.43.unused_ref.own_ref, ...), custom_call_target="tpu_custom_call" | custom-call | tf_op jit(solution)/shard_map/pallas_call | solution.py:415
  21.0 0.4 collective-permute-done.6.recv_ref
  21.5 0.3 collective-permute-start.9
  21.8 0.3 collective-permute-start.8
  22.1 1.5 %collective-permute-start.7 = (f32[128,256]{1,0:T(8,128)S(1)}, f32[128,256]{1,0:T(8,128)S(1)}, u32[]{:S(2)}, u32[]{:S(2)}) collective-permute-start(f32[128,256]{1,0:T(8,128)S(1)} %get-tuple-element.45), channel_id=1, source_target_pairs={{0,2},{1,5},{2,0},{3,7},{4,6},{5,1},{6,4},{7,3},{8,10},{9,13},{10,... | collective-permute-start | bytes 393224 | tf_op jit(solution)/shard_map/ppermute | solution.py:441
  23.6 0.0 collective-permute-done.8.other_note_ref
  23.6 0.0 collective-permute-done.9.recv_ref
  23.6 1.2 %shard_map.77 = (f32[512,256]{1,0:T(8,128)S(1)}, f32[512,128]{1,0:T(8,128)S(1)}) custom-call(f32[8,128]{1,0:T(8,128)S(1)} %get-tuple-element.29.note_ref, f32[8,128]{1,0:T(8,128)S(1)} %collective-permute-done.8.other_note_ref, f32[2,256,256]{2,1,0:T(8,128)S(1)} %get-tuple-element.43.unused_ref.own_ref, f32[2,256,256]{2,1,0:T(8,128)S(1)} %collective-permute-done.9.recv_ref, ...), custom_call_target="tpu_custom_call" | custom-call | tf_op jit(solution)/shard_map/pallas_call | solution.py:415
  24.8 1.5 %collective-permute-start.12 = (f32[512,128]{1,0:T(8,128)S(1)}, f32[512,128]{1,0:T(8,128)S(1)}, u32[]{:S(2)}, u32[]{:S(2)}) collective-permute-start(f32[512,128]{1,0:T(8,128)S(1)} %get-tuple-element.48), channel_id=1, source_target_pairs={{0,2},{1,3},{2,0},{3,1},{4,6},{5,7},{6,4},{7,5},{8,10},{9,11},{10,... | collective-permute-start | bytes 786440 | tf_op jit(solution)/shard_map/ppermute | solution.py:441
  26.3 0.8 %collective-permute-done.7.b_ref = f32[128,256]{1,0:T(8,128)S(1)} collective-permute-done((f32[128,256]{1,0:T(8,128)S(1)}, f32[128,256]{1,0:T(8,128)S(1)}, u32[]{:S(2)}, u32[]{:S(2)}) %collective-permute-start.7) | collective-permute-done | bytes 131104 | tf_op jit(solution)/shard_map/ppermute | solution.py:441
  27.1 3.0 %collective-permute-start.10 = (f32[128,256]{1,0:T(8,128)S(1)}, f32[128,256]{1,0:T(8,128)S(1)}, u32[]{:S(2)}, u32[]{:S(2)}) collective-permute-start(f32[128,256]{1,0:T(8,128)S(1)} %shard_map.78.a_ref), channel_id=1, source_target_pairs={{0,4},{1,9},{2,6},{3,11},{4,0},{5,13},{6,2},{7,15},{8,12},{9,1},{1... | collective-permute-start | bytes 393224 | tf_op jit(solution)/shard_map/ppermute | solution.py:441
  30.0 0.0 collective-permute-start.13
  30.0 3.9 %collective-permute-done.10.b_ref = f32[128,256]{1,0:T(8,128)S(1)} collective-permute-done((f32[128,256]{1,0:T(8,128)S(1)}, f32[128,256]{1,0:T(8,128)S(1)}, u32[]{:S(2)}, u32[]{:S(2)}) %collective-permute-start.10) | collective-permute-done | bytes 131104 | tf_op jit(solution)/shard_map/ppermute | solution.py:441
  33.9 2.0 %collective-permute-start.11 = (f32[128,256]{1,0:T(8,128)S(1)}, f32[128,256]{1,0:T(8,128)S(1)}, u32[]{:S(2)}, u32[]{:S(2)}) collective-permute-start(f32[128,256]{1,0:T(8,128)S(1)} %shard_map.79.a_ref.unused_ref), channel_id=1, source_target_pairs={{0,8},{1,3},{2,10},{3,1},{4,12},{5,7},{6,14},{7,5},{8,0},{9,11},{1... | collective-permute-start | bytes 393224 | tf_op jit(solution)/shard_map/ppermute | solution.py:441
  35.9 0.0 collective-permute-done.12.refs_0_
  35.9 0.1 shard_map.81
  36.0 0.4 collective-permute-start.14
  36.5 0.2 collective-permute-start.15
  36.6 5.5 %collective-permute-done.11.b_ref = f32[128,256]{1,0:T(8,128)S(1)} collective-permute-done((f32[128,256]{1,0:T(8,128)S(1)}, f32[128,256]{1,0:T(8,128)S(1)}, u32[]{:S(2)}, u32[]{:S(2)}) %collective-permute-start.11) | collective-permute-done | bytes 131104 | tf_op jit(solution)/shard_map/ppermute | solution.py:441
  42.2 0.0 collective-permute-done.13.other_light_ref
  42.2 0.0 collective-permute-done.14.edge_a
  42.2 0.0 collective-permute-done.15.edge_b
  42.2 0.1 shard_map.82.part_ref
  42.3 0.1 collective-permute-start.16
  42.4 1.9 %collective-permute-start.17 = (f32[128,256]{1,0:T(8,128)S(1)}, f32[128,256]{1,0:T(8,128)S(1)}, u32[]{:S(2)}, u32[]{:S(2)}) collective-permute-start(f32[128,256]{1,0:T(8,128)S(1)} %shard_map.80.unused_ref.keep_ref), channel_id=1, source_target_pairs={{0,2},{1,5},{2,0},{3,7},{4,6},{5,1},{6,4},{7,3},{8,10},{9,13},{10,... | collective-permute-start | bytes 393224 | tf_op jit(solution)/shard_map/ppermute | solution.py:441
  44.3 0.8 %collective-permute-start.18 = (f32[128,256]{1,0:T(8,128)S(1)}, f32[128,256]{1,0:T(8,128)S(1)}, u32[]{:S(2)}, u32[]{:S(2)}) collective-permute-start(f32[128,256]{1,0:T(8,128)S(1)} %shard_map.80.unused_ref.keep_ref), channel_id=1, source_target_pairs={{0,1},{1,0},{2,3},{3,2},{4,5},{5,4},{6,7},{7,6},{8,9},{9,8},{10,11... | collective-permute-start | bytes 393224 | tf_op jit(solution)/shard_map/ppermute | solution.py:444
  45.1 2.4 %collective-permute-done.17.away_ref = f32[128,256]{1,0:T(8,128)S(1)} collective-permute-done((f32[128,256]{1,0:T(8,128)S(1)}, f32[128,256]{1,0:T(8,128)S(1)}, u32[]{:S(2)}, u32[]{:S(2)}) %collective-permute-start.17) | collective-permute-done | bytes 131104 | tf_op jit(solution)/shard_map/ppermute | solution.py:441
  47.5 0.1 collective-permute-start.19
  47.6 0.0 collective-permute-done.16.part_other_ref
  47.6 0.8 %shard_map.83 = (f32[2,256,256]{2,1,0:T(8,128)}, f32[8,128]{1,0:T(8,128)S(1)}) custom-call(f32[256,256]{1,0:T(8,128)S(1)} %shard_map.82.part_ref, f32[256,256]{1,0:T(8,128)S(1)} %collective-permute-done.16.part_other_ref), custom_call_target="tpu_custom_call" | custom-call | tf_op jit(solution)/shard_map/pallas_call | solution.py:415
  48.4 0.0 collective-permute-done.18.keep_other_ref
  48.4 0.4 collective-permute-done.19.away_other_ref
  48.8 0.9 %shard_map.84 = f32[2,256,256]{2,1,0:T(8,128)} custom-call(f32[2,256,256]{2,1,0:T(8,128)S(1)} %get-tuple-element.30.unused_ref.probe_ref, f32[128,256]{1,0:T(8,128)S(1)} %shard_map.80.unused_ref.keep_ref, f32[128,256]{1,0:T(8,128)S(1)} %collective-permute-done.17.away_ref, f32[128,256]{1,0:T(8,128)S(1)} %collective-permute-done.18.keep_other_ref, ...), custom_call_target="tpu_custom_call" | custom-call | tf_op jit(solution)/shard_map/pallas_call | solution.py:415
  (5 shorter events, 0.1 us)
Async XLA Ops:
  0.6 9.7 %copy-start.2 = (bf16[3,256,256]{2,1,0:T(8,128)(2,1)S(1)}, bf16[3,256,256]{2,1,0:T(8,128)(2,1)}, u32[]{:S(2)}) copy-start(bf16[3,256,256]{2,1,0:T(8,128)(2,1)} %constant.2.clone.refs_4_) | copy-start | bytes 1179652
  2.6 11.0 %collective-permute-start.1 = (f32[136,256]{1,0:T(8,128)}, f32[136,256]{1,0:T(8,128)S(1)}, u32[]{:S(2)}, u32[]{:S(2)}) collective-permute-start(f32[136,256]{1,0:T(8,128)} %get-tuple-element.32), channel_id=1, source_target_pairs={{0,4},{1,5},{2,6},{3,7},{4,0},{5,1},{6,2},{7,3},{8,12},{9,13},{10,... | collective-permute-start | bytes 417800 | tf_op jit(solution)/shard_map/ppermute | solution.py:441
  5.7 4.6 %copy-start.4 = (f32[8,128]{1,0:T(8,128)S(1)}, f32[8,128]{1,0:T(8,128)}, u32[]{:S(2)}) copy-start(f32[8,128]{1,0:T(8,128)} %get-tuple-element.28.refs_0_) | copy-start | bytes 12292
  5.7 7.9 %collective-permute-start.2 = (f32[136,256]{1,0:T(8,128)}, f32[136,256]{1,0:T(8,128)S(1)}, u32[]{:S(2)}, u32[]{:S(2)}) collective-permute-start(f32[136,256]{1,0:T(8,128)} %get-tuple-element.33), channel_id=1, source_target_pairs={{0,1},{1,0},{2,3},{3,2},{4,8},{5,9},{6,10},{7,11},{8,4},{9,5},{10,... | collective-permute-start | bytes 417800 | tf_op jit(solution)/shard_map/ppermute | solution.py:441
  5.7 7.9 %collective-permute-start = (f32[264,128]{1,0:T(8,128)}, f32[264,128]{1,0:T(8,128)S(1)}, u32[]{:S(2)}, u32[]{:S(2)}) collective-permute-start(f32[264,128]{1,0:T(8,128)} %get-tuple-element.31), channel_id=1, source_target_pairs={{0,2},{1,3},{2,0},{3,1},{4,6},{5,7},{6,4},{7,5},{8,10},{9,11},{10,... | collective-permute-start | bytes 405512 | tf_op jit(solution)/shard_map/ppermute | solution.py:441
  7.2 6.4 %collective-permute-start.3 = (f32[136,128]{1,0:T(8,128)}, f32[136,128]{1,0:T(8,128)S(1)}, u32[]{:S(2)}, u32[]{:S(2)}) collective-permute-start(f32[136,128]{1,0:T(8,128)} %get-tuple-element.34), channel_id=1, source_target_pairs={{0,6},{1,7},{2,4},{3,5},{4,2},{5,3},{6,0},{7,1},{8,14},{9,15},{10,... | collective-permute-start | bytes 208904 | tf_op jit(solution)/shard_map/ppermute | solution.py:441
  10.3 3.3 %collective-permute-start.4 = (f32[136,128]{1,0:T(8,128)}, f32[136,128]{1,0:T(8,128)S(1)}, u32[]{:S(2)}, u32[]{:S(2)}) collective-permute-start(f32[136,128]{1,0:T(8,128)} %get-tuple-element.35), channel_id=1, source_target_pairs={{0,1},{1,0},{2,3},{3,2},{4,10},{5,11},{6,8},{7,9},{8,6},{9,7},{10,... | collective-permute-start | bytes 208904 | tf_op jit(solution)/shard_map/ppermute | solution.py:441
  10.3 1.0 %copy-start = (f32[2,256,256]{2,1,0:T(8,128)S(1)}, f32[2,256,256]{2,1,0:T(8,128)}, u32[]{:S(2)}) copy-start(f32[2,256,256]{2,1,0:T(8,128)} %refs_1_.1) | copy-start | bytes 1572868
  11.4 1.0 %copy-start.1 = (f32[2,256,256]{2,1,0:T(8,128)S(1)}, f32[2,256,256]{2,1,0:T(8,128)}, u32[]{:S(2)}) copy-start(f32[2,256,256]{2,1,0:T(8,128)} %refs_2_.1) | copy-start | bytes 1572868
  12.4 0.9 %copy-start.3 = (bf16[2,256,256]{2,1,0:T(8,128)(2,1)S(1)}, bf16[2,256,256]{2,1,0:T(8,128)(2,1)}, u32[]{:S(2)}) copy-start(bf16[2,256,256]{2,1,0:T(8,128)(2,1)} %refs_3_.1) | copy-start | bytes 786436
  13.7 2.8 %collective-permute-start.5 = (f32[1024,128]{1,0:T(8,128)S(1)}, f32[1024,128]{1,0:T(8,128)S(1)}, u32[]{:S(2)}, u32[]{:S(2)}) collective-permute-start(f32[1024,128]{1,0:T(8,128)S(1)} %shard_map.70.unused_ref.before_ref), channel_id=1, source_target_pairs={{0,1},{1,0},{2,3},{3,2},{4,5},{5,4},{6,7},{7,6},{8,9},{9,8},{10,11... | collective-permute-start | bytes 1572872 | tf_op jit(solution)/shard_map/ppermute | solution.py:444
  19.9 1.6 %collective-permute-start.6 = (f32[256,256]{1,0:T(8,128)S(1)}, f32[256,256]{1,0:T(8,128)S(1)}, u32[]{:S(2)}, u32[]{:S(2)}) collective-permute-start(f32[256,256]{1,0:T(8,128)S(1)} %get-tuple-element.41), channel_id=1, source_target_pairs={{0,1},{1,0},{2,3},{3,2},{4,5},{5,4},{6,7},{7,6},{8,9},{9,8},{10,11... | collective-permute-start | bytes 786440 | tf_op jit(solution)/shard_map/ppermute | solution.py:444
  21.5 2.1 %collective-permute-start.9 = (f32[2,256,256]{2,1,0:T(8,128)S(1)}, f32[2,256,256]{2,1,0:T(8,128)S(1)}, u32[]{:S(2)}, u32[]{:S(2)}) collective-permute-start(f32[2,256,256]{2,1,0:T(8,128)S(1)} %get-tuple-element.46), channel_id=1, source_target_pairs={{0,1},{1,0},{2,3},{3,2},{4,5},{5,4},{6,7},{7,6},{8,9},{9,8},{10,11... | collective-permute-start | bytes 1572872 | tf_op jit(solution)/shard_map/ppermute | solution.py:444
  21.8 1.8 %collective-permute-start.8 = (f32[8,128]{1,0:T(8,128)S(1)}, f32[8,128]{1,0:T(8,128)S(1)}, u32[]{:S(2)}, u32[]{:S(2)}) collective-permute-start(f32[8,128]{1,0:T(8,128)S(1)} %get-tuple-element.29.note_ref), channel_id=1, source_target_pairs={{0,1},{1,0},{2,3},{3,2},{4,5},{5,4},{6,7},{7,6},{8,9},{9,8},{10,11... | collective-permute-start | bytes 12296 | tf_op jit(solution)/shard_map/ppermute | solution.py:444
  22.1 5.0 %collective-permute-start.7 = (f32[128,256]{1,0:T(8,128)S(1)}, f32[128,256]{1,0:T(8,128)S(1)}, u32[]{:S(2)}, u32[]{:S(2)}) collective-permute-start(f32[128,256]{1,0:T(8,128)S(1)} %get-tuple-element.45), channel_id=1, source_target_pairs={{0,2},{1,5},{2,0},{3,7},{4,6},{5,1},{6,4},{7,3},{8,10},{9,13},{10,... | collective-permute-start | bytes 393224 | tf_op jit(solution)/shard_map/ppermute | solution.py:441
  24.8 11.1 %collective-permute-start.12 = (f32[512,128]{1,0:T(8,128)S(1)}, f32[512,128]{1,0:T(8,128)S(1)}, u32[]{:S(2)}, u32[]{:S(2)}) collective-permute-start(f32[512,128]{1,0:T(8,128)S(1)} %get-tuple-element.48), channel_id=1, source_target_pairs={{0,2},{1,3},{2,0},{3,1},{4,6},{5,7},{6,4},{7,5},{8,10},{9,11},{10,... | collective-permute-start | bytes 786440 | tf_op jit(solution)/shard_map/ppermute | solution.py:441
  27.1 6.8 %collective-permute-start.10 = (f32[128,256]{1,0:T(8,128)S(1)}, f32[128,256]{1,0:T(8,128)S(1)}, u32[]{:S(2)}, u32[]{:S(2)}) collective-permute-start(f32[128,256]{1,0:T(8,128)S(1)} %shard_map.78.a_ref), channel_id=1, source_target_pairs={{0,4},{1,9},{2,6},{3,11},{4,0},{5,13},{6,2},{7,15},{8,12},{9,1},{1... | collective-permute-start | bytes 393224 | tf_op jit(solution)/shard_map/ppermute | solution.py:441
  30.0 12.1 %collective-permute-start.13 = (f32[256,256]{1,0:T(8,128)S(1)}, f32[256,256]{1,0:T(8,128)S(1)}, u32[]{:S(2)}, u32[]{:S(2)}) collective-permute-start(f32[256,256]{1,0:T(8,128)S(1)} %shard_map.75.unused_light_ref.light_ref), channel_id=1, source_target_pairs={{0,1},{1,0},{2,3},{3,2},{4,5},{5,4},{6,7},{7,6},{8,9},{9,8},{10,11... | collective-permute-start | bytes 786440 | tf_op jit(solution)/shard_map/ppermute | solution.py:444
  33.9 8.2 %collective-permute-start.11 = (f32[128,256]{1,0:T(8,128)S(1)}, f32[128,256]{1,0:T(8,128)S(1)}, u32[]{:S(2)}, u32[]{:S(2)}) collective-permute-start(f32[128,256]{1,0:T(8,128)S(1)} %shard_map.79.a_ref.unused_ref), channel_id=1, source_target_pairs={{0,8},{1,3},{2,10},{3,1},{4,12},{5,7},{6,14},{7,5},{8,0},{9,11},{1... | collective-permute-start | bytes 393224 | tf_op jit(solution)/shard_map/ppermute | solution.py:441
  36.0 6.1 %collective-permute-start.14 = (f32[128,256]{1,0:T(8,128)S(1)}, f32[128,256]{1,0:T(8,128)S(1)}, u32[]{:S(2)}, u32[]{:S(2)}) collective-permute-start(f32[128,256]{1,0:T(8,128)S(1)} %get-tuple-element.50), channel_id=1, source_target_pairs={{0,4},{1,5},{2,6},{3,7},{4,0},{5,1},{6,2},{7,3},{8,12},{9,13},{10,... | collective-permute-start | bytes 393224 | tf_op jit(solution)/shard_map/ppermute | solution.py:441
  36.5 5.7 %collective-permute-start.15 = (f32[128,256]{1,0:T(8,128)S(1)}, f32[128,256]{1,0:T(8,128)S(1)}, u32[]{:S(2)}, u32[]{:S(2)}) collective-permute-start(f32[128,256]{1,0:T(8,128)S(1)} %get-tuple-element.51), channel_id=1, source_target_pairs={{0,1},{1,0},{2,3},{3,2},{4,8},{5,9},{6,10},{7,11},{8,4},{9,5},{10,... | collective-permute-start | bytes 393224 | tf_op jit(solution)/shard_map/ppermute | solution.py:441
  42.3 5.2 %collective-permute-start.16 = (f32[256,256]{1,0:T(8,128)S(1)}, f32[256,256]{1,0:T(8,128)S(1)}, u32[]{:S(2)}, u32[]{:S(2)}) collective-permute-start(f32[256,256]{1,0:T(8,128)S(1)} %shard_map.82.part_ref), channel_id=1, source_target_pairs={{0,1},{1,0},{2,3},{3,2},{4,5},{5,4},{6,7},{7,6},{8,9},{9,8},{10,11... | collective-permute-start | bytes 786440 | tf_op jit(solution)/shard_map/ppermute | solution.py:444
  42.4 5.0 %collective-permute-start.17 = (f32[128,256]{1,0:T(8,128)S(1)}, f32[128,256]{1,0:T(8,128)S(1)}, u32[]{:S(2)}, u32[]{:S(2)}) collective-permute-start(f32[128,256]{1,0:T(8,128)S(1)} %shard_map.80.unused_ref.keep_ref), channel_id=1, source_target_pairs={{0,2},{1,5},{2,0},{3,7},{4,6},{5,1},{6,4},{7,3},{8,10},{9,13},{10,... | collective-permute-start | bytes 393224 | tf_op jit(solution)/shard_map/ppermute | solution.py:441
  44.3 4.1 %collective-permute-start.18 = (f32[128,256]{1,0:T(8,128)S(1)}, f32[128,256]{1,0:T(8,128)S(1)}, u32[]{:S(2)}, u32[]{:S(2)}) collective-permute-start(f32[128,256]{1,0:T(8,128)S(1)} %shard_map.80.unused_ref.keep_ref), channel_id=1, source_target_pairs={{0,1},{1,0},{2,3},{3,2},{4,5},{5,4},{6,7},{7,6},{8,9},{9,8},{10,11... | collective-permute-start | bytes 393224 | tf_op jit(solution)/shard_map/ppermute | solution.py:444
  47.5 1.3 %collective-permute-start.19 = (f32[128,256]{1,0:T(8,128)S(1)}, f32[128,256]{1,0:T(8,128)S(1)}, u32[]{:S(2)}, u32[]{:S(2)}) collective-permute-start(f32[128,256]{1,0:T(8,128)S(1)} %collective-permute-done.17.away_ref), channel_id=1, source_target_pairs={{0,1},{1,0},{2,3},{3,2},{4,5},{5,4},{6,7},{7,6},{8,9},{9,8},{10,11... | collective-permute-start | bytes 393224 | tf_op jit(solution)/shard_map/ppermute | solution.py:444

commit v7 on v6

--- a/solution.py
+++ b/solution.py
@@ -59,8 +59,13 @@
     return [tuple(tile if way is None else tile // 2 for way in ways) for ways in block_ways(nz, nx)]
 
 
+def packing_order(nz, nx):
+    ways = block_ways(nz, nx)
+    return [[k for k, (_, w) in enumerate(ways) if (w is None) == later] for later in (False, True)]
+
+
 def packed_places(shapes):
-    lanes = min(width for _, width in shapes)
+    lanes = min(min(shape) for shape in shapes)
     at, places = 0, []
     for height, width in shapes:
         places.append([])
@@ -217,7 +222,10 @@
         padded[:, far_cols] = jnp.zeros((padded.shape[0], margin), jnp.float32)
     places = block_places(z, x, nz, nx, margin, margin + tile, margin)
     shapes = block_shapes(nz, nx, tile)
-    pieces = packed_places(shapes)
+    pieces = {}
+    for which, array in zip(packing_order(nz, nx), blocks):
+        for k, places_of in zip(which, packed_places([shapes[k] for k in which])):
+            pieces[k] = [(array, at) for at, _, _ in places_of]
     for k, ((height, width), (rows, cols), ok) in enumerate(zip(shapes, places, block_valid(z, x, nz, nx))):
 
         @pl.when(ok)
@@ -225,7 +233,7 @@
             if ours:
                 padded[rows, cols] = blocks[k][:height, :]
             else:
-                parts = [blocks[0][at : at + height, :] for at, _, _ in pieces[k]]
+                parts = [array[at : at + height, :] for array, at in pieces[k]]
                 padded[rows, cols] = parts[0] if len(parts) == 1 else jnp.concatenate(parts, axis=1)
 
         @pl.when(jnp.logical_not(ok))
@@ -236,9 +244,10 @@
     cut_patches(note, padded, out)
 
 
-def pack_kernel(nz, nx, tile, unused_ref, *refs):
-    *blocks, out = refs
-    for block, pieces in zip(blocks, packed_places(block_shapes(nz, nx, tile))):
+def pack_kernel(shapes, note_ref, unused_ref, *refs):
+    *blocks, out, note_out = refs
+    note_out[...] = note_ref[...]
+    for block, pieces in zip(blocks, packed_places(shapes)):
         for at, col, height in pieces:
             out[at : at + height, :] = block[:height, col : col + out.shape[1]]
 
@@ -339,7 +348,7 @@
 
 def update_kernel(nz, unused_ref, spec_ref, center_ref, light_ref, other_light_ref, edge_a, edge_b, *refs):
     z, c = lax.axis_index("scanx"), lax.axis_index("pos")
-    part_ref, grad = refs
+    upper_ref, lower_ref, grad = refs
     tile = center_ref.shape[0]
     grad[...] = center_ref[...]
     for way, edge in enumerate((edge_a, edge_b)):
@@ -350,18 +359,22 @@
         def _():
             grad[pl.ds(at, margin), :] += edge[...]
 
-    part_ref[...] = spec_ref[c] + grad[...] / (light_ref[...] + other_light_ref[...] + 1.0)
+    for at, out in ((0, upper_ref), (tile // 2, lower_ref)):
+        span = pl.ds(at, tile // 2)
+        out[...] = spec_ref[c, span, :] + grad[span, :] / (light_ref[span, :] + other_light_ref[span, :] + 1.0)
 
 
 def add_kernel(a_ref, b_ref, *refs):
     refs[-1][...] = a_ref[...] + b_ref[...]
 
 
-def specimen_kernel(part_ref, part_other_ref, out_ref, done_ref):
+def specimen_kernel(upper_ref, lower_ref, other_upper_ref, other_lower_ref, out_ref, done_ref):
+    c = lax.axis_index("pos")
+    rows = upper_ref.shape[0]
+    for part, upper, lower in ((c, upper_ref, lower_ref), (1 - c, other_upper_ref, other_lower_ref)):
+        out_ref[part, :rows, :] = upper[...]
+        out_ref[part, rows:, :] = lower[...]
     done_ref[...] = jnp.zeros(done_ref.shape, done_ref.dtype)
-    c = lax.axis_index("pos")
-    out_ref[c] = part_ref[...]
-    out_ref[1 - c] = part_other_ref[...]
 
 
 def probe_kernel(step_size, probe_ref, keep_ref, away_ref, keep_other_ref, away_other_ref, unused_ref, out_ref):
@@ -466,14 +479,16 @@
         waves,
         scratch=[dma(len(late))],
     )
-    lanes = min(w for _, w in shapes)
-    (packed,) = call(
-        functools.partial(pack_kernel, nz, nx, tile),
-        [f32(sum(h * w for h, w in shapes) // lanes, lanes)],
-        [ANY] + [VMEM] * len(recv),
-        probe_v,
-        *recv,
-    )
+    def packed(which, note, after):
+        chosen = [shapes[k] for k in which]
+        return call(
+            functools.partial(pack_kernel, chosen),
+            [f32(sum(h * w for h, w in chosen) // margin, margin), f32(*NOTE)],
+            [VMEM, ANY] + [VMEM] * len(which),
+            note,
+            after,
+            *[recv[k] for k in which],
+        )
 
     def patches_from(ours, after, *arrays):
         return call(
@@ -505,9 +520,12 @@
             ],
         )[0]
 
-    patches = patches_from(True, packed, *recv)
-    light = light_from([k for k, (_, w) in enumerate(ways) if w is None], True, packed, patches)
-    patches_other = patches_from(False, light, to_core(packed))
+    along_x, along_z = packing_order(nz, nx)
+    packed_x, handed_on = packed(along_x, note, probe_v)
+    light = light_from(along_x, True, packed_x, packed_x)
+    packed_z, other_note = packed(along_z, to_core(handed_on), light)
+    patches = patches_from(True, packed_z, *recv)
+    patches_other = patches_from(False, patches, to_core(packed_x), to_core(packed_z))
     own, other, probe_own, probe_other = call(
         positions_kernel,
         [f32(npos, size, size)] * 2 + [f32(size, size)] * 2,
@@ -519,8 +537,7 @@
         ta_v,
         tb_v,
     )
-    other_note = to_core(note)
-    light = light_from([k for k, (_, w) in enumerate(ways) if w is not None], False, light, own)
+    light = light_from(along_z, False, light, own)
 
     zbits = [("z", 1 << k) for k in range(nz.bit_length() - 1)]
     xbits = [("x", 1 << k) for k in range(nx.bit_length() - 1)]
@@ -572,9 +589,9 @@
     arrived = [send(edge, targets[ways.index((way, None))]) for way, edge in enumerate(edges)]
     for k in range(2, len(orders[0])):
         (keep,) = call(add_kernel, [half], [VMEM] * 2, keep, send(keep, stage(k)))
-    (part,) = call(
+    updated = call(
         functools.partial(update_kernel, nz),
-        [f32(tile, tile)],
+        [f32(tile // 2, tile)] * 2,
         [ANY] + [VMEM] * (4 + len(arrived)),
         keep,
         specimen_v,
@@ -585,7 +602,9 @@
         scratch=[pltpu.VMEM((tile, tile), jnp.float32)],
     )
     away = send(keep, stage(0))
-    new_specimen, done = call(specimen_kernel, [f32(2, tile, tile), f32(*NOTE)], [VMEM] * 2, part, to_core(part))
+    new_specimen, done = call(
+        specimen_kernel, [f32(2, tile, tile), f32(*NOTE)], [VMEM] * 4, *updated, *[to_core(u) for u in updated]
+    )
     step_size = 1.0 / math.sqrt(npos * nz * nx * nc)
     (new_probe,) = call(
         functools.partial(probe_kernel, step_size),

time: 50.1 us -> 50.6 us (level)
  waiting for transfers between devices: 13.4 us -> 15.1 us
  starting transfers between devices: 20.3 us -> 19.5 us
    ppermute x12, starting transfers between devices: 18.1 us -> 16.6 us  [send(): return lax.ppermute(value, GROUP, permutation(sizes, target))]
    ppermute x12, waiting for transfers between devices: 12.6 us -> 13.6 us  [send(): return lax.ppermute(value, GROUP, permutation(sizes, target))]
    ppermute x8 -> x10, starting transfers between devices: 2.16 us -> 2.83 us  [to_core(): return lax.ppermute(value, 'pos', PART_SWAP)]
    ppermute x8 -> x10, waiting for transfers between devices: 0.84 us -> 1.46 us  [to_core(): return lax.ppermute(value, 'pos', PART_SWAP)]
    pallas_call x17 -> x18, Pallas kernels: 12.1 us -> 11.8 us  [call(): pl.pallas_call(kernel, out_shape=out_shape, in_specs=specs, out_specs=out...]
  transfers between devices with their start and end apart: 20 -> 22, of which waited for: 6 -> 8; matrix products, arithmetic and copies ran while one was open for 0% -> 0% of each run, Pallas kernels for 11% -> 11%
where the time goes in v7:
time: 50.6 us; the launch traced here: 50.2 us
  starting transfers between devices  19.5 us (39%)
  waiting for transfers between devices  15.1 us (30%)
  Pallas kernels  11.8 us (23%)
  local copies, waits for them, and re-layouts  3.04 us (6%)
  between operations  0.84 us (2%)
    ppermute x12, starting transfers between devices, send(): return lax.ppermute(value, GROUP, permutation(sizes, target))  16.6 us
    ppermute x12, waiting for transfers between devices, send(): return lax.ppermute(value, GROUP, permutation(sizes, target))  13.6 us
    pallas_call x18, Pallas kernels, call(): pl.pallas_call(kernel, out_shape=out_shape, in_specs=specs, out_specs=out...  11.8 us
    unnamed x10, local copies, waits for them, and re-layouts  3.04 us
    ppermute x10, starting transfers between devices, to_core(): return lax.ppermute(value, 'pos', PART_SWAP)  2.83 us
    ppermute x10, waiting for transfers between devices, to_core(): return lax.ppermute(value, 'pos', PART_SWAP)  1.46 us
  transfers between devices with their start and end apart: 22, of which 8 were waited for; matrix products, arithmetic and copies ran while one was open for 0% of the time, Pallas kernels for 11%

profile of v7, /device:TPU:0, one launch (start us, length us, event | category | flops | bytes accessed | tf_op | source)
XLA Modules:
  0.0 50.2 jit_solution(11905033272991305402)
XLA Ops:
  0.6 0.0 copy-start.2
  0.6 2.0 %shard_map.68 = (f32[264,128]{1,0:T(8,128)}, f32[136,256]{1,0:T(8,128)}, f32[136,256]{1,0:T(8,128)}, f32[136,128]{1,0:T(8,128)}, f32[136,128]{1,0:T(8,128)}, /*index=5*/f32[8,128]{1,0:T(8,128)}) custom-call(s32[2,2]{1,0:T(2,128)} %off_hbm.1, f32[2,256,256]{2,1,0:T(8,128)} %refs_1_.1), custom_call_target="tpu_custom_call" | custom-call | tf_op jit(solution)/shard_map/pallas_call | solution.py:428
  2.6 3.0 %collective-permute-start = (f32[264,128]{1,0:T(8,128)}, f32[264,128]{1,0:T(8,128)S(1)}, u32[]{:S(2)}, u32[]{:S(2)}) collective-permute-start(f32[264,128]{1,0:T(8,128)} %get-tuple-element.37), channel_id=1, source_target_pairs={{0,2},{1,3},{2,0},{3,1},{4,6},{5,7},{6,4},{7,5},{8,10},{9,11},{10,... | collective-permute-start | bytes 405512 | tf_op jit(solution)/shard_map/ppermute | solution.py:454
  5.6 0.0 copy-start.4
  5.6 1.6 %collective-permute-start.4 = (f32[136,256]{1,0:T(8,128)}, f32[136,256]{1,0:T(8,128)S(1)}, u32[]{:S(2)}, u32[]{:S(2)}) collective-permute-start(f32[136,256]{1,0:T(8,128)} %get-tuple-element.42), channel_id=1, source_target_pairs={{0,4},{1,5},{2,6},{3,7},{4,0},{5,1},{6,2},{7,3},{8,12},{9,13},{10,... | collective-permute-start | bytes 417800 | tf_op jit(solution)/shard_map/ppermute | solution.py:454
  7.2 0.0 collective-permute-start.5
  7.2 3.1 %collective-permute-start.1 = (f32[136,128]{1,0:T(8,128)}, f32[136,128]{1,0:T(8,128)S(1)}, u32[]{:S(2)}, u32[]{:S(2)}) collective-permute-start(f32[136,128]{1,0:T(8,128)} %get-tuple-element.38), channel_id=1, source_target_pairs={{0,6},{1,7},{2,4},{3,5},{4,2},{5,3},{6,0},{7,1},{8,14},{9,15},{10,... | collective-permute-start | bytes 208904 | tf_op jit(solution)/shard_map/ppermute | solution.py:454
  10.3 0.0 collective-permute-start.2
  10.3 0.0 copy-done.2
  10.3 0.0 copy-done.4
  10.3 0.0 copy-start
  10.4 1.0 %copy-done = f32[2,256,256]{2,1,0:T(8,128)S(1)} copy-done((f32[2,256,256]{2,1,0:T(8,128)S(1)}, f32[2,256,256]{2,1,0:T(8,128)}, u32[]{:S(2)}) %copy-start) | copy-done | bytes 524312
  11.4 1.0 %copy-done.1 = f32[2,256,256]{2,1,0:T(8,128)S(1)} copy-done((f32[2,256,256]{2,1,0:T(8,128)S(1)}, f32[2,256,256]{2,1,0:T(8,128)}, u32[]{:S(2)}) %copy-start.1) | copy-done | bytes 524312
  12.4 0.9 %copy-done.3 = bf16[2,256,256]{2,1,0:T(8,128)(2,1)S(1)} copy-done((bf16[2,256,256]{2,1,0:T(8,128)(2,1)S(1)}, bf16[2,256,256]{2,1,0:T(8,128)(2,1)}, u32[]{:S(2)}) %copy-start.3) | copy-done | bytes 262168
  13.4 0.2 shard_map.69
  13.6 0.0 collective-permute-done.1.refs_1_.refs_3_
  13.6 0.0 collective-permute-done.2.refs_2_.refs_4_
  13.6 0.0 collective-permute-done.refs_0_
  13.6 0.6 %collective-permute-start.3 = (f32[8,128]{1,0:T(8,128)S(1)}, f32[8,128]{1,0:T(8,128)S(1)}, u32[]{:S(2)}, u32[]{:S(2)}) collective-permute-start(f32[8,128]{1,0:T(8,128)S(1)} %get-tuple-element.40), channel_id=1, source_target_pairs={{0,1},{1,0},{2,3},{3,2},{4,5},{5,4},{6,7},{7,6},{8,9},{9,8},{10,11... | collective-permute-start | bytes 12296 | tf_op jit(solution)/shard_map/ppermute | solution.py:457
  14.2 0.1 collective-permute-start.6
  14.3 1.3 %shard_map.71.unused_ref.before_ref = f32[256,256]{1,0:T(8,128)S(1)} custom-call(f32[8,128]{1,0:T(8,128)S(1)} %get-tuple-element.35.note_ref, f32[2,256,256]{2,1,0:T(8,128)S(1)} %get-tuple-element.36.unused_ref.probe_ref, f32[512,128]{1,0:T(8,128)S(1)} %get-tuple-element.41.before_ref.unused_ref, f32[512,128]{1,0:T(8,128)S(1)} %get-tuple-element.41.before_ref.unused_ref, ...), custom_call_target="tpu_custom_call" | custom-call | tf_op jit(solution)/shard_map/pallas_call | solution.py:428
  15.6 0.0 collective-permute-done.4.refs_0_.refs_1_
  15.6 0.0 collective-permute-done.5.refs_1_.refs_2_
  15.6 0.0 collective-permute-done.3.note_ref
  15.6 0.7 %collective-permute-start.7 = (f32[512,128]{1,0:T(8,128)S(1)}, f32[512,128]{1,0:T(8,128)S(1)}, u32[]{:S(2)}, u32[]{:S(2)}) collective-permute-start(f32[512,128]{1,0:T(8,128)S(1)} %get-tuple-element.44.unused_ref), channel_id=1, source_target_pairs={{0,1},{1,0},{2,3},{3,2},{4,5},{5,4},{6,7},{7,6},{8,9},{9,8},{10,11... | collective-permute-start | bytes 786440 | tf_op jit(solution)/shard_map/ppermute | solution.py:457
  16.3 0.8 %shard_map.73.unused_ref.patch_ref = f32[2,256,256]{2,1,0:T(8,128)S(1)} custom-call(f32[8,128]{1,0:T(8,128)S(1)} %get-tuple-element.35.note_ref, f32[512,128]{1,0:T(8,128)S(1)} %get-tuple-element.44.unused_ref, f32[2,256,256]{2,1,0:T(8,128)S(1)} %get-tuple-element.45.spec_ref, f32[264,128]{1,0:T(8,128)S(1)} %collective-permute-done.refs_0_, ...), custom_call_target="tpu_custom_call" | custom-call | tf_op jit(solution)/shard_map/pallas_call | solution.py:428
  17.1 0.0 collective-permute-done.6.refs_0_
  17.1 0.3 collective-permute-done.7.refs_1_
  17.4 0.8 %shard_map.74.patch_other_ref = f32[2,256,256]{2,1,0:T(8,128)S(1)} custom-call(f32[8,128]{1,0:T(8,128)S(1)} %get-tuple-element.35.note_ref, f32[2,256,256]{2,1,0:T(8,128)S(1)} %shard_map.73.unused_ref.patch_ref, f32[2,256,256]{2,1,0:T(8,128)S(1)} %get-tuple-element.45.spec_ref, f32[512,128]{1,0:T(8,128)S(1)} %collective-permute-done.6.refs_0_, ...), custom_call_target="tpu_custom_call" | custom-call | tf_op jit(solution)/shard_map/pallas_call | solution.py:428
  18.3 2.5 %shard_map.75 = (f32[2,256,256]{2,1,0:T(8,128)S(1)}, f32[2,256,256]{2,1,0:T(8,128)S(1)}, f32[256,256]{1,0:T(8,128)S(1)}, f32[256,256]{1,0:T(8,128)S(1)}) custom-call(f32[2,256,256]{2,1,0:T(8,128)S(1)} %shard_map.73.unused_ref.patch_ref, f32[2,256,256]{2,1,0:T(8,128)S(1)} %shard_map.74.patch_other_ref, ...), custom_call_target="tpu_custom_call" | custom-call | tf_op jit(solution)/shard_map/pallas_call | solution.py:428
  20.8 0.4 collective-permute-start.8
  21.3 0.9 %shard_map.76.unused_light_ref.light_ref = f32[256,256]{1,0:T(8,128)S(1)} custom-call(f32[8,128]{1,0:T(8,128)S(1)} %get-tuple-element.35.note_ref, f32[2,256,256]{2,1,0:T(8,128)S(1)} %get-tuple-element.36.unused_ref.probe_ref, f32[256,256]{1,0:T(8,128)S(1)} %shard_map.71.unused_ref.before_ref, f32[2,256,256]{2,1,0:T(8,128)S(1)} %get-tuple-element.52.unused_ref.own_ref, ...), custom_call_target="tpu_custom_call" | custom-call | tf_op jit(solution)/shard_map/pallas_call | solution.py:428
  22.1 0.3 collective-permute-done.8.recv_ref
  22.5 0.4 collective-permute-start.10
  22.9 1.2 %collective-permute-start.9 = (f32[128,256]{1,0:T(8,128)S(1)}, f32[128,256]{1,0:T(8,128)S(1)}, u32[]{:S(2)}, u32[]{:S(2)}) collective-permute-start(f32[128,256]{1,0:T(8,128)S(1)} %get-tuple-element.54), channel_id=1, source_target_pairs={{0,2},{1,5},{2,0},{3,7},{4,6},{5,1},{6,4},{7,3},{8,10},{9,13},{10,... | collective-permute-start | bytes 393224 | tf_op jit(solution)/shard_map/ppermute | solution.py:454
  24.1 0.4 collective-permute-done.10.recv_ref
  24.4 1.2 %shard_map.78 = (f32[512,256]{1,0:T(8,128)S(1)}, f32[512,128]{1,0:T(8,128)S(1)}) custom-call(f32[8,128]{1,0:T(8,128)S(1)} %get-tuple-element.35.note_ref, f32[8,128]{1,0:T(8,128)S(1)} %get-tuple-element.55.other_note_ref, f32[2,256,256]{2,1,0:T(8,128)S(1)} %get-tuple-element.52.unused_ref.own_ref, f32[2,256,256]{2,1,0:T(8,128)S(1)} %collective-permute-done.10.recv_ref, ...), custom_call_target="tpu_custom_call" | custom-call | tf_op jit(solution)/shard_map/pallas_call | solution.py:428
  25.7 1.3 %collective-permute-start.13 = (f32[512,128]{1,0:T(8,128)S(1)}, f32[512,128]{1,0:T(8,128)S(1)}, u32[]{:S(2)}, u32[]{:S(2)}) collective-permute-start(f32[512,128]{1,0:T(8,128)S(1)} %get-tuple-element.58), channel_id=1, source_target_pairs={{0,2},{1,3},{2,0},{3,1},{4,6},{5,7},{6,4},{7,5},{8,10},{9,11},{10,... | collective-permute-start | bytes 786440 | tf_op jit(solution)/shard_map/ppermute | solution.py:454
  27.0 0.9 %collective-permute-done.9.b_ref = f32[128,256]{1,0:T(8,128)S(1)} collective-permute-done((f32[128,256]{1,0:T(8,128)S(1)}, f32[128,256]{1,0:T(8,128)S(1)}, u32[]{:S(2)}, u32[]{:S(2)}) %collective-permute-start.9) | collective-permute-done | bytes 131104 | tf_op jit(solution)/shard_map/ppermute | solution.py:454
  27.9 2.5 %collective-permute-start.11 = (f32[128,256]{1,0:T(8,128)S(1)}, f32[128,256]{1,0:T(8,128)S(1)}, u32[]{:S(2)}, u32[]{:S(2)}) collective-permute-start(f32[128,256]{1,0:T(8,128)S(1)} %shard_map.79.a_ref), channel_id=1, source_target_pairs={{0,4},{1,9},{2,6},{3,11},{4,0},{5,13},{6,2},{7,15},{8,12},{9,1},{1... | collective-permute-start | bytes 393224 | tf_op jit(solution)/shard_map/ppermute | solution.py:454
  30.4 0.0 collective-permute-start.14
  30.4 3.9 %collective-permute-done.11.b_ref = f32[128,256]{1,0:T(8,128)S(1)} collective-permute-done((f32[128,256]{1,0:T(8,128)S(1)}, f32[128,256]{1,0:T(8,128)S(1)}, u32[]{:S(2)}, u32[]{:S(2)}) %collective-permute-start.11) | collective-permute-done | bytes 131104 | tf_op jit(solution)/shard_map/ppermute | solution.py:454
  34.4 1.9 %collective-permute-start.12 = (f32[128,256]{1,0:T(8,128)S(1)}, f32[128,256]{1,0:T(8,128)S(1)}, u32[]{:S(2)}, u32[]{:S(2)}) collective-permute-start(f32[128,256]{1,0:T(8,128)S(1)} %shard_map.80.a_ref.unused_ref), channel_id=1, source_target_pairs={{0,8},{1,3},{2,10},{3,1},{4,12},{5,7},{6,14},{7,5},{8,0},{9,11},{1... | collective-permute-start | bytes 393224 | tf_op jit(solution)/shard_map/ppermute | solution.py:454
  36.2 0.0 collective-permute-done.13.refs_0_
  36.2 0.1 shard_map.82
  36.3 0.7 %collective-permute-start.15 = (f32[128,256]{1,0:T(8,128)S(1)}, f32[128,256]{1,0:T(8,128)S(1)}, u32[]{:S(2)}, u32[]{:S(2)}) collective-permute-start(f32[128,256]{1,0:T(8,128)S(1)} %get-tuple-element.60), channel_id=1, source_target_pairs={{0,4},{1,5},{2,6},{3,7},{4,0},{5,1},{6,2},{7,3},{8,12},{9,13},{10,... | collective-permute-start | bytes 393224 | tf_op jit(solution)/shard_map/ppermute | solution.py:454
  37.0 0.0 collective-permute-start.16
  37.0 5.9 %collective-permute-done.12.b_ref = f32[128,256]{1,0:T(8,128)S(1)} collective-permute-done((f32[128,256]{1,0:T(8,128)S(1)}, f32[128,256]{1,0:T(8,128)S(1)}, u32[]{:S(2)}, u32[]{:S(2)}) %collective-permute-start.12) | collective-permute-done | bytes 131104 | tf_op jit(solution)/shard_map/ppermute | solution.py:454
  43.0 1.3 %collective-permute-start.19 = (f32[128,256]{1,0:T(8,128)S(1)}, f32[128,256]{1,0:T(8,128)S(1)}, u32[]{:S(2)}, u32[]{:S(2)}) collective-permute-start(f32[128,256]{1,0:T(8,128)S(1)} %shard_map.81.unused_ref.keep_ref), channel_id=1, source_target_pairs={{0,2},{1,5},{2,0},{3,7},{4,6},{5,1},{6,4},{7,3},{8,10},{9,13},{10,... | collective-permute-start | bytes 393224 | tf_op jit(solution)/shard_map/ppermute | solution.py:454
  44.3 0.0 collective-permute-done.14.other_light_ref
  44.3 0.0 collective-permute-done.15.edge_a
  44.3 0.0 collective-permute-done.16.edge_b
  44.3 0.1 shard_map.83
  44.4 0.1 collective-permute-start.17
  44.5 0.5 collective-permute-start.18
  45.0 0.1 collective-permute-start.20
  45.1 2.9 %collective-permute-done.19.away_ref = f32[128,256]{1,0:T(8,128)S(1)} collective-permute-done((f32[128,256]{1,0:T(8,128)S(1)}, f32[128,256]{1,0:T(8,128)S(1)}, u32[]{:S(2)}, u32[]{:S(2)}) %collective-permute-start.19) | collective-permute-done | bytes 131104 | tf_op jit(solution)/shard_map/ppermute | solution.py:454
  48.0 0.0 collective-permute-start.21
  48.0 0.0 collective-permute-done.17.other_upper_ref
  48.0 0.0 collective-permute-done.18.other_lower_ref
  48.0 0.8 %shard_map.84 = (f32[2,256,256]{2,1,0:T(8,128)}, f32[8,128]{1,0:T(8,128)S(1)}) custom-call(f32[128,256]{1,0:T(8,128)S(1)} %get-tuple-element.62.upper_ref, f32[128,256]{1,0:T(8,128)S(1)} %get-tuple-element.63.lower_ref, f32[128,256]{1,0:T(8,128)S(1)} %collective-permute-done.17.other_upper_ref, f32[128,256]{1,0:T(8,128)S(1)} %collective-permute-done.18.other_lower_ref), custom_call_target="tpu_custom_call" | custom-call | tf_op jit(solution)/shard_map/pallas_call | solution.py:428
  48.8 0.0 collective-permute-done.20.keep_other_ref
  48.8 0.5 collective-permute-done.21.away_other_ref
  49.3 0.9 %shard_map.85 = f32[2,256,256]{2,1,0:T(8,128)} custom-call(f32[2,256,256]{2,1,0:T(8,128)S(1)} %get-tuple-element.36.unused_ref.probe_ref, f32[128,256]{1,0:T(8,128)S(1)} %shard_map.81.unused_ref.keep_ref, f32[128,256]{1,0:T(8,128)S(1)} %collective-permute-done.19.away_ref, f32[128,256]{1,0:T(8,128)S(1)} %collective-permute-done.20.keep_other_ref, ...), custom_call_target="tpu_custom_call" | custom-call | tf_op jit(solution)/shard_map/pallas_call | solution.py:428
  (8 shorter events, 0.1 us)
Async XLA Ops:
  0.6 9.7 %copy-start.2 = (bf16[3,256,256]{2,1,0:T(8,128)(2,1)S(1)}, bf16[3,256,256]{2,1,0:T(8,128)(2,1)}, u32[]{:S(2)}) copy-start(bf16[3,256,256]{2,1,0:T(8,128)(2,1)} %constant.2.clone.refs_4_) | copy-start | bytes 1179652
  2.6 11.0 %collective-permute-start = (f32[264,128]{1,0:T(8,128)}, f32[264,128]{1,0:T(8,128)S(1)}, u32[]{:S(2)}, u32[]{:S(2)}) collective-permute-start(f32[264,128]{1,0:T(8,128)} %get-tuple-element.37), channel_id=1, source_target_pairs={{0,2},{1,3},{2,0},{3,1},{4,6},{5,7},{6,4},{7,5},{8,10},{9,11},{10,... | collective-permute-start | bytes 405512 | tf_op jit(solution)/shard_map/ppermute | solution.py:454
  5.6 4.7 %copy-start.4 = (f32[8,128]{1,0:T(8,128)S(1)}, f32[8,128]{1,0:T(8,128)}, u32[]{:S(2)}) copy-start(f32[8,128]{1,0:T(8,128)} %get-tuple-element.34.refs_0_) | copy-start | bytes 12292
  5.6 9.9 %collective-permute-start.4 = (f32[136,256]{1,0:T(8,128)}, f32[136,256]{1,0:T(8,128)S(1)}, u32[]{:S(2)}, u32[]{:S(2)}) collective-permute-start(f32[136,256]{1,0:T(8,128)} %get-tuple-element.42), channel_id=1, source_target_pairs={{0,4},{1,5},{2,6},{3,7},{4,0},{5,1},{6,2},{7,3},{8,12},{9,13},{10,... | collective-permute-start | bytes 417800 | tf_op jit(solution)/shard_map/ppermute | solution.py:454
  7.2 8.4 %collective-permute-start.5 = (f32[136,256]{1,0:T(8,128)}, f32[136,256]{1,0:T(8,128)S(1)}, u32[]{:S(2)}, u32[]{:S(2)}) collective-permute-start(f32[136,256]{1,0:T(8,128)} %get-tuple-element.43), channel_id=1, source_target_pairs={{0,1},{1,0},{2,3},{3,2},{4,8},{5,9},{6,10},{7,11},{8,4},{9,5},{10,... | collective-permute-start | bytes 417800 | tf_op jit(solution)/shard_map/ppermute | solution.py:454
  7.2 6.4 %collective-permute-start.1 = (f32[136,128]{1,0:T(8,128)}, f32[136,128]{1,0:T(8,128)S(1)}, u32[]{:S(2)}, u32[]{:S(2)}) collective-permute-start(f32[136,128]{1,0:T(8,128)} %get-tuple-element.38), channel_id=1, source_target_pairs={{0,6},{1,7},{2,4},{3,5},{4,2},{5,3},{6,0},{7,1},{8,14},{9,15},{10,... | collective-permute-start | bytes 208904 | tf_op jit(solution)/shard_map/ppermute | solution.py:454
  10.3 3.3 %collective-permute-start.2 = (f32[136,128]{1,0:T(8,128)}, f32[136,128]{1,0:T(8,128)S(1)}, u32[]{:S(2)}, u32[]{:S(2)}) collective-permute-start(f32[136,128]{1,0:T(8,128)} %get-tuple-element.39), channel_id=1, source_target_pairs={{0,1},{1,0},{2,3},{3,2},{4,10},{5,11},{6,8},{7,9},{8,6},{9,7},{10,... | collective-permute-start | bytes 208904 | tf_op jit(solution)/shard_map/ppermute | solution.py:454
  10.3 1.0 %copy-start = (f32[2,256,256]{2,1,0:T(8,128)S(1)}, f32[2,256,256]{2,1,0:T(8,128)}, u32[]{:S(2)}) copy-start(f32[2,256,256]{2,1,0:T(8,128)} %refs_1_.1) | copy-start | bytes 1572868
  11.4 1.0 %copy-start.1 = (f32[2,256,256]{2,1,0:T(8,128)S(1)}, f32[2,256,256]{2,1,0:T(8,128)}, u32[]{:S(2)}) copy-start(f32[2,256,256]{2,1,0:T(8,128)} %refs_2_.1) | copy-start | bytes 1572868
  12.4 0.9 %copy-start.3 = (bf16[2,256,256]{2,1,0:T(8,128)(2,1)S(1)}, bf16[2,256,256]{2,1,0:T(8,128)(2,1)}, u32[]{:S(2)}) copy-start(bf16[2,256,256]{2,1,0:T(8,128)(2,1)} %refs_3_.1) | copy-start | bytes 786436
  13.6 1.9 %collective-permute-start.3 = (f32[8,128]{1,0:T(8,128)S(1)}, f32[8,128]{1,0:T(8,128)S(1)}, u32[]{:S(2)}, u32[]{:S(2)}) collective-permute-start(f32[8,128]{1,0:T(8,128)S(1)} %get-tuple-element.40), channel_id=1, source_target_pairs={{0,1},{1,0},{2,3},{3,2},{4,5},{5,4},{6,7},{7,6},{8,9},{9,8},{10,11... | collective-permute-start | bytes 12296 | tf_op jit(solution)/shard_map/ppermute | solution.py:457
  14.2 2.9 %collective-permute-start.6 = (f32[512,128]{1,0:T(8,128)S(1)}, f32[512,128]{1,0:T(8,128)S(1)}, u32[]{:S(2)}, u32[]{:S(2)}) collective-permute-start(f32[512,128]{1,0:T(8,128)S(1)} %get-tuple-element.41.before_ref.unused_ref), channel_id=1, source_target_pairs={{0,1},{1,0},{2,3},{3,2},{4,5},{5,4},{6,7},{7,6},{8,9},{9,8},{10,11... | collective-permute-start | bytes 786440 | tf_op jit(solution)/shard_map/ppermute | solution.py:457
  15.6 1.8 %collective-permute-start.7 = (f32[512,128]{1,0:T(8,128)S(1)}, f32[512,128]{1,0:T(8,128)S(1)}, u32[]{:S(2)}, u32[]{:S(2)}) collective-permute-start(f32[512,128]{1,0:T(8,128)S(1)} %get-tuple-element.44.unused_ref), channel_id=1, source_target_pairs={{0,1},{1,0},{2,3},{3,2},{4,5},{5,4},{6,7},{7,6},{8,9},{9,8},{10,11... | collective-permute-start | bytes 786440 | tf_op jit(solution)/shard_map/ppermute | solution.py:457
  20.8 1.6 %collective-permute-start.8 = (f32[256,256]{1,0:T(8,128)S(1)}, f32[256,256]{1,0:T(8,128)S(1)}, u32[]{:S(2)}, u32[]{:S(2)}) collective-permute-start(f32[256,256]{1,0:T(8,128)S(1)} %get-tuple-element.50), channel_id=1, source_target_pairs={{0,1},{1,0},{2,3},{3,2},{4,5},{5,4},{6,7},{7,6},{8,9},{9,8},{10,11... | collective-permute-start | bytes 786440 | tf_op jit(solution)/shard_map/ppermute | solution.py:457
  22.5 2.0 %collective-permute-start.10 = (f32[2,256,256]{2,1,0:T(8,128)S(1)}, f32[2,256,256]{2,1,0:T(8,128)S(1)}, u32[]{:S(2)}, u32[]{:S(2)}) collective-permute-start(f32[2,256,256]{2,1,0:T(8,128)S(1)} %get-tuple-element.56), channel_id=1, source_target_pairs={{0,1},{1,0},{2,3},{3,2},{4,5},{5,4},{6,7},{7,6},{8,9},{9,8},{10,11... | collective-permute-start | bytes 1572872 | tf_op jit(solution)/shard_map/ppermute | solution.py:457
  22.9 5.0 %collective-permute-start.9 = (f32[128,256]{1,0:T(8,128)S(1)}, f32[128,256]{1,0:T(8,128)S(1)}, u32[]{:S(2)}, u32[]{:S(2)}) collective-permute-start(f32[128,256]{1,0:T(8,128)S(1)} %get-tuple-element.54), channel_id=1, source_target_pairs={{0,2},{1,5},{2,0},{3,7},{4,6},{5,1},{6,4},{7,3},{8,10},{9,13},{10,... | collective-permute-start | bytes 393224 | tf_op jit(solution)/shard_map/ppermute | solution.py:454
  25.7 10.6 %collective-permute-start.13 = (f32[512,128]{1,0:T(8,128)S(1)}, f32[512,128]{1,0:T(8,128)S(1)}, u32[]{:S(2)}, u32[]{:S(2)}) collective-permute-start(f32[512,128]{1,0:T(8,128)S(1)} %get-tuple-element.58), channel_id=1, source_target_pairs={{0,2},{1,3},{2,0},{3,1},{4,6},{5,7},{6,4},{7,5},{8,10},{9,11},{10,... | collective-permute-start | bytes 786440 | tf_op jit(solution)/shard_map/ppermute | solution.py:454
  27.9 6.5 %collective-permute-start.11 = (f32[128,256]{1,0:T(8,128)S(1)}, f32[128,256]{1,0:T(8,128)S(1)}, u32[]{:S(2)}, u32[]{:S(2)}) collective-permute-start(f32[128,256]{1,0:T(8,128)S(1)} %shard_map.79.a_ref), channel_id=1, source_target_pairs={{0,4},{1,9},{2,6},{3,11},{4,0},{5,13},{6,2},{7,15},{8,12},{9,1},{1... | collective-permute-start | bytes 393224 | tf_op jit(solution)/shard_map/ppermute | solution.py:454
  30.4 13.9 %collective-permute-start.14 = (f32[256,256]{1,0:T(8,128)S(1)}, f32[256,256]{1,0:T(8,128)S(1)}, u32[]{:S(2)}, u32[]{:S(2)}) collective-permute-start(f32[256,256]{1,0:T(8,128)S(1)} %shard_map.76.unused_light_ref.light_ref), channel_id=1, source_target_pairs={{0,1},{1,0},{2,3},{3,2},{4,5},{5,4},{6,7},{7,6},{8,9},{9,8},{10,11... | collective-permute-start | bytes 786440 | tf_op jit(solution)/shard_map/ppermute | solution.py:457
  34.4 8.5 %collective-permute-start.12 = (f32[128,256]{1,0:T(8,128)S(1)}, f32[128,256]{1,0:T(8,128)S(1)}, u32[]{:S(2)}, u32[]{:S(2)}) collective-permute-start(f32[128,256]{1,0:T(8,128)S(1)} %shard_map.80.a_ref.unused_ref), channel_id=1, source_target_pairs={{0,8},{1,3},{2,10},{3,1},{4,12},{5,7},{6,14},{7,5},{8,0},{9,11},{1... | collective-permute-start | bytes 393224 | tf_op jit(solution)/shard_map/ppermute | solution.py:454
  36.3 7.9 %collective-permute-start.15 = (f32[128,256]{1,0:T(8,128)S(1)}, f32[128,256]{1,0:T(8,128)S(1)}, u32[]{:S(2)}, u32[]{:S(2)}) collective-permute-start(f32[128,256]{1,0:T(8,128)S(1)} %get-tuple-element.60), channel_id=1, source_target_pairs={{0,4},{1,5},{2,6},{3,7},{4,0},{5,1},{6,2},{7,3},{8,12},{9,13},{10,... | collective-permute-start | bytes 393224 | tf_op jit(solution)/shard_map/ppermute | solution.py:454
  37.0 7.3 %collective-permute-start.16 = (f32[128,256]{1,0:T(8,128)S(1)}, f32[128,256]{1,0:T(8,128)S(1)}, u32[]{:S(2)}, u32[]{:S(2)}) collective-permute-start(f32[128,256]{1,0:T(8,128)S(1)} %get-tuple-element.61), channel_id=1, source_target_pairs={{0,1},{1,0},{2,3},{3,2},{4,8},{5,9},{6,10},{7,11},{8,4},{9,5},{10,... | collective-permute-start | bytes 393224 | tf_op jit(solution)/shard_map/ppermute | solution.py:454
  43.0 5.0 %collective-permute-start.19 = (f32[128,256]{1,0:T(8,128)S(1)}, f32[128,256]{1,0:T(8,128)S(1)}, u32[]{:S(2)}, u32[]{:S(2)}) collective-permute-start(f32[128,256]{1,0:T(8,128)S(1)} %shard_map.81.unused_ref.keep_ref), channel_id=1, source_target_pairs={{0,2},{1,5},{2,0},{3,7},{4,6},{5,1},{6,4},{7,3},{8,10},{9,13},{10,... | collective-permute-start | bytes 393224 | tf_op jit(solution)/shard_map/ppermute | solution.py:454
  44.4 3.6 %collective-permute-start.17 = (f32[128,256]{1,0:T(8,128)S(1)}, f32[128,256]{1,0:T(8,128)S(1)}, u32[]{:S(2)}, u32[]{:S(2)}) collective-permute-start(f32[128,256]{1,0:T(8,128)S(1)} %get-tuple-element.62.upper_ref), channel_id=1, source_target_pairs={{0,1},{1,0},{2,3},{3,2},{4,5},{5,4},{6,7},{7,6},{8,9},{9,8},{10,11... | collective-permute-start | bytes 393224 | tf_op jit(solution)/shard_map/ppermute | solution.py:457
  44.5 3.5 %collective-permute-start.18 = (f32[128,256]{1,0:T(8,128)S(1)}, f32[128,256]{1,0:T(8,128)S(1)}, u32[]{:S(2)}, u32[]{:S(2)}) collective-permute-start(f32[128,256]{1,0:T(8,128)S(1)} %get-tuple-element.63.lower_ref), channel_id=1, source_target_pairs={{0,1},{1,0},{2,3},{3,2},{4,5},{5,4},{6,7},{7,6},{8,9},{9,8},{10,11... | collective-permute-start | bytes 393224 | tf_op jit(solution)/shard_map/ppermute | solution.py:457
  45.0 3.9 %collective-permute-start.20 = (f32[128,256]{1,0:T(8,128)S(1)}, f32[128,256]{1,0:T(8,128)S(1)}, u32[]{:S(2)}, u32[]{:S(2)}) collective-permute-start(f32[128,256]{1,0:T(8,128)S(1)} %shard_map.81.unused_ref.keep_ref), channel_id=1, source_target_pairs={{0,1},{1,0},{2,3},{3,2},{4,5},{5,4},{6,7},{7,6},{8,9},{9,8},{10,11... | collective-permute-start | bytes 393224 | tf_op jit(solution)/shard_map/ppermute | solution.py:457
  48.0 1.3 %collective-permute-start.21 = (f32[128,256]{1,0:T(8,128)S(1)}, f32[128,256]{1,0:T(8,128)S(1)}, u32[]{:S(2)}, u32[]{:S(2)}) collective-permute-start(f32[128,256]{1,0:T(8,128)S(1)} %collective-permute-done.19.away_ref), channel_id=1, source_target_pairs={{0,1},{1,0},{2,3},{3,2},{4,5},{5,4},{6,7},{7,6},{8,9},{9,8},{10,11... | collective-permute-start | bytes 393224 | tf_op jit(solution)/shard_map/ppermute | solution.py:457

commit v8 on v7

--- a/solution.py
+++ b/solution.py
@@ -16,6 +16,7 @@
 ANY = pl.BlockSpec(memory_space=pl.ANY)
 HBM = pl.BlockSpec(memory_space=pltpu.HBM)
 NOTE = (8, 128)
+FILL_ROWS = 16
 NOTE_SMEM = pltpu.SMEM(NOTE, jnp.float32)
 
 
@@ -61,7 +62,8 @@
 
 def packing_order(nz, nx):
     ways = block_ways(nz, nx)
-    return [[k for k, (_, w) in enumerate(ways) if (w is None) == later] for later in (False, True)]
+    kinds = [(v is not None, w is not None) for v, w in ways]
+    return [[k for k, kind in enumerate(kinds) if kind == which] for which in ((True, True), (True, False), (False, True))]
 
 
 def packed_places(shapes):
@@ -161,8 +163,11 @@
         for k in range(2):
             note = jnp.where(lane == 2 * j + k, off_ref[j, k].astype(jnp.float32), note)
     note_ref[...] = note
-    for out in outs:
-        out[out.shape[0] - NOTE[0] :, : NOTE[1]] = note
+    for out, (height, width) in zip(outs, block_shapes(nz, nx, tile)):
+        fill = out.shape[0] - NOTE[0] - height
+        if fill:
+            out[height : height + fill, :] = jnp.zeros((fill, width), jnp.float32)
+        out[height + fill :, : NOTE[1]] = note
     for copy in copies:
         copy.wait()
 
@@ -222,8 +227,9 @@
         padded[:, far_cols] = jnp.zeros((padded.shape[0], margin), jnp.float32)
     places = block_places(z, x, nz, nx, margin, margin + tile, margin)
     shapes = block_shapes(nz, nx, tile)
-    pieces = {}
-    for which, array in zip(packing_order(nz, nx), blocks):
+    corners, along_z, along_x = packing_order(nz, nx)
+    pieces = {k: [(block, 0)] for k, block in zip(along_x, blocks[2:])}
+    for which, array in zip((corners, along_z), blocks):
         for k, places_of in zip(which, packed_places([shapes[k] for k in which])):
             pieces[k] = [(array, at) for at, _, _ in places_of]
     for k, ((height, width), (rows, cols), ok) in enumerate(zip(shapes, places, block_valid(z, x, nz, nx))):
@@ -244,9 +250,8 @@
     cut_patches(note, padded, out)
 
 
-def pack_kernel(shapes, note_ref, unused_ref, *refs):
-    *blocks, out, note_out = refs
-    note_out[...] = note_ref[...]
+def pack_kernel(shapes, waits, *refs):
+    *blocks, out = refs[waits:]
     for block, pieces in zip(blocks, packed_places(shapes)):
         for at, col, height in pieces:
             out[at : at + height, :] = block[:height, col : col + out.shape[1]]
@@ -459,7 +464,7 @@
     shapes = block_shapes(nz, nx, tile)
     *blocks, note = call(
         functools.partial(halo_blocks_kernel, nz, nx),
-        [f32(h + NOTE[0], w) for h, w in shapes] + [f32(*NOTE)],
+        [f32(h + NOTE[0] + (FILL_ROWS if v is None else 0), w) for (h, w), (v, _) in zip(shapes, ways)] + [f32(*NOTE)],
         [HBM, HBM],
         offsets,
         specimen,
@@ -479,17 +484,6 @@
         waves,
         scratch=[dma(len(late))],
     )
-    def packed(which, note, after):
-        chosen = [shapes[k] for k in which]
-        return call(
-            functools.partial(pack_kernel, chosen),
-            [f32(sum(h * w for h, w in chosen) // margin, margin), f32(*NOTE)],
-            [VMEM, ANY] + [VMEM] * len(which),
-            note,
-            after,
-            *[recv[k] for k in which],
-        )
-
     def patches_from(ours, after, *arrays):
         return call(
             functools.partial(patches_kernel, nz, nx, ours),
@@ -520,12 +514,22 @@
             ],
         )[0]
 
-    along_x, along_z = packing_order(nz, nx)
-    packed_x, handed_on = packed(along_x, note, probe_v)
-    light = light_from(along_x, True, packed_x, packed_x)
-    packed_z, other_note = packed(along_z, to_core(handed_on), light)
+    corners, along_z, along_x = packing_order(nz, nx)
+    def packed(which, *after):
+        chosen = [shapes[k] for k in which]
+        return call(
+            functools.partial(pack_kernel, chosen, len(after)),
+            [f32(sum(h * w for h, w in chosen) // margin, margin)],
+            [ANY] * len(after) + [VMEM] * len(which),
+            *after,
+            *[recv[k] for k in which],
+        )[0]
+
+    other_corners = to_core(packed(corners, probe_v))
+    light = light_from(corners + along_x, True, probe_v, probe_v)
+    packed_z = packed(along_z, light, other_corners)
     patches = patches_from(True, packed_z, *recv)
-    patches_other = patches_from(False, patches, to_core(packed_x), to_core(packed_z))
+    patches_other = patches_from(False, patches, other_corners, to_core(packed_z), *[to_core(recv[k]) for k in along_x])
     own, other, probe_own, probe_other = call(
         positions_kernel,
         [f32(npos, size, size)] * 2 + [f32(size, size)] * 2,
@@ -537,6 +541,7 @@
         ta_v,
         tb_v,
     )
+    other_note = to_core(note)
     light = light_from(along_z, False, light, own)
 
     zbits = [("z", 1 << k) for k in range(nz.bit_length() - 1)]

time: 50.6 us -> 50.3 us (level)
  starting transfers between devices: 19.5 us -> 16.8 us
  waiting for transfers between devices: 15.1 us -> 17.7 us
    ppermute x12, starting transfers between devices: 16.6 us -> 14.2 us  [send(): return lax.ppermute(value, GROUP, permutation(sizes, target))]
    ppermute x12, waiting for transfers between devices: 13.6 us -> 15.2 us  [send(): return lax.ppermute(value, GROUP, permutation(sizes, target))]
    ppermute x10 -> x11, waiting for transfers between devices: 1.46 us -> 2.53 us  [to_core(): return lax.ppermute(value, 'pos', PART_SWAP)]
    ppermute x10 -> x11, starting transfers between devices: 2.83 us -> 2.63 us  [to_core(): return lax.ppermute(value, 'pos', PART_SWAP)]
  transfers between devices with their start and end apart: 22 -> 23, of which waited for: 8 -> 8; matrix products, arithmetic and copies ran while one was open for 0% -> 0% of each run, Pallas kernels for 11% -> 11%
where the time goes in v8:
time: 50.3 us; the launch traced here: 50.1 us
  waiting for transfers between devices  17.7 us (35%)
  starting transfers between devices  16.8 us (33%)
  Pallas kernels  11.6 us (23%)
  local copies, waits for them, and re-layouts  3.04 us (6%)
  between operations  0.86 us (2%)
    ppermute x12, waiting for transfers between devices, send(): return lax.ppermute(value, GROUP, permutation(sizes, target))  15.2 us
    ppermute x12, starting transfers between devices, send(): return lax.ppermute(value, GROUP, permutation(sizes, target))  14.2 us
    pallas_call x18, Pallas kernels, call(): pl.pallas_call(kernel, out_shape=out_shape, in_specs=specs, out_specs=out...  11.6 us
    unnamed x10, local copies, waits for them, and re-layouts  3.04 us
    ppermute x11, starting transfers between devices, to_core(): return lax.ppermute(value, 'pos', PART_SWAP)  2.63 us
    ppermute x11, waiting for transfers between devices, to_core(): return lax.ppermute(value, 'pos', PART_SWAP)  2.53 us
  transfers between devices with their start and end apart: 23, of which 8 were waited for; matrix products, arithmetic and copies ran while one was open for 0% of the time, Pallas kernels for 11%

profile of v8, /device:TPU:0, one launch (start us, length us, event | category | flops | bytes accessed | tf_op | source)
XLA Modules:
  0.0 50.1 jit_solution(7009884480950690029)
XLA Ops:
  0.6 0.0 copy-start.2
  0.6 2.0 %shard_map.68 = (f32[280,128]{1,0:T(8,128)}, f32[136,256]{1,0:T(8,128)}, f32[136,256]{1,0:T(8,128)}, f32[136,128]{1,0:T(8,128)}, f32[136,128]{1,0:T(8,128)}, /*index=5*/f32[8,128]{1,0:T(8,128)}) custom-call(s32[2,2]{1,0:T(2,128)} %off_hbm.1, f32[2,256,256]{2,1,0:T(8,128)} %refs_1_.1), custom_call_target="tpu_custom_call" | custom-call | tf_op jit(solution)/shard_map/pallas_call | solution.py:433
  2.6 4.0 %collective-permute-start = (f32[136,128]{1,0:T(8,128)}, f32[136,128]{1,0:T(8,128)S(1)}, u32[]{:S(2)}, u32[]{:S(2)}) collective-permute-start(f32[136,128]{1,0:T(8,128)} %get-tuple-element.33), channel_id=1, source_target_pairs={{0,6},{1,7},{2,4},{3,5},{4,2},{5,3},{6,0},{7,1},{8,14},{9,15},{10,... | collective-permute-start | bytes 208904 | tf_op jit(solution)/shard_map/ppermute | solution.py:459
  6.6 0.0 collective-permute-start.1
  6.6 0.5 %collective-permute-start.2 = (f32[280,128]{1,0:T(8,128)}, f32[280,128]{1,0:T(8,128)S(1)}, u32[]{:S(2)}, u32[]{:S(2)}) collective-permute-start(f32[280,128]{1,0:T(8,128)} %get-tuple-element.35), channel_id=1, source_target_pairs={{0,2},{1,3},{2,0},{3,1},{4,6},{5,7},{6,4},{7,5},{8,10},{9,11},{10,... | collective-permute-start | bytes 430088 | tf_op jit(solution)/shard_map/ppermute | solution.py:459
  7.2 4.1 %collective-permute-start.4 = (f32[136,256]{1,0:T(8,128)}, f32[136,256]{1,0:T(8,128)S(1)}, u32[]{:S(2)}, u32[]{:S(2)}) collective-permute-start(f32[136,256]{1,0:T(8,128)} %get-tuple-element.36), channel_id=1, source_target_pairs={{0,4},{1,5},{2,6},{3,7},{4,0},{5,1},{6,2},{7,3},{8,12},{9,13},{10,... | collective-permute-start | bytes 417800 | tf_op jit(solution)/shard_map/ppermute | solution.py:459
  11.2 0.0 collective-permute-start.5
  11.2 0.0 copy-done.4
  11.3 0.0 copy-start
  11.3 1.0 %copy-done = f32[2,256,256]{2,1,0:T(8,128)S(1)} copy-done((f32[2,256,256]{2,1,0:T(8,128)S(1)}, f32[2,256,256]{2,1,0:T(8,128)}, u32[]{:S(2)}) %copy-start) | copy-done | bytes 524312
  12.3 1.0 %copy-done.1 = f32[2,256,256]{2,1,0:T(8,128)S(1)} copy-done((f32[2,256,256]{2,1,0:T(8,128)S(1)}, f32[2,256,256]{2,1,0:T(8,128)}, u32[]{:S(2)}) %copy-start.1) | copy-done | bytes 524312
  13.3 0.9 %copy-done.3 = bf16[2,256,256]{2,1,0:T(8,128)(2,1)S(1)} copy-done((bf16[2,256,256]{2,1,0:T(8,128)(2,1)S(1)}, bf16[2,256,256]{2,1,0:T(8,128)(2,1)}, u32[]{:S(2)}) %copy-start.3) | copy-done | bytes 262168
  14.3 0.2 shard_map.69
  14.5 0.0 collective-permute-done.refs_0_.refs_1_.refs_3_
  14.5 0.0 collective-permute-done.1.refs_1_.refs_2_.refs_4_
  14.5 0.6 %collective-permute-start.3 = (f32[256,128]{1,0:T(8,128)S(1)}, f32[256,128]{1,0:T(8,128)S(1)}, u32[]{:S(2)}, u32[]{:S(2)}) collective-permute-start(f32[256,128]{1,0:T(8,128)S(1)} %shard_map.71), channel_id=1, source_target_pairs={{0,1},{1,0},{2,3},{3,2},{4,5},{5,4},{6,7},{7,6},{8,9},{9,8},{10,11... | collective-permute-start | bytes 393224 | tf_op jit(solution)/shard_map/ppermute | solution.py:462
  15.1 0.0 collective-permute-done.2.refs_2_.refs_0_
  15.1 1.3 %shard_map.70.refs_0_.before_ref = f32[256,256]{1,0:T(8,128)S(1)} custom-call(f32[8,128]{1,0:T(8,128)S(1)} %get-tuple-element.31.note_ref, f32[2,256,256]{2,1,0:T(8,128)S(1)} %get-tuple-element.32.probe_ref.before_ref.unused_ref.refs_0_, f32[2,256,256]{2,1,0:T(8,128)S(1)} %get-tuple-element.32.probe_ref.before_ref.unused_ref.refs_0_, ...), custom_call_target="tpu_custom_call" | custom-call | tf_op jit(solution)/shard_map/pallas_call | solution.py:433
  16.4 0.0 collective-permute-done.4.refs_2_.refs_1_.refs_0_
  16.4 0.0 collective-permute-done.5.refs_3_.refs_2_.refs_1_
  16.4 0.0 collective-permute-done.3.refs_1_.refs_0_
  16.4 0.1 collective-permute-start.6
  16.5 0.5 collective-permute-start.7
  17.0 0.8 %shard_map.73.unused_ref.patch_ref = f32[2,256,256]{2,1,0:T(8,128)S(1)} custom-call(f32[8,128]{1,0:T(8,128)S(1)} %get-tuple-element.31.note_ref, f32[512,128]{1,0:T(8,128)S(1)} %shard_map.72.unused_ref, f32[2,256,256]{2,1,0:T(8,128)S(1)} %get-tuple-element.38.spec_ref, f32[280,128]{1,0:T(8,128)S(1)} %collective-permute-done.2.refs_2_.refs_0_, ...), custom_call_target="tpu_custom_call" | custom-call | tf_op jit(solution)/shard_map/pallas_call | solution.py:433
  17.9 0.4 collective-permute-done.7.refs_2_
  18.2 0.0 collective-permute-done.6.refs_1_
  18.3 0.8 %shard_map.74.patch_other_ref = f32[2,256,256]{2,1,0:T(8,128)S(1)} custom-call(f32[8,128]{1,0:T(8,128)S(1)} %get-tuple-element.31.note_ref, f32[2,256,256]{2,1,0:T(8,128)S(1)} %shard_map.73.unused_ref.patch_ref, f32[2,256,256]{2,1,0:T(8,128)S(1)} %get-tuple-element.38.spec_ref, f32[256,128]{1,0:T(8,128)S(1)} %collective-permute-done.3.refs_1_.refs_0_, ...), custom_call_target="tpu_custom_call" | custom-call | tf_op jit(solution)/shard_map/pallas_call | solution.py:433
  19.1 2.5 %shard_map.75 = (f32[2,256,256]{2,1,0:T(8,128)S(1)}, f32[2,256,256]{2,1,0:T(8,128)S(1)}, f32[256,256]{1,0:T(8,128)S(1)}, f32[256,256]{1,0:T(8,128)S(1)}) custom-call(f32[2,256,256]{2,1,0:T(8,128)S(1)} %shard_map.73.unused_ref.patch_ref, f32[2,256,256]{2,1,0:T(8,128)S(1)} %shard_map.74.patch_other_ref, ...), custom_call_target="tpu_custom_call" | custom-call | tf_op jit(solution)/shard_map/pallas_call | solution.py:433
  21.6 0.2 collective-permute-start.8
  21.8 0.7 %shard_map.76.unused_light_ref.light_ref = f32[256,256]{1,0:T(8,128)S(1)} custom-call(f32[8,128]{1,0:T(8,128)S(1)} %get-tuple-element.31.note_ref, f32[2,256,256]{2,1,0:T(8,128)S(1)} %get-tuple-element.32.probe_ref.before_ref.unused_ref.refs_0_, f32[256,256]{1,0:T(8,128)S(1)} %shard_map.70.refs_0_.before_ref, ...), custom_call_target="tpu_custom_call" | custom-call | tf_op jit(solution)/shard_map/pallas_call | solution.py:433
  22.6 0.7 %collective-permute-done.8.recv_ref = f32[256,256]{1,0:T(8,128)S(1)} collective-permute-done((f32[256,256]{1,0:T(8,128)S(1)}, f32[256,256]{1,0:T(8,128)S(1)}, u32[]{:S(2)}, u32[]{:S(2)}) %collective-permute-start.8) | collective-permute-done | bytes 262176 | tf_op jit(solution)/shard_map/ppermute | solution.py:462
  23.3 0.2 collective-permute-start.11
  23.5 0.6 %collective-permute-start.9 = (f32[128,256]{1,0:T(8,128)S(1)}, f32[128,256]{1,0:T(8,128)S(1)}, u32[]{:S(2)}, u32[]{:S(2)}) collective-permute-start(f32[128,256]{1,0:T(8,128)S(1)} %get-tuple-element.47), channel_id=1, source_target_pairs={{0,2},{1,5},{2,0},{3,7},{4,6},{5,1},{6,4},{7,3},{8,10},{9,13},{10,... | collective-permute-start | bytes 393224 | tf_op jit(solution)/shard_map/ppermute | solution.py:459
  24.1 0.2 collective-permute-start.10
  24.3 1.0 %collective-permute-done.10.other_note_ref = f32[8,128]{1,0:T(8,128)S(1)} collective-permute-done((f32[8,128]{1,0:T(8,128)S(1)}, f32[8,128]{1,0:T(8,128)S(1)}, u32[]{:S(2)}, u32[]{:S(2)}) %collective-permute-start.10) | collective-permute-done | bytes 4128 | tf_op jit(solution)/shard_map/ppermute | solution.py:462
  25.3 0.0 collective-permute-done.11.recv_ref
  25.3 1.2 %shard_map.78 = (f32[512,256]{1,0:T(8,128)S(1)}, f32[512,128]{1,0:T(8,128)S(1)}) custom-call(f32[8,128]{1,0:T(8,128)S(1)} %get-tuple-element.31.note_ref, f32[8,128]{1,0:T(8,128)S(1)} %collective-permute-done.10.other_note_ref, f32[2,256,256]{2,1,0:T(8,128)S(1)} %get-tuple-element.45.unused_ref.own_ref, f32[2,256,256]{2,1,0:T(8,128)S(1)} %collective-permute-done.11.recv_ref, ...), custom_call_target="tpu_custom_call" | custom-call | tf_op jit(solution)/shard_map/pallas_call | solution.py:433
  26.5 1.5 %collective-permute-start.14 = (f32[512,128]{1,0:T(8,128)S(1)}, f32[512,128]{1,0:T(8,128)S(1)}, u32[]{:S(2)}, u32[]{:S(2)}) collective-permute-start(f32[512,128]{1,0:T(8,128)S(1)} %get-tuple-element.50), channel_id=1, source_target_pairs={{0,2},{1,3},{2,0},{3,1},{4,6},{5,7},{6,4},{7,5},{8,10},{9,11},{10,... | collective-permute-start | bytes 786440 | tf_op jit(solution)/shard_map/ppermute | solution.py:459
  28.0 0.5 collective-permute-done.9.b_ref
  28.5 0.8 %collective-permute-start.12 = (f32[128,256]{1,0:T(8,128)S(1)}, f32[128,256]{1,0:T(8,128)S(1)}, u32[]{:S(2)}, u32[]{:S(2)}) collective-permute-start(f32[128,256]{1,0:T(8,128)S(1)} %shard_map.79.a_ref), channel_id=1, source_target_pairs={{0,4},{1,9},{2,6},{3,11},{4,0},{5,13},{6,2},{7,15},{8,12},{9,1},{1... | collective-permute-start | bytes 393224 | tf_op jit(solution)/shard_map/ppermute | solution.py:459
  29.3 0.2 collective-permute-start.15
  29.5 5.2 %collective-permute-done.12.b_ref = f32[128,256]{1,0:T(8,128)S(1)} collective-permute-done((f32[128,256]{1,0:T(8,128)S(1)}, f32[128,256]{1,0:T(8,128)S(1)}, u32[]{:S(2)}, u32[]{:S(2)}) %collective-permute-start.12) | collective-permute-done | bytes 131104 | tf_op jit(solution)/shard_map/ppermute | solution.py:459
  34.7 0.6 %collective-permute-start.13 = (f32[128,256]{1,0:T(8,128)S(1)}, f32[128,256]{1,0:T(8,128)S(1)}, u32[]{:S(2)}, u32[]{:S(2)}) collective-permute-start(f32[128,256]{1,0:T(8,128)S(1)} %shard_map.80.a_ref.unused_ref), channel_id=1, source_target_pairs={{0,8},{1,3},{2,10},{3,1},{4,12},{5,7},{6,14},{7,5},{8,0},{9,11},{1... | collective-permute-start | bytes 393224 | tf_op jit(solution)/shard_map/ppermute | solution.py:459
  35.3 0.0 collective-permute-done.14.refs_0_
  35.3 0.1 shard_map.82
  35.4 2.0 %collective-permute-start.16 = (f32[128,256]{1,0:T(8,128)S(1)}, f32[128,256]{1,0:T(8,128)S(1)}, u32[]{:S(2)}, u32[]{:S(2)}) collective-permute-start(f32[128,256]{1,0:T(8,128)S(1)} %get-tuple-element.52), channel_id=1, source_target_pairs={{0,4},{1,5},{2,6},{3,7},{4,0},{5,1},{6,2},{7,3},{8,12},{9,13},{10,... | collective-permute-start | bytes 393224 | tf_op jit(solution)/shard_map/ppermute | solution.py:459
  37.4 0.0 collective-permute-start.17
  37.4 5.4 %collective-permute-done.13.b_ref = f32[128,256]{1,0:T(8,128)S(1)} collective-permute-done((f32[128,256]{1,0:T(8,128)S(1)}, f32[128,256]{1,0:T(8,128)S(1)}, u32[]{:S(2)}, u32[]{:S(2)}) %collective-permute-start.13) | collective-permute-done | bytes 131104 | tf_op jit(solution)/shard_map/ppermute | solution.py:459
  42.8 0.1 collective-permute-start.20
  42.9 0.0 collective-permute-done.15.other_light_ref
  42.9 0.0 collective-permute-done.16.edge_a
  42.9 0.0 collective-permute-done.17.edge_b
  42.9 0.1 shard_map.83
  43.0 0.1 collective-permute-start.18
  43.1 0.5 collective-permute-start.19
  43.6 0.1 collective-permute-start.21
  43.7 4.1 %collective-permute-done.20.away_ref = f32[128,256]{1,0:T(8,128)S(1)} collective-permute-done((f32[128,256]{1,0:T(8,128)S(1)}, f32[128,256]{1,0:T(8,128)S(1)}, u32[]{:S(2)}, u32[]{:S(2)}) %collective-permute-start.20) | collective-permute-done | bytes 131104 | tf_op jit(solution)/shard_map/ppermute | solution.py:459
  47.8 0.0 collective-permute-start.22
  47.8 0.0 collective-permute-done.18.other_upper_ref
  47.8 0.0 collective-permute-done.19.other_lower_ref
  47.9 0.8 %shard_map.84 = (f32[2,256,256]{2,1,0:T(8,128)}, f32[8,128]{1,0:T(8,128)S(1)}) custom-call(f32[128,256]{1,0:T(8,128)S(1)} %get-tuple-element.54.upper_ref, f32[128,256]{1,0:T(8,128)S(1)} %get-tuple-element.55.lower_ref, f32[128,256]{1,0:T(8,128)S(1)} %collective-permute-done.18.other_upper_ref, f32[128,256]{1,0:T(8,128)S(1)} %collective-permute-done.19.other_lower_ref), custom_call_target="tpu_custom_call" | custom-call | tf_op jit(solution)/shard_map/pallas_call | solution.py:433
  48.7 0.0 collective-permute-done.21.keep_other_ref
  48.7 0.5 collective-permute-done.22.away_other_ref
  49.2 0.9 %shard_map.85 = f32[2,256,256]{2,1,0:T(8,128)} custom-call(f32[2,256,256]{2,1,0:T(8,128)S(1)} %get-tuple-element.32.probe_ref.before_ref.unused_ref.refs_0_, f32[128,256]{1,0:T(8,128)S(1)} %shard_map.81.unused_ref.keep_ref, f32[128,256]{1,0:T(8,128)S(1)} %collective-permute-done.20.away_ref, f32[128,256]{1,0:T(8,128)S(1)} %collective-permute-done.21.keep_other_ref, ...), custom_call_target="tpu_custom_call" | custom-call | tf_op jit(solution)/shard_map/pallas_call | solution.py:433
  (10 shorter events, 0.1 us)
Async XLA Ops:
  0.6 10.6 %copy-start.2 = (bf16[3,256,256]{2,1,0:T(8,128)(2,1)S(1)}, bf16[3,256,256]{2,1,0:T(8,128)(2,1)}, u32[]{:S(2)}) copy-start(bf16[3,256,256]{2,1,0:T(8,128)(2,1)} %constant.2.clone.refs_4_) | copy-start | bytes 1179652
  2.6 11.9 %collective-permute-start = (f32[136,128]{1,0:T(8,128)}, f32[136,128]{1,0:T(8,128)S(1)}, u32[]{:S(2)}, u32[]{:S(2)}) collective-permute-start(f32[136,128]{1,0:T(8,128)} %get-tuple-element.33), channel_id=1, source_target_pairs={{0,6},{1,7},{2,4},{3,5},{4,2},{5,3},{6,0},{7,1},{8,14},{9,15},{10,... | collective-permute-start | bytes 208904 | tf_op jit(solution)/shard_map/ppermute | solution.py:459
  6.6 4.6 %copy-start.4 = (f32[8,128]{1,0:T(8,128)S(1)}, f32[8,128]{1,0:T(8,128)}, u32[]{:S(2)}) copy-start(f32[8,128]{1,0:T(8,128)} %get-tuple-element.30.refs_0_) | copy-start | bytes 12292
  6.6 7.9 %collective-permute-start.1 = (f32[136,128]{1,0:T(8,128)}, f32[136,128]{1,0:T(8,128)S(1)}, u32[]{:S(2)}, u32[]{:S(2)}) collective-permute-start(f32[136,128]{1,0:T(8,128)} %get-tuple-element.34), channel_id=1, source_target_pairs={{0,1},{1,0},{2,3},{3,2},{4,10},{5,11},{6,8},{7,9},{8,6},{9,7},{10,... | collective-permute-start | bytes 208904 | tf_op jit(solution)/shard_map/ppermute | solution.py:459
  6.6 8.5 %collective-permute-start.2 = (f32[280,128]{1,0:T(8,128)}, f32[280,128]{1,0:T(8,128)S(1)}, u32[]{:S(2)}, u32[]{:S(2)}) collective-permute-start(f32[280,128]{1,0:T(8,128)} %get-tuple-element.35), channel_id=1, source_target_pairs={{0,2},{1,3},{2,0},{3,1},{4,6},{5,7},{6,4},{7,5},{8,10},{9,11},{10,... | collective-permute-start | bytes 430088 | tf_op jit(solution)/shard_map/ppermute | solution.py:459
  7.2 9.2 %collective-permute-start.4 = (f32[136,256]{1,0:T(8,128)}, f32[136,256]{1,0:T(8,128)S(1)}, u32[]{:S(2)}, u32[]{:S(2)}) collective-permute-start(f32[136,256]{1,0:T(8,128)} %get-tuple-element.36), channel_id=1, source_target_pairs={{0,4},{1,5},{2,6},{3,7},{4,0},{5,1},{6,2},{7,3},{8,12},{9,13},{10,... | collective-permute-start | bytes 417800 | tf_op jit(solution)/shard_map/ppermute | solution.py:459
  11.2 5.2 %collective-permute-start.5 = (f32[136,256]{1,0:T(8,128)}, f32[136,256]{1,0:T(8,128)S(1)}, u32[]{:S(2)}, u32[]{:S(2)}) collective-permute-start(f32[136,256]{1,0:T(8,128)} %get-tuple-element.37), channel_id=1, source_target_pairs={{0,1},{1,0},{2,3},{3,2},{4,8},{5,9},{6,10},{7,11},{8,4},{9,5},{10,... | collective-permute-start | bytes 417800 | tf_op jit(solution)/shard_map/ppermute | solution.py:459
  11.3 1.0 %copy-start = (f32[2,256,256]{2,1,0:T(8,128)S(1)}, f32[2,256,256]{2,1,0:T(8,128)}, u32[]{:S(2)}) copy-start(f32[2,256,256]{2,1,0:T(8,128)} %refs_1_.1) | copy-start | bytes 1572868
  12.3 1.0 %copy-start.1 = (f32[2,256,256]{2,1,0:T(8,128)S(1)}, f32[2,256,256]{2,1,0:T(8,128)}, u32[]{:S(2)}) copy-start(f32[2,256,256]{2,1,0:T(8,128)} %refs_2_.1) | copy-start | bytes 1572868
  13.3 0.9 %copy-start.3 = (bf16[2,256,256]{2,1,0:T(8,128)(2,1)S(1)}, bf16[2,256,256]{2,1,0:T(8,128)(2,1)}, u32[]{:S(2)}) copy-start(bf16[2,256,256]{2,1,0:T(8,128)(2,1)} %refs_3_.1) | copy-start | bytes 786436
  14.5 1.9 %collective-permute-start.3 = (f32[256,128]{1,0:T(8,128)S(1)}, f32[256,128]{1,0:T(8,128)S(1)}, u32[]{:S(2)}, u32[]{:S(2)}) collective-permute-start(f32[256,128]{1,0:T(8,128)S(1)} %shard_map.71), channel_id=1, source_target_pairs={{0,1},{1,0},{2,3},{3,2},{4,5},{5,4},{6,7},{7,6},{8,9},{9,8},{10,11... | collective-permute-start | bytes 393224 | tf_op jit(solution)/shard_map/ppermute | solution.py:462
  16.4 1.8 %collective-permute-start.6 = (f32[512,128]{1,0:T(8,128)S(1)}, f32[512,128]{1,0:T(8,128)S(1)}, u32[]{:S(2)}, u32[]{:S(2)}) collective-permute-start(f32[512,128]{1,0:T(8,128)S(1)} %shard_map.72.unused_ref), channel_id=1, source_target_pairs={{0,1},{1,0},{2,3},{3,2},{4,5},{5,4},{6,7},{7,6},{8,9},{9,8},{10,11... | collective-permute-start | bytes 786440 | tf_op jit(solution)/shard_map/ppermute | solution.py:462
  16.5 1.7 %collective-permute-start.7 = (f32[280,128]{1,0:T(8,128)S(1)}, f32[280,128]{1,0:T(8,128)S(1)}, u32[]{:S(2)}, u32[]{:S(2)}) collective-permute-start(f32[280,128]{1,0:T(8,128)S(1)} %collective-permute-done.2.refs_2_.refs_0_), channel_id=1, source_target_pairs={{0,1},{1,0},{2,3},{3,2},{4,5},{5,4},{6,7},{7,6},{8,9},{9,8},{10,11... | collective-permute-start | bytes 430088 | tf_op jit(solution)/shard_map/ppermute | solution.py:462
  21.6 1.6 %collective-permute-start.8 = (f32[256,256]{1,0:T(8,128)S(1)}, f32[256,256]{1,0:T(8,128)S(1)}, u32[]{:S(2)}, u32[]{:S(2)}) collective-permute-start(f32[256,256]{1,0:T(8,128)S(1)} %get-tuple-element.43), channel_id=1, source_target_pairs={{0,1},{1,0},{2,3},{3,2},{4,5},{5,4},{6,7},{7,6},{8,9},{9,8},{10,11... | collective-permute-start | bytes 786440 | tf_op jit(solution)/shard_map/ppermute | solution.py:462
  23.3 2.0 %collective-permute-start.11 = (f32[2,256,256]{2,1,0:T(8,128)S(1)}, f32[2,256,256]{2,1,0:T(8,128)S(1)}, u32[]{:S(2)}, u32[]{:S(2)}) collective-permute-start(f32[2,256,256]{2,1,0:T(8,128)S(1)} %get-tuple-element.48), channel_id=1, source_target_pairs={{0,1},{1,0},{2,3},{3,2},{4,5},{5,4},{6,7},{7,6},{8,9},{9,8},{10,11... | collective-permute-start | bytes 1572872 | tf_op jit(solution)/shard_map/ppermute | solution.py:462
  23.5 5.0 %collective-permute-start.9 = (f32[128,256]{1,0:T(8,128)S(1)}, f32[128,256]{1,0:T(8,128)S(1)}, u32[]{:S(2)}, u32[]{:S(2)}) collective-permute-start(f32[128,256]{1,0:T(8,128)S(1)} %get-tuple-element.47), channel_id=1, source_target_pairs={{0,2},{1,5},{2,0},{3,7},{4,6},{5,1},{6,4},{7,3},{8,10},{9,13},{10,... | collective-permute-start | bytes 393224 | tf_op jit(solution)/shard_map/ppermute | solution.py:459
  24.1 1.2 %collective-permute-start.10 = (f32[8,128]{1,0:T(8,128)S(1)}, f32[8,128]{1,0:T(8,128)S(1)}, u32[]{:S(2)}, u32[]{:S(2)}) collective-permute-start(f32[8,128]{1,0:T(8,128)S(1)} %get-tuple-element.31.note_ref), channel_id=1, source_target_pairs={{0,1},{1,0},{2,3},{3,2},{4,5},{5,4},{6,7},{7,6},{8,9},{9,8},{10,11... | collective-permute-start | bytes 12296 | tf_op jit(solution)/shard_map/ppermute | solution.py:462
  26.5 8.8 %collective-permute-start.14 = (f32[512,128]{1,0:T(8,128)S(1)}, f32[512,128]{1,0:T(8,128)S(1)}, u32[]{:S(2)}, u32[]{:S(2)}) collective-permute-start(f32[512,128]{1,0:T(8,128)S(1)} %get-tuple-element.50), channel_id=1, source_target_pairs={{0,2},{1,3},{2,0},{3,1},{4,6},{5,7},{6,4},{7,5},{8,10},{9,11},{10,... | collective-permute-start | bytes 786440 | tf_op jit(solution)/shard_map/ppermute | solution.py:459
  28.5 6.2 %collective-permute-start.12 = (f32[128,256]{1,0:T(8,128)S(1)}, f32[128,256]{1,0:T(8,128)S(1)}, u32[]{:S(2)}, u32[]{:S(2)}) collective-permute-start(f32[128,256]{1,0:T(8,128)S(1)} %shard_map.79.a_ref), channel_id=1, source_target_pairs={{0,4},{1,9},{2,6},{3,11},{4,0},{5,13},{6,2},{7,15},{8,12},{9,1},{1... | collective-permute-start | bytes 393224 | tf_op jit(solution)/shard_map/ppermute | solution.py:459
  29.3 13.6 %collective-permute-start.15 = (f32[256,256]{1,0:T(8,128)S(1)}, f32[256,256]{1,0:T(8,128)S(1)}, u32[]{:S(2)}, u32[]{:S(2)}) collective-permute-start(f32[256,256]{1,0:T(8,128)S(1)} %shard_map.76.unused_light_ref.light_ref), channel_id=1, source_target_pairs={{0,1},{1,0},{2,3},{3,2},{4,5},{5,4},{6,7},{7,6},{8,9},{9,8},{10,11... | collective-permute-start | bytes 786440 | tf_op jit(solution)/shard_map/ppermute | solution.py:462
  34.7 8.1 %collective-permute-start.13 = (f32[128,256]{1,0:T(8,128)S(1)}, f32[128,256]{1,0:T(8,128)S(1)}, u32[]{:S(2)}, u32[]{:S(2)}) collective-permute-start(f32[128,256]{1,0:T(8,128)S(1)} %shard_map.80.a_ref.unused_ref), channel_id=1, source_target_pairs={{0,8},{1,3},{2,10},{3,1},{4,12},{5,7},{6,14},{7,5},{8,0},{9,11},{1... | collective-permute-start | bytes 393224 | tf_op jit(solution)/shard_map/ppermute | solution.py:459
  35.4 7.5 %collective-permute-start.16 = (f32[128,256]{1,0:T(8,128)S(1)}, f32[128,256]{1,0:T(8,128)S(1)}, u32[]{:S(2)}, u32[]{:S(2)}) collective-permute-start(f32[128,256]{1,0:T(8,128)S(1)} %get-tuple-element.52), channel_id=1, source_target_pairs={{0,4},{1,5},{2,6},{3,7},{4,0},{5,1},{6,2},{7,3},{8,12},{9,13},{10,... | collective-permute-start | bytes 393224 | tf_op jit(solution)/shard_map/ppermute | solution.py:459
  37.4 5.5 %collective-permute-start.17 = (f32[128,256]{1,0:T(8,128)S(1)}, f32[128,256]{1,0:T(8,128)S(1)}, u32[]{:S(2)}, u32[]{:S(2)}) collective-permute-start(f32[128,256]{1,0:T(8,128)S(1)} %get-tuple-element.53), channel_id=1, source_target_pairs={{0,1},{1,0},{2,3},{3,2},{4,8},{5,9},{6,10},{7,11},{8,4},{9,5},{10,... | collective-permute-start | bytes 393224 | tf_op jit(solution)/shard_map/ppermute | solution.py:459
  42.8 5.0 %collective-permute-start.20 = (f32[128,256]{1,0:T(8,128)S(1)}, f32[128,256]{1,0:T(8,128)S(1)}, u32[]{:S(2)}, u32[]{:S(2)}) collective-permute-start(f32[128,256]{1,0:T(8,128)S(1)} %shard_map.81.unused_ref.keep_ref), channel_id=1, source_target_pairs={{0,2},{1,5},{2,0},{3,7},{4,6},{5,1},{6,4},{7,3},{8,10},{9,13},{10,... | collective-permute-start | bytes 393224 | tf_op jit(solution)/shard_map/ppermute | solution.py:459
  43.0 4.8 %collective-permute-start.18 = (f32[128,256]{1,0:T(8,128)S(1)}, f32[128,256]{1,0:T(8,128)S(1)}, u32[]{:S(2)}, u32[]{:S(2)}) collective-permute-start(f32[128,256]{1,0:T(8,128)S(1)} %get-tuple-element.54.upper_ref), channel_id=1, source_target_pairs={{0,1},{1,0},{2,3},{3,2},{4,5},{5,4},{6,7},{7,6},{8,9},{9,8},{10,11... | collective-permute-start | bytes 393224 | tf_op jit(solution)/shard_map/ppermute | solution.py:462
  43.1 4.7 %collective-permute-start.19 = (f32[128,256]{1,0:T(8,128)S(1)}, f32[128,256]{1,0:T(8,128)S(1)}, u32[]{:S(2)}, u32[]{:S(2)}) collective-permute-start(f32[128,256]{1,0:T(8,128)S(1)} %get-tuple-element.55.lower_ref), channel_id=1, source_target_pairs={{0,1},{1,0},{2,3},{3,2},{4,5},{5,4},{6,7},{7,6},{8,9},{9,8},{10,11... | collective-permute-start | bytes 393224 | tf_op jit(solution)/shard_map/ppermute | solution.py:462
  43.6 5.1 %collective-permute-start.21 = (f32[128,256]{1,0:T(8,128)S(1)}, f32[128,256]{1,0:T(8,128)S(1)}, u32[]{:S(2)}, u32[]{:S(2)}) collective-permute-start(f32[128,256]{1,0:T(8,128)S(1)} %shard_map.81.unused_ref.keep_ref), channel_id=1, source_target_pairs={{0,1},{1,0},{2,3},{3,2},{4,5},{5,4},{6,7},{7,6},{8,9},{9,8},{10,11... | collective-permute-start | bytes 393224 | tf_op jit(solution)/shard_map/ppermute | solution.py:462
  47.8 1.3 %collective-permute-start.22 = (f32[128,256]{1,0:T(8,128)S(1)}, f32[128,256]{1,0:T(8,128)S(1)}, u32[]{:S(2)}, u32[]{:S(2)}) collective-permute-start(f32[128,256]{1,0:T(8,128)S(1)} %collective-permute-done.20.away_ref), channel_id=1, source_target_pairs={{0,1},{1,0},{2,3},{3,2},{4,5},{5,4},{6,7},{7,6},{8,9},{9,8},{10,11... | collective-permute-start | bytes 393224 | tf_op jit(solution)/shard_map/ppermute | solution.py:462

commit v9 on v8

--- a/solution.py
+++ b/solution.py
@@ -525,8 +525,9 @@
             *[recv[k] for k in which],
         )[0]
 
-    other_corners = to_core(packed(corners, probe_v))
-    light = light_from(corners + along_x, True, probe_v, probe_v)
+    packed_corners = packed(corners, probe_v, *[recv[k] for k in along_x])
+    other_corners = to_core(packed_corners)
+    light = light_from(corners + along_x, True, packed_corners, packed_corners)
     packed_z = packed(along_z, light, other_corners)
     patches = patches_from(True, packed_z, *recv)
     patches_other = patches_from(False, patches, other_corners, to_core(packed_z), *[to_core(recv[k]) for k in along_x])

time: 50.3 us -> 50.5 us (level)
  starting transfers between devices: 16.8 us -> 15.4 us
  waiting for transfers between devices: 17.7 us -> 18.9 us
    ppermute x12, starting transfers between devices: 14.2 us -> 12.6 us  [send(): return lax.ppermute(value, GROUP, permutation(sizes, target))]
    ppermute x12, waiting for transfers between devices: 15.2 us -> 16.4 us  [send(): return lax.ppermute(value, GROUP, permutation(sizes, target))]
  transfers between devices with their start and end apart: 23 -> 23, of which waited for: 8 -> 8; matrix products, arithmetic and copies ran while one was open for 0% -> 0% of each run, Pallas kernels for 11% -> 12%
where the time goes in v9:
time: 50.5 us; the launch traced here: 50.2 us
  waiting for transfers between devices  18.9 us (37%)
  starting transfers between devices  15.4 us (30%)
  Pallas kernels  12.1 us (24%)
  local copies, waits for them, and re-layouts  3.04 us (6%)
  between operations  0.84 us (2%)
    ppermute x12, waiting for transfers between devices, send(): return lax.ppermute(value, GROUP, permutation(sizes, target))  16.4 us
    ppermute x12, starting transfers between devices, send(): return lax.ppermute(value, GROUP, permutation(sizes, target))  12.6 us
    pallas_call x18, Pallas kernels, call(): pl.pallas_call(kernel, out_shape=out_shape, in_specs=specs, out_specs=out...  12.1 us
    unnamed x10, local copies, waits for them, and re-layouts  3.04 us
    ppermute x11, starting transfers between devices, to_core(): return lax.ppermute(value, 'pos', PART_SWAP)  2.79 us
    ppermute x11, waiting for transfers between devices, to_core(): return lax.ppermute(value, 'pos', PART_SWAP)  2.52 us
  transfers between devices with their start and end apart: 23, of which 8 were waited for; matrix products, arithmetic and copies ran while one was open for 0% of the time, Pallas kernels for 12%

profile of v9, /device:TPU:0, one launch (start us, length us, event | category | flops | bytes accessed | tf_op | source)
XLA Modules:
  0.0 50.2 jit_solution(10178407823247972341)
XLA Ops:
  0.6 0.0 copy-start.2
  0.6 2.0 %shard_map.68 = (f32[280,128]{1,0:T(8,128)}, f32[136,256]{1,0:T(8,128)}, f32[136,256]{1,0:T(8,128)}, f32[136,128]{1,0:T(8,128)}, f32[136,128]{1,0:T(8,128)}, /*index=5*/f32[8,128]{1,0:T(8,128)}) custom-call(s32[2,2]{1,0:T(2,128)} %off_hbm.1, f32[2,256,256]{2,1,0:T(8,128)} %refs_1_.1), custom_call_target="tpu_custom_call" | custom-call | tf_op jit(solution)/shard_map/pallas_call | solution.py:433
  2.6 3.0 %collective-permute-start = (f32[280,128]{1,0:T(8,128)}, f32[280,128]{1,0:T(8,128)S(1)}, u32[]{:S(2)}, u32[]{:S(2)}) collective-permute-start(f32[280,128]{1,0:T(8,128)} %get-tuple-element.33), channel_id=1, source_target_pairs={{0,2},{1,3},{2,0},{3,1},{4,6},{5,7},{6,4},{7,5},{8,10},{9,11},{10,... | collective-permute-start | bytes 430088 | tf_op jit(solution)/shard_map/ppermute | solution.py:459
  5.6 1.5 %collective-permute-start.1 = (f32[136,128]{1,0:T(8,128)}, f32[136,128]{1,0:T(8,128)S(1)}, u32[]{:S(2)}, u32[]{:S(2)}) collective-permute-start(f32[136,128]{1,0:T(8,128)} %get-tuple-element.34), channel_id=1, source_target_pairs={{0,6},{1,7},{2,4},{3,5},{4,2},{5,3},{6,0},{7,1},{8,14},{9,15},{10,... | collective-permute-start | bytes 208904 | tf_op jit(solution)/shard_map/ppermute | solution.py:459
  7.2 0.0 collective-permute-start.2
  7.2 4.1 %collective-permute-start.4 = (f32[136,256]{1,0:T(8,128)}, f32[136,256]{1,0:T(8,128)S(1)}, u32[]{:S(2)}, u32[]{:S(2)}) collective-permute-start(f32[136,256]{1,0:T(8,128)} %get-tuple-element.36), channel_id=1, source_target_pairs={{0,4},{1,5},{2,6},{3,7},{4,0},{5,1},{6,2},{7,3},{8,12},{9,13},{10,... | collective-permute-start | bytes 417800 | tf_op jit(solution)/shard_map/ppermute | solution.py:459
  11.2 0.0 collective-permute-start.5
  11.2 0.0 copy-done.4
  11.3 0.0 copy-start
  11.3 1.0 %copy-done = f32[2,256,256]{2,1,0:T(8,128)S(1)} copy-done((f32[2,256,256]{2,1,0:T(8,128)S(1)}, f32[2,256,256]{2,1,0:T(8,128)}, u32[]{:S(2)}) %copy-start) | copy-done | bytes 524312
  12.3 1.0 %copy-done.1 = f32[2,256,256]{2,1,0:T(8,128)S(1)} copy-done((f32[2,256,256]{2,1,0:T(8,128)S(1)}, f32[2,256,256]{2,1,0:T(8,128)}, u32[]{:S(2)}) %copy-start.1) | copy-done | bytes 524312
  13.3 0.9 %copy-done.3 = bf16[2,256,256]{2,1,0:T(8,128)(2,1)S(1)} copy-done((bf16[2,256,256]{2,1,0:T(8,128)(2,1)S(1)}, bf16[2,256,256]{2,1,0:T(8,128)(2,1)}, u32[]{:S(2)}) %copy-start.3) | copy-done | bytes 262168
  14.3 0.2 shard_map.69
  14.5 0.0 collective-permute-done.1.refs_2_.refs_0_.refs_3_
  14.5 0.0 collective-permute-done.2.refs_3_.refs_1_.refs_4_
  14.5 0.0 collective-permute-done.refs_1_.refs_2_.refs_0_
  14.6 0.6 %collective-permute-start.3 = (f32[256,128]{1,0:T(8,128)S(1)}, f32[256,128]{1,0:T(8,128)S(1)}, u32[]{:S(2)}, u32[]{:S(2)}) collective-permute-start(f32[256,128]{1,0:T(8,128)S(1)} %shard_map.70.before_ref.unused_ref), channel_id=1, source_target_pairs={{0,1},{1,0},{2,3},{3,2},{4,5},{5,4},{6,7},{7,6},{8,9},{9,8},{10,11... | collective-permute-start | bytes 393224 | tf_op jit(solution)/shard_map/ppermute | solution.py:462
  15.1 1.4 %shard_map.71.refs_0_.before_ref = f32[256,256]{1,0:T(8,128)S(1)} custom-call(f32[8,128]{1,0:T(8,128)S(1)} %get-tuple-element.31.note_ref, f32[2,256,256]{2,1,0:T(8,128)S(1)} %get-tuple-element.32.refs_0_.probe_ref, f32[256,128]{1,0:T(8,128)S(1)} %shard_map.70.before_ref.unused_ref, f32[256,128]{1,0:T(8,128)S(1)} %shard_map.70.before_ref.unused_ref, ...), custom_call_target="tpu_custom_call" | custom-call | tf_op jit(solution)/shard_map/pallas_call | solution.py:433
  16.5 0.0 collective-permute-done.4.refs_2_.refs_1_.refs_0_
  16.6 0.0 collective-permute-done.5.refs_3_.refs_2_.refs_1_
  16.6 0.0 collective-permute-done.3.refs_1_.refs_0_
  16.6 0.1 collective-permute-start.6
  16.7 0.5 collective-permute-start.7
  17.2 0.8 %shard_map.73.unused_ref.patch_ref = f32[2,256,256]{2,1,0:T(8,128)S(1)} custom-call(f32[8,128]{1,0:T(8,128)S(1)} %get-tuple-element.31.note_ref, f32[512,128]{1,0:T(8,128)S(1)} %shard_map.72.unused_ref, f32[2,256,256]{2,1,0:T(8,128)S(1)} %get-tuple-element.38.spec_ref, f32[280,128]{1,0:T(8,128)S(1)} %collective-permute-done.refs_1_.refs_2_.refs_0_, ...), custom_call_target="tpu_custom_call" | custom-call | tf_op jit(solution)/shard_map/pallas_call | solution.py:433
  18.0 0.4 collective-permute-done.7.refs_2_
  18.4 0.0 collective-permute-done.6.refs_1_
  18.4 0.8 %shard_map.74.patch_other_ref = f32[2,256,256]{2,1,0:T(8,128)S(1)} custom-call(f32[8,128]{1,0:T(8,128)S(1)} %get-tuple-element.31.note_ref, f32[2,256,256]{2,1,0:T(8,128)S(1)} %shard_map.73.unused_ref.patch_ref, f32[2,256,256]{2,1,0:T(8,128)S(1)} %get-tuple-element.38.spec_ref, f32[256,128]{1,0:T(8,128)S(1)} %collective-permute-done.3.refs_1_.refs_0_, ...), custom_call_target="tpu_custom_call" | custom-call | tf_op jit(solution)/shard_map/pallas_call | solution.py:433
  19.3 2.5 %shard_map.75 = (f32[2,256,256]{2,1,0:T(8,128)S(1)}, f32[2,256,256]{2,1,0:T(8,128)S(1)}, f32[256,256]{1,0:T(8,128)S(1)}, f32[256,256]{1,0:T(8,128)S(1)}) custom-call(f32[2,256,256]{2,1,0:T(8,128)S(1)} %shard_map.73.unused_ref.patch_ref, f32[2,256,256]{2,1,0:T(8,128)S(1)} %shard_map.74.patch_other_ref, ...), custom_call_target="tpu_custom_call" | custom-call | tf_op jit(solution)/shard_map/pallas_call | solution.py:433
  21.8 0.2 collective-permute-start.8
  22.0 1.0 %shard_map.76.unused_light_ref.light_ref = f32[256,256]{1,0:T(8,128)S(1)} custom-call(f32[8,128]{1,0:T(8,128)S(1)} %get-tuple-element.31.note_ref, f32[2,256,256]{2,1,0:T(8,128)S(1)} %get-tuple-element.32.refs_0_.probe_ref, f32[256,256]{1,0:T(8,128)S(1)} %shard_map.71.refs_0_.before_ref, f32[2,256,256]{2,1,0:T(8,128)S(1)} %get-tuple-element.45.unused_ref.own_ref, ...), custom_call_target="tpu_custom_call" | custom-call | tf_op jit(solution)/shard_map/pallas_call | solution.py:433
  23.0 0.4 collective-permute-done.8.recv_ref
  23.4 0.2 collective-permute-start.11
  23.6 0.5 %collective-permute-start.9 = (f32[128,256]{1,0:T(8,128)S(1)}, f32[128,256]{1,0:T(8,128)S(1)}, u32[]{:S(2)}, u32[]{:S(2)}) collective-permute-start(f32[128,256]{1,0:T(8,128)S(1)} %get-tuple-element.47), channel_id=1, source_target_pairs={{0,2},{1,5},{2,0},{3,7},{4,6},{5,1},{6,4},{7,3},{8,10},{9,13},{10,... | collective-permute-start | bytes 393224 | tf_op jit(solution)/shard_map/ppermute | solution.py:459
  24.2 0.0 collective-permute-start.10
  24.2 1.2 %collective-permute-done.10.other_note_ref = f32[8,128]{1,0:T(8,128)S(1)} collective-permute-done((f32[8,128]{1,0:T(8,128)S(1)}, f32[8,128]{1,0:T(8,128)S(1)}, u32[]{:S(2)}, u32[]{:S(2)}) %collective-permute-start.10) | collective-permute-done | bytes 4128 | tf_op jit(solution)/shard_map/ppermute | solution.py:462
  25.4 0.0 collective-permute-done.11.recv_ref
  25.4 1.2 %shard_map.78 = (f32[512,256]{1,0:T(8,128)S(1)}, f32[512,128]{1,0:T(8,128)S(1)}) custom-call(f32[8,128]{1,0:T(8,128)S(1)} %get-tuple-element.31.note_ref, f32[8,128]{1,0:T(8,128)S(1)} %collective-permute-done.10.other_note_ref, f32[2,256,256]{2,1,0:T(8,128)S(1)} %get-tuple-element.45.unused_ref.own_ref, f32[2,256,256]{2,1,0:T(8,128)S(1)} %collective-permute-done.11.recv_ref, ...), custom_call_target="tpu_custom_call" | custom-call | tf_op jit(solution)/shard_map/pallas_call | solution.py:433
  26.7 1.5 %collective-permute-start.14 = (f32[512,128]{1,0:T(8,128)S(1)}, f32[512,128]{1,0:T(8,128)S(1)}, u32[]{:S(2)}, u32[]{:S(2)}) collective-permute-start(f32[512,128]{1,0:T(8,128)S(1)} %get-tuple-element.50), channel_id=1, source_target_pairs={{0,2},{1,3},{2,0},{3,1},{4,6},{5,7},{6,4},{7,5},{8,10},{9,11},{10,... | collective-permute-start | bytes 786440 | tf_op jit(solution)/shard_map/ppermute | solution.py:459
  28.1 0.5 collective-permute-done.9.b_ref
  28.6 0.1 collective-permute-start.12
  28.7 0.6 %collective-permute-start.15 = (f32[256,256]{1,0:T(8,128)S(1)}, f32[256,256]{1,0:T(8,128)S(1)}, u32[]{:S(2)}, u32[]{:S(2)}) collective-permute-start(f32[256,256]{1,0:T(8,128)S(1)} %shard_map.76.unused_light_ref.light_ref), channel_id=1, source_target_pairs={{0,1},{1,0},{2,3},{3,2},{4,5},{5,4},{6,7},{7,6},{8,9},{9,8},{10,11... | collective-permute-start | bytes 786440 | tf_op jit(solution)/shard_map/ppermute | solution.py:462
  29.3 5.7 %collective-permute-done.12.b_ref = f32[128,256]{1,0:T(8,128)S(1)} collective-permute-done((f32[128,256]{1,0:T(8,128)S(1)}, f32[128,256]{1,0:T(8,128)S(1)}, u32[]{:S(2)}, u32[]{:S(2)}) %collective-permute-start.12) | collective-permute-done | bytes 131104 | tf_op jit(solution)/shard_map/ppermute | solution.py:459
  35.0 0.2 collective-permute-start.13
  35.2 0.0 collective-permute-done.14.refs_0_
  35.2 0.1 shard_map.82
  35.3 1.5 %collective-permute-start.16 = (f32[128,256]{1,0:T(8,128)S(1)}, f32[128,256]{1,0:T(8,128)S(1)}, u32[]{:S(2)}, u32[]{:S(2)}) collective-permute-start(f32[128,256]{1,0:T(8,128)S(1)} %get-tuple-element.52), channel_id=1, source_target_pairs={{0,4},{1,5},{2,6},{3,7},{4,0},{5,1},{6,2},{7,3},{8,12},{9,13},{10,... | collective-permute-start | bytes 393224 | tf_op jit(solution)/shard_map/ppermute | solution.py:459
  36.9 0.0 collective-permute-start.17
  36.9 6.1 %collective-permute-done.13.b_ref = f32[128,256]{1,0:T(8,128)S(1)} collective-permute-done((f32[128,256]{1,0:T(8,128)S(1)}, f32[128,256]{1,0:T(8,128)S(1)}, u32[]{:S(2)}, u32[]{:S(2)}) %collective-permute-start.13) | collective-permute-done | bytes 131104 | tf_op jit(solution)/shard_map/ppermute | solution.py:459
  43.0 0.1 collective-permute-start.20
  43.1 0.0 collective-permute-done.15.other_light_ref
  43.1 0.0 collective-permute-done.16.edge_a
  43.1 0.0 collective-permute-done.17.edge_b
  43.1 0.1 shard_map.83
  43.2 0.1 collective-permute-start.18
  43.3 0.5 collective-permute-start.19
  43.8 0.1 collective-permute-start.21
  43.9 4.1 %collective-permute-done.20.away_ref = f32[128,256]{1,0:T(8,128)S(1)} collective-permute-done((f32[128,256]{1,0:T(8,128)S(1)}, f32[128,256]{1,0:T(8,128)S(1)}, u32[]{:S(2)}, u32[]{:S(2)}) %collective-permute-start.20) | collective-permute-done | bytes 131104 | tf_op jit(solution)/shard_map/ppermute | solution.py:459
  48.0 0.0 collective-permute-start.22
  48.0 0.0 collective-permute-done.18.other_upper_ref
  48.0 0.0 collective-permute-done.19.other_lower_ref
  48.0 0.8 %shard_map.84 = (f32[2,256,256]{2,1,0:T(8,128)}, f32[8,128]{1,0:T(8,128)S(1)}) custom-call(f32[128,256]{1,0:T(8,128)S(1)} %get-tuple-element.54.upper_ref, f32[128,256]{1,0:T(8,128)S(1)} %get-tuple-element.55.lower_ref, f32[128,256]{1,0:T(8,128)S(1)} %collective-permute-done.18.other_upper_ref, f32[128,256]{1,0:T(8,128)S(1)} %collective-permute-done.19.other_lower_ref), custom_call_target="tpu_custom_call" | custom-call | tf_op jit(solution)/shard_map/pallas_call | solution.py:433
  48.8 0.0 collective-permute-done.21.keep_other_ref
  48.8 0.5 collective-permute-done.22.away_other_ref
  49.3 0.9 %shard_map.85 = f32[2,256,256]{2,1,0:T(8,128)} custom-call(f32[2,256,256]{2,1,0:T(8,128)S(1)} %get-tuple-element.32.refs_0_.probe_ref, f32[128,256]{1,0:T(8,128)S(1)} %shard_map.81.unused_ref.keep_ref, f32[128,256]{1,0:T(8,128)S(1)} %collective-permute-done.20.away_ref, f32[128,256]{1,0:T(8,128)S(1)} %collective-permute-done.21.keep_other_ref, ...), custom_call_target="tpu_custom_call" | custom-call | tf_op jit(solution)/shard_map/pallas_call | solution.py:433
  (10 shorter events, 0.1 us)
Async XLA Ops:
  0.6 10.6 %copy-start.2 = (bf16[3,256,256]{2,1,0:T(8,128)(2,1)S(1)}, bf16[3,256,256]{2,1,0:T(8,128)(2,1)}, u32[]{:S(2)}) copy-start(bf16[3,256,256]{2,1,0:T(8,128)(2,1)} %constant.2.clone.refs_4_) | copy-start | bytes 1179652
  2.6 11.9 %collective-permute-start = (f32[280,128]{1,0:T(8,128)}, f32[280,128]{1,0:T(8,128)S(1)}, u32[]{:S(2)}, u32[]{:S(2)}) collective-permute-start(f32[280,128]{1,0:T(8,128)} %get-tuple-element.33), channel_id=1, source_target_pairs={{0,2},{1,3},{2,0},{3,1},{4,6},{5,7},{6,4},{7,5},{8,10},{9,11},{10,... | collective-permute-start | bytes 430088 | tf_op jit(solution)/shard_map/ppermute | solution.py:459
  5.6 5.6 %copy-start.4 = (f32[8,128]{1,0:T(8,128)S(1)}, f32[8,128]{1,0:T(8,128)}, u32[]{:S(2)}) copy-start(f32[8,128]{1,0:T(8,128)} %get-tuple-element.30.refs_0_) | copy-start | bytes 12292
  5.6 8.9 %collective-permute-start.1 = (f32[136,128]{1,0:T(8,128)}, f32[136,128]{1,0:T(8,128)S(1)}, u32[]{:S(2)}, u32[]{:S(2)}) collective-permute-start(f32[136,128]{1,0:T(8,128)} %get-tuple-element.34), channel_id=1, source_target_pairs={{0,6},{1,7},{2,4},{3,5},{4,2},{5,3},{6,0},{7,1},{8,14},{9,15},{10,... | collective-permute-start | bytes 208904 | tf_op jit(solution)/shard_map/ppermute | solution.py:459
  7.2 7.4 %collective-permute-start.2 = (f32[136,128]{1,0:T(8,128)}, f32[136,128]{1,0:T(8,128)S(1)}, u32[]{:S(2)}, u32[]{:S(2)}) collective-permute-start(f32[136,128]{1,0:T(8,128)} %get-tuple-element.35), channel_id=1, source_target_pairs={{0,1},{1,0},{2,3},{3,2},{4,10},{5,11},{6,8},{7,9},{8,6},{9,7},{10,... | collective-permute-start | bytes 208904 | tf_op jit(solution)/shard_map/ppermute | solution.py:459
  7.2 9.4 %collective-permute-start.4 = (f32[136,256]{1,0:T(8,128)}, f32[136,256]{1,0:T(8,128)S(1)}, u32[]{:S(2)}, u32[]{:S(2)}) collective-permute-start(f32[136,256]{1,0:T(8,128)} %get-tuple-element.36), channel_id=1, source_target_pairs={{0,4},{1,5},{2,6},{3,7},{4,0},{5,1},{6,2},{7,3},{8,12},{9,13},{10,... | collective-permute-start | bytes 417800 | tf_op jit(solution)/shard_map/ppermute | solution.py:459
  11.2 5.3 %collective-permute-start.5 = (f32[136,256]{1,0:T(8,128)}, f32[136,256]{1,0:T(8,128)S(1)}, u32[]{:S(2)}, u32[]{:S(2)}) collective-permute-start(f32[136,256]{1,0:T(8,128)} %get-tuple-element.37), channel_id=1, source_target_pairs={{0,1},{1,0},{2,3},{3,2},{4,8},{5,9},{6,10},{7,11},{8,4},{9,5},{10,... | collective-permute-start | bytes 417800 | tf_op jit(solution)/shard_map/ppermute | solution.py:459
  11.3 1.0 %copy-start = (f32[2,256,256]{2,1,0:T(8,128)S(1)}, f32[2,256,256]{2,1,0:T(8,128)}, u32[]{:S(2)}) copy-start(f32[2,256,256]{2,1,0:T(8,128)} %refs_1_.1) | copy-start | bytes 1572868
  12.3 1.0 %copy-start.1 = (f32[2,256,256]{2,1,0:T(8,128)S(1)}, f32[2,256,256]{2,1,0:T(8,128)}, u32[]{:S(2)}) copy-start(f32[2,256,256]{2,1,0:T(8,128)} %refs_2_.1) | copy-start | bytes 1572868
  13.3 0.9 %copy-start.3 = (bf16[2,256,256]{2,1,0:T(8,128)(2,1)S(1)}, bf16[2,256,256]{2,1,0:T(8,128)(2,1)}, u32[]{:S(2)}) copy-start(bf16[2,256,256]{2,1,0:T(8,128)(2,1)} %refs_3_.1) | copy-start | bytes 786436
  14.6 2.0 %collective-permute-start.3 = (f32[256,128]{1,0:T(8,128)S(1)}, f32[256,128]{1,0:T(8,128)S(1)}, u32[]{:S(2)}, u32[]{:S(2)}) collective-permute-start(f32[256,128]{1,0:T(8,128)S(1)} %shard_map.70.before_ref.unused_ref), channel_id=1, source_target_pairs={{0,1},{1,0},{2,3},{3,2},{4,5},{5,4},{6,7},{7,6},{8,9},{9,8},{10,11... | collective-permute-start | bytes 393224 | tf_op jit(solution)/shard_map/ppermute | solution.py:462
  16.6 1.8 %collective-permute-start.6 = (f32[512,128]{1,0:T(8,128)S(1)}, f32[512,128]{1,0:T(8,128)S(1)}, u32[]{:S(2)}, u32[]{:S(2)}) collective-permute-start(f32[512,128]{1,0:T(8,128)S(1)} %shard_map.72.unused_ref), channel_id=1, source_target_pairs={{0,1},{1,0},{2,3},{3,2},{4,5},{5,4},{6,7},{7,6},{8,9},{9,8},{10,11... | collective-permute-start | bytes 786440 | tf_op jit(solution)/shard_map/ppermute | solution.py:462
  16.7 1.7 %collective-permute-start.7 = (f32[280,128]{1,0:T(8,128)S(1)}, f32[280,128]{1,0:T(8,128)S(1)}, u32[]{:S(2)}, u32[]{:S(2)}) collective-permute-start(f32[280,128]{1,0:T(8,128)S(1)} %collective-permute-done.refs_1_.refs_2_.refs_0_), channel_id=1, source_target_pairs={{0,1},{1,0},{2,3},{3,2},{4,5},{5,4},{6,7},{7,6},{8,9},{9,8},{10,11... | collective-permute-start | bytes 430088 | tf_op jit(solution)/shard_map/ppermute | solution.py:462
  21.8 1.6 %collective-permute-start.8 = (f32[256,256]{1,0:T(8,128)S(1)}, f32[256,256]{1,0:T(8,128)S(1)}, u32[]{:S(2)}, u32[]{:S(2)}) collective-permute-start(f32[256,256]{1,0:T(8,128)S(1)} %get-tuple-element.43), channel_id=1, source_target_pairs={{0,1},{1,0},{2,3},{3,2},{4,5},{5,4},{6,7},{7,6},{8,9},{9,8},{10,11... | collective-permute-start | bytes 786440 | tf_op jit(solution)/shard_map/ppermute | solution.py:462
  23.4 2.0 %collective-permute-start.11 = (f32[2,256,256]{2,1,0:T(8,128)S(1)}, f32[2,256,256]{2,1,0:T(8,128)S(1)}, u32[]{:S(2)}, u32[]{:S(2)}) collective-permute-start(f32[2,256,256]{2,1,0:T(8,128)S(1)} %get-tuple-element.48), channel_id=1, source_target_pairs={{0,1},{1,0},{2,3},{3,2},{4,5},{5,4},{6,7},{7,6},{8,9},{9,8},{10,11... | collective-permute-start | bytes 1572872 | tf_op jit(solution)/shard_map/ppermute | solution.py:462
  23.6 5.0 %collective-permute-start.9 = (f32[128,256]{1,0:T(8,128)S(1)}, f32[128,256]{1,0:T(8,128)S(1)}, u32[]{:S(2)}, u32[]{:S(2)}) collective-permute-start(f32[128,256]{1,0:T(8,128)S(1)} %get-tuple-element.47), channel_id=1, source_target_pairs={{0,2},{1,5},{2,0},{3,7},{4,6},{5,1},{6,4},{7,3},{8,10},{9,13},{10,... | collective-permute-start | bytes 393224 | tf_op jit(solution)/shard_map/ppermute | solution.py:459
  24.2 1.2 %collective-permute-start.10 = (f32[8,128]{1,0:T(8,128)S(1)}, f32[8,128]{1,0:T(8,128)S(1)}, u32[]{:S(2)}, u32[]{:S(2)}) collective-permute-start(f32[8,128]{1,0:T(8,128)S(1)} %get-tuple-element.31.note_ref), channel_id=1, source_target_pairs={{0,1},{1,0},{2,3},{3,2},{4,5},{5,4},{6,7},{7,6},{8,9},{9,8},{10,11... | collective-permute-start | bytes 12296 | tf_op jit(solution)/shard_map/ppermute | solution.py:462
  26.7 8.6 %collective-permute-start.14 = (f32[512,128]{1,0:T(8,128)S(1)}, f32[512,128]{1,0:T(8,128)S(1)}, u32[]{:S(2)}, u32[]{:S(2)}) collective-permute-start(f32[512,128]{1,0:T(8,128)S(1)} %get-tuple-element.50), channel_id=1, source_target_pairs={{0,2},{1,3},{2,0},{3,1},{4,6},{5,7},{6,4},{7,5},{8,10},{9,11},{10,... | collective-permute-start | bytes 786440 | tf_op jit(solution)/shard_map/ppermute | solution.py:459
  28.6 6.4 %collective-permute-start.12 = (f32[128,256]{1,0:T(8,128)S(1)}, f32[128,256]{1,0:T(8,128)S(1)}, u32[]{:S(2)}, u32[]{:S(2)}) collective-permute-start(f32[128,256]{1,0:T(8,128)S(1)} %shard_map.79.a_ref), channel_id=1, source_target_pairs={{0,4},{1,9},{2,6},{3,11},{4,0},{5,13},{6,2},{7,15},{8,12},{9,1},{1... | collective-permute-start | bytes 393224 | tf_op jit(solution)/shard_map/ppermute | solution.py:459
  28.7 14.4 %collective-permute-start.15 = (f32[256,256]{1,0:T(8,128)S(1)}, f32[256,256]{1,0:T(8,128)S(1)}, u32[]{:S(2)}, u32[]{:S(2)}) collective-permute-start(f32[256,256]{1,0:T(8,128)S(1)} %shard_map.76.unused_light_ref.light_ref), channel_id=1, source_target_pairs={{0,1},{1,0},{2,3},{3,2},{4,5},{5,4},{6,7},{7,6},{8,9},{9,8},{10,11... | collective-permute-start | bytes 786440 | tf_op jit(solution)/shard_map/ppermute | solution.py:462
  35.0 7.9 %collective-permute-start.13 = (f32[128,256]{1,0:T(8,128)S(1)}, f32[128,256]{1,0:T(8,128)S(1)}, u32[]{:S(2)}, u32[]{:S(2)}) collective-permute-start(f32[128,256]{1,0:T(8,128)S(1)} %shard_map.80.a_ref.unused_ref), channel_id=1, source_target_pairs={{0,8},{1,3},{2,10},{3,1},{4,12},{5,7},{6,14},{7,5},{8,0},{9,11},{1... | collective-permute-start | bytes 393224 | tf_op jit(solution)/shard_map/ppermute | solution.py:459
  35.3 7.8 %collective-permute-start.16 = (f32[128,256]{1,0:T(8,128)S(1)}, f32[128,256]{1,0:T(8,128)S(1)}, u32[]{:S(2)}, u32[]{:S(2)}) collective-permute-start(f32[128,256]{1,0:T(8,128)S(1)} %get-tuple-element.52), channel_id=1, source_target_pairs={{0,4},{1,5},{2,6},{3,7},{4,0},{5,1},{6,2},{7,3},{8,12},{9,13},{10,... | collective-permute-start | bytes 393224 | tf_op jit(solution)/shard_map/ppermute | solution.py:459
  36.9 6.2 %collective-permute-start.17 = (f32[128,256]{1,0:T(8,128)S(1)}, f32[128,256]{1,0:T(8,128)S(1)}, u32[]{:S(2)}, u32[]{:S(2)}) collective-permute-start(f32[128,256]{1,0:T(8,128)S(1)} %get-tuple-element.53), channel_id=1, source_target_pairs={{0,1},{1,0},{2,3},{3,2},{4,8},{5,9},{6,10},{7,11},{8,4},{9,5},{10,... | collective-permute-start | bytes 393224 | tf_op jit(solution)/shard_map/ppermute | solution.py:459
  43.0 5.0 %collective-permute-start.20 = (f32[128,256]{1,0:T(8,128)S(1)}, f32[128,256]{1,0:T(8,128)S(1)}, u32[]{:S(2)}, u32[]{:S(2)}) collective-permute-start(f32[128,256]{1,0:T(8,128)S(1)} %shard_map.81.unused_ref.keep_ref), channel_id=1, source_target_pairs={{0,2},{1,5},{2,0},{3,7},{4,6},{5,1},{6,4},{7,3},{8,10},{9,13},{10,... | collective-permute-start | bytes 393224 | tf_op jit(solution)/shard_map/ppermute | solution.py:459
  43.2 4.8 %collective-permute-start.18 = (f32[128,256]{1,0:T(8,128)S(1)}, f32[128,256]{1,0:T(8,128)S(1)}, u32[]{:S(2)}, u32[]{:S(2)}) collective-permute-start(f32[128,256]{1,0:T(8,128)S(1)} %get-tuple-element.54.upper_ref), channel_id=1, source_target_pairs={{0,1},{1,0},{2,3},{3,2},{4,5},{5,4},{6,7},{7,6},{8,9},{9,8},{10,11... | collective-permute-start | bytes 393224 | tf_op jit(solution)/shard_map/ppermute | solution.py:462
  43.3 4.7 %collective-permute-start.19 = (f32[128,256]{1,0:T(8,128)S(1)}, f32[128,256]{1,0:T(8,128)S(1)}, u32[]{:S(2)}, u32[]{:S(2)}) collective-permute-start(f32[128,256]{1,0:T(8,128)S(1)} %get-tuple-element.55.lower_ref), channel_id=1, source_target_pairs={{0,1},{1,0},{2,3},{3,2},{4,5},{5,4},{6,7},{7,6},{8,9},{9,8},{10,11... | collective-permute-start | bytes 393224 | tf_op jit(solution)/shard_map/ppermute | solution.py:462
  43.8 5.0 %collective-permute-start.21 = (f32[128,256]{1,0:T(8,128)S(1)}, f32[128,256]{1,0:T(8,128)S(1)}, u32[]{:S(2)}, u32[]{:S(2)}) collective-permute-start(f32[128,256]{1,0:T(8,128)S(1)} %shard_map.81.unused_ref.keep_ref), channel_id=1, source_target_pairs={{0,1},{1,0},{2,3},{3,2},{4,5},{5,4},{6,7},{7,6},{8,9},{9,8},{10,11... | collective-permute-start | bytes 393224 | tf_op jit(solution)/shard_map/ppermute | solution.py:462
  48.0 1.3 %collective-permute-start.22 = (f32[128,256]{1,0:T(8,128)S(1)}, f32[128,256]{1,0:T(8,128)S(1)}, u32[]{:S(2)}, u32[]{:S(2)}) collective-permute-start(f32[128,256]{1,0:T(8,128)S(1)} %collective-permute-done.20.away_ref), channel_id=1, source_target_pairs={{0,1},{1,0},{2,3},{3,2},{4,5},{5,4},{6,7},{7,6},{8,9},{9,8},{10,11... | collective-permute-start | bytes 393224 | tf_op jit(solution)/shard_map/ppermute | solution.py:462

commit v10 on v9

--- a/solution.py
+++ b/solution.py
@@ -474,8 +474,8 @@
     recv = [send(block, target) for block, target in zip(blocks, targets)]
 
     waves = jnp.asarray(dft_waves(size))
-    late = (note, specimen, probe_wave, amplitudes)
-    note, specimen_v, probe_v, amp_v, ta_v, tb_v = call(
+    late = (note, probe_wave)
+    note, probe_v, ta_v, tb_v = call(
         fetch_kernel,
         [jax.ShapeDtypeStruct(a.shape, a.dtype) for a in late]
         + [jax.ShapeDtypeStruct((2 * size, 2 * size), jnp.bfloat16)] * 2,
@@ -491,7 +491,7 @@
             [VMEM, ANY] + [VMEM] * (1 + len(arrays)),
             note,
             after,
-            specimen_v,
+            specimen,
             *arrays,
             scratch=[pltpu.VMEM((tile + size, tile + size), jnp.float32), NOTE_SMEM, dma(1)],
         )[0]
@@ -538,7 +538,7 @@
         patches,
         patches_other,
         probe_v,
-        amp_v,
+        amplitudes,
         ta_v,
         tb_v,
     )
@@ -600,7 +600,7 @@
         [f32(tile // 2, tile)] * 2,
         [ANY] + [VMEM] * (4 + len(arrived)),
         keep,
-        specimen_v,
+        specimen,
         center,
         light,
         to_core(light),

time: 50.5 us -> 47.7 us (0.945)
  waiting for transfers between devices: 18.9 us -> 10.6 us
  starting transfers between devices: 15.4 us -> 23.6 us
  local copies, waits for them, and re-layouts: 3.04 us -> 1.18 us
  Pallas kernels: 12.1 us -> 11.4 us
    ppermute x12, waiting for transfers between devices: 16.4 us -> 8.38 us  [send(): return lax.ppermute(value, GROUP, permutation(sizes, target))]
    ppermute x12, starting transfers between devices: 12.6 us -> 19.4 us  [send(): return lax.ppermute(value, GROUP, permutation(sizes, target))]
    unnamed x10, local copies, waits for them, and re-layouts: 3.04 us -> 1.18 us
    ppermute x11, starting transfers between devices: 2.79 us -> 4.15 us  [to_core(): return lax.ppermute(value, 'pos', PART_SWAP)]
    pallas_call x18, Pallas kernels: 12.1 us -> 11.4 us  [call(): pl.pallas_call(kernel, out_shape=out_shape, in_specs=specs, out_specs=out...]
  transfers between devices with their start and end apart: 23 -> 23, of which waited for: 8 -> 8; matrix products, arithmetic and copies ran while one was open for 0% -> 0% of each run, Pallas kernels for 12% -> 11%
where the time goes in v10:
time: 47.7 us; the launch traced here: 47.6 us
  starting transfers between devices  23.6 us (49%)
  Pallas kernels  11.4 us (24%)
  waiting for transfers between devices  10.6 us (22%)
  local copies, waits for them, and re-layouts  1.18 us (2%)
  between operations  0.83 us (2%)
    ppermute x12, starting transfers between devices, send(): return lax.ppermute(value, GROUP, permutation(sizes, target))  19.4 us
    pallas_call x18, Pallas kernels, call(): pl.pallas_call(kernel, out_shape=out_shape, in_specs=specs, out_specs=out...  11.4 us
    ppermute x12, waiting for transfers between devices, send(): return lax.ppermute(value, GROUP, permutation(sizes, target))  8.38 us
    ppermute x11, starting transfers between devices, to_core(): return lax.ppermute(value, 'pos', PART_SWAP)  4.15 us
    ppermute x11, waiting for transfers between devices, to_core(): return lax.ppermute(value, 'pos', PART_SWAP)  2.23 us
    unnamed x10, local copies, waits for them, and re-layouts  1.18 us
  transfers between devices with their start and end apart: 23, of which 8 were waited for; matrix products, arithmetic and copies ran while one was open for 0% of the time, Pallas kernels for 11%

profile of v10, /device:TPU:0, one launch (start us, length us, event | category | flops | bytes accessed | tf_op | source)
XLA Modules:
  0.0 47.6 jit_solution(261259322933105741)
XLA Ops:
  0.6 0.0 copy-start.2
  0.6 2.0 %shard_map.68 = (f32[280,128]{1,0:T(8,128)}, f32[136,256]{1,0:T(8,128)}, f32[136,256]{1,0:T(8,128)}, f32[136,128]{1,0:T(8,128)}, f32[136,128]{1,0:T(8,128)}, /*index=5*/f32[8,128]{1,0:T(8,128)}) custom-call(s32[2,2]{1,0:T(2,128)} %off_hbm.1, f32[2,256,256]{2,1,0:T(8,128)} %spec_ref.7), custom_call_target="tpu_custom_call" | custom-call | tf_op jit(solution)/shard_map/pallas_call | solution.py:433
  2.6 3.0 %collective-permute-start = (f32[280,128]{1,0:T(8,128)}, f32[280,128]{1,0:T(8,128)S(1)}, u32[]{:S(2)}, u32[]{:S(2)}) collective-permute-start(f32[280,128]{1,0:T(8,128)} %get-tuple-element.31), channel_id=1, source_target_pairs={{0,2},{1,3},{2,0},{3,1},{4,6},{5,7},{6,4},{7,5},{8,10},{9,11},{10,... | collective-permute-start | bytes 430088 | tf_op jit(solution)/shard_map/ppermute | solution.py:459
  5.6 1.5 %collective-permute-start.1 = (f32[136,128]{1,0:T(8,128)}, f32[136,128]{1,0:T(8,128)S(1)}, u32[]{:S(2)}, u32[]{:S(2)}) collective-permute-start(f32[136,128]{1,0:T(8,128)} %get-tuple-element.32), channel_id=1, source_target_pairs={{0,6},{1,7},{2,4},{3,5},{4,2},{5,3},{6,0},{7,1},{8,14},{9,15},{10,... | collective-permute-start | bytes 208904 | tf_op jit(solution)/shard_map/ppermute | solution.py:459
  7.2 0.0 collective-permute-start.2
  7.2 4.1 %collective-permute-start.4 = (f32[136,256]{1,0:T(8,128)}, f32[136,256]{1,0:T(8,128)S(1)}, u32[]{:S(2)}, u32[]{:S(2)}) collective-permute-start(f32[136,256]{1,0:T(8,128)} %get-tuple-element.34), channel_id=1, source_target_pairs={{0,4},{1,5},{2,6},{3,7},{4,0},{5,1},{6,2},{7,3},{8,12},{9,13},{10,... | collective-permute-start | bytes 417800 | tf_op jit(solution)/shard_map/ppermute | solution.py:459
  11.2 0.0 collective-permute-start.5
  11.3 0.0 copy-start.1
  11.3 1.0 %copy-done.1 = f32[2,256,256]{2,1,0:T(8,128)S(1)} copy-done((f32[2,256,256]{2,1,0:T(8,128)S(1)}, f32[2,256,256]{2,1,0:T(8,128)}, u32[]{:S(2)}) %copy-start.1) | copy-done | bytes 524312
  12.3 0.1 shard_map.69
  12.4 0.0 collective-permute-done.1.refs_2_.refs_0_.refs_3_
  12.4 0.0 collective-permute-done.2.refs_3_.refs_1_.refs_4_
  12.5 0.0 collective-permute-done.refs_1_.refs_2_.refs_0_
  12.5 0.6 %collective-permute-start.3 = (f32[256,128]{1,0:T(8,128)S(1)}, f32[256,128]{1,0:T(8,128)S(1)}, u32[]{:S(2)}, u32[]{:S(2)}) collective-permute-start(f32[256,128]{1,0:T(8,128)S(1)} %shard_map.70.before_ref.unused_ref), channel_id=1, source_target_pairs={{0,1},{1,0},{2,3},{3,2},{4,5},{5,4},{6,7},{7,6},{8,9},{9,8},{10,11... | collective-permute-start | bytes 393224 | tf_op jit(solution)/shard_map/ppermute | solution.py:462
  13.1 1.1 %shard_map.71.refs_0_.before_ref = f32[256,256]{1,0:T(8,128)S(1)} custom-call(f32[8,128]{1,0:T(8,128)S(1)} %get-tuple-element.29.note_ref, f32[2,256,256]{2,1,0:T(8,128)S(1)} %get-tuple-element.30.refs_0_.probe_ref, f32[256,128]{1,0:T(8,128)S(1)} %shard_map.70.before_ref.unused_ref, f32[256,128]{1,0:T(8,128)S(1)} %shard_map.70.before_ref.unused_ref, ...), custom_call_target="tpu_custom_call" | custom-call | tf_op jit(solution)/shard_map/pallas_call | solution.py:433
  14.2 0.0 copy-start
  14.2 0.3 collective-permute-done.4.refs_2_.refs_1_.refs_0_
  14.5 0.0 collective-permute-done.5.refs_3_.refs_2_.refs_1_
  14.5 0.0 collective-permute-done.3.refs_1_.refs_0_
  14.5 0.1 collective-permute-start.6
  14.6 0.5 collective-permute-start.7
  15.1 0.1 copy-done
  15.2 0.8 %shard_map.73.unused_ref.patch_ref = f32[2,256,256]{2,1,0:T(8,128)S(1)} custom-call(f32[8,128]{1,0:T(8,128)S(1)} %get-tuple-element.29.note_ref, f32[512,128]{1,0:T(8,128)S(1)} %shard_map.72.unused_ref, f32[2,256,256]{2,1,0:T(8,128)S(1)} %copy-done, f32[280,128]{1,0:T(8,128)S(1)} %collective-permute-done.refs_1_.refs_2_.refs_0_, ...), custom_call_target="tpu_custom_call" | custom-call | tf_op jit(solution)/shard_map/pallas_call | solution.py:433
  16.1 0.0 copy-start.3
  16.1 0.3 collective-permute-done.7.refs_2_
  16.3 0.0 collective-permute-done.6.refs_1_
  16.3 0.8 %shard_map.74.patch_other_ref = f32[2,256,256]{2,1,0:T(8,128)S(1)} custom-call(f32[8,128]{1,0:T(8,128)S(1)} %get-tuple-element.29.note_ref, f32[2,256,256]{2,1,0:T(8,128)S(1)} %shard_map.73.unused_ref.patch_ref, f32[2,256,256]{2,1,0:T(8,128)S(1)} %copy-done, f32[256,128]{1,0:T(8,128)S(1)} %collective-permute-done.3.refs_1_.refs_0_, ...), custom_call_target="tpu_custom_call" | custom-call | tf_op jit(solution)/shard_map/pallas_call | solution.py:433
  17.2 2.5 %shard_map.75 = (f32[2,256,256]{2,1,0:T(8,128)S(1)}, f32[2,256,256]{2,1,0:T(8,128)S(1)}, f32[256,256]{1,0:T(8,128)S(1)}, f32[256,256]{1,0:T(8,128)S(1)}) custom-call(f32[2,256,256]{2,1,0:T(8,128)S(1)} %shard_map.73.unused_ref.patch_ref, f32[2,256,256]{2,1,0:T(8,128)S(1)} %shard_map.74.patch_other_ref, ...), custom_call_target="tpu_custom_call" | custom-call | tf_op jit(solution)/shard_map/pallas_call | solution.py:433
  19.7 0.2 collective-permute-start.8
  19.9 0.7 %shard_map.76.unused_light_ref.light_ref = f32[256,256]{1,0:T(8,128)S(1)} custom-call(f32[8,128]{1,0:T(8,128)S(1)} %get-tuple-element.29.note_ref, f32[2,256,256]{2,1,0:T(8,128)S(1)} %get-tuple-element.30.refs_0_.probe_ref, f32[256,256]{1,0:T(8,128)S(1)} %shard_map.71.refs_0_.before_ref, f32[2,256,256]{2,1,0:T(8,128)S(1)} %get-tuple-element.41.unused_ref.own_ref, ...), custom_call_target="tpu_custom_call" | custom-call | tf_op jit(solution)/shard_map/pallas_call | solution.py:433
  20.7 0.6 %collective-permute-done.8.recv_ref = f32[256,256]{1,0:T(8,128)S(1)} collective-permute-done((f32[256,256]{1,0:T(8,128)S(1)}, f32[256,256]{1,0:T(8,128)S(1)}, u32[]{:S(2)}, u32[]{:S(2)}) %collective-permute-start.8) | collective-permute-done | bytes 262176 | tf_op jit(solution)/shard_map/ppermute | solution.py:462
  21.4 0.2 collective-permute-start.11
  21.6 0.7 %collective-permute-start.9 = (f32[128,256]{1,0:T(8,128)S(1)}, f32[128,256]{1,0:T(8,128)S(1)}, u32[]{:S(2)}, u32[]{:S(2)}) collective-permute-start(f32[128,256]{1,0:T(8,128)S(1)} %get-tuple-element.43), channel_id=1, source_target_pairs={{0,2},{1,5},{2,0},{3,7},{4,6},{5,1},{6,4},{7,3},{8,10},{9,13},{10,... | collective-permute-start | bytes 393224 | tf_op jit(solution)/shard_map/ppermute | solution.py:459
  22.3 1.4 %collective-permute-start.10 = (f32[8,128]{1,0:T(8,128)S(1)}, f32[8,128]{1,0:T(8,128)S(1)}, u32[]{:S(2)}, u32[]{:S(2)}) collective-permute-start(f32[8,128]{1,0:T(8,128)S(1)} %get-tuple-element.29.note_ref), channel_id=1, source_target_pairs={{0,1},{1,0},{2,3},{3,2},{4,5},{5,4},{6,7},{7,6},{8,9},{9,8},{10,11... | collective-permute-start | bytes 12296 | tf_op jit(solution)/shard_map/ppermute | solution.py:462
  23.7 0.8 %collective-permute-done.10.other_note_ref = f32[8,128]{1,0:T(8,128)S(1)} collective-permute-done((f32[8,128]{1,0:T(8,128)S(1)}, f32[8,128]{1,0:T(8,128)S(1)}, u32[]{:S(2)}, u32[]{:S(2)}) %collective-permute-start.10) | collective-permute-done | bytes 4128 | tf_op jit(solution)/shard_map/ppermute | solution.py:462
  24.5 0.0 collective-permute-done.11.recv_ref
  24.5 1.2 %shard_map.78 = (f32[512,256]{1,0:T(8,128)S(1)}, f32[512,128]{1,0:T(8,128)S(1)}) custom-call(f32[8,128]{1,0:T(8,128)S(1)} %get-tuple-element.29.note_ref, f32[8,128]{1,0:T(8,128)S(1)} %collective-permute-done.10.other_note_ref, f32[2,256,256]{2,1,0:T(8,128)S(1)} %get-tuple-element.41.unused_ref.own_ref, f32[2,256,256]{2,1,0:T(8,128)S(1)} %collective-permute-done.11.recv_ref, ...), custom_call_target="tpu_custom_call" | custom-call | tf_op jit(solution)/shard_map/pallas_call | solution.py:433
  25.7 1.6 %collective-permute-start.14 = (f32[512,128]{1,0:T(8,128)S(1)}, f32[512,128]{1,0:T(8,128)S(1)}, u32[]{:S(2)}, u32[]{:S(2)}) collective-permute-start(f32[512,128]{1,0:T(8,128)S(1)} %get-tuple-element.46), channel_id=1, source_target_pairs={{0,2},{1,3},{2,0},{3,1},{4,6},{5,7},{6,4},{7,5},{8,10},{9,11},{10,... | collective-permute-start | bytes 786440 | tf_op jit(solution)/shard_map/ppermute | solution.py:459
  27.3 0.0 collective-permute-done.9.b_ref
  27.4 1.3 %collective-permute-start.12 = (f32[128,256]{1,0:T(8,128)S(1)}, f32[128,256]{1,0:T(8,128)S(1)}, u32[]{:S(2)}, u32[]{:S(2)}) collective-permute-start(f32[128,256]{1,0:T(8,128)S(1)} %shard_map.79.a_ref), channel_id=1, source_target_pairs={{0,4},{1,9},{2,6},{3,11},{4,0},{5,13},{6,2},{7,15},{8,12},{9,1},{1... | collective-permute-start | bytes 393224 | tf_op jit(solution)/shard_map/ppermute | solution.py:459
  28.7 0.5 %collective-permute-start.15 = (f32[256,256]{1,0:T(8,128)S(1)}, f32[256,256]{1,0:T(8,128)S(1)}, u32[]{:S(2)}, u32[]{:S(2)}) collective-permute-start(f32[256,256]{1,0:T(8,128)S(1)} %shard_map.76.unused_light_ref.light_ref), channel_id=1, source_target_pairs={{0,1},{1,0},{2,3},{3,2},{4,5},{5,4},{6,7},{7,6},{8,9},{9,8},{10,11... | collective-permute-start | bytes 786440 | tf_op jit(solution)/shard_map/ppermute | solution.py:462
  29.2 3.5 %collective-permute-done.12.b_ref = f32[128,256]{1,0:T(8,128)S(1)} collective-permute-done((f32[128,256]{1,0:T(8,128)S(1)}, f32[128,256]{1,0:T(8,128)S(1)}, u32[]{:S(2)}, u32[]{:S(2)}) %collective-permute-start.12) | collective-permute-done | bytes 131104 | tf_op jit(solution)/shard_map/ppermute | solution.py:459
  32.8 2.4 %collective-permute-start.13 = (f32[128,256]{1,0:T(8,128)S(1)}, f32[128,256]{1,0:T(8,128)S(1)}, u32[]{:S(2)}, u32[]{:S(2)}) collective-permute-start(f32[128,256]{1,0:T(8,128)S(1)} %shard_map.80.a_ref.unused_ref), channel_id=1, source_target_pairs={{0,8},{1,3},{2,10},{3,1},{4,12},{5,7},{6,14},{7,5},{8,0},{9,11},{1... | collective-permute-start | bytes 393224 | tf_op jit(solution)/shard_map/ppermute | solution.py:459
  35.1 0.0 collective-permute-done.14.refs_0_
  35.1 0.1 shard_map.82
  35.2 2.0 %collective-permute-start.16 = (f32[128,256]{1,0:T(8,128)S(1)}, f32[128,256]{1,0:T(8,128)S(1)}, u32[]{:S(2)}, u32[]{:S(2)}) collective-permute-start(f32[128,256]{1,0:T(8,128)S(1)} %get-tuple-element.48), channel_id=1, source_target_pairs={{0,4},{1,5},{2,6},{3,7},{4,0},{5,1},{6,2},{7,3},{8,12},{9,13},{10,... | collective-permute-start | bytes 393224 | tf_op jit(solution)/shard_map/ppermute | solution.py:459
  37.2 0.0 collective-permute-start.17
  37.2 2.4 %collective-permute-done.13.b_ref = f32[128,256]{1,0:T(8,128)S(1)} collective-permute-done((f32[128,256]{1,0:T(8,128)S(1)}, f32[128,256]{1,0:T(8,128)S(1)}, u32[]{:S(2)}, u32[]{:S(2)}) %collective-permute-start.13) | collective-permute-done | bytes 131104 | tf_op jit(solution)/shard_map/ppermute | solution.py:459
  39.6 2.8 %collective-permute-start.20 = (f32[128,256]{1,0:T(8,128)S(1)}, f32[128,256]{1,0:T(8,128)S(1)}, u32[]{:S(2)}, u32[]{:S(2)}) collective-permute-start(f32[128,256]{1,0:T(8,128)S(1)} %shard_map.81.unused_ref.keep_ref), channel_id=1, source_target_pairs={{0,2},{1,5},{2,0},{3,7},{4,6},{5,1},{6,4},{7,3},{8,10},{9,13},{10,... | collective-permute-start | bytes 393224 | tf_op jit(solution)/shard_map/ppermute | solution.py:459
  42.4 0.0 collective-permute-done.15.other_light_ref
  42.4 0.0 collective-permute-done.16.edge_a
  42.4 0.0 collective-permute-done.17.edge_b
  42.4 0.1 shard_map.83
  42.6 0.1 collective-permute-start.18
  42.7 0.5 %collective-permute-start.19 = (f32[128,256]{1,0:T(8,128)S(1)}, f32[128,256]{1,0:T(8,128)S(1)}, u32[]{:S(2)}, u32[]{:S(2)}) collective-permute-start(f32[128,256]{1,0:T(8,128)S(1)} %get-tuple-element.51.lower_ref), channel_id=1, source_target_pairs={{0,1},{1,0},{2,3},{3,2},{4,5},{5,4},{6,7},{7,6},{8,9},{9,8},{10,11... | collective-permute-start | bytes 393224 | tf_op jit(solution)/shard_map/ppermute | solution.py:462
  43.2 0.1 collective-permute-start.21
  43.2 2.2 %collective-permute-done.20.away_ref = f32[128,256]{1,0:T(8,128)S(1)} collective-permute-done((f32[128,256]{1,0:T(8,128)S(1)}, f32[128,256]{1,0:T(8,128)S(1)}, u32[]{:S(2)}, u32[]{:S(2)}) %collective-permute-start.20) | collective-permute-done | bytes 131104 | tf_op jit(solution)/shard_map/ppermute | solution.py:459
  45.4 0.0 collective-permute-start.22
  45.4 0.0 collective-permute-done.18.other_upper_ref
  45.4 0.0 collective-permute-done.19.other_lower_ref
  45.4 0.8 %shard_map.84 = (f32[2,256,256]{2,1,0:T(8,128)}, f32[8,128]{1,0:T(8,128)S(1)}) custom-call(f32[128,256]{1,0:T(8,128)S(1)} %get-tuple-element.50.upper_ref, f32[128,256]{1,0:T(8,128)S(1)} %get-tuple-element.51.lower_ref, f32[128,256]{1,0:T(8,128)S(1)} %collective-permute-done.18.other_upper_ref, f32[128,256]{1,0:T(8,128)S(1)} %collective-permute-done.19.other_lower_ref), custom_call_target="tpu_custom_call" | custom-call | tf_op jit(solution)/shard_map/pallas_call | solution.py:433
  46.2 0.0 collective-permute-done.21.keep_other_ref
  46.2 0.5 %collective-permute-done.22.away_other_ref = f32[128,256]{1,0:T(8,128)S(1)} collective-permute-done((f32[128,256]{1,0:T(8,128)S(1)}, f32[128,256]{1,0:T(8,128)S(1)}, u32[]{:S(2)}, u32[]{:S(2)}) %collective-permute-start.22) | collective-permute-done | bytes 131104 | tf_op jit(solution)/shard_map/ppermute | solution.py:462
  46.7 0.9 %shard_map.85 = f32[2,256,256]{2,1,0:T(8,128)} custom-call(f32[2,256,256]{2,1,0:T(8,128)S(1)} %get-tuple-element.30.refs_0_.probe_ref, f32[128,256]{1,0:T(8,128)S(1)} %shard_map.81.unused_ref.keep_ref, f32[128,256]{1,0:T(8,128)S(1)} %collective-permute-done.20.away_ref, f32[128,256]{1,0:T(8,128)S(1)} %collective-permute-done.21.keep_other_ref, ...), custom_call_target="tpu_custom_call" | custom-call | tf_op jit(solution)/shard_map/pallas_call | solution.py:433
  (10 shorter events, 0.1 us)
Async XLA Ops:
  0.6 10.6 %copy-start.2 = (bf16[3,256,256]{2,1,0:T(8,128)(2,1)S(1)}, bf16[3,256,256]{2,1,0:T(8,128)(2,1)}, u32[]{:S(2)}) copy-start(bf16[3,256,256]{2,1,0:T(8,128)(2,1)} %constant.2.clone.refs_2_) | copy-start | bytes 1179652
  2.6 9.8 %collective-permute-start = (f32[280,128]{1,0:T(8,128)}, f32[280,128]{1,0:T(8,128)S(1)}, u32[]{:S(2)}, u32[]{:S(2)}) collective-permute-start(f32[280,128]{1,0:T(8,128)} %get-tuple-element.31), channel_id=1, source_target_pairs={{0,2},{1,3},{2,0},{3,1},{4,6},{5,7},{6,4},{7,5},{8,10},{9,11},{10,... | collective-permute-start | bytes 430088 | tf_op jit(solution)/shard_map/ppermute | solution.py:459
  5.6 5.6 %copy-start.4 = (f32[8,128]{1,0:T(8,128)S(1)}, f32[8,128]{1,0:T(8,128)}, u32[]{:S(2)}) copy-start(f32[8,128]{1,0:T(8,128)} %get-tuple-element.28.refs_0_) | copy-start | bytes 12292
  5.6 6.8 %collective-permute-start.1 = (f32[136,128]{1,0:T(8,128)}, f32[136,128]{1,0:T(8,128)S(1)}, u32[]{:S(2)}, u32[]{:S(2)}) collective-permute-start(f32[136,128]{1,0:T(8,128)} %get-tuple-element.32), channel_id=1, source_target_pairs={{0,6},{1,7},{2,4},{3,5},{4,2},{5,3},{6,0},{7,1},{8,14},{9,15},{10,... | collective-permute-start | bytes 208904 | tf_op jit(solution)/shard_map/ppermute | solution.py:459
  7.2 5.3 %collective-permute-start.2 = (f32[136,128]{1,0:T(8,128)}, f32[136,128]{1,0:T(8,128)S(1)}, u32[]{:S(2)}, u32[]{:S(2)}) collective-permute-start(f32[136,128]{1,0:T(8,128)} %get-tuple-element.33), channel_id=1, source_target_pairs={{0,1},{1,0},{2,3},{3,2},{4,10},{5,11},{6,8},{7,9},{8,6},{9,7},{10,... | collective-permute-start | bytes 208904 | tf_op jit(solution)/shard_map/ppermute | solution.py:459
  7.2 7.3 %collective-permute-start.4 = (f32[136,256]{1,0:T(8,128)}, f32[136,256]{1,0:T(8,128)S(1)}, u32[]{:S(2)}, u32[]{:S(2)}) collective-permute-start(f32[136,256]{1,0:T(8,128)} %get-tuple-element.34), channel_id=1, source_target_pairs={{0,4},{1,5},{2,6},{3,7},{4,0},{5,1},{6,2},{7,3},{8,12},{9,13},{10,... | collective-permute-start | bytes 417800 | tf_op jit(solution)/shard_map/ppermute | solution.py:459
  11.2 3.2 %collective-permute-start.5 = (f32[136,256]{1,0:T(8,128)}, f32[136,256]{1,0:T(8,128)S(1)}, u32[]{:S(2)}, u32[]{:S(2)}) collective-permute-start(f32[136,256]{1,0:T(8,128)} %get-tuple-element.35), channel_id=1, source_target_pairs={{0,1},{1,0},{2,3},{3,2},{4,8},{5,9},{6,10},{7,11},{8,4},{9,5},{10,... | collective-permute-start | bytes 417800 | tf_op jit(solution)/shard_map/ppermute | solution.py:459
  11.3 1.0 %copy-start.1 = (f32[2,256,256]{2,1,0:T(8,128)S(1)}, f32[2,256,256]{2,1,0:T(8,128)}, u32[]{:S(2)}) copy-start(f32[2,256,256]{2,1,0:T(8,128)} %refs_1_.1) | copy-start | bytes 1572868
  12.5 2.0 %collective-permute-start.3 = (f32[256,128]{1,0:T(8,128)S(1)}, f32[256,128]{1,0:T(8,128)S(1)}, u32[]{:S(2)}, u32[]{:S(2)}) collective-permute-start(f32[256,128]{1,0:T(8,128)S(1)} %shard_map.70.before_ref.unused_ref), channel_id=1, source_target_pairs={{0,1},{1,0},{2,3},{3,2},{4,5},{5,4},{6,7},{7,6},{8,9},{9,8},{10,11... | collective-permute-start | bytes 393224 | tf_op jit(solution)/shard_map/ppermute | solution.py:462
  14.2 1.0 %copy-start = (f32[2,256,256]{2,1,0:T(8,128)S(1)}, f32[2,256,256]{2,1,0:T(8,128)}, u32[]{:S(2)}) copy-start(f32[2,256,256]{2,1,0:T(8,128)} %spec_ref.7) | copy-start | bytes 1572868
  14.5 1.8 %collective-permute-start.6 = (f32[512,128]{1,0:T(8,128)S(1)}, f32[512,128]{1,0:T(8,128)S(1)}, u32[]{:S(2)}, u32[]{:S(2)}) collective-permute-start(f32[512,128]{1,0:T(8,128)S(1)} %shard_map.72.unused_ref), channel_id=1, source_target_pairs={{0,1},{1,0},{2,3},{3,2},{4,5},{5,4},{6,7},{7,6},{8,9},{9,8},{10,11... | collective-permute-start | bytes 786440 | tf_op jit(solution)/shard_map/ppermute | solution.py:462
  14.6 1.7 %collective-permute-start.7 = (f32[280,128]{1,0:T(8,128)S(1)}, f32[280,128]{1,0:T(8,128)S(1)}, u32[]{:S(2)}, u32[]{:S(2)}) collective-permute-start(f32[280,128]{1,0:T(8,128)S(1)} %collective-permute-done.refs_1_.refs_2_.refs_0_), channel_id=1, source_target_pairs={{0,1},{1,0},{2,3},{3,2},{4,5},{5,4},{6,7},{7,6},{8,9},{9,8},{10,11... | collective-permute-start | bytes 430088 | tf_op jit(solution)/shard_map/ppermute | solution.py:462
  16.1 1.1 %copy-start.3 = (bf16[2,256,256]{2,1,0:T(8,128)(2,1)S(1)}, bf16[2,256,256]{2,1,0:T(8,128)(2,1)}, u32[]{:S(2)}) copy-start(bf16[2,256,256]{2,1,0:T(8,128)(2,1)} %amp_ref.1) | copy-start | bytes 786436
  19.7 1.6 %collective-permute-start.8 = (f32[256,256]{1,0:T(8,128)S(1)}, f32[256,256]{1,0:T(8,128)S(1)}, u32[]{:S(2)}, u32[]{:S(2)}) collective-permute-start(f32[256,256]{1,0:T(8,128)S(1)} %get-tuple-element.39), channel_id=1, source_target_pairs={{0,1},{1,0},{2,3},{3,2},{4,5},{5,4},{6,7},{7,6},{8,9},{9,8},{10,11... | collective-permute-start | bytes 786440 | tf_op jit(solution)/shard_map/ppermute | solution.py:462
  21.4 3.1 %collective-permute-start.11 = (f32[2,256,256]{2,1,0:T(8,128)S(1)}, f32[2,256,256]{2,1,0:T(8,128)S(1)}, u32[]{:S(2)}, u32[]{:S(2)}) collective-permute-start(f32[2,256,256]{2,1,0:T(8,128)S(1)} %get-tuple-element.44), channel_id=1, source_target_pairs={{0,1},{1,0},{2,3},{3,2},{4,5},{5,4},{6,7},{7,6},{8,9},{9,8},{10,11... | collective-permute-start | bytes 1572872 | tf_op jit(solution)/shard_map/ppermute | solution.py:462
  21.6 5.8 %collective-permute-start.9 = (f32[128,256]{1,0:T(8,128)S(1)}, f32[128,256]{1,0:T(8,128)S(1)}, u32[]{:S(2)}, u32[]{:S(2)}) collective-permute-start(f32[128,256]{1,0:T(8,128)S(1)} %get-tuple-element.43), channel_id=1, source_target_pairs={{0,2},{1,5},{2,0},{3,7},{4,6},{5,1},{6,4},{7,3},{8,10},{9,13},{10,... | collective-permute-start | bytes 393224 | tf_op jit(solution)/shard_map/ppermute | solution.py:459
  22.3 2.2 %collective-permute-start.10 = (f32[8,128]{1,0:T(8,128)S(1)}, f32[8,128]{1,0:T(8,128)S(1)}, u32[]{:S(2)}, u32[]{:S(2)}) collective-permute-start(f32[8,128]{1,0:T(8,128)S(1)} %get-tuple-element.29.note_ref), channel_id=1, source_target_pairs={{0,1},{1,0},{2,3},{3,2},{4,5},{5,4},{6,7},{7,6},{8,9},{9,8},{10,11... | collective-permute-start | bytes 12296 | tf_op jit(solution)/shard_map/ppermute | solution.py:462
  25.7 9.4 %collective-permute-start.14 = (f32[512,128]{1,0:T(8,128)S(1)}, f32[512,128]{1,0:T(8,128)S(1)}, u32[]{:S(2)}, u32[]{:S(2)}) collective-permute-start(f32[512,128]{1,0:T(8,128)S(1)} %get-tuple-element.46), channel_id=1, source_target_pairs={{0,2},{1,3},{2,0},{3,1},{4,6},{5,7},{6,4},{7,5},{8,10},{9,11},{10,... | collective-permute-start | bytes 786440 | tf_op jit(solution)/shard_map/ppermute | solution.py:459
  27.4 5.4 %collective-permute-start.12 = (f32[128,256]{1,0:T(8,128)S(1)}, f32[128,256]{1,0:T(8,128)S(1)}, u32[]{:S(2)}, u32[]{:S(2)}) collective-permute-start(f32[128,256]{1,0:T(8,128)S(1)} %shard_map.79.a_ref), channel_id=1, source_target_pairs={{0,4},{1,9},{2,6},{3,11},{4,0},{5,13},{6,2},{7,15},{8,12},{9,1},{1... | collective-permute-start | bytes 393224 | tf_op jit(solution)/shard_map/ppermute | solution.py:459
  28.7 13.7 %collective-permute-start.15 = (f32[256,256]{1,0:T(8,128)S(1)}, f32[256,256]{1,0:T(8,128)S(1)}, u32[]{:S(2)}, u32[]{:S(2)}) collective-permute-start(f32[256,256]{1,0:T(8,128)S(1)} %shard_map.76.unused_light_ref.light_ref), channel_id=1, source_target_pairs={{0,1},{1,0},{2,3},{3,2},{4,5},{5,4},{6,7},{7,6},{8,9},{9,8},{10,11... | collective-permute-start | bytes 786440 | tf_op jit(solution)/shard_map/ppermute | solution.py:462
  32.8 6.8 %collective-permute-start.13 = (f32[128,256]{1,0:T(8,128)S(1)}, f32[128,256]{1,0:T(8,128)S(1)}, u32[]{:S(2)}, u32[]{:S(2)}) collective-permute-start(f32[128,256]{1,0:T(8,128)S(1)} %shard_map.80.a_ref.unused_ref), channel_id=1, source_target_pairs={{0,8},{1,3},{2,10},{3,1},{4,12},{5,7},{6,14},{7,5},{8,0},{9,11},{1... | collective-permute-start | bytes 393224 | tf_op jit(solution)/shard_map/ppermute | solution.py:459
  35.2 7.2 %collective-permute-start.16 = (f32[128,256]{1,0:T(8,128)S(1)}, f32[128,256]{1,0:T(8,128)S(1)}, u32[]{:S(2)}, u32[]{:S(2)}) collective-permute-start(f32[128,256]{1,0:T(8,128)S(1)} %get-tuple-element.48), channel_id=1, source_target_pairs={{0,4},{1,5},{2,6},{3,7},{4,0},{5,1},{6,2},{7,3},{8,12},{9,13},{10,... | collective-permute-start | bytes 393224 | tf_op jit(solution)/shard_map/ppermute | solution.py:459
  37.2 5.2 %collective-permute-start.17 = (f32[128,256]{1,0:T(8,128)S(1)}, f32[128,256]{1,0:T(8,128)S(1)}, u32[]{:S(2)}, u32[]{:S(2)}) collective-permute-start(f32[128,256]{1,0:T(8,128)S(1)} %get-tuple-element.49), channel_id=1, source_target_pairs={{0,1},{1,0},{2,3},{3,2},{4,8},{5,9},{6,10},{7,11},{8,4},{9,5},{10,... | collective-permute-start | bytes 393224 | tf_op jit(solution)/shard_map/ppermute | solution.py:459
  39.6 5.8 %collective-permute-start.20 = (f32[128,256]{1,0:T(8,128)S(1)}, f32[128,256]{1,0:T(8,128)S(1)}, u32[]{:S(2)}, u32[]{:S(2)}) collective-permute-start(f32[128,256]{1,0:T(8,128)S(1)} %shard_map.81.unused_ref.keep_ref), channel_id=1, source_target_pairs={{0,2},{1,5},{2,0},{3,7},{4,6},{5,1},{6,4},{7,3},{8,10},{9,13},{10,... | collective-permute-start | bytes 393224 | tf_op jit(solution)/shard_map/ppermute | solution.py:459
  42.6 2.8 %collective-permute-start.18 = (f32[128,256]{1,0:T(8,128)S(1)}, f32[128,256]{1,0:T(8,128)S(1)}, u32[]{:S(2)}, u32[]{:S(2)}) collective-permute-start(f32[128,256]{1,0:T(8,128)S(1)} %get-tuple-element.50.upper_ref), channel_id=1, source_target_pairs={{0,1},{1,0},{2,3},{3,2},{4,5},{5,4},{6,7},{7,6},{8,9},{9,8},{10,11... | collective-permute-start | bytes 393224 | tf_op jit(solution)/shard_map/ppermute | solution.py:462
  42.7 2.7 %collective-permute-start.19 = (f32[128,256]{1,0:T(8,128)S(1)}, f32[128,256]{1,0:T(8,128)S(1)}, u32[]{:S(2)}, u32[]{:S(2)}) collective-permute-start(f32[128,256]{1,0:T(8,128)S(1)} %get-tuple-element.51.lower_ref), channel_id=1, source_target_pairs={{0,1},{1,0},{2,3},{3,2},{4,5},{5,4},{6,7},{7,6},{8,9},{9,8},{10,11... | collective-permute-start | bytes 393224 | tf_op jit(solution)/shard_map/ppermute | solution.py:462
  43.2 3.1 %collective-permute-start.21 = (f32[128,256]{1,0:T(8,128)S(1)}, f32[128,256]{1,0:T(8,128)S(1)}, u32[]{:S(2)}, u32[]{:S(2)}) collective-permute-start(f32[128,256]{1,0:T(8,128)S(1)} %shard_map.81.unused_ref.keep_ref), channel_id=1, source_target_pairs={{0,1},{1,0},{2,3},{3,2},{4,5},{5,4},{6,7},{7,6},{8,9},{9,8},{10,11... | collective-permute-start | bytes 393224 | tf_op jit(solution)/shard_map/ppermute | solution.py:462
  45.4 1.3 %collective-permute-start.22 = (f32[128,256]{1,0:T(8,128)S(1)}, f32[128,256]{1,0:T(8,128)S(1)}, u32[]{:S(2)}, u32[]{:S(2)}) collective-permute-start(f32[128,256]{1,0:T(8,128)S(1)} %collective-permute-done.20.away_ref), channel_id=1, source_target_pairs={{0,1},{1,0},{2,3},{3,2},{4,5},{5,4},{6,7},{7,6},{8,9},{9,8},{10,11... | collective-permute-start | bytes 393224 | tf_op jit(solution)/shard_map/ppermute | solution.py:462

commit v11 on v10

--- a/solution.py
+++ b/solution.py
@@ -227,9 +227,8 @@
         padded[:, far_cols] = jnp.zeros((padded.shape[0], margin), jnp.float32)
     places = block_places(z, x, nz, nx, margin, margin + tile, margin)
     shapes = block_shapes(nz, nx, tile)
-    corners, along_z, along_x = packing_order(nz, nx)
-    pieces = {k: [(block, 0)] for k, block in zip(along_x, blocks[2:])}
-    for which, array in zip((corners, along_z), blocks):
+    pieces = {}
+    for which, array in zip(packing_order(nz, nx), blocks):
         for k, places_of in zip(which, packed_places([shapes[k] for k in which])):
             pieces[k] = [(array, at) for at, _, _ in places_of]
     for k, ((height, width), (rows, cols), ok) in enumerate(zip(shapes, places, block_valid(z, x, nz, nx))):
@@ -528,9 +527,10 @@
     packed_corners = packed(corners, probe_v, *[recv[k] for k in along_x])
     other_corners = to_core(packed_corners)
     light = light_from(corners + along_x, True, packed_corners, packed_corners)
-    packed_z = packed(along_z, light, other_corners)
+    other_x = to_core(packed(along_x, packed_corners))
+    packed_z = packed(along_z, light, other_corners, other_x)
     patches = patches_from(True, packed_z, *recv)
-    patches_other = patches_from(False, patches, other_corners, to_core(packed_z), *[to_core(recv[k]) for k in along_x])
+    patches_other = patches_from(False, patches, other_corners, to_core(packed_z), other_x)
     own, other, probe_own, probe_other = call(
         positions_kernel,
         [f32(npos, size, size)] * 2 + [f32(size, size)] * 2,

time: 47.7 us -> 47.9 us (level); the launches traced: 47.6 us -> 47 us
  waiting for transfers between devices: 10.6 us -> 9.52 us
  local copies, waits for them, and re-layouts: 1.18 us -> 1.77 us
  starting transfers between devices: 23.6 us -> 23.1 us
    ppermute x12, waiting for transfers between devices: 8.38 us -> 7.67 us  [send(): return lax.ppermute(value, GROUP, permutation(sizes, target))]
    unnamed x10, local copies, waits for them, and re-layouts: 1.18 us -> 1.77 us
    pallas_call x18 -> x19, Pallas kernels: 11.4 us -> 11.7 us  [call(): pl.pallas_call(kernel, out_shape=out_shape, in_specs=specs, out_specs=out...]
  transfers between devices with their start and end apart: 23 -> 23, of which waited for: 8 -> 7; matrix products, arithmetic and copies ran while one was open for 0% -> 0% of each run, Pallas kernels for 11% -> 12%
where the time goes in v11:
time: 47.9 us; the launch traced here: 47 us
  starting transfers between devices  23.1 us (48%)
  Pallas kernels  11.7 us (24%)
  waiting for transfers between devices  9.52 us (20%)
  local copies, waits for them, and re-layouts  1.77 us (4%)
  between operations  0.87 us (2%)
    ppermute x12, starting transfers between devices, send(): return lax.ppermute(value, GROUP, permutation(sizes, target))  19.2 us
    pallas_call x19, Pallas kernels, call(): pl.pallas_call(kernel, out_shape=out_shape, in_specs=specs, out_specs=out...  11.7 us
    ppermute x12, waiting for transfers between devices, send(): return lax.ppermute(value, GROUP, permutation(sizes, target))  7.67 us
    ppermute x11, starting transfers between devices, to_core(): return lax.ppermute(value, 'pos', PART_SWAP)  3.97 us
    ppermute x11, waiting for transfers between devices, to_core(): return lax.ppermute(value, 'pos', PART_SWAP)  1.85 us
    unnamed x10, local copies, waits for them, and re-layouts  1.77 us
  transfers between devices with their start and end apart: 23, of which 7 were waited for; matrix products, arithmetic and copies ran while one was open for 0% of the time, Pallas kernels for 12%

profile of v11, /device:TPU:0, one launch (start us, length us, event | category | flops | bytes accessed | tf_op | source)
XLA Modules:
  0.0 47.0 jit_solution(8045495585634826395)
XLA Ops:
  0.6 0.0 copy-start.2
  0.6 2.0 %shard_map.68 = (f32[280,128]{1,0:T(8,128)}, f32[136,256]{1,0:T(8,128)}, f32[136,256]{1,0:T(8,128)}, f32[136,128]{1,0:T(8,128)}, f32[136,128]{1,0:T(8,128)}, /*index=5*/f32[8,128]{1,0:T(8,128)}) custom-call(s32[2,2]{1,0:T(2,128)} %off_hbm.1, f32[2,256,256]{2,1,0:T(8,128)} %spec_ref.7), custom_call_target="tpu_custom_call" | custom-call | tf_op jit(solution)/shard_map/pallas_call | solution.py:432
  2.6 3.0 %collective-permute-start = (f32[280,128]{1,0:T(8,128)}, f32[280,128]{1,0:T(8,128)S(1)}, u32[]{:S(2)}, u32[]{:S(2)}) collective-permute-start(f32[280,128]{1,0:T(8,128)} %get-tuple-element.31), channel_id=1, source_target_pairs={{0,2},{1,3},{2,0},{3,1},{4,6},{5,7},{6,4},{7,5},{8,10},{9,11},{10,... | collective-permute-start | bytes 430088 | tf_op jit(solution)/shard_map/ppermute | solution.py:458
  5.6 1.5 %collective-permute-start.1 = (f32[136,128]{1,0:T(8,128)}, f32[136,128]{1,0:T(8,128)S(1)}, u32[]{:S(2)}, u32[]{:S(2)}) collective-permute-start(f32[136,128]{1,0:T(8,128)} %get-tuple-element.32), channel_id=1, source_target_pairs={{0,6},{1,7},{2,4},{3,5},{4,2},{5,3},{6,0},{7,1},{8,14},{9,15},{10,... | collective-permute-start | bytes 208904 | tf_op jit(solution)/shard_map/ppermute | solution.py:458
  7.2 0.0 collective-permute-start.2
  7.2 4.1 %collective-permute-start.5 = (f32[136,256]{1,0:T(8,128)}, f32[136,256]{1,0:T(8,128)S(1)}, u32[]{:S(2)}, u32[]{:S(2)}) collective-permute-start(f32[136,256]{1,0:T(8,128)} %get-tuple-element.34), channel_id=1, source_target_pairs={{0,4},{1,5},{2,6},{3,7},{4,0},{5,1},{6,2},{7,3},{8,12},{9,13},{10,... | collective-permute-start | bytes 417800 | tf_op jit(solution)/shard_map/ppermute | solution.py:458
  11.2 0.0 collective-permute-start.6
  11.3 0.0 copy-start.1
  11.3 1.0 %copy-done.1 = f32[2,256,256]{2,1,0:T(8,128)S(1)} copy-done((f32[2,256,256]{2,1,0:T(8,128)S(1)}, f32[2,256,256]{2,1,0:T(8,128)}, u32[]{:S(2)}) %copy-start.1) | copy-done | bytes 524312
  12.3 0.1 shard_map.69
  12.4 0.0 collective-permute-done.1.refs_2_.refs_0_.refs_3_
  12.4 0.0 collective-permute-done.2.refs_3_.refs_1_.refs_4_
  12.5 0.0 collective-permute-done.refs_1_.refs_2_.refs_0_
  12.5 0.6 %collective-permute-start.4 = (f32[256,128]{1,0:T(8,128)S(1)}, f32[256,128]{1,0:T(8,128)S(1)}, u32[]{:S(2)}, u32[]{:S(2)}) collective-permute-start(f32[256,128]{1,0:T(8,128)S(1)} %shard_map.72), channel_id=1, source_target_pairs={{0,1},{1,0},{2,3},{3,2},{4,5},{5,4},{6,7},{7,6},{8,9},{9,8},{10,11... | collective-permute-start | bytes 393224 | tf_op jit(solution)/shard_map/ppermute | solution.py:461
  13.1 0.1 collective-permute-start.3
  13.2 1.4 %shard_map.71.refs_0_.before_ref = f32[256,256]{1,0:T(8,128)S(1)} custom-call(f32[8,128]{1,0:T(8,128)S(1)} %get-tuple-element.29.note_ref, f32[2,256,256]{2,1,0:T(8,128)S(1)} %get-tuple-element.30.refs_0_.probe_ref, f32[256,128]{1,0:T(8,128)S(1)} %shard_map.70.before_ref.unused_ref.refs_0_, f32[256,128]{1,0:T(8,128)S(1)} %shard_map.70.before_ref.unused_ref.refs_0_, ...), custom_call_target="tpu_custom_call" | custom-call | tf_op jit(solution)/shard_map/pallas_call | solution.py:432
  14.6 0.0 copy-start
  14.6 0.0 collective-permute-done.5.refs_3_.refs_1_.refs_0_
  14.6 0.0 collective-permute-done.6.refs_4_.refs_2_.refs_1_
  14.6 0.0 collective-permute-done.4.refs_2_
  14.6 0.0 collective-permute-done.3.refs_1_.refs_0_
  14.7 0.3 collective-permute-start.7
  15.0 0.6 %copy-done = f32[2,256,256]{2,1,0:T(8,128)S(1)} copy-done((f32[2,256,256]{2,1,0:T(8,128)S(1)}, f32[2,256,256]{2,1,0:T(8,128)}, u32[]{:S(2)}) %copy-start) | copy-done | bytes 524312
  15.6 0.8 %shard_map.74.unused_ref.patch_ref = f32[2,256,256]{2,1,0:T(8,128)S(1)} custom-call(f32[8,128]{1,0:T(8,128)S(1)} %get-tuple-element.29.note_ref, f32[512,128]{1,0:T(8,128)S(1)} %shard_map.73.unused_ref, f32[2,256,256]{2,1,0:T(8,128)S(1)} %copy-done, f32[280,128]{1,0:T(8,128)S(1)} %collective-permute-done.refs_1_.refs_2_.refs_0_, ...), custom_call_target="tpu_custom_call" | custom-call | tf_op jit(solution)/shard_map/pallas_call | solution.py:432
  16.5 0.0 copy-start.3
  16.5 0.0 collective-permute-done.7.refs_1_
  16.5 0.8 %shard_map.75.patch_other_ref = f32[2,256,256]{2,1,0:T(8,128)S(1)} custom-call(f32[8,128]{1,0:T(8,128)S(1)} %get-tuple-element.29.note_ref, f32[2,256,256]{2,1,0:T(8,128)S(1)} %shard_map.74.unused_ref.patch_ref, f32[2,256,256]{2,1,0:T(8,128)S(1)} %copy-done, f32[256,128]{1,0:T(8,128)S(1)} %collective-permute-done.3.refs_1_.refs_0_, ...), custom_call_target="tpu_custom_call" | custom-call | tf_op jit(solution)/shard_map/pallas_call | solution.py:432
  17.3 0.1 copy-done.3
  17.4 2.5 %shard_map.76 = (f32[2,256,256]{2,1,0:T(8,128)S(1)}, f32[2,256,256]{2,1,0:T(8,128)S(1)}, f32[256,256]{1,0:T(8,128)S(1)}, f32[256,256]{1,0:T(8,128)S(1)}) custom-call(f32[2,256,256]{2,1,0:T(8,128)S(1)} %shard_map.74.unused_ref.patch_ref, f32[2,256,256]{2,1,0:T(8,128)S(1)} %shard_map.75.patch_other_ref, ...), custom_call_target="tpu_custom_call" | custom-call | tf_op jit(solution)/shard_map/pallas_call | solution.py:432
  20.0 0.3 collective-permute-start.8
  20.3 0.7 %shard_map.77.unused_light_ref.light_ref = f32[256,256]{1,0:T(8,128)S(1)} custom-call(f32[8,128]{1,0:T(8,128)S(1)} %get-tuple-element.29.note_ref, f32[2,256,256]{2,1,0:T(8,128)S(1)} %get-tuple-element.30.refs_0_.probe_ref, f32[256,256]{1,0:T(8,128)S(1)} %shard_map.71.refs_0_.before_ref, f32[2,256,256]{2,1,0:T(8,128)S(1)} %get-tuple-element.41.unused_ref.own_ref, ...), custom_call_target="tpu_custom_call" | custom-call | tf_op jit(solution)/shard_map/pallas_call | solution.py:432
  21.1 0.5 %collective-permute-done.8.recv_ref = f32[256,256]{1,0:T(8,128)S(1)} collective-permute-done((f32[256,256]{1,0:T(8,128)S(1)}, f32[256,256]{1,0:T(8,128)S(1)}, u32[]{:S(2)}, u32[]{:S(2)}) %collective-permute-start.8) | collective-permute-done | bytes 262176 | tf_op jit(solution)/shard_map/ppermute | solution.py:461
  21.6 0.3 collective-permute-start.11
  21.9 0.8 %collective-permute-start.9 = (f32[128,256]{1,0:T(8,128)S(1)}, f32[128,256]{1,0:T(8,128)S(1)}, u32[]{:S(2)}, u32[]{:S(2)}) collective-permute-start(f32[128,256]{1,0:T(8,128)S(1)} %get-tuple-element.43), channel_id=1, source_target_pairs={{0,2},{1,5},{2,0},{3,7},{4,6},{5,1},{6,4},{7,3},{8,10},{9,13},{10,... | collective-permute-start | bytes 393224 | tf_op jit(solution)/shard_map/ppermute | solution.py:458
  22.8 0.8 %collective-permute-start.10 = (f32[8,128]{1,0:T(8,128)S(1)}, f32[8,128]{1,0:T(8,128)S(1)}, u32[]{:S(2)}, u32[]{:S(2)}) collective-permute-start(f32[8,128]{1,0:T(8,128)S(1)} %get-tuple-element.29.note_ref), channel_id=1, source_target_pairs={{0,1},{1,0},{2,3},{3,2},{4,5},{5,4},{6,7},{7,6},{8,9},{9,8},{10,11... | collective-permute-start | bytes 12296 | tf_op jit(solution)/shard_map/ppermute | solution.py:461
  23.6 0.8 %collective-permute-done.10.other_note_ref = f32[8,128]{1,0:T(8,128)S(1)} collective-permute-done((f32[8,128]{1,0:T(8,128)S(1)}, f32[8,128]{1,0:T(8,128)S(1)}, u32[]{:S(2)}, u32[]{:S(2)}) %collective-permute-start.10) | collective-permute-done | bytes 4128 | tf_op jit(solution)/shard_map/ppermute | solution.py:461
  24.4 0.0 collective-permute-done.11.recv_ref
  24.4 1.2 %shard_map.79 = (f32[512,256]{1,0:T(8,128)S(1)}, f32[512,128]{1,0:T(8,128)S(1)}) custom-call(f32[8,128]{1,0:T(8,128)S(1)} %get-tuple-element.29.note_ref, f32[8,128]{1,0:T(8,128)S(1)} %collective-permute-done.10.other_note_ref, f32[2,256,256]{2,1,0:T(8,128)S(1)} %get-tuple-element.41.unused_ref.own_ref, f32[2,256,256]{2,1,0:T(8,128)S(1)} %collective-permute-done.11.recv_ref, ...), custom_call_target="tpu_custom_call" | custom-call | tf_op jit(solution)/shard_map/pallas_call | solution.py:432
  25.7 1.6 %collective-permute-start.14 = (f32[512,128]{1,0:T(8,128)S(1)}, f32[512,128]{1,0:T(8,128)S(1)}, u32[]{:S(2)}, u32[]{:S(2)}) collective-permute-start(f32[512,128]{1,0:T(8,128)S(1)} %get-tuple-element.46), channel_id=1, source_target_pairs={{0,2},{1,3},{2,0},{3,1},{4,6},{5,7},{6,4},{7,5},{8,10},{9,11},{10,... | collective-permute-start | bytes 786440 | tf_op jit(solution)/shard_map/ppermute | solution.py:458
  27.2 0.0 collective-permute-done.9.b_ref
  27.2 1.4 %collective-permute-start.12 = (f32[128,256]{1,0:T(8,128)S(1)}, f32[128,256]{1,0:T(8,128)S(1)}, u32[]{:S(2)}, u32[]{:S(2)}) collective-permute-start(f32[128,256]{1,0:T(8,128)S(1)} %shard_map.80.a_ref), channel_id=1, source_target_pairs={{0,4},{1,9},{2,6},{3,11},{4,0},{5,13},{6,2},{7,15},{8,12},{9,1},{1... | collective-permute-start | bytes 393224 | tf_op jit(solution)/shard_map/ppermute | solution.py:458
  28.6 0.8 %collective-permute-start.15 = (f32[256,256]{1,0:T(8,128)S(1)}, f32[256,256]{1,0:T(8,128)S(1)}, u32[]{:S(2)}, u32[]{:S(2)}) collective-permute-start(f32[256,256]{1,0:T(8,128)S(1)} %shard_map.77.unused_light_ref.light_ref), channel_id=1, source_target_pairs={{0,1},{1,0},{2,3},{3,2},{4,5},{5,4},{6,7},{7,6},{8,9},{9,8},{10,11... | collective-permute-start | bytes 786440 | tf_op jit(solution)/shard_map/ppermute | solution.py:461
  29.5 3.2 %collective-permute-done.12.b_ref = f32[128,256]{1,0:T(8,128)S(1)} collective-permute-done((f32[128,256]{1,0:T(8,128)S(1)}, f32[128,256]{1,0:T(8,128)S(1)}, u32[]{:S(2)}, u32[]{:S(2)}) %collective-permute-start.12) | collective-permute-done | bytes 131104 | tf_op jit(solution)/shard_map/ppermute | solution.py:458
  32.7 2.7 %collective-permute-start.13 = (f32[128,256]{1,0:T(8,128)S(1)}, f32[128,256]{1,0:T(8,128)S(1)}, u32[]{:S(2)}, u32[]{:S(2)}) collective-permute-start(f32[128,256]{1,0:T(8,128)S(1)} %shard_map.81.a_ref.unused_ref), channel_id=1, source_target_pairs={{0,8},{1,3},{2,10},{3,1},{4,12},{5,7},{6,14},{7,5},{8,0},{9,11},{1... | collective-permute-start | bytes 393224 | tf_op jit(solution)/shard_map/ppermute | solution.py:458
  35.4 0.0 collective-permute-done.14.refs_0_
  35.4 0.1 shard_map.83
  35.5 1.6 %collective-permute-start.16 = (f32[128,256]{1,0:T(8,128)S(1)}, f32[128,256]{1,0:T(8,128)S(1)}, u32[]{:S(2)}, u32[]{:S(2)}) collective-permute-start(f32[128,256]{1,0:T(8,128)S(1)} %get-tuple-element.48), channel_id=1, source_target_pairs={{0,4},{1,5},{2,6},{3,7},{4,0},{5,1},{6,2},{7,3},{8,12},{9,13},{10,... | collective-permute-start | bytes 393224 | tf_op jit(solution)/shard_map/ppermute | solution.py:458
  37.1 0.0 collective-permute-start.17
  37.1 2.3 %collective-permute-done.13.b_ref = f32[128,256]{1,0:T(8,128)S(1)} collective-permute-done((f32[128,256]{1,0:T(8,128)S(1)}, f32[128,256]{1,0:T(8,128)S(1)}, u32[]{:S(2)}, u32[]{:S(2)}) %collective-permute-start.13) | collective-permute-done | bytes 131104 | tf_op jit(solution)/shard_map/ppermute | solution.py:458
  39.4 2.4 %collective-permute-start.20 = (f32[128,256]{1,0:T(8,128)S(1)}, f32[128,256]{1,0:T(8,128)S(1)}, u32[]{:S(2)}, u32[]{:S(2)}) collective-permute-start(f32[128,256]{1,0:T(8,128)S(1)} %shard_map.82.unused_ref.keep_ref), channel_id=1, source_target_pairs={{0,2},{1,5},{2,0},{3,7},{4,6},{5,1},{6,4},{7,3},{8,10},{9,13},{10,... | collective-permute-start | bytes 393224 | tf_op jit(solution)/shard_map/ppermute | solution.py:458
  41.8 0.0 collective-permute-done.15.other_light_ref
  41.8 0.1 collective-permute-done.16.edge_a
  41.9 0.0 collective-permute-done.17.edge_b
  41.9 0.1 shard_map.84
  42.0 0.1 collective-permute-start.18
  42.1 0.5 %collective-permute-start.19 = (f32[128,256]{1,0:T(8,128)S(1)}, f32[128,256]{1,0:T(8,128)S(1)}, u32[]{:S(2)}, u32[]{:S(2)}) collective-permute-start(f32[128,256]{1,0:T(8,128)S(1)} %get-tuple-element.51.lower_ref), channel_id=1, source_target_pairs={{0,1},{1,0},{2,3},{3,2},{4,5},{5,4},{6,7},{7,6},{8,9},{9,8},{10,11... | collective-permute-start | bytes 393224 | tf_op jit(solution)/shard_map/ppermute | solution.py:461
  42.6 0.1 collective-permute-start.21
  42.7 2.1 %collective-permute-done.20.away_ref = f32[128,256]{1,0:T(8,128)S(1)} collective-permute-done((f32[128,256]{1,0:T(8,128)S(1)}, f32[128,256]{1,0:T(8,128)S(1)}, u32[]{:S(2)}, u32[]{:S(2)}) %collective-permute-start.20) | collective-permute-done | bytes 131104 | tf_op jit(solution)/shard_map/ppermute | solution.py:458
  44.8 0.0 collective-permute-start.22
  44.8 0.0 collective-permute-done.18.other_upper_ref
  44.8 0.0 collective-permute-done.19.other_lower_ref
  44.8 0.8 %shard_map.85 = (f32[2,256,256]{2,1,0:T(8,128)}, f32[8,128]{1,0:T(8,128)S(1)}) custom-call(f32[128,256]{1,0:T(8,128)S(1)} %get-tuple-element.50.upper_ref, f32[128,256]{1,0:T(8,128)S(1)} %get-tuple-element.51.lower_ref, f32[128,256]{1,0:T(8,128)S(1)} %collective-permute-done.18.other_upper_ref, f32[128,256]{1,0:T(8,128)S(1)} %collective-permute-done.19.other_lower_ref), custom_call_target="tpu_custom_call" | custom-call | tf_op jit(solution)/shard_map/pallas_call | solution.py:432
  45.6 0.5 %collective-permute-done.22.away_other_ref = f32[128,256]{1,0:T(8,128)S(1)} collective-permute-done((f32[128,256]{1,0:T(8,128)S(1)}, f32[128,256]{1,0:T(8,128)S(1)}, u32[]{:S(2)}, u32[]{:S(2)}) %collective-permute-start.22) | collective-permute-done | bytes 131104 | tf_op jit(solution)/shard_map/ppermute | solution.py:461
  46.1 0.9 %shard_map.86 = f32[2,256,256]{2,1,0:T(8,128)} custom-call(f32[2,256,256]{2,1,0:T(8,128)S(1)} %get-tuple-element.30.refs_0_.probe_ref, f32[128,256]{1,0:T(8,128)S(1)} %shard_map.82.unused_ref.keep_ref, f32[128,256]{1,0:T(8,128)S(1)} %collective-permute-done.20.away_ref, f32[128,256]{1,0:T(8,128)S(1)} %collective-permute-done.21.keep_other_ref, ...), custom_call_target="tpu_custom_call" | custom-call | tf_op jit(solution)/shard_map/pallas_call | solution.py:432
  (11 shorter events, 0.1 us)
Async XLA Ops:
  0.6 10.6 %copy-start.2 = (bf16[3,256,256]{2,1,0:T(8,128)(2,1)S(1)}, bf16[3,256,256]{2,1,0:T(8,128)(2,1)}, u32[]{:S(2)}) copy-start(bf16[3,256,256]{2,1,0:T(8,128)(2,1)} %constant.2.clone.refs_2_) | copy-start | bytes 1179652
  2.6 9.8 %collective-permute-start = (f32[280,128]{1,0:T(8,128)}, f32[280,128]{1,0:T(8,128)S(1)}, u32[]{:S(2)}, u32[]{:S(2)}) collective-permute-start(f32[280,128]{1,0:T(8,128)} %get-tuple-element.31), channel_id=1, source_target_pairs={{0,2},{1,3},{2,0},{3,1},{4,6},{5,7},{6,4},{7,5},{8,10},{9,11},{10,... | collective-permute-start | bytes 430088 | tf_op jit(solution)/shard_map/ppermute | solution.py:458
  5.6 5.6 %copy-start.4 = (f32[8,128]{1,0:T(8,128)S(1)}, f32[8,128]{1,0:T(8,128)}, u32[]{:S(2)}) copy-start(f32[8,128]{1,0:T(8,128)} %get-tuple-element.28.refs_0_) | copy-start | bytes 12292
  5.6 6.8 %collective-permute-start.1 = (f32[136,128]{1,0:T(8,128)}, f32[136,128]{1,0:T(8,128)S(1)}, u32[]{:S(2)}, u32[]{:S(2)}) collective-permute-start(f32[136,128]{1,0:T(8,128)} %get-tuple-element.32), channel_id=1, source_target_pairs={{0,6},{1,7},{2,4},{3,5},{4,2},{5,3},{6,0},{7,1},{8,14},{9,15},{10,... | collective-permute-start | bytes 208904 | tf_op jit(solution)/shard_map/ppermute | solution.py:458
  7.2 5.3 %collective-permute-start.2 = (f32[136,128]{1,0:T(8,128)}, f32[136,128]{1,0:T(8,128)S(1)}, u32[]{:S(2)}, u32[]{:S(2)}) collective-permute-start(f32[136,128]{1,0:T(8,128)} %get-tuple-element.33), channel_id=1, source_target_pairs={{0,1},{1,0},{2,3},{3,2},{4,10},{5,11},{6,8},{7,9},{8,6},{9,7},{10,... | collective-permute-start | bytes 208904 | tf_op jit(solution)/shard_map/ppermute | solution.py:458
  7.2 7.4 %collective-permute-start.5 = (f32[136,256]{1,0:T(8,128)}, f32[136,256]{1,0:T(8,128)S(1)}, u32[]{:S(2)}, u32[]{:S(2)}) collective-permute-start(f32[136,256]{1,0:T(8,128)} %get-tuple-element.34), channel_id=1, source_target_pairs={{0,4},{1,5},{2,6},{3,7},{4,0},{5,1},{6,2},{7,3},{8,12},{9,13},{10,... | collective-permute-start | bytes 417800 | tf_op jit(solution)/shard_map/ppermute | solution.py:458
  11.2 3.4 %collective-permute-start.6 = (f32[136,256]{1,0:T(8,128)}, f32[136,256]{1,0:T(8,128)S(1)}, u32[]{:S(2)}, u32[]{:S(2)}) collective-permute-start(f32[136,256]{1,0:T(8,128)} %get-tuple-element.35), channel_id=1, source_target_pairs={{0,1},{1,0},{2,3},{3,2},{4,8},{5,9},{6,10},{7,11},{8,4},{9,5},{10,... | collective-permute-start | bytes 417800 | tf_op jit(solution)/shard_map/ppermute | solution.py:458
  11.3 1.0 %copy-start.1 = (f32[2,256,256]{2,1,0:T(8,128)S(1)}, f32[2,256,256]{2,1,0:T(8,128)}, u32[]{:S(2)}) copy-start(f32[2,256,256]{2,1,0:T(8,128)} %refs_1_.1) | copy-start | bytes 1572868
  12.5 2.1 %collective-permute-start.4 = (f32[256,128]{1,0:T(8,128)S(1)}, f32[256,128]{1,0:T(8,128)S(1)}, u32[]{:S(2)}, u32[]{:S(2)}) collective-permute-start(f32[256,128]{1,0:T(8,128)S(1)} %shard_map.72), channel_id=1, source_target_pairs={{0,1},{1,0},{2,3},{3,2},{4,5},{5,4},{6,7},{7,6},{8,9},{9,8},{10,11... | collective-permute-start | bytes 393224 | tf_op jit(solution)/shard_map/ppermute | solution.py:461
  13.1 1.6 %collective-permute-start.3 = (f32[256,128]{1,0:T(8,128)S(1)}, f32[256,128]{1,0:T(8,128)S(1)}, u32[]{:S(2)}, u32[]{:S(2)}) collective-permute-start(f32[256,128]{1,0:T(8,128)S(1)} %shard_map.70.before_ref.unused_ref.refs_0_), channel_id=1, source_target_pairs={{0,1},{1,0},{2,3},{3,2},{4,5},{5,4},{6,7},{7,6},{8,9},{9,8},{10,11... | collective-permute-start | bytes 393224 | tf_op jit(solution)/shard_map/ppermute | solution.py:461
  14.6 1.0 %copy-start = (f32[2,256,256]{2,1,0:T(8,128)S(1)}, f32[2,256,256]{2,1,0:T(8,128)}, u32[]{:S(2)}) copy-start(f32[2,256,256]{2,1,0:T(8,128)} %spec_ref.7) | copy-start | bytes 1572868
  14.7 1.8 %collective-permute-start.7 = (f32[512,128]{1,0:T(8,128)S(1)}, f32[512,128]{1,0:T(8,128)S(1)}, u32[]{:S(2)}, u32[]{:S(2)}) collective-permute-start(f32[512,128]{1,0:T(8,128)S(1)} %shard_map.73.unused_ref), channel_id=1, source_target_pairs={{0,1},{1,0},{2,3},{3,2},{4,5},{5,4},{6,7},{7,6},{8,9},{9,8},{10,11... | collective-permute-start | bytes 786440 | tf_op jit(solution)/shard_map/ppermute | solution.py:461
  16.5 1.0 %copy-start.3 = (bf16[2,256,256]{2,1,0:T(8,128)(2,1)S(1)}, bf16[2,256,256]{2,1,0:T(8,128)(2,1)}, u32[]{:S(2)}) copy-start(bf16[2,256,256]{2,1,0:T(8,128)(2,1)} %amp_ref.1) | copy-start | bytes 786436
  20.0 1.6 %collective-permute-start.8 = (f32[256,256]{1,0:T(8,128)S(1)}, f32[256,256]{1,0:T(8,128)S(1)}, u32[]{:S(2)}, u32[]{:S(2)}) collective-permute-start(f32[256,256]{1,0:T(8,128)S(1)} %get-tuple-element.39), channel_id=1, source_target_pairs={{0,1},{1,0},{2,3},{3,2},{4,5},{5,4},{6,7},{7,6},{8,9},{9,8},{10,11... | collective-permute-start | bytes 786440 | tf_op jit(solution)/shard_map/ppermute | solution.py:461
  21.6 2.8 %collective-permute-start.11 = (f32[2,256,256]{2,1,0:T(8,128)S(1)}, f32[2,256,256]{2,1,0:T(8,128)S(1)}, u32[]{:S(2)}, u32[]{:S(2)}) collective-permute-start(f32[2,256,256]{2,1,0:T(8,128)S(1)} %get-tuple-element.44), channel_id=1, source_target_pairs={{0,1},{1,0},{2,3},{3,2},{4,5},{5,4},{6,7},{7,6},{8,9},{9,8},{10,11... | collective-permute-start | bytes 1572872 | tf_op jit(solution)/shard_map/ppermute | solution.py:461
  21.9 5.3 %collective-permute-start.9 = (f32[128,256]{1,0:T(8,128)S(1)}, f32[128,256]{1,0:T(8,128)S(1)}, u32[]{:S(2)}, u32[]{:S(2)}) collective-permute-start(f32[128,256]{1,0:T(8,128)S(1)} %get-tuple-element.43), channel_id=1, source_target_pairs={{0,2},{1,5},{2,0},{3,7},{4,6},{5,1},{6,4},{7,3},{8,10},{9,13},{10,... | collective-permute-start | bytes 393224 | tf_op jit(solution)/shard_map/ppermute | solution.py:458
  22.8 1.6 %collective-permute-start.10 = (f32[8,128]{1,0:T(8,128)S(1)}, f32[8,128]{1,0:T(8,128)S(1)}, u32[]{:S(2)}, u32[]{:S(2)}) collective-permute-start(f32[8,128]{1,0:T(8,128)S(1)} %get-tuple-element.29.note_ref), channel_id=1, source_target_pairs={{0,1},{1,0},{2,3},{3,2},{4,5},{5,4},{6,7},{7,6},{8,9},{9,8},{10,11... | collective-permute-start | bytes 12296 | tf_op jit(solution)/shard_map/ppermute | solution.py:461
  25.7 9.7 %collective-permute-start.14 = (f32[512,128]{1,0:T(8,128)S(1)}, f32[512,128]{1,0:T(8,128)S(1)}, u32[]{:S(2)}, u32[]{:S(2)}) collective-permute-start(f32[512,128]{1,0:T(8,128)S(1)} %get-tuple-element.46), channel_id=1, source_target_pairs={{0,2},{1,3},{2,0},{3,1},{4,6},{5,7},{6,4},{7,5},{8,10},{9,11},{10,... | collective-permute-start | bytes 786440 | tf_op jit(solution)/shard_map/ppermute | solution.py:458
  27.2 5.5 %collective-permute-start.12 = (f32[128,256]{1,0:T(8,128)S(1)}, f32[128,256]{1,0:T(8,128)S(1)}, u32[]{:S(2)}, u32[]{:S(2)}) collective-permute-start(f32[128,256]{1,0:T(8,128)S(1)} %shard_map.80.a_ref), channel_id=1, source_target_pairs={{0,4},{1,9},{2,6},{3,11},{4,0},{5,13},{6,2},{7,15},{8,12},{9,1},{1... | collective-permute-start | bytes 393224 | tf_op jit(solution)/shard_map/ppermute | solution.py:458
  28.6 13.2 %collective-permute-start.15 = (f32[256,256]{1,0:T(8,128)S(1)}, f32[256,256]{1,0:T(8,128)S(1)}, u32[]{:S(2)}, u32[]{:S(2)}) collective-permute-start(f32[256,256]{1,0:T(8,128)S(1)} %shard_map.77.unused_light_ref.light_ref), channel_id=1, source_target_pairs={{0,1},{1,0},{2,3},{3,2},{4,5},{5,4},{6,7},{7,6},{8,9},{9,8},{10,11... | collective-permute-start | bytes 786440 | tf_op jit(solution)/shard_map/ppermute | solution.py:461
  32.7 6.7 %collective-permute-start.13 = (f32[128,256]{1,0:T(8,128)S(1)}, f32[128,256]{1,0:T(8,128)S(1)}, u32[]{:S(2)}, u32[]{:S(2)}) collective-permute-start(f32[128,256]{1,0:T(8,128)S(1)} %shard_map.81.a_ref.unused_ref), channel_id=1, source_target_pairs={{0,8},{1,3},{2,10},{3,1},{4,12},{5,7},{6,14},{7,5},{8,0},{9,11},{1... | collective-permute-start | bytes 393224 | tf_op jit(solution)/shard_map/ppermute | solution.py:458
  35.5 6.4 %collective-permute-start.16 = (f32[128,256]{1,0:T(8,128)S(1)}, f32[128,256]{1,0:T(8,128)S(1)}, u32[]{:S(2)}, u32[]{:S(2)}) collective-permute-start(f32[128,256]{1,0:T(8,128)S(1)} %get-tuple-element.48), channel_id=1, source_target_pairs={{0,4},{1,5},{2,6},{3,7},{4,0},{5,1},{6,2},{7,3},{8,12},{9,13},{10,... | collective-permute-start | bytes 393224 | tf_op jit(solution)/shard_map/ppermute | solution.py:458
  37.1 4.8 %collective-permute-start.17 = (f32[128,256]{1,0:T(8,128)S(1)}, f32[128,256]{1,0:T(8,128)S(1)}, u32[]{:S(2)}, u32[]{:S(2)}) collective-permute-start(f32[128,256]{1,0:T(8,128)S(1)} %get-tuple-element.49), channel_id=1, source_target_pairs={{0,1},{1,0},{2,3},{3,2},{4,8},{5,9},{6,10},{7,11},{8,4},{9,5},{10,... | collective-permute-start | bytes 393224 | tf_op jit(solution)/shard_map/ppermute | solution.py:458
  39.4 5.4 %collective-permute-start.20 = (f32[128,256]{1,0:T(8,128)S(1)}, f32[128,256]{1,0:T(8,128)S(1)}, u32[]{:S(2)}, u32[]{:S(2)}) collective-permute-start(f32[128,256]{1,0:T(8,128)S(1)} %shard_map.82.unused_ref.keep_ref), channel_id=1, source_target_pairs={{0,2},{1,5},{2,0},{3,7},{4,6},{5,1},{6,4},{7,3},{8,10},{9,13},{10,... | collective-permute-start | bytes 393224 | tf_op jit(solution)/shard_map/ppermute | solution.py:458
  42.0 2.8 %collective-permute-start.18 = (f32[128,256]{1,0:T(8,128)S(1)}, f32[128,256]{1,0:T(8,128)S(1)}, u32[]{:S(2)}, u32[]{:S(2)}) collective-permute-start(f32[128,256]{1,0:T(8,128)S(1)} %get-tuple-element.50.upper_ref), channel_id=1, source_target_pairs={{0,1},{1,0},{2,3},{3,2},{4,5},{5,4},{6,7},{7,6},{8,9},{9,8},{10,11... | collective-permute-start | bytes 393224 | tf_op jit(solution)/shard_map/ppermute | solution.py:461
  42.1 2.7 %collective-permute-start.19 = (f32[128,256]{1,0:T(8,128)S(1)}, f32[128,256]{1,0:T(8,128)S(1)}, u32[]{:S(2)}, u32[]{:S(2)}) collective-permute-start(f32[128,256]{1,0:T(8,128)S(1)} %get-tuple-element.51.lower_ref), channel_id=1, source_target_pairs={{0,1},{1,0},{2,3},{3,2},{4,5},{5,4},{6,7},{7,6},{8,9},{9,8},{10,11... | collective-permute-start | bytes 393224 | tf_op jit(solution)/shard_map/ppermute | solution.py:461
  42.6 3.0 %collective-permute-start.21 = (f32[128,256]{1,0:T(8,128)S(1)}, f32[128,256]{1,0:T(8,128)S(1)}, u32[]{:S(2)}, u32[]{:S(2)}) collective-permute-start(f32[128,256]{1,0:T(8,128)S(1)} %shard_map.82.unused_ref.keep_ref), channel_id=1, source_target_pairs={{0,1},{1,0},{2,3},{3,2},{4,5},{5,4},{6,7},{7,6},{8,9},{9,8},{10,11... | collective-permute-start | bytes 393224 | tf_op jit(solution)/shard_map/ppermute | solution.py:461
  44.8 1.3 %collective-permute-start.22 = (f32[128,256]{1,0:T(8,128)S(1)}, f32[128,256]{1,0:T(8,128)S(1)}, u32[]{:S(2)}, u32[]{:S(2)}) collective-permute-start(f32[128,256]{1,0:T(8,128)S(1)} %collective-permute-done.20.away_ref), channel_id=1, source_target_pairs={{0,1},{1,0},{2,3},{3,2},{4,5},{5,4},{6,7},{7,6},{8,9},{9,8},{10,11... | collective-permute-start | bytes 393224 | tf_op jit(solution)/shard_map/ppermute | solution.py:461

commit v12 on v11

--- a/solution.py
+++ b/solution.py
@@ -473,8 +473,8 @@
     recv = [send(block, target) for block, target in zip(blocks, targets)]
 
     waves = jnp.asarray(dft_waves(size))
-    late = (note, probe_wave)
-    note, probe_v, ta_v, tb_v = call(
+    late = (note, specimen, probe_wave)
+    note, specimen_v, probe_v, ta_v, tb_v = call(
         fetch_kernel,
         [jax.ShapeDtypeStruct(a.shape, a.dtype) for a in late]
         + [jax.ShapeDtypeStruct((2 * size, 2 * size), jnp.bfloat16)] * 2,
@@ -600,7 +600,7 @@
         [f32(tile // 2, tile)] * 2,
         [ANY] + [VMEM] * (4 + len(arrived)),
         keep,
-        specimen,
+        specimen_v,
         center,
         light,
         to_core(light),

time: 47.9 us -> 50.2 us (1.048); the launches traced: 47 us -> 49.9 us
  waiting for transfers between devices: 9.52 us -> 16.6 us
  starting transfers between devices: 23.1 us -> 17.8 us
  local copies, waits for them, and re-layouts: 1.77 us -> 2.66 us
    ppermute x12, waiting for transfers between devices: 7.67 us -> 14.8 us  [send(): return lax.ppermute(value, GROUP, permutation(sizes, target))]
    ppermute x12, starting transfers between devices: 19.2 us -> 14.3 us  [send(): return lax.ppermute(value, GROUP, permutation(sizes, target))]
    unnamed x10 -> x12, local copies, waits for them, and re-layouts: 1.77 us -> 2.66 us
  transfers between devices with their start and end apart: 23 -> 23, of which waited for: 7 -> 7; matrix products, arithmetic and copies ran while one was open for 0% -> 0% of each run, Pallas kernels for 12% -> 11%
where the time goes in v12:
time: 50.2 us; the launch traced here: 49.9 us
  starting transfers between devices  17.8 us (35%)
  waiting for transfers between devices  16.6 us (33%)
  Pallas kernels  11.9 us (24%)
  local copies, waits for them, and re-layouts  2.66 us (5%)
  between operations  0.9 us (2%)
    ppermute x12, waiting for transfers between devices, send(): return lax.ppermute(value, GROUP, permutation(sizes, target))  14.8 us
    ppermute x12, starting transfers between devices, send(): return lax.ppermute(value, GROUP, permutation(sizes, target))  14.3 us
    pallas_call x19, Pallas kernels, call(): pl.pallas_call(kernel, out_shape=out_shape, in_specs=specs, out_specs=out...  11.9 us
    ppermute x11, starting transfers between devices, to_core(): return lax.ppermute(value, 'pos', PART_SWAP)  3.51 us
    unnamed x12, local copies, waits for them, and re-layouts  2.66 us
    ppermute x11, waiting for transfers between devices, to_core(): return lax.ppermute(value, 'pos', PART_SWAP)  1.79 us
  transfers between devices with their start and end apart: 23, of which 7 were waited for; matrix products, arithmetic and copies ran while one was open for 0% of the time, Pallas kernels for 11%

profile of v12, /device:TPU:0, one launch (start us, length us, event | category | flops | bytes accessed | tf_op | source)
XLA Modules:
  0.0 49.9 jit_solution(12177708015728358647)
XLA Ops:
  0.6 0.0 copy-start.3
  0.6 2.0 %shard_map.68 = (f32[280,128]{1,0:T(8,128)}, f32[136,256]{1,0:T(8,128)}, f32[136,256]{1,0:T(8,128)}, f32[136,128]{1,0:T(8,128)}, f32[136,128]{1,0:T(8,128)}, /*index=5*/f32[8,128]{1,0:T(8,128)}) custom-call(s32[2,2]{1,0:T(2,128)} %off_hbm.1, f32[2,256,256]{2,1,0:T(8,128)} %spec_ref.5), custom_call_target="tpu_custom_call" | custom-call | tf_op jit(solution)/shard_map/pallas_call | solution.py:432
  2.6 3.0 %collective-permute-start = (f32[280,128]{1,0:T(8,128)}, f32[280,128]{1,0:T(8,128)S(1)}, u32[]{:S(2)}, u32[]{:S(2)}) collective-permute-start(f32[280,128]{1,0:T(8,128)} %get-tuple-element.32), channel_id=1, source_target_pairs={{0,2},{1,3},{2,0},{3,1},{4,6},{5,7},{6,4},{7,5},{8,10},{9,11},{10,... | collective-permute-start | bytes 430088 | tf_op jit(solution)/shard_map/ppermute | solution.py:458
  5.6 1.5 %collective-permute-start.1 = (f32[136,128]{1,0:T(8,128)}, f32[136,128]{1,0:T(8,128)S(1)}, u32[]{:S(2)}, u32[]{:S(2)}) collective-permute-start(f32[136,128]{1,0:T(8,128)} %get-tuple-element.33), channel_id=1, source_target_pairs={{0,6},{1,7},{2,4},{3,5},{4,2},{5,3},{6,0},{7,1},{8,14},{9,15},{10,... | collective-permute-start | bytes 208904 | tf_op jit(solution)/shard_map/ppermute | solution.py:458
  7.2 0.0 collective-permute-start.2
  7.2 4.1 %collective-permute-start.5 = (f32[136,256]{1,0:T(8,128)}, f32[136,256]{1,0:T(8,128)S(1)}, u32[]{:S(2)}, u32[]{:S(2)}) collective-permute-start(f32[136,256]{1,0:T(8,128)} %get-tuple-element.35), channel_id=1, source_target_pairs={{0,4},{1,5},{2,6},{3,7},{4,0},{5,1},{6,2},{7,3},{8,12},{9,13},{10,... | collective-permute-start | bytes 417800 | tf_op jit(solution)/shard_map/ppermute | solution.py:458
  11.3 0.0 collective-permute-start.6
  11.3 0.0 copy-start
  11.3 1.0 %copy-done = f32[2,256,256]{2,1,0:T(8,128)S(1)} copy-done((f32[2,256,256]{2,1,0:T(8,128)S(1)}, f32[2,256,256]{2,1,0:T(8,128)}, u32[]{:S(2)}) %copy-start) | copy-done | bytes 524312
  12.3 1.0 %copy-done.2 = f32[2,256,256]{2,1,0:T(8,128)S(1)} copy-done((f32[2,256,256]{2,1,0:T(8,128)S(1)}, f32[2,256,256]{2,1,0:T(8,128)}, u32[]{:S(2)}) %copy-start.2) | copy-done | bytes 524312
  13.4 0.2 shard_map.69
  13.5 0.0 collective-permute-done.1.refs_2_.refs_0_.refs_3_
  13.5 0.0 collective-permute-done.2.refs_3_.refs_1_.refs_4_
  13.6 0.0 collective-permute-done.refs_1_.refs_2_.refs_0_
  13.6 0.6 %collective-permute-start.4 = (f32[256,128]{1,0:T(8,128)S(1)}, f32[256,128]{1,0:T(8,128)S(1)}, u32[]{:S(2)}, u32[]{:S(2)}) collective-permute-start(f32[256,128]{1,0:T(8,128)S(1)} %shard_map.72), channel_id=1, source_target_pairs={{0,1},{1,0},{2,3},{3,2},{4,5},{5,4},{6,7},{7,6},{8,9},{9,8},{10,11... | collective-permute-start | bytes 393224 | tf_op jit(solution)/shard_map/ppermute | solution.py:461
  14.2 0.1 collective-permute-start.3
  14.3 1.4 %shard_map.71.refs_0_.before_ref = f32[256,256]{1,0:T(8,128)S(1)} custom-call(f32[8,128]{1,0:T(8,128)S(1)} %get-tuple-element.30.note_ref, f32[2,256,256]{2,1,0:T(8,128)S(1)} %get-tuple-element.31.refs_0_.probe_ref, f32[256,128]{1,0:T(8,128)S(1)} %shard_map.70.before_ref.unused_ref.refs_0_, f32[256,128]{1,0:T(8,128)S(1)} %shard_map.70.before_ref.unused_ref.refs_0_, ...), custom_call_target="tpu_custom_call" | custom-call | tf_op jit(solution)/shard_map/pallas_call | solution.py:432
  15.7 0.0 copy-start.1
  15.7 0.0 collective-permute-done.5.refs_3_.refs_1_.refs_0_
  15.7 0.0 collective-permute-done.6.refs_4_.refs_2_.refs_1_
  15.7 0.0 collective-permute-done.4.refs_2_
  15.7 0.0 collective-permute-done.3.refs_1_.refs_0_
  15.8 0.5 collective-permute-start.7
  16.3 0.5 copy-done.1
  16.7 0.8 %shard_map.74.unused_ref.patch_ref = f32[2,256,256]{2,1,0:T(8,128)S(1)} custom-call(f32[8,128]{1,0:T(8,128)S(1)} %get-tuple-element.30.note_ref, f32[512,128]{1,0:T(8,128)S(1)} %shard_map.73.unused_ref, f32[2,256,256]{2,1,0:T(8,128)S(1)} %copy-done.1, f32[280,128]{1,0:T(8,128)S(1)} %collective-permute-done.refs_1_.refs_2_.refs_0_, ...), custom_call_target="tpu_custom_call" | custom-call | tf_op jit(solution)/shard_map/pallas_call | solution.py:432
  17.6 0.0 copy-start.4
  17.6 0.0 collective-permute-done.7.refs_1_
  17.6 0.8 %shard_map.75.patch_other_ref = f32[2,256,256]{2,1,0:T(8,128)S(1)} custom-call(f32[8,128]{1,0:T(8,128)S(1)} %get-tuple-element.30.note_ref, f32[2,256,256]{2,1,0:T(8,128)S(1)} %shard_map.74.unused_ref.patch_ref, f32[2,256,256]{2,1,0:T(8,128)S(1)} %copy-done.1, f32[256,128]{1,0:T(8,128)S(1)} %collective-permute-done.3.refs_1_.refs_0_, ...), custom_call_target="tpu_custom_call" | custom-call | tf_op jit(solution)/shard_map/pallas_call | solution.py:432
  18.4 0.1 copy-done.4
  18.5 2.5 %shard_map.76 = (f32[2,256,256]{2,1,0:T(8,128)S(1)}, f32[2,256,256]{2,1,0:T(8,128)S(1)}, f32[256,256]{1,0:T(8,128)S(1)}, f32[256,256]{1,0:T(8,128)S(1)}) custom-call(f32[2,256,256]{2,1,0:T(8,128)S(1)} %shard_map.74.unused_ref.patch_ref, f32[2,256,256]{2,1,0:T(8,128)S(1)} %shard_map.75.patch_other_ref, ...), custom_call_target="tpu_custom_call" | custom-call | tf_op jit(solution)/shard_map/pallas_call | solution.py:432
  21.1 0.5 collective-permute-start.8
  21.6 0.9 %shard_map.77.unused_light_ref.light_ref = f32[256,256]{1,0:T(8,128)S(1)} custom-call(f32[8,128]{1,0:T(8,128)S(1)} %get-tuple-element.30.note_ref, f32[2,256,256]{2,1,0:T(8,128)S(1)} %get-tuple-element.31.refs_0_.probe_ref, f32[256,256]{1,0:T(8,128)S(1)} %shard_map.71.refs_0_.before_ref, f32[2,256,256]{2,1,0:T(8,128)S(1)} %get-tuple-element.42.unused_ref.own_ref, ...), custom_call_target="tpu_custom_call" | custom-call | tf_op jit(solution)/shard_map/pallas_call | solution.py:432
  22.4 0.3 collective-permute-done.8.recv_ref
  22.8 0.4 collective-permute-start.11
  23.2 0.5 %collective-permute-start.9 = (f32[128,256]{1,0:T(8,128)S(1)}, f32[128,256]{1,0:T(8,128)S(1)}, u32[]{:S(2)}, u32[]{:S(2)}) collective-permute-start(f32[128,256]{1,0:T(8,128)S(1)} %get-tuple-element.44), channel_id=1, source_target_pairs={{0,2},{1,5},{2,0},{3,7},{4,6},{5,1},{6,4},{7,3},{8,10},{9,13},{10,... | collective-permute-start | bytes 393224 | tf_op jit(solution)/shard_map/ppermute | solution.py:458
  23.7 0.2 collective-permute-start.10
  23.9 1.0 %collective-permute-done.10.other_note_ref = f32[8,128]{1,0:T(8,128)S(1)} collective-permute-done((f32[8,128]{1,0:T(8,128)S(1)}, f32[8,128]{1,0:T(8,128)S(1)}, u32[]{:S(2)}, u32[]{:S(2)}) %collective-permute-start.10) | collective-permute-done | bytes 4128 | tf_op jit(solution)/shard_map/ppermute | solution.py:461
  24.9 0.0 collective-permute-done.11.recv_ref
  24.9 1.2 %shard_map.79 = (f32[512,256]{1,0:T(8,128)S(1)}, f32[512,128]{1,0:T(8,128)S(1)}) custom-call(f32[8,128]{1,0:T(8,128)S(1)} %get-tuple-element.30.note_ref, f32[8,128]{1,0:T(8,128)S(1)} %collective-permute-done.10.other_note_ref, f32[2,256,256]{2,1,0:T(8,128)S(1)} %get-tuple-element.42.unused_ref.own_ref, f32[2,256,256]{2,1,0:T(8,128)S(1)} %collective-permute-done.11.recv_ref, ...), custom_call_target="tpu_custom_call" | custom-call | tf_op jit(solution)/shard_map/pallas_call | solution.py:432
  26.1 1.6 %collective-permute-start.14 = (f32[512,128]{1,0:T(8,128)S(1)}, f32[512,128]{1,0:T(8,128)S(1)}, u32[]{:S(2)}, u32[]{:S(2)}) collective-permute-start(f32[512,128]{1,0:T(8,128)S(1)} %get-tuple-element.48), channel_id=1, source_target_pairs={{0,2},{1,3},{2,0},{3,1},{4,6},{5,7},{6,4},{7,5},{8,10},{9,11},{10,... | collective-permute-start | bytes 786440 | tf_op jit(solution)/shard_map/ppermute | solution.py:458
  27.7 0.5 collective-permute-done.9.b_ref
  28.2 0.7 %collective-permute-start.12 = (f32[128,256]{1,0:T(8,128)S(1)}, f32[128,256]{1,0:T(8,128)S(1)}, u32[]{:S(2)}, u32[]{:S(2)}) collective-permute-start(f32[128,256]{1,0:T(8,128)S(1)} %shard_map.80.a_ref), channel_id=1, source_target_pairs={{0,4},{1,9},{2,6},{3,11},{4,0},{5,13},{6,2},{7,15},{8,12},{9,1},{1... | collective-permute-start | bytes 393224 | tf_op jit(solution)/shard_map/ppermute | solution.py:458
  28.9 0.6 %collective-permute-start.15 = (f32[256,256]{1,0:T(8,128)S(1)}, f32[256,256]{1,0:T(8,128)S(1)}, u32[]{:S(2)}, u32[]{:S(2)}) collective-permute-start(f32[256,256]{1,0:T(8,128)S(1)} %shard_map.77.unused_light_ref.light_ref), channel_id=1, source_target_pairs={{0,1},{1,0},{2,3},{3,2},{4,5},{5,4},{6,7},{7,6},{8,9},{9,8},{10,11... | collective-permute-start | bytes 786440 | tf_op jit(solution)/shard_map/ppermute | solution.py:461
  29.5 4.9 %collective-permute-done.12.b_ref = f32[128,256]{1,0:T(8,128)S(1)} collective-permute-done((f32[128,256]{1,0:T(8,128)S(1)}, f32[128,256]{1,0:T(8,128)S(1)}, u32[]{:S(2)}, u32[]{:S(2)}) %collective-permute-start.12) | collective-permute-done | bytes 131104 | tf_op jit(solution)/shard_map/ppermute | solution.py:458
  34.4 0.9 %collective-permute-start.13 = (f32[128,256]{1,0:T(8,128)S(1)}, f32[128,256]{1,0:T(8,128)S(1)}, u32[]{:S(2)}, u32[]{:S(2)}) collective-permute-start(f32[128,256]{1,0:T(8,128)S(1)} %shard_map.81.a_ref.unused_ref), channel_id=1, source_target_pairs={{0,8},{1,3},{2,10},{3,1},{4,12},{5,7},{6,14},{7,5},{8,0},{9,11},{1... | collective-permute-start | bytes 393224 | tf_op jit(solution)/shard_map/ppermute | solution.py:458
  35.3 0.0 collective-permute-done.14.refs_0_
  35.3 0.1 shard_map.83
  35.4 1.9 %collective-permute-start.16 = (f32[128,256]{1,0:T(8,128)S(1)}, f32[128,256]{1,0:T(8,128)S(1)}, u32[]{:S(2)}, u32[]{:S(2)}) collective-permute-start(f32[128,256]{1,0:T(8,128)S(1)} %get-tuple-element.50), channel_id=1, source_target_pairs={{0,4},{1,5},{2,6},{3,7},{4,0},{5,1},{6,2},{7,3},{8,12},{9,13},{10,... | collective-permute-start | bytes 393224 | tf_op jit(solution)/shard_map/ppermute | solution.py:458
  37.3 0.0 collective-permute-start.17
  37.3 5.3 %collective-permute-done.13.b_ref = f32[128,256]{1,0:T(8,128)S(1)} collective-permute-done((f32[128,256]{1,0:T(8,128)S(1)}, f32[128,256]{1,0:T(8,128)S(1)}, u32[]{:S(2)}, u32[]{:S(2)}) %collective-permute-start.13) | collective-permute-done | bytes 131104 | tf_op jit(solution)/shard_map/ppermute | solution.py:458
  42.6 0.1 collective-permute-start.20
  42.7 0.0 collective-permute-done.15.other_light_ref
  42.7 0.0 collective-permute-done.16.edge_a
  42.7 0.0 collective-permute-done.17.edge_b
  42.7 0.1 shard_map.84
  42.9 0.1 collective-permute-start.18
  42.9 0.5 collective-permute-start.19
  43.4 0.1 collective-permute-start.21
  43.5 4.1 %collective-permute-done.20.away_ref = f32[128,256]{1,0:T(8,128)S(1)} collective-permute-done((f32[128,256]{1,0:T(8,128)S(1)}, f32[128,256]{1,0:T(8,128)S(1)}, u32[]{:S(2)}, u32[]{:S(2)}) %collective-permute-start.20) | collective-permute-done | bytes 131104 | tf_op jit(solution)/shard_map/ppermute | solution.py:458
  47.6 0.0 collective-permute-start.22
  47.7 0.0 collective-permute-done.19.other_lower_ref
  47.7 0.8 %shard_map.85 = (f32[2,256,256]{2,1,0:T(8,128)}, f32[8,128]{1,0:T(8,128)S(1)}) custom-call(f32[128,256]{1,0:T(8,128)S(1)} %get-tuple-element.52.upper_ref, f32[128,256]{1,0:T(8,128)S(1)} %get-tuple-element.53.lower_ref, f32[128,256]{1,0:T(8,128)S(1)} %collective-permute-done.18.other_upper_ref, f32[128,256]{1,0:T(8,128)S(1)} %collective-permute-done.19.other_lower_ref), custom_call_target="tpu_custom_call" | custom-call | tf_op jit(solution)/shard_map/pallas_call | solution.py:432
  48.5 0.5 collective-permute-done.22.away_other_ref
  49.0 0.9 %shard_map.86 = f32[2,256,256]{2,1,0:T(8,128)} custom-call(f32[2,256,256]{2,1,0:T(8,128)S(1)} %get-tuple-element.31.refs_0_.probe_ref, f32[128,256]{1,0:T(8,128)S(1)} %shard_map.82.unused_ref.keep_ref, f32[128,256]{1,0:T(8,128)S(1)} %collective-permute-done.20.away_ref, f32[128,256]{1,0:T(8,128)S(1)} %collective-permute-done.21.keep_other_ref, ...), custom_call_target="tpu_custom_call" | custom-call | tf_op jit(solution)/shard_map/pallas_call | solution.py:432
  (13 shorter events, 0.1 us)
Async XLA Ops:
  0.6 10.6 %copy-start.3 = (bf16[3,256,256]{2,1,0:T(8,128)(2,1)S(1)}, bf16[3,256,256]{2,1,0:T(8,128)(2,1)}, u32[]{:S(2)}) copy-start(bf16[3,256,256]{2,1,0:T(8,128)(2,1)} %constant.2.clone.refs_3_) | copy-start | bytes 1179652
  2.6 10.9 %collective-permute-start = (f32[280,128]{1,0:T(8,128)}, f32[280,128]{1,0:T(8,128)S(1)}, u32[]{:S(2)}, u32[]{:S(2)}) collective-permute-start(f32[280,128]{1,0:T(8,128)} %get-tuple-element.32), channel_id=1, source_target_pairs={{0,2},{1,3},{2,0},{3,1},{4,6},{5,7},{6,4},{7,5},{8,10},{9,11},{10,... | collective-permute-start | bytes 430088 | tf_op jit(solution)/shard_map/ppermute | solution.py:458
  5.6 5.6 %copy-start.5 = (f32[8,128]{1,0:T(8,128)S(1)}, f32[8,128]{1,0:T(8,128)}, u32[]{:S(2)}) copy-start(f32[8,128]{1,0:T(8,128)} %get-tuple-element.29.refs_0_) | copy-start | bytes 12292
  5.6 7.9 %collective-permute-start.1 = (f32[136,128]{1,0:T(8,128)}, f32[136,128]{1,0:T(8,128)S(1)}, u32[]{:S(2)}, u32[]{:S(2)}) collective-permute-start(f32[136,128]{1,0:T(8,128)} %get-tuple-element.33), channel_id=1, source_target_pairs={{0,6},{1,7},{2,4},{3,5},{4,2},{5,3},{6,0},{7,1},{8,14},{9,15},{10,... | collective-permute-start | bytes 208904 | tf_op jit(solution)/shard_map/ppermute | solution.py:458
  7.2 6.4 %collective-permute-start.2 = (f32[136,128]{1,0:T(8,128)}, f32[136,128]{1,0:T(8,128)S(1)}, u32[]{:S(2)}, u32[]{:S(2)}) collective-permute-start(f32[136,128]{1,0:T(8,128)} %get-tuple-element.34), channel_id=1, source_target_pairs={{0,1},{1,0},{2,3},{3,2},{4,10},{5,11},{6,8},{7,9},{8,6},{9,7},{10,... | collective-permute-start | bytes 208904 | tf_op jit(solution)/shard_map/ppermute | solution.py:458
  7.2 8.5 %collective-permute-start.5 = (f32[136,256]{1,0:T(8,128)}, f32[136,256]{1,0:T(8,128)S(1)}, u32[]{:S(2)}, u32[]{:S(2)}) collective-permute-start(f32[136,256]{1,0:T(8,128)} %get-tuple-element.35), channel_id=1, source_target_pairs={{0,4},{1,5},{2,6},{3,7},{4,0},{5,1},{6,2},{7,3},{8,12},{9,13},{10,... | collective-permute-start | bytes 417800 | tf_op jit(solution)/shard_map/ppermute | solution.py:458
  11.3 4.5 %collective-permute-start.6 = (f32[136,256]{1,0:T(8,128)}, f32[136,256]{1,0:T(8,128)S(1)}, u32[]{:S(2)}, u32[]{:S(2)}) collective-permute-start(f32[136,256]{1,0:T(8,128)} %get-tuple-element.36), channel_id=1, source_target_pairs={{0,1},{1,0},{2,3},{3,2},{4,8},{5,9},{6,10},{7,11},{8,4},{9,5},{10,... | collective-permute-start | bytes 417800 | tf_op jit(solution)/shard_map/ppermute | solution.py:458
  11.3 1.0 %copy-start = (f32[2,256,256]{2,1,0:T(8,128)S(1)}, f32[2,256,256]{2,1,0:T(8,128)}, u32[]{:S(2)}) copy-start(f32[2,256,256]{2,1,0:T(8,128)} %spec_ref.5) | copy-start | bytes 1572868
  12.3 1.0 %copy-start.2 = (f32[2,256,256]{2,1,0:T(8,128)S(1)}, f32[2,256,256]{2,1,0:T(8,128)}, u32[]{:S(2)}) copy-start(f32[2,256,256]{2,1,0:T(8,128)} %refs_2_.1) | copy-start | bytes 1572868
  13.6 2.1 %collective-permute-start.4 = (f32[256,128]{1,0:T(8,128)S(1)}, f32[256,128]{1,0:T(8,128)S(1)}, u32[]{:S(2)}, u32[]{:S(2)}) collective-permute-start(f32[256,128]{1,0:T(8,128)S(1)} %shard_map.72), channel_id=1, source_target_pairs={{0,1},{1,0},{2,3},{3,2},{4,5},{5,4},{6,7},{7,6},{8,9},{9,8},{10,11... | collective-permute-start | bytes 393224 | tf_op jit(solution)/shard_map/ppermute | solution.py:461
  14.2 1.6 %collective-permute-start.3 = (f32[256,128]{1,0:T(8,128)S(1)}, f32[256,128]{1,0:T(8,128)S(1)}, u32[]{:S(2)}, u32[]{:S(2)}) collective-permute-start(f32[256,128]{1,0:T(8,128)S(1)} %shard_map.70.before_ref.unused_ref.refs_0_), channel_id=1, source_target_pairs={{0,1},{1,0},{2,3},{3,2},{4,5},{5,4},{6,7},{7,6},{8,9},{9,8},{10,11... | collective-permute-start | bytes 393224 | tf_op jit(solution)/shard_map/ppermute | solution.py:461
  15.7 1.0 %copy-start.1 = (f32[2,256,256]{2,1,0:T(8,128)S(1)}, f32[2,256,256]{2,1,0:T(8,128)}, u32[]{:S(2)}) copy-start(f32[2,256,256]{2,1,0:T(8,128)} %spec_ref.5) | copy-start | bytes 1572868
  15.8 1.8 %collective-permute-start.7 = (f32[512,128]{1,0:T(8,128)S(1)}, f32[512,128]{1,0:T(8,128)S(1)}, u32[]{:S(2)}, u32[]{:S(2)}) collective-permute-start(f32[512,128]{1,0:T(8,128)S(1)} %shard_map.73.unused_ref), channel_id=1, source_target_pairs={{0,1},{1,0},{2,3},{3,2},{4,5},{5,4},{6,7},{7,6},{8,9},{9,8},{10,11... | collective-permute-start | bytes 786440 | tf_op jit(solution)/shard_map/ppermute | solution.py:461
  17.6 1.0 %copy-start.4 = (bf16[2,256,256]{2,1,0:T(8,128)(2,1)S(1)}, bf16[2,256,256]{2,1,0:T(8,128)(2,1)}, u32[]{:S(2)}) copy-start(bf16[2,256,256]{2,1,0:T(8,128)(2,1)} %amp_ref.1) | copy-start | bytes 786436
  21.1 1.7 %collective-permute-start.8 = (f32[256,256]{1,0:T(8,128)S(1)}, f32[256,256]{1,0:T(8,128)S(1)}, u32[]{:S(2)}, u32[]{:S(2)}) collective-permute-start(f32[256,256]{1,0:T(8,128)S(1)} %get-tuple-element.40), channel_id=1, source_target_pairs={{0,1},{1,0},{2,3},{3,2},{4,5},{5,4},{6,7},{7,6},{8,9},{9,8},{10,11... | collective-permute-start | bytes 786440 | tf_op jit(solution)/shard_map/ppermute | solution.py:461
  22.8 2.1 %collective-permute-start.11 = (f32[2,256,256]{2,1,0:T(8,128)S(1)}, f32[2,256,256]{2,1,0:T(8,128)S(1)}, u32[]{:S(2)}, u32[]{:S(2)}) collective-permute-start(f32[2,256,256]{2,1,0:T(8,128)S(1)} %get-tuple-element.45), channel_id=1, source_target_pairs={{0,1},{1,0},{2,3},{3,2},{4,5},{5,4},{6,7},{7,6},{8,9},{9,8},{10,11... | collective-permute-start | bytes 1572872 | tf_op jit(solution)/shard_map/ppermute | solution.py:461
  23.2 5.0 %collective-permute-start.9 = (f32[128,256]{1,0:T(8,128)S(1)}, f32[128,256]{1,0:T(8,128)S(1)}, u32[]{:S(2)}, u32[]{:S(2)}) collective-permute-start(f32[128,256]{1,0:T(8,128)S(1)} %get-tuple-element.44), channel_id=1, source_target_pairs={{0,2},{1,5},{2,0},{3,7},{4,6},{5,1},{6,4},{7,3},{8,10},{9,13},{10,... | collective-permute-start | bytes 393224 | tf_op jit(solution)/shard_map/ppermute | solution.py:458
  23.7 1.2 %collective-permute-start.10 = (f32[8,128]{1,0:T(8,128)S(1)}, f32[8,128]{1,0:T(8,128)S(1)}, u32[]{:S(2)}, u32[]{:S(2)}) collective-permute-start(f32[8,128]{1,0:T(8,128)S(1)} %get-tuple-element.30.note_ref), channel_id=1, source_target_pairs={{0,1},{1,0},{2,3},{3,2},{4,5},{5,4},{6,7},{7,6},{8,9},{9,8},{10,11... | collective-permute-start | bytes 12296 | tf_op jit(solution)/shard_map/ppermute | solution.py:461
  26.1 9.2 %collective-permute-start.14 = (f32[512,128]{1,0:T(8,128)S(1)}, f32[512,128]{1,0:T(8,128)S(1)}, u32[]{:S(2)}, u32[]{:S(2)}) collective-permute-start(f32[512,128]{1,0:T(8,128)S(1)} %get-tuple-element.48), channel_id=1, source_target_pairs={{0,2},{1,3},{2,0},{3,1},{4,6},{5,7},{6,4},{7,5},{8,10},{9,11},{10,... | collective-permute-start | bytes 786440 | tf_op jit(solution)/shard_map/ppermute | solution.py:458
  28.2 6.2 %collective-permute-start.12 = (f32[128,256]{1,0:T(8,128)S(1)}, f32[128,256]{1,0:T(8,128)S(1)}, u32[]{:S(2)}, u32[]{:S(2)}) collective-permute-start(f32[128,256]{1,0:T(8,128)S(1)} %shard_map.80.a_ref), channel_id=1, source_target_pairs={{0,4},{1,9},{2,6},{3,11},{4,0},{5,13},{6,2},{7,15},{8,12},{9,1},{1... | collective-permute-start | bytes 393224 | tf_op jit(solution)/shard_map/ppermute | solution.py:458
  28.9 13.8 %collective-permute-start.15 = (f32[256,256]{1,0:T(8,128)S(1)}, f32[256,256]{1,0:T(8,128)S(1)}, u32[]{:S(2)}, u32[]{:S(2)}) collective-permute-start(f32[256,256]{1,0:T(8,128)S(1)} %shard_map.77.unused_light_ref.light_ref), channel_id=1, source_target_pairs={{0,1},{1,0},{2,3},{3,2},{4,5},{5,4},{6,7},{7,6},{8,9},{9,8},{10,11... | collective-permute-start | bytes 786440 | tf_op jit(solution)/shard_map/ppermute | solution.py:461
  34.4 8.2 %collective-permute-start.13 = (f32[128,256]{1,0:T(8,128)S(1)}, f32[128,256]{1,0:T(8,128)S(1)}, u32[]{:S(2)}, u32[]{:S(2)}) collective-permute-start(f32[128,256]{1,0:T(8,128)S(1)} %shard_map.81.a_ref.unused_ref), channel_id=1, source_target_pairs={{0,8},{1,3},{2,10},{3,1},{4,12},{5,7},{6,14},{7,5},{8,0},{9,11},{1... | collective-permute-start | bytes 393224 | tf_op jit(solution)/shard_map/ppermute | solution.py:458
  35.4 7.3 %collective-permute-start.16 = (f32[128,256]{1,0:T(8,128)S(1)}, f32[128,256]{1,0:T(8,128)S(1)}, u32[]{:S(2)}, u32[]{:S(2)}) collective-permute-start(f32[128,256]{1,0:T(8,128)S(1)} %get-tuple-element.50), channel_id=1, source_target_pairs={{0,4},{1,5},{2,6},{3,7},{4,0},{5,1},{6,2},{7,3},{8,12},{9,13},{10,... | collective-permute-start | bytes 393224 | tf_op jit(solution)/shard_map/ppermute | solution.py:458
  37.3 5.4 %collective-permute-start.17 = (f32[128,256]{1,0:T(8,128)S(1)}, f32[128,256]{1,0:T(8,128)S(1)}, u32[]{:S(2)}, u32[]{:S(2)}) collective-permute-start(f32[128,256]{1,0:T(8,128)S(1)} %get-tuple-element.51), channel_id=1, source_target_pairs={{0,1},{1,0},{2,3},{3,2},{4,8},{5,9},{6,10},{7,11},{8,4},{9,5},{10,... | collective-permute-start | bytes 393224 | tf_op jit(solution)/shard_map/ppermute | solution.py:458
  42.6 5.0 %collective-permute-start.20 = (f32[128,256]{1,0:T(8,128)S(1)}, f32[128,256]{1,0:T(8,128)S(1)}, u32[]{:S(2)}, u32[]{:S(2)}) collective-permute-start(f32[128,256]{1,0:T(8,128)S(1)} %shard_map.82.unused_ref.keep_ref), channel_id=1, source_target_pairs={{0,2},{1,5},{2,0},{3,7},{4,6},{5,1},{6,4},{7,3},{8,10},{9,13},{10,... | collective-permute-start | bytes 393224 | tf_op jit(solution)/shard_map/ppermute | solution.py:458
  42.9 4.8 %collective-permute-start.18 = (f32[128,256]{1,0:T(8,128)S(1)}, f32[128,256]{1,0:T(8,128)S(1)}, u32[]{:S(2)}, u32[]{:S(2)}) collective-permute-start(f32[128,256]{1,0:T(8,128)S(1)} %get-tuple-element.52.upper_ref), channel_id=1, source_target_pairs={{0,1},{1,0},{2,3},{3,2},{4,5},{5,4},{6,7},{7,6},{8,9},{9,8},{10,11... | collective-permute-start | bytes 393224 | tf_op jit(solution)/shard_map/ppermute | solution.py:461
  42.9 4.7 %collective-permute-start.19 = (f32[128,256]{1,0:T(8,128)S(1)}, f32[128,256]{1,0:T(8,128)S(1)}, u32[]{:S(2)}, u32[]{:S(2)}) collective-permute-start(f32[128,256]{1,0:T(8,128)S(1)} %get-tuple-element.53.lower_ref), channel_id=1, source_target_pairs={{0,1},{1,0},{2,3},{3,2},{4,5},{5,4},{6,7},{7,6},{8,9},{9,8},{10,11... | collective-permute-start | bytes 393224 | tf_op jit(solution)/shard_map/ppermute | solution.py:461
  43.4 5.1 %collective-permute-start.21 = (f32[128,256]{1,0:T(8,128)S(1)}, f32[128,256]{1,0:T(8,128)S(1)}, u32[]{:S(2)}, u32[]{:S(2)}) collective-permute-start(f32[128,256]{1,0:T(8,128)S(1)} %shard_map.82.unused_ref.keep_ref), channel_id=1, source_target_pairs={{0,1},{1,0},{2,3},{3,2},{4,5},{5,4},{6,7},{7,6},{8,9},{9,8},{10,11... | collective-permute-start | bytes 393224 | tf_op jit(solution)/shard_map/ppermute | solution.py:461
  47.6 1.3 %collective-permute-start.22 = (f32[128,256]{1,0:T(8,128)S(1)}, f32[128,256]{1,0:T(8,128)S(1)}, u32[]{:S(2)}, u32[]{:S(2)}) collective-permute-start(f32[128,256]{1,0:T(8,128)S(1)} %collective-permute-done.20.away_ref), channel_id=1, source_target_pairs={{0,1},{1,0},{2,3},{3,2},{4,5},{5,4},{6,7},{7,6},{8,9},{9,8},{10,11... | collective-permute-start | bytes 393224 | tf_op jit(solution)/shard_map/ppermute | solution.py:461
